TPU v7x, 32 devices: a whole 2x2x4 slice. The times are simulated.
32 devices in a mesh: seq: 4 (over z), dp: 8 (over y, x, core).
Axes of the slice: x: 2, y: 2, z: 4, core: 2. Of those that a mesh axis runs over, the one named last changes fastest.
Arguments:
- tokens: bfloat16 [8, 3072, 512], P('dp', 'seq'), may hold values from -6 to 6
- cotangent: bfloat16 [8, 3072, 512], P('dp', 'seq'), may hold values from -6 to 6
- first_length: int32 [8], P('dp'), may hold values from 384 to 2688, as said below
- ln1_gain: bfloat16 [512], P(('seq', 'dp')), may hold values from 0.099609375 to 1.8984375
- ln2_gain: bfloat16 [512], P(('seq', 'dp')), may hold values from 0.099609375 to 1.8984375
- ln3_gain: bfloat16 [2048], P(('seq', 'dp')), may hold values from 0.099609375 to 1.8984375
- ln4_gain: bfloat16 [512], P(('seq', 'dp')), may hold values from 0.099609375 to 1.8984375
- ln5_gain: bfloat16 [512], P(('seq', 'dp')), may hold values from 0.099609375 to 1.8984375
- glu_weight: bfloat16 [512, 1024], P(('seq', 'dp')), may hold values from -0.25 to 0.25
- wide_weight: bfloat16 [512, 2048], P(('seq', 'dp')), may hold values from -0.25 to 0.25
- narrow_weight: bfloat16 [1536, 256], P(('seq', 'dp')), may hold values from -0.15625 to 0.15625
- depth_weight: bfloat16 [18432], P(('seq', 'dp')), may hold values from -2 to 2
- point_weight: bfloat16 [2048, 256], P(('seq', 'dp')), may hold values from -0.125 to 0.125
- qkv_weight: bfloat16 [512, 1536], P(('seq', 'dp')), may hold values from -0.25 to 0.25
- attn_weight: bfloat16 [512, 512], P(('seq', 'dp')), may hold values from -6 to 6
- up_weight: bfloat16 [512, 2048], P(('seq', 'dp')), may hold values from -0.25 to 0.25
- down_weight: bfloat16 [2048, 512], P(('seq', 'dp')), may hold values from -0.125 to 0.125
Outputs:
- mixed: bfloat16 [8, 3072, 512], P('dp', 'seq')
- tokens_grad: float32 [8, 3072, 512], P('dp', 'seq')
- ln1_grad: float32 [512], P(('seq', 'dp'))
- ln2_grad: float32 [512], P(('seq', 'dp'))
- ln3_grad: float32 [2048], P(('seq', 'dp'))
- ln4_grad: float32 [512], P(('seq', 'dp'))
- ln5_grad: float32 [512], P(('seq', 'dp'))
- glu_grad: float32 [512, 1024], P(('seq', 'dp'))
- wide_grad: float32 [512, 2048], P(('seq', 'dp'))
- narrow_grad: float32 [1536, 256], P(('seq', 'dp'))
- depth_grad: float32 [18432], P(('seq', 'dp'))
- point_grad: float32 [2048, 256], P(('seq', 'dp'))
- qkv_grad: float32 [512, 1536], P(('seq', 'dp'))
- attn_grad: float32 [512, 512], P(('seq', 'dp'))
- up_grad: float32 [512, 2048], P(('seq', 'dp'))
- down_grad: float32 [2048, 512], P(('seq', 'dp'))
Inputs may be any that keep to these rules, and one draw needn't show every extreme that they name: A group's first sequence has first_length tokens and its second the remaining 3072 minus first_length; the shorter of the two has half of 768 to 767 tokens.
All inputs are finite; a program needn't handle non-finite values.
Results may differ from a plain program's by a relative error of at most 0.017.
Values may be sent and summed in bfloat16 or wider, within the bound.
No kernel may reach another device: no remote copies, remote signals or barrier semaphores. Data moves between devices by JAX's collectives and lax.ppermute only.
A program may use at most 256 MiB of HBM per device.

v0:
```python
import jax
import jax.numpy as jnp
from jax import lax
from jax.sharding import PartitionSpec as P

D = 512
HEADS = 8
FF = 2048
KERNEL = 9
HEAD = 64
NARROW = 256


def with_halo(block, sides, width):
    for axis, dim in sides:
        count = lax.axis_size(axis)
        forward = [(i, i + 1) for i in range(count - 1)]
        backward = [(target, source) for source, target in forward]
        low = lax.ppermute(
            lax.slice_in_dim(block, block.shape[dim] - width, None, axis=dim), axis, forward
        )
        high = lax.ppermute(lax.slice_in_dim(block, 0, width, axis=dim), axis, backward)
        block = jnp.concatenate([low, block, high], axis=dim)
    return block


def for_sending(value):
    return jax.tree.map(lambda a: a.astype(jnp.bfloat16) if a.dtype == jnp.float32 else a, value)


def value_rounding(v):
    return lax.optimization_barrier(v.astype(jnp.bfloat16)).astype(jnp.float32)


def value_passing(v):
    return v


def make_rounders():
    rounding = jax.custom_vjp(value_rounding)
    back_rounder = jax.custom_vjp(value_passing)

    def rounding_keep(v):
        return (rounding(v), None)

    def rounding_pass(kept, grad):
        return (grad,)

    def back_keep(v):
        return (v, None)

    def back_apply(kept, grad):
        return (rounding(grad),)

    rounding.defvjp(rounding_keep, rounding_pass)
    back_rounder.defvjp(back_keep, back_apply)
    return (rounding, back_rounder)


def low(v):
    return make_rounders()[0](v)


def low_back(v):
    return make_rounders()[1](v)


def product(left, right):
    return jnp.dot(left, right, preferred_element_type=jnp.float32)


def norm_rows(values, gain):
    row_mean = jnp.mean(values, axis=-1, keepdims=True)
    centred = values - row_mean
    spread = jnp.mean(centred * centred, axis=-1, keepdims=True)
    return centred * lax.rsqrt(spread + 1e-05) * gain


def from_padded(padded, ids_pad, width, offset):
    count = padded.shape[0] - 2 * width
    moved = padded[width + offset : width + offset + count]
    own_ids = ids_pad[width : width + count]
    there_ids = ids_pad[width + offset : width + offset + count]
    return jnp.where((there_ids == own_ids)[:, None], moved, 0.0)


def first_part(inputs, params):
    normed = low(norm_rows(inputs, params[0]))
    joined = low_back(product(normed, params[5]))
    hidden1 = inputs + joined[:, :D] * jax.nn.sigmoid(joined[:, D:])
    return (hidden1, low(norm_rows(hidden1, params[1])))


def second_part(padded, ids_pad, params):
    normed = padded[1:-1]
    left = jax.nn.gelu(low_back(product(normed, params[6])))
    stacked = jnp.concatenate(
        [from_padded(padded, ids_pad, 1, -1), normed, from_padded(padded, ids_pad, 1, 1)], axis=1
    )
    right = jax.nn.gelu(low_back(product(stacked, params[7])))
    joined = left + jnp.pad(right, ((0, 0), (0, FF - NARROW)))
    return low(norm_rows(joined, params[2]))


def third_part(hidden1, padded, ids_pad, params):
    half = KERNEL // 2
    taps = params[8].reshape(KERNEL, FF)
    spread = from_padded(padded, ids_pad, half, -half) * taps[0]
    for offset in range(1, KERNEL):
        spread = spread + from_padded(padded, ids_pad, half, offset - half) * taps[offset]
    branch = low_back(product(low(spread), params[9]))
    hidden2 = hidden1 + jnp.pad(branch, ((0, 0), (0, D - NARROW)))
    qkv = low(low_back(product(low(norm_rows(hidden2, params[3])), params[10])))
    return (hidden2, qkv)


def fourth_part(hidden2, attended, params):
    hidden3 = hidden2 + low_back(product(low(low_back(attended)), params[11]))
    inner = low(jax.nn.gelu(low_back(product(low(norm_rows(hidden3, params[4])), params[12]))))
    return hidden3 + low_back(product(inner, params[13]))


def padded_ids(first_len, width, local_rows):
    places = lax.axis_index("seq") * local_rows + jnp.arange(-width, local_rows + width)
    group_rows = local_rows * lax.axis_size("seq")
    inside = (places >= 0) & (places < group_rows)
    return jnp.where(inside, (places >= first_len).astype(jnp.int32), -1)


def fold_rims(grad_pad, arrived, width):
    core = grad_pad[width:-width]
    upper = core[:width] + arrived[:width]
    lower = core[-width:] + arrived[3 * width :]
    return jnp.concatenate([upper, core[width:-width], lower])


def scores_of(query, keys, query_ids, key_ids):
    scores = jnp.einsum("qhd,khd->hqk", query, keys, preferred_element_type=jnp.float32) * HEAD ** (
        -0.5
    )
    same = (query_ids[:, None] == key_ids[None, :])[None]
    return (scores, same)


def key_blocks_of(keys, values, key_ids):
    total_rows = keys.shape[0]
    block = 512 if total_rows % 512 == 0 else total_rows
    count = total_rows // block
    return (
        keys.reshape(count, block, HEADS, HEAD),
        values.reshape(count, block, HEADS, HEAD),
        key_ids.reshape(count, block),
    )


def attend_forward(query, keys, values, query_ids, key_ids):
    blocks = key_blocks_of(keys, values, key_ids)
    start = jnp.full((HEADS, query.shape[0]), -1e30, jnp.float32)

    def peak_step(carry, item):
        peak, total = carry
        scores, same = scores_of(query, item[0], query_ids, item[2])
        new_peak = jnp.maximum(peak, jnp.max(jnp.where(same, scores, -1e30), axis=-1))
        weights = jnp.where(same, jnp.exp(scores - new_peak[..., None]), 0.0)
        return ((new_peak, total * jnp.exp(peak - new_peak) + jnp.sum(weights, axis=-1)), None)

    (peak, total), unused = lax.scan(peak_step, (start, jnp.zeros_like(start)), blocks)
    log_total = peak + jnp.log(total)

    def value_step(acc, item):
        scores, same = scores_of(query, item[0], query_ids, item[2])
        probs = jnp.where(same, jnp.exp(scores - log_total[..., None]), 0.0).astype(jnp.bfloat16)
        return (
            acc + jnp.einsum("hqk,khd->qhd", probs, item[1], preferred_element_type=jnp.float32),
            None,
        )

    attended, unused = lax.scan(value_step, jnp.zeros(query.shape, jnp.float32), blocks)
    return (attended.reshape(query.shape[0], D), log_total)


def probs_and_grads(query, key_block, value_block, query_ids, key_ids, log_total, grad_out):
    scores, same = scores_of(query, key_block, query_ids, key_ids)
    probs = jnp.where(same, jnp.exp(scores - log_total[..., None]), 0.0)
    grad_probs = jnp.einsum(
        "qhd,khd->hqk", grad_out, value_block, preferred_element_type=jnp.float32
    )
    return (probs, grad_probs)


def inner_of(query, blocks, query_ids, log_total, grad_out):

    def inner_step(acc, item):
        probs, grad_probs = probs_and_grads(
            query, item[0], item[1], query_ids, item[2], log_total, grad_out
        )
        return (acc + jnp.sum(probs * grad_probs, axis=-1), None)

    inner_sum, unused = lax.scan(
        inner_step, jnp.zeros((HEADS, query.shape[0]), jnp.float32), blocks
    )
    return inner_sum


def attend_backward(query, keys, values, query_ids, key_ids, log_total, grad_out):
    blocks = key_blocks_of(keys, values, key_ids)
    scale = HEAD ** (-0.5)
    inner_sum = inner_of(query, blocks, query_ids, log_total, grad_out)

    def grad_step(acc, item):
        probs, grad_probs = probs_and_grads(
            query, item[0], item[1], query_ids, item[2], log_total, grad_out
        )
        grad_scores = (probs * (grad_probs - inner_sum[..., None])).astype(jnp.bfloat16)
        acc = acc + scale * jnp.einsum(
            "hqk,khd->qhd", grad_scores, item[0], preferred_element_type=jnp.float32
        )
        key_grad = scale * jnp.einsum(
            "hqk,qhd->khd", grad_scores, query, preferred_element_type=jnp.float32
        )
        value_grad = jnp.einsum(
            "hqk,qhd->khd", probs.astype(jnp.bfloat16), grad_out, preferred_element_type=jnp.float32
        )
        block_rows = item[0].shape[0]
        return (
            acc,
            jnp.concatenate(
                [key_grad.reshape(block_rows, D), value_grad.reshape(block_rows, D)], axis=1
            ),
        )

    query_grad, pieces = lax.scan(grad_step, jnp.zeros(query.shape, jnp.float32), blocks)
    return (query_grad.reshape(query.shape[0], D), pieces.reshape(keys.shape[0], 2 * D))


def on_device(
    tokens,
    cotangent,
    first_length,
    ln1_gain,
    ln2_gain,
    ln3_gain,
    ln4_gain,
    ln5_gain,
    glu_weight,
    wide_weight,
    narrow_weight,
    depth_weight,
    point_weight,
    qkv_weight,
    attn_weight,
    up_weight,
    down_weight,
):
    inputs = tokens[0].astype(jnp.float32)
    local_rows = inputs.shape[0]
    first_len = first_length[0]
    half = KERNEL // 2
    narrow_ids = padded_ids(first_len, 1, local_rows)
    wide_ids = padded_ids(first_len, half, local_rows)
    own_ids = narrow_ids[1:-1]
    group_rows = local_rows * lax.axis_size("seq")
    key_ids = (jnp.arange(group_rows) >= first_len).astype(jnp.int32)
    gathered = (
        lax.all_gather(ln1_gain, ("seq", "dp"), axis=0, tiled=True),
        lax.all_gather(ln2_gain, ("seq", "dp"), axis=0, tiled=True),
        lax.all_gather(ln3_gain, ("seq", "dp"), axis=0, tiled=True),
        lax.all_gather(ln4_gain, ("seq", "dp"), axis=0, tiled=True),
        lax.all_gather(ln5_gain, ("seq", "dp"), axis=0, tiled=True),
        lax.all_gather(glu_weight, ("seq", "dp"), axis=0, tiled=True),
        lax.all_gather(wide_weight, ("seq", "dp"), axis=0, tiled=True),
        lax.all_gather(narrow_weight, ("seq", "dp"), axis=0, tiled=True),
        lax.all_gather(depth_weight, ("seq", "dp"), axis=0, tiled=True),
        lax.all_gather(point_weight, ("seq", "dp"), axis=0, tiled=True),
        lax.all_gather(qkv_weight, ("seq", "dp"), axis=0, tiled=True),
        lax.all_gather(attn_weight, ("seq", "dp"), axis=0, tiled=True),
        lax.all_gather(up_weight, ("seq", "dp"), axis=0, tiled=True),
        lax.all_gather(down_weight, ("seq", "dp"), axis=0, tiled=True),
    )
    params = tuple((weight.astype(jnp.float32) for weight in gathered))
    hidden1, normed2 = first_part(inputs, params)
    narrow_pad = with_halo(normed2.astype(jnp.bfloat16), (("seq", 0),), 1).astype(jnp.float32)
    middle = second_part(narrow_pad, narrow_ids, params)
    wide_pad = with_halo(middle.astype(jnp.bfloat16), (("seq", 0),), half).astype(jnp.float32)
    hidden2, qkv = third_part(hidden1, wide_pad, wide_ids, params)
    qkv_low = qkv.astype(jnp.bfloat16)
    query = qkv_low[:, :D].reshape(local_rows, HEADS, HEAD)
    keys_all, values_all = (
        lax.all_gather(qkv_low[:, D : 2 * D], "seq", axis=0, tiled=True),
        lax.all_gather(qkv_low[:, 2 * D :], "seq", axis=0, tiled=True),
    )
    attended, log_total = attend_forward(
        query,
        keys_all.reshape(group_rows, HEADS, HEAD),
        values_all.reshape(group_rows, HEADS, HEAD),
        own_ids,
        key_ids,
    )
    output = fourth_part(hidden2, attended, params)
    regathered = (
        lax.all_gather(ln1_gain, ("seq", "dp"), axis=0, tiled=True),
        lax.all_gather(ln2_gain, ("seq", "dp"), axis=0, tiled=True),
        lax.all_gather(ln3_gain, ("seq", "dp"), axis=0, tiled=True),
        lax.all_gather(ln4_gain, ("seq", "dp"), axis=0, tiled=True),
        lax.all_gather(ln5_gain, ("seq", "dp"), axis=0, tiled=True),
        lax.all_gather(glu_weight, ("seq", "dp"), axis=0, tiled=True),
        lax.all_gather(wide_weight, ("seq", "dp"), axis=0, tiled=True),
        lax.all_gather(narrow_weight, ("seq", "dp"), axis=0, tiled=True),
        lax.all_gather(depth_weight, ("seq", "dp"), axis=0, tiled=True),
        lax.all_gather(point_weight, ("seq", "dp"), axis=0, tiled=True),
        lax.all_gather(qkv_weight, ("seq", "dp"), axis=0, tiled=True),
        lax.all_gather(attn_weight, ("seq", "dp"), axis=0, tiled=True),
        lax.all_gather(up_weight, ("seq", "dp"), axis=0, tiled=True),
        lax.all_gather(down_weight, ("seq", "dp"), axis=0, tiled=True),
    )
    params = tuple((weight.astype(jnp.float32) for weight in regathered))
    keys_all, values_all = (
        lax.all_gather(qkv_low[:, D : 2 * D], "seq", axis=0, tiled=True),
        lax.all_gather(qkv_low[:, 2 * D :], "seq", axis=0, tiled=True),
    )
    cot_out = cotangent[0].astype(jnp.float32)
    unused, pull_fourth = jax.vjp(fourth_part, hidden2, attended, params)
    grad_hidden2, grad_attended, grads_fourth = pull_fourth(cot_out)
    grad_low = grad_attended.astype(jnp.bfloat16)
    query_grad, key_terms = attend_backward(
        query,
        keys_all.reshape(group_rows, HEADS, HEAD),
        values_all.reshape(group_rows, HEADS, HEAD),
        own_ids,
        key_ids,
        log_total,
        grad_low.reshape(local_rows, HEADS, HEAD),
    )
    key_grads = lax.psum_scatter(
        key_terms.astype(jnp.bfloat16), "seq", scatter_dimension=0, tiled=True
    ).astype(jnp.float32)
    unused, pull_third = jax.vjp(
        lambda first, padded, weights: third_part(first, padded, wide_ids, weights),
        hidden1,
        wide_pad,
        params,
    )
    grad_hidden1, grad_wide_pad, grads_third = pull_third(
        (grad_hidden2, jnp.concatenate([query_grad, key_grads], axis=1))
    )
    rim_rows = jnp.concatenate([grad_wide_pad[:half], grad_wide_pad[-half:]])
    arrived = with_halo(for_sending(rim_rows), (("seq", 0),), half).astype(rim_rows.dtype)
    grad_middle = fold_rims(grad_wide_pad, arrived, half)
    unused, pull_second = jax.vjp(
        lambda padded, weights: second_part(padded, narrow_ids, weights), narrow_pad, params
    )
    grad_narrow_pad, grads_second = pull_second(grad_middle)
    rim_rows = jnp.concatenate([grad_narrow_pad[:1], grad_narrow_pad[-1:]])
    arrived = with_halo(rim_rows, (("seq", 0),), 1)
    grad_normed2 = fold_rims(grad_narrow_pad, arrived, 1)
    unused, pull_first = jax.vjp(first_part, inputs, params)
    grad_inputs, grads_first = pull_first((grad_hidden1, grad_normed2))
    totals = jax.tree.map(
        lambda a, b, c, e: a + b + c + e, grads_first, grads_second, grads_third, grads_fourth
    )
    summed = (
        lax.psum_scatter(totals[0], ("seq", "dp"), scatter_dimension=0, tiled=True),
        lax.psum_scatter(totals[1], ("seq", "dp"), scatter_dimension=0, tiled=True),
        lax.psum_scatter(totals[2], ("seq", "dp"), scatter_dimension=0, tiled=True),
        lax.psum_scatter(totals[3], ("seq", "dp"), scatter_dimension=0, tiled=True),
        lax.psum_scatter(totals[4], ("seq", "dp"), scatter_dimension=0, tiled=True),
        lax.psum_scatter(totals[5], ("seq", "dp"), scatter_dimension=0, tiled=True),
        lax.psum_scatter(totals[6], ("seq", "dp"), scatter_dimension=0, tiled=True),
        lax.psum_scatter(totals[7], ("seq", "dp"), scatter_dimension=0, tiled=True),
        lax.psum_scatter(totals[8], ("seq", "dp"), scatter_dimension=0, tiled=True),
        lax.psum_scatter(totals[9], ("seq", "dp"), scatter_dimension=0, tiled=True),
        lax.psum_scatter(totals[10], ("seq", "dp"), scatter_dimension=0, tiled=True),
        lax.psum_scatter(totals[11], ("seq", "dp"), scatter_dimension=0, tiled=True),
        lax.psum_scatter(totals[12], ("seq", "dp"), scatter_dimension=0, tiled=True),
        lax.psum_scatter(totals[13], ("seq", "dp"), scatter_dimension=0, tiled=True),
    )
    return (
        output.astype(jnp.bfloat16)[None],
        grad_inputs[None],
        summed[0],
        summed[1],
        summed[2],
        summed[3],
        summed[4],
        summed[5],
        summed[6],
        summed[7],
        summed[8],
        summed[9],
        summed[10],
        summed[11],
        summed[12],
        summed[13],
    )


def solution(mesh):
    in_specs = (
        P("dp", "seq", None),
        P("dp", "seq", None),
        P("dp"),
        P(("seq", "dp")),
        P(("seq", "dp")),
        P(("seq", "dp")),
        P(("seq", "dp")),
        P(("seq", "dp")),
        P(("seq", "dp"), None),
        P(("seq", "dp"), None),
        P(("seq", "dp"), None),
        P(("seq", "dp")),
        P(("seq", "dp"), None),
        P(("seq", "dp"), None),
        P(("seq", "dp"), None),
        P(("seq", "dp"), None),
        P(("seq", "dp"), None),
    )
    out_specs = (
        P("dp", "seq", None),
        P("dp", "seq", None),
        P(("seq", "dp")),
        P(("seq", "dp")),
        P(("seq", "dp")),
        P(("seq", "dp")),
        P(("seq", "dp")),
        P(("seq", "dp"), None),
        P(("seq", "dp"), None),
        P(("seq", "dp"), None),
        P(("seq", "dp")),
        P(("seq", "dp"), None),
        P(("seq", "dp"), None),
        P(("seq", "dp"), None),
        P(("seq", "dp"), None),
        P(("seq", "dp"), None),
    )
    return jax.shard_map(
        on_device, mesh=mesh, in_specs=in_specs, out_specs=out_specs, check_vma=False
    )
```

profile of v0, /device:TPU:0, one launch (start us, length us, event | category | flops | bytes accessed | tf_op | source)
XLA Modules:
  0.0 2013.1 jit_solution(10959599223459754245)
XLA Ops:
  18.8 42.5 %all-reduce.38 = (bf16[512]{0:T(512)(128)(2,1)S(1)}, bf16[2048]{0:T(1024)(128)(2,1)S(1)}, bf16[512]{0:T(512)(128)(2,1)S(1)}, bf16[18432]{0:T(1024)(128)(2,1)S(1)...) all-reduce(bf16[512]{0:T(512)(128)(2,1)S(1)} %dynamic-update-slice,, ...), channel_id=1, replica_groups=mesh['seq'=4,'dp'=8] {'seq','dp'}, use_global_device_ids=true, to_apply=%add.25 | all-reduce | flops 22528 | bytes 90112
  61.5 45.5 %all_gather.68 = bf16[1536,256]{1,0:T(8,128)(2,1)} all-gather(bf16[48,256]{1,0:T(8,128)(2,1)} %param.35), channel_id=1, replica_groups=mesh['seq'=4,'dp'=8] {'seq','dp'}, dimensions={0}, use_global_device_ids=true | all-gather | bytes 811008 | tf_op jit(solution)/shard_map/all_gather | solution.py:272
  126.2 4.5 fusion.111
  148.7 12.5 add_convert_fusion
  161.3 20.3 %all-gather.13.cloned.1.call-done = bf16[2048,256]{1,0:T(8,128)(2,1)} async-done(((bf16[64,256]{1,0:T(8,128)(2,1)}), bf16[2048,256]{1,0:T(8,128)(2,1)}) %all-gather.13.cloned.1.call-update) | async-done | bytes 1048592 | tf_op jit(solution)/shard_map/all_gather | solution.py:274
  185.7 52.5 %all-gather.15.cloned.1.call-done = bf16[512,1536]{1,0:T(8,128)(2,1)} async-done(((bf16[16,1536]{1,0:T(8,128)(2,1)}), bf16[512,1536]{1,0:T(8,128)(2,1)}) %all-gather.15.cloned.1.call-update) | async-done | bytes 1572880 | tf_op jit(solution)/shard_map/all_gather | solution.py:275
  244.7 46.0 %all_gather.76 = bf16[512,512]{1,0:T(8,128)(2,1)} all-gather(bf16[16,512]{1,0:T(8,128)(2,1)S(1)} %copy-done.106), channel_id=1, replica_groups=mesh['seq'=4,'dp'=8] {'seq','dp'}, dimensions={0}, use_global_device_ids=true | all-gather | bytes 540672 | tf_op jit(solution)/shard_map/all_gather | solution.py:276
  291.0 15.7 all-gather.17.cloned.1.call-done
  306.7 8.9 reshape.418
  315.6 7.7 copy.138
  323.3 47.6 %all-gather.19.cloned.1.call-done = bf16[3072,512]{1,0:T(8,128)(2,1)} async-done(((bf16[768,512]{1,0:T(8,128)(2,1)}), bf16[3072,512]{1,0:T(8,128)(2,1)}) %all-gather.19.cloned.1.call-update) | async-done | bytes 3145744 | tf_op jit(solution)/shard_map/all_gather | solution.py:289
  370.9 8.9 reshape.419
  379.7 7.6 copy.139
  387.4 36.8 %while.48 = (s32[]{:T(128)}, f32[8,768]{1,0:T(8,128)S(1)}, f32[8,768]{1,0:T(8,128)S(1)}, s32[768]{0:T(1024)S(1)}, s32[6,512]{1,0:T(8,128)S(1)}, /*index=5*/bf16[...) while((s32[]{:T(128)}, f32[8,768]{1,0:T(8,128)S(1)}, ...), condition=%wide.region_11.12_spmd.clone, body=%wide.region_8.11_spmd.clone.sunk | while | flops 425097216 | bytes 27985016 | solution.py:167
  424.2 50.6 %while.49 = (s32[]{:T(128)}, f32[768,8,64]{0,2,1:T(8,128)}, bf16[6,512,8,64]{1,3,2,0:T(8,128)(2,1)}, s32[768]{0:T(1024)S(1)}, s32[6,512]{1,0:T(8,128)S(1)}, /*in...) while((s32[]{:T(128)}, f32[768,8,64]{0,2,1:T(8,128)}, ...), condition=%wide.region_13.14_spmd.clone, body=%wide.region_12.13_spmd.clone.sunk | while | flops 819068928 | bytes 5802618 | solution.py:178
  424.5 6.1 bitcast_add_fusion.4
  430.8 6.6 bitcast_add_fusion.4
  437.7 6.6 bitcast_add_fusion.4
  444.6 6.6 bitcast_add_fusion.4
  451.5 6.6 bitcast_add_fusion.4
  458.4 6.6 bitcast_add_fusion.4
  479.8 7.2 multiply_convert_fusion
  487.0 7.8 fusion.65
  502.1 50.0 %while.50 = (s32[]{:T(128)}, f32[8,768]{1,0:T(8,128)S(1)}, s32[768]{0:T(1024)S(1)}, s32[6,512]{1,0:T(8,128)S(1)}, bf16[6,512,8,64]{1,3,2,0:T(8,128)(2,1)}, /*ind...) while((s32[]{:T(128)}, f32[8,768]{1,0:T(8,128)S(1)}, ...), condition=%wide.region_20.21_spmd.clone, body=%wide.region_18.20_spmd.clone.sunk | while | flops 821434368 | bytes 28705928 | solution.py:199
  505.3 5.1 fusion.232
  513.7 5.1 fusion.232
  522.0 5.1 fusion.232
  530.3 5.1 fusion.232
  538.7 5.1 fusion.232
  547.0 5.1 fusion.232
  552.1 141.4 %while.51 = (s32[]{:T(128)}, f32[768,8,64]{0,2,1:T(8,128)}, bf16[6,512,1024]{2,1,0:T(8,128)(2,1)}, bf16[6,512,8,64]{1,3,2,0:T(8,128)(2,1)}, s32[768]{0:T(1024)S(...) while((s32[]{:T(128)}, f32[768,8,64]{0,2,1:T(8,128)}, ...), condition=%wide.region_22.23_spmd.clone, body=%wide.region_21.22_spmd.clone.sunk | while | flops 2048917504 | bytes 94061864 | solution.py:232
  556.7 4.5 fusion.245
  561.1 5.3 fusion.244
  580.2 4.5 fusion.245
  584.7 5.3 fusion.244
  603.8 4.5 fusion.245
  608.2 5.3 fusion.244
  627.3 4.5 fusion.245
  631.8 5.3 fusion.244
  650.8 4.5 fusion.245
  655.3 5.3 fusion.244
  674.3 4.5 fusion.245
  678.8 5.3 fusion.244
  695.4 107.9 %reduce-scatter.10.cloned.1.call-done = bf16[768,1024]{1,0:T(8,128)(2,1)} async-done(((bf16[3072,1024]{1,0:T(8,128)(2,1)}), bf16[768,1024]{1,0:T(8,128)(2,1)}) %reduce-scatter.10.cloned.1.call-update) | async-done | bytes 1572880 | tf_op jit(solution)/shard_map/reduce_scatter | solution.py:334
  810.3 36.1 %multiply_reduce_fusion.8 = (f32[2048]{0:T(1024)S(1)}, f32[2048]{0:T(1024)S(1)}, f32[2048]{0:T(1024)S(1)}, f32[2048]{0:T(1024)S(1)}, f32[2048]{0:T(1024)S(1)}, /...) fusion(f32[776,2048]{1,0:T(8,128)} %copy-done, ...), kind=kOutput, calls=%fused_computation.104 | convolution fusion | flops 849328128 | bytes 70735872 | tf_op jit(solution)/shard_map/transpose(jvp())/dot_general | solution.py:69
  850.3 4.9 fusion.134
  856.3 5.7 fusion.135
  862.9 15.5 multiply_select_fusion.7
  878.4 17.7 fusion.114
  906.1 5.9 multiply_reduce_fusion.9
  911.9 5.9 fusion.113
  917.9 4.8 fusion.58
  925.4 5.0 fusion.132
  960.3 5.0 fusion.130
  966.7 5.4 fusion.84
  975.3 40.9 %all-reduce.37 = (f32[512]{0:T(512)S(1)}, f32[512]{0:T(512)S(1)}, f32[2048]{0:T(1024)S(1)}, f32[512]{0:T(512)S(1)}, f32[512]{0:T(512)S(1)}) all-reduce(f32[512]{0:T(512)S(1)} %get-tuple-element.481, f32[512]{0:T(512)S(1)} %get-tuple-element.475, ...), channel_id=3, replica_groups=mesh['seq'=4,'dp'=8] {'seq','dp'}, use_global_device_ids=true, to_apply=%region_33.34.clone | all-reduce | flops 4096 | bytes 32768
  1023.6 82.2 %reduce-scatter.22.cloned.1.call-done = f32[16,512]{1,0:T(8,128)} async-done(((f32[512,512]{1,0:T(8,128)}), f32[16,512]{1,0:T(8,128)}) %reduce-scatter.22.cloned.1.call-update) | async-done | bytes 32784 | tf_op jit(solution)/shard_map/reduce_scatter | solution.py:373
  1105.8 139.8 %reduce-scatter.24.cloned.1.call-done = f32[16,2048]{1,0:T(8,128)} async-done(((f32[512,2048]{1,0:T(8,128)}), f32[16,2048]{1,0:T(8,128)}) %reduce-scatter.24.cloned.1.call-update) | async-done | bytes 131088 | tf_op jit(solution)/shard_map/reduce_scatter | solution.py:374
  1245.6 139.9 %reduce-scatter.26.cloned.1.call-done = f32[64,512]{1,0:T(8,128)} async-done(((f32[2048,512]{1,0:T(8,128)}), f32[64,512]{1,0:T(8,128)}) %reduce-scatter.26.cloned.1.call-update) | async-done | bytes 131088 | tf_op jit(solution)/shard_map/reduce_scatter | solution.py:375
  1385.5 99.5 %reduce-scatter.16.cloned.1.call-done = f32[48,256]{1,0:T(8,128)} async-done(((f32[1536,256]{1,0:T(8,128)}), f32[48,256]{1,0:T(8,128)}) %reduce-scatter.16.cloned.1.call-update) | async-done | bytes 49168 | tf_op jit(solution)/shard_map/reduce_scatter | solution.py:369
  1484.9 107.3 %reduce-scatter.20.cloned.1.call-done = f32[16,1536]{1,0:T(8,128)} async-done(((f32[512,1536]{1,0:T(8,128)}), f32[16,1536]{1,0:T(8,128)}) %reduce-scatter.20.cloned.1.call-update) | async-done | bytes 98320 | tf_op jit(solution)/shard_map/reduce_scatter | solution.py:372
  1592.3 138.5 %reduce-scatter.18.cloned.1.call-done = f32[64,256]{1,0:T(8,128)} async-done(((f32[2048,256]{1,0:T(8,128)}), f32[64,256]{1,0:T(8,128)}) %reduce-scatter.18.cloned.1.call-update) | async-done | bytes 65552 | tf_op jit(solution)/shard_map/reduce_scatter | solution.py:371
  1730.7 135.3 %reduce-scatter.12.cloned.1.call-done = f32[16,1024]{1,0:T(8,128)} async-done(((f32[512,1024]{1,0:T(8,128)}), f32[16,1024]{1,0:T(8,128)}) %reduce-scatter.12.cloned.1.call-update) | async-done | bytes 65552 | tf_op jit(solution)/shard_map/reduce_scatter | solution.py:367
  1866.1 139.8 %reduce-scatter.14.cloned.1.call-done = f32[16,2048]{1,0:T(8,128)} async-done(((f32[512,2048]{1,0:T(8,128)}), f32[16,2048]{1,0:T(8,128)}) %reduce-scatter.14.cloned.1.call-update) | async-done | bytes 131088 | tf_op jit(solution)/shard_map/reduce_scatter | solution.py:368
  (623 shorter events, 277.8 us)
Async XLA Ops:
  7.2 99.8 %copy-start.13 = (bf16[1,768,512]{2,1,0:T(8,128)(2,1)S(1)}, bf16[1,768,512]{2,1,0:T(8,128)(2,1)}, u32[]{:S(2)}) copy-start(bf16[1,768,512]{2,1,0:T(8,128)(2,1)} %param.25) | copy-start | bytes 2359300
  7.2 100.2 %all-gather.9.cloned.1.call-start = ((), (), s32[]{:S(2)}) async-start(), calls=%async_computation.9 | async-start | bytes 1081344 | tf_op jit(solution)/shard_map/all_gather | solution.py:270
  7.9 118.2 %all-gather.11.cloned.1.call-start = ((), (), s32[]{:S(2)}) async-start(), calls=%async_computation.10 | async-start | bytes 2162688 | tf_op jit(solution)/shard_map/all_gather | solution.py:271
  8.7 172.9 %all-gather.13.cloned.1.call-start = ((), (), s32[]{:S(2)}) async-start(), calls=%async_computation.11 | async-start | bytes 1081344 | tf_op jit(solution)/shard_map/all_gather | solution.py:274
  9.4 228.8 %all-gather.15.cloned.1.call-start = ((), (), s32[]{:S(2)}) async-start(), calls=%async_computation.12 | async-start | bytes 1622016 | tf_op jit(solution)/shard_map/all_gather | solution.py:275
  10.0 296.7 %all-gather.17.cloned.1.call-start = ((), (), s32[]{:S(2)}) async-start(), calls=%async_computation.13 | async-start | bytes 3932160 | tf_op jit(solution)/shard_map/all_gather | solution.py:290
  10.8 108.6 %copy-start.107 = (pred[768]{0:T(1024)(128)(4,1)}, pred[768]{0:T(1024)(128)(4,1)S(1)}, u32[]{:S(2)}) copy-start(pred[768]{0:T(1024)(128)(4,1)S(1)} %get-tuple-element.628) | copy-start | bytes 2308
  10.8 108.7 %copy-start.109 = (pred[768]{0:T(1024)(128)(4,1)}, pred[768]{0:T(1024)(128)(4,1)S(1)}, u32[]{:S(2)}) copy-start(pred[768]{0:T(1024)(128)(4,1)S(1)} %get-tuple-element.629) | copy-start | bytes 2308
  12.1 95.3 %copy-start.56 = (f32[768]{0:T(1024)}, f32[768]{0:T(1024)S(1)}, u32[]{:S(2)}) copy-start(f32[768]{0:T(1024)S(1)} %broadcast_multiply_fusion.5) | copy-start | bytes 9220
  13.6 93.8 %copy-start.86 = (f32[768]{0:T(1024)}, f32[768]{0:T(1024)S(1)}, u32[]{:S(2)}) copy-start(f32[768]{0:T(1024)S(1)} %fusion.78) | copy-start | bytes 9220
  13.6 93.8 %copy-start.78 = (f32[768]{0:T(1024)}, f32[768]{0:T(1024)S(1)}, u32[]{:S(2)}) copy-start(f32[768]{0:T(1024)S(1)} %fusion.102) | copy-start | bytes 9220
  61.3 46.1 %copy-start.98 = (f32[512]{0:T(512)}, f32[512]{0:T(512)S(1)}, u32[]{:S(2)}) copy-start(f32[512]{0:T(512)S(1)} %convert_element_type.90) | copy-start | bytes 6148
  61.3 50.8 %copy-start.100 = (f32[512]{0:T(512)}, f32[512]{0:T(512)S(1)}, u32[]{:S(2)}) copy-start(f32[512]{0:T(512)S(1)} %convert_element_type.93) | copy-start | bytes 6148
  61.3 84.7 %copy-start.62 = (f32[2048]{0:T(1024)}, f32[2048]{0:T(1024)S(1)}, u32[]{:S(2)}) copy-start(f32[2048]{0:T(1024)S(1)} %get-tuple-element.612) | copy-start | bytes 24580
  61.4 84.7 %copy-start.64 = (f32[2048]{0:T(1024)}, f32[2048]{0:T(1024)S(1)}, u32[]{:S(2)}) copy-start(f32[2048]{0:T(1024)S(1)} %get-tuple-element.613) | copy-start | bytes 24580
  61.4 84.7 %copy-start.66 = (f32[2048]{0:T(1024)}, f32[2048]{0:T(1024)S(1)}, u32[]{:S(2)}) copy-start(f32[2048]{0:T(1024)S(1)} %get-tuple-element.614) | copy-start | bytes 24580
  61.4 84.7 %copy-start.68 = (f32[2048]{0:T(1024)}, f32[2048]{0:T(1024)S(1)}, u32[]{:S(2)}) copy-start(f32[2048]{0:T(1024)S(1)} %get-tuple-element.615) | copy-start | bytes 24580
  61.4 84.7 %copy-start.70 = (f32[2048]{0:T(1024)}, f32[2048]{0:T(1024)S(1)}, u32[]{:S(2)}) copy-start(f32[2048]{0:T(1024)S(1)} %get-tuple-element.616) | copy-start | bytes 24580
  61.4 84.7 %copy-start.72 = (f32[2048]{0:T(1024)}, f32[2048]{0:T(1024)S(1)}, u32[]{:S(2)}) copy-start(f32[2048]{0:T(1024)S(1)} %get-tuple-element.617) | copy-start | bytes 24580
  61.4 84.7 %copy-start.74 = (f32[2048]{0:T(1024)}, f32[2048]{0:T(1024)S(1)}, u32[]{:S(2)}) copy-start(f32[2048]{0:T(1024)S(1)} %get-tuple-element.618) | copy-start | bytes 24580
  61.4 84.7 %copy-start.76 = (f32[2048]{0:T(1024)}, f32[2048]{0:T(1024)S(1)}, u32[]{:S(2)}) copy-start(f32[2048]{0:T(1024)S(1)} %get-tuple-element.619) | copy-start | bytes 24580
  61.4 84.7 %copy-start.102 = (f32[2048]{0:T(1024)}, f32[2048]{0:T(1024)S(1)}, u32[]{:S(2)}) copy-start(f32[2048]{0:T(1024)S(1)} %get-tuple-element.611) | copy-start | bytes 24580
  111.0 73.7 %copy-start.7 = (f32[768,512]{1,0:T(8,128)}, f32[768,512]{1,0:T(8,128)S(1)}, u32[]{:S(2)}) copy-start(f32[768,512]{1,0:T(8,128)S(1)} %get-tuple-element.581) | copy-start | bytes 4718596
  111.0 9.3 copy-start.58
  112.4 13.7 copy-start.25
  112.4 2.7 collective-permute-start
  113.7 5.5 collective-permute-start.1
  115.1 18.6 copy-start.54
  123.4 10.3 copy-start.23
  137.0 4.2 collective-permute-start.2
  139.5 5.6 collective-permute-start.3
  141.2 44.2 %copy-start.104 = (f32[512]{0:T(512)}, f32[512]{0:T(512)S(1)}, u32[]{:S(2)}) copy-start(f32[512]{0:T(512)S(1)} %convert_element_type.103) | copy-start | bytes 6148
  185.0 291.3 %copy-start.11 = (f32[768,512]{1,0:T(8,128)}, f32[768,512]{1,0:T(8,128)S(1)}, u32[]{:S(2)}) copy-start(f32[768,512]{1,0:T(8,128)S(1)} %get-tuple-element.579) | copy-start | bytes 4718596
  185.0 56.0 %copy-start.82 = (f32[768]{0:T(1024)}, f32[768]{0:T(1024)S(1)}, u32[]{:S(2)}) copy-start(f32[768]{0:T(1024)S(1)} %broadcast_multiply_fusion.3) | copy-start | bytes 9220
  185.3 55.7 %copy-start.92 = (f32[768]{0:T(1024)}, f32[768]{0:T(1024)S(1)}, u32[]{:S(2)}) copy-start(f32[768]{0:T(1024)S(1)} %multiply_reduce_fusion.19) | copy-start | bytes 9220
  185.4 55.7 %copy-start.94 = (f32[768]{0:T(1024)}, f32[768]{0:T(1024)S(1)}, u32[]{:S(2)}) copy-start(f32[768]{0:T(1024)S(1)} %fusion.105) | copy-start | bytes 9220
  185.7 55.4 %copy-start.37 = (bf16[768,512]{1,0:T(8,128)(2,1)}, bf16[768,512]{1,0:T(8,128)(2,1)S(1)}, u32[]{:S(2)}) copy-start(bf16[768,512]{1,0:T(8,128)(2,1)S(1)} %multiply_convert_fusion.3) | copy-start | bytes 2359300
  242.5 128.4 %all-gather.19.cloned.1.call-start = ((), (), s32[]{:S(2)}) async-start(), calls=%async_computation.14 | async-start | bytes 3932160 | tf_op jit(solution)/shard_map/all_gather | solution.py:289
  243.0 236.7 %all-gather.21.cloned.1.call-start = ((), (), s32[]{:S(2)}) async-start(), calls=%async_computation.15 | async-start | bytes 2162688 | tf_op jit(solution)/shard_map/all_gather | solution.py:277
  243.8 243.2 %all-gather.23.cloned.1.call-start = ((), (), s32[]{:S(2)}) async-start(), calls=%async_computation.16 | async-start | bytes 2162688 | tf_op jit(solution)/shard_map/all_gather | solution.py:278
  244.5 558.7 %reduce-scatter.10.cloned.1.call-start = ((), (), s32[]{:S(2)}) async-start(), calls=%async_computation.17 | async-start | bytes 7864320 | tf_op jit(solution)/shard_map/reduce_scatter | solution.py:334
  479.7 7.2 copy-start.35
  479.7 7.2 copy-start.39
  487.0 7.8 copy-start.16
  487.0 7.8 copy-start.129
  693.6 328.6 %all-reduce.41.cloned.1.call-start = ((), (), s32[]{:S(2)}) async-start(), calls=%async_computation.26 | async-start | bytes 147456
  695.1 109.9 %copy-start.12 = (f32[768,512]{1,0:T(8,128)S(1)}, f32[768,512]{1,0:T(8,128)}, u32[]{:S(2)}) copy-start(f32[768,512]{1,0:T(8,128)} %copy-done.11) | copy-start | bytes 4718596
  695.1 109.9 %copy-start.83 = (f32[768]{0:T(1024)S(1)}, f32[768]{0:T(1024)}, u32[]{:S(2)}) copy-start(f32[768]{0:T(1024)} %copy-done.82) | copy-start | bytes 9220
  695.1 109.9 %copy-start.95 = (f32[768]{0:T(1024)S(1)}, f32[768]{0:T(1024)}, u32[]{:S(2)}) copy-start(f32[768]{0:T(1024)} %copy-done.94) | copy-start | bytes 9220
  695.1 109.9 %copy-start.105 = (f32[512]{0:T(512)S(1)}, f32[512]{0:T(512)}, u32[]{:S(2)}) copy-start(f32[512]{0:T(512)} %copy-done.104) | copy-start | bytes 6148
  810.3 36.1 %copy-start.53 = (bf16[768,256]{1,0:T(8,128)(2,1)}, bf16[768,256]{1,0:T(8,128)(2,1)S(1)}, u32[]{:S(2)}) copy-start(bf16[768,256]{1,0:T(8,128)(2,1)S(1)} %pad.289) | copy-start | bytes 1179652
  847.1 258.7 %reduce-scatter.22.cloned.1.call-start = ((), (), s32[]{:S(2)}) async-start(), calls=%async_computation.23 | async-start | bytes 1081344 | tf_op jit(solution)/shard_map/reduce_scatter | solution.py:373
  850.2 395.3 %reduce-scatter.24.cloned.1.call-start = ((), (), s32[]{:S(2)}) async-start(), calls=%async_computation.24 | async-start | bytes 4325376 | tf_op jit(solution)/shard_map/reduce_scatter | solution.py:374
  855.2 530.2 %reduce-scatter.26.cloned.1.call-start = ((), (), s32[]{:S(2)}) async-start(), calls=%async_computation.25 | async-start | bytes 4325376 | tf_op jit(solution)/shard_map/reduce_scatter | solution.py:375
  862.1 622.8 %reduce-scatter.16.cloned.1.call-start = ((), (), s32[]{:S(2)}) async-start(), calls=%async_computation.20 | async-start | bytes 1622016 | tf_op jit(solution)/shard_map/reduce_scatter | solution.py:369
  896.8 5.6 collective-permute-start.4
  900.3 5.6 collective-permute-start.5
  925.3 666.9 %reduce-scatter.20.cloned.1.call-start = ((), (), s32[]{:S(2)}) async-start(), calls=%async_computation.22 | async-start | bytes 3244032 | tf_op jit(solution)/shard_map/reduce_scatter | solution.py:372
  930.5 800.3 %reduce-scatter.18.cloned.1.call-start = ((), (), s32[]{:S(2)}) async-start(), calls=%async_computation.21 | async-start | bytes 2162688 | tf_op jit(solution)/shard_map/reduce_scatter | solution.py:371
  935.0 931.0 %reduce-scatter.12.cloned.1.call-start = ((), (), s32[]{:S(2)}) async-start(), calls=%async_computation.18 | async-start | bytes 2162688 | tf_op jit(solution)/shard_map/reduce_scatter | solution.py:367
  940.5 5.2 collective-permute-start.6
  945.7 5.7 collective-permute-start.7
  960.0 1045.8 %reduce-scatter.14.cloned.1.call-start = ((), (), s32[]{:S(2)}) async-start(), calls=%async_computation.19 | async-start | bytes 4325376 | tf_op jit(solution)/shard_map/reduce_scatter | solution.py:368
  972.2 47.0 %copy-start.21 = (f32[768,512]{1,0:T(8,128)S(1)}, f32[768,512]{1,0:T(8,128)}, u32[]{:S(2)}) copy-start(f32[768,512]{1,0:T(8,128)} %copy-done.20) | copy-start | bytes 4718596
  (121 other events, 341.7 us)
Sparse Core Ops, SparseCore 0:
  10.9 56.6 all-gather.8
  70.5 55.6 all-gather.10
  129.0 52.4 all-gather.12
  184.3 53.8 all-gather.14
  242.6 64.0 all-gather.16
  308.1 62.6 all-gather.18
  373.7 55.0 all-gather.20
  431.6 55.2 all-gather.22
  693.7 109.5 reduce-scatter.9
  847.3 118.9 all-reduce.40
  969.1 136.6 reduce-scatter.21
  1108.6 136.9 reduce-scatter.23
  1248.5 136.8 reduce-scatter.25
  1392.0 92.8 reduce-scatter.15
  1491.7 100.5 reduce-scatter.19
  1595.0 135.6 reduce-scatter.17
  1733.4 132.6 reduce-scatter.11
  1868.9 136.9 reduce-scatter.13
where the time goes:
time: 2030 us; the launch traced here: 2010 us
  waiting for transfers between devices  1250 us (62%)
  matrix products  332 us (16%)
  blocking collectives  175 us (9%)
  other arithmetic  119 us (6%)
  local copies, waits for them, and re-layouts  90.1 us (4%)
    reduce_scatter x1, waiting for transfers between devices, on_device(): lax.psum_scatter(totals[13], ('seq', 'dp'), scatter_dimension=0, tiled=True)  140 us
    reduce_scatter x1, waiting for transfers between devices, on_device(): lax.psum_scatter(totals[12], ('seq', 'dp'), scatter_dimension=0, tiled=True)  140 us
    reduce_scatter x1, waiting for transfers between devices, on_device(): lax.psum_scatter(totals[6], ('seq', 'dp'), scatter_dimension=0, tiled=True)  140 us
    reduce_scatter x1, waiting for transfers between devices, on_device(): lax.psum_scatter(totals[9], ('seq', 'dp'), scatter_dimension=0, tiled=True)  138 us
    reduce_scatter x1, waiting for transfers between devices, on_device(): lax.psum_scatter(totals[5], ('seq', 'dp'), scatter_dimension=0, tiled=True)  135 us
    dot_general x24, matrix products, product(): return jnp.dot(left, right, preferred_element_type=jnp.float32)  115 us
    reduce_scatter x1, waiting for transfers between devices, on_device(): lax.psum_scatter(key_terms.astype(jnp.bfloat16), 'seq', scatter_dimension...  108 us
    reduce_scatter x1, waiting for transfers between devices, on_device(): lax.psum_scatter(totals[10], ('seq', 'dp'), scatter_dimension=0, tiled=True)  107 us
  transfers between devices with their start and end apart: 26, of which 19 were waited for; matrix products, arithmetic and copies ran while one was open for 13% of the time, Pallas kernels for 0%

commit v1 on v0

--- a/solution.py
+++ b/solution.py
@@ -9,6 +9,72 @@
 KERNEL = 9
 HEAD = 64
 NARROW = 256
+
+
+PACK = 256
+
+
+def pack_block(block):
+    rows, columns = block.shape
+    return block.reshape(rows, columns // PACK, PACK).transpose(1, 0, 2).reshape(-1, PACK)
+
+
+def pack_small(blocks):
+    flat = jnp.concatenate(blocks, axis=-1)
+    rows = -(-flat.shape[-1] // (16 * PACK)) * 16
+    pad = [(0, 0)] * (flat.ndim - 1) + [(0, rows * PACK - flat.shape[-1])]
+    return jnp.pad(flat, pad).reshape(flat.shape[:-1] + (rows, PACK))
+
+
+def gather_all(weights):
+    small = [w for w in weights if w.ndim == 1]
+    packed = [pack_block(w) for w in weights if w.ndim == 2] + [pack_small(small)]
+    local = jnp.concatenate(packed, axis=0)
+    whole = lax.all_gather(local, ("seq", "dp"), axis=0, tiled=False)
+    count = whole.shape[0]
+    tail = whole[:, -packed[-1].shape[0] :].reshape(count, -1)
+    result, start, place = [], 0, 0
+    for w in weights:
+        if w.ndim == 1:
+            result.append(tail[:, place : place + w.shape[0]].reshape(-1))
+            place += w.shape[0]
+        else:
+            rows, columns = w.shape
+            chunks = columns // PACK
+            part = whole[:, start : start + rows * chunks].reshape(count, chunks, rows, PACK)
+            result.append(part.transpose(0, 2, 1, 3).reshape(count * rows, columns))
+            start += rows * chunks
+    return result
+
+
+def scatter_all(grads, weights):
+    count = lax.axis_size("seq") * lax.axis_size("dp")
+    packed, small = [], []
+    for grad, w in zip(grads, weights):
+        if w.ndim == 1:
+            small.append(grad.reshape(count, -1))
+        else:
+            rows, columns = w.shape
+            chunks = columns // PACK
+            part = grad.astype(jnp.bfloat16).reshape(count, rows, chunks, PACK)
+            packed.append(part.transpose(0, 2, 1, 3).reshape(count, rows * chunks, PACK))
+    packed.append(pack_small(small).astype(jnp.bfloat16))
+    send = jnp.concatenate(packed, axis=1)
+    total = lax.psum_scatter(send, ("seq", "dp"), scatter_dimension=0, tiled=False)
+    total = total.astype(jnp.float32)
+    tail = total[-packed[-1].shape[1] :].reshape(-1)
+    result, start, place = [], 0, 0
+    for w in weights:
+        if w.ndim == 1:
+            result.append(tail[place : place + w.shape[0]])
+            place += w.shape[0]
+        else:
+            rows, columns = w.shape
+            chunks = columns // PACK
+            part = total[start : start + rows * chunks].reshape(chunks, rows, PACK)
+            result.append(part.transpose(1, 0, 2).reshape(rows, columns))
+            start += rows * chunks
+    return result
 
 
 def with_halo(block, sides, width):
@@ -261,22 +327,23 @@
     own_ids = narrow_ids[1:-1]
     group_rows = local_rows * lax.axis_size("seq")
     key_ids = (jnp.arange(group_rows) >= first_len).astype(jnp.int32)
-    gathered = (
-        lax.all_gather(ln1_gain, ("seq", "dp"), axis=0, tiled=True),
-        lax.all_gather(ln2_gain, ("seq", "dp"), axis=0, tiled=True),
-        lax.all_gather(ln3_gain, ("seq", "dp"), axis=0, tiled=True),
-        lax.all_gather(ln4_gain, ("seq", "dp"), axis=0, tiled=True),
-        lax.all_gather(ln5_gain, ("seq", "dp"), axis=0, tiled=True),
-        lax.all_gather(glu_weight, ("seq", "dp"), axis=0, tiled=True),
-        lax.all_gather(wide_weight, ("seq", "dp"), axis=0, tiled=True),
-        lax.all_gather(narrow_weight, ("seq", "dp"), axis=0, tiled=True),
-        lax.all_gather(depth_weight, ("seq", "dp"), axis=0, tiled=True),
-        lax.all_gather(point_weight, ("seq", "dp"), axis=0, tiled=True),
-        lax.all_gather(qkv_weight, ("seq", "dp"), axis=0, tiled=True),
-        lax.all_gather(attn_weight, ("seq", "dp"), axis=0, tiled=True),
-        lax.all_gather(up_weight, ("seq", "dp"), axis=0, tiled=True),
-        lax.all_gather(down_weight, ("seq", "dp"), axis=0, tiled=True),
-    )
+    weights = (
+        ln1_gain,
+        ln2_gain,
+        ln3_gain,
+        ln4_gain,
+        ln5_gain,
+        glu_weight,
+        wide_weight,
+        narrow_weight,
+        depth_weight,
+        point_weight,
+        qkv_weight,
+        attn_weight,
+        up_weight,
+        down_weight,
+    )
+    gathered = gather_all(weights)
     params = tuple((weight.astype(jnp.float32) for weight in gathered))
     hidden1, normed2 = first_part(inputs, params)
     narrow_pad = with_halo(normed2.astype(jnp.bfloat16), (("seq", 0),), 1).astype(jnp.float32)
@@ -297,27 +364,6 @@
         key_ids,
     )
     output = fourth_part(hidden2, attended, params)
-    regathered = (
-        lax.all_gather(ln1_gain, ("seq", "dp"), axis=0, tiled=True),
-        lax.all_gather(ln2_gain, ("seq", "dp"), axis=0, tiled=True),
-        lax.all_gather(ln3_gain, ("seq", "dp"), axis=0, tiled=True),
-        lax.all_gather(ln4_gain, ("seq", "dp"), axis=0, tiled=True),
-        lax.all_gather(ln5_gain, ("seq", "dp"), axis=0, tiled=True),
-        lax.all_gather(glu_weight, ("seq", "dp"), axis=0, tiled=True),
-        lax.all_gather(wide_weight, ("seq", "dp"), axis=0, tiled=True),
-        lax.all_gather(narrow_weight, ("seq", "dp"), axis=0, tiled=True),
-        lax.all_gather(depth_weight, ("seq", "dp"), axis=0, tiled=True),
-        lax.all_gather(point_weight, ("seq", "dp"), axis=0, tiled=True),
-        lax.all_gather(qkv_weight, ("seq", "dp"), axis=0, tiled=True),
-        lax.all_gather(attn_weight, ("seq", "dp"), axis=0, tiled=True),
-        lax.all_gather(up_weight, ("seq", "dp"), axis=0, tiled=True),
-        lax.all_gather(down_weight, ("seq", "dp"), axis=0, tiled=True),
-    )
-    params = tuple((weight.astype(jnp.float32) for weight in regathered))
-    keys_all, values_all = (
-        lax.all_gather(qkv_low[:, D : 2 * D], "seq", axis=0, tiled=True),
-        lax.all_gather(qkv_low[:, 2 * D :], "seq", axis=0, tiled=True),
-    )
     cot_out = cotangent[0].astype(jnp.float32)
     unused, pull_fourth = jax.vjp(fourth_part, hidden2, attended, params)
     grad_hidden2, grad_attended, grads_fourth = pull_fourth(cot_out)
@@ -358,22 +404,7 @@
     totals = jax.tree.map(
         lambda a, b, c, e: a + b + c + e, grads_first, grads_second, grads_third, grads_fourth
     )
-    summed = (
-        lax.psum_scatter(totals[0], ("seq", "dp"), scatter_dimension=0, tiled=True),
-        lax.psum_scatter(totals[1], ("seq", "dp"), scatter_dimension=0, tiled=True),
-        lax.psum_scatter(totals[2], ("seq", "dp"), scatter_dimension=0, tiled=True),
-        lax.psum_scatter(totals[3], ("seq", "dp"), scatter_dimension=0, tiled=True),
-        lax.psum_scatter(totals[4], ("seq", "dp"), scatter_dimension=0, tiled=True),
-        lax.psum_scatter(totals[5], ("seq", "dp"), scatter_dimension=0, tiled=True),
-        lax.psum_scatter(totals[6], ("seq", "dp"), scatter_dimension=0, tiled=True),
-        lax.psum_scatter(totals[7], ("seq", "dp"), scatter_dimension=0, tiled=True),
-        lax.psum_scatter(totals[8], ("seq", "dp"), scatter_dimension=0, tiled=True),
-        lax.psum_scatter(totals[9], ("seq", "dp"), scatter_dimension=0, tiled=True),
-        lax.psum_scatter(totals[10], ("seq", "dp"), scatter_dimension=0, tiled=True),
-        lax.psum_scatter(totals[11], ("seq", "dp"), scatter_dimension=0, tiled=True),
-        lax.psum_scatter(totals[12], ("seq", "dp"), scatter_dimension=0, tiled=True),
-        lax.psum_scatter(totals[13], ("seq", "dp"), scatter_dimension=0, tiled=True),
-    )
+    summed = scatter_all(totals, weights)
     return (
         output.astype(jnp.bfloat16)[None],
         grad_inputs[None],

time: 2030 us -> 1070 us (0.53)
  waiting for transfers between devices: 1250 us -> 431 us
  blocking collectives: 175 us -> 0 us
  local copies, waits for them, and re-layouts: 90.1 us -> 164 us
  matrix products: 332 us -> 305 us
    reduce_scatter x8 -> x1, waiting for transfers between devices: 982 us -> 150 us  [scatter_all(): lax.psum_scatter(send, ('seq', 'dp'), scatter_dimension=0, tiled=False)]
    all_gather x2 -> x0, blocking collectives: 91.5 us -> none  [the longest x1 46 us: on_device(): lax.all_gather(attn_weight, ('seq', 'dp'), axis=0, tiled=True)]
    unnamed x2 -> x0, blocking collectives: 83.4 us -> none
    all_gather x1, waiting for transfers between devices: 15.7 us -> 51.7 us  [on_device(): lax.all_gather(qkv_low[:, 2 * D:], 'seq', axis=0, tiled=True)]
    dot_general x24, matrix products: 115 us -> 88.2 us  [product(): return jnp.dot(left, right, preferred_element_type=jnp.float32)]
    transpose x0 -> x20, local copies, waits for them, and re-layouts: none -> 20.6 us  [the longest x8 12.9 us: scatter_all(): part.transpose(0, 2, 1, 3).reshape(count, rows * chunks, PACK)]
    all_gather x6 -> x1, waiting for transfers between devices: 75.6 us -> 90.7 us  [gather_all(): whole = lax.all_gather(local, ('seq', 'dp'), axis=0, tiled=False)]
    unnamed x278 -> x306, local copies, waits for them, and re-layouts: 45.2 us -> 59.9 us
  transfers between devices with their start and end apart: 26 -> 13, of which waited for: 19 -> 6; matrix products, arithmetic and copies ran while one was open for 13% -> 7% of each run, Pallas kernels for 0% -> 0%
where the time goes in v1:
time: 1070 us; the launch traced here: 1060 us
  waiting for transfers between devices  431 us (40%)
  matrix products  305 us (29%)
  local copies, waits for them, and re-layouts  164 us (15%)
  other arithmetic  122 us (11%)
  starting transfers between devices  21.9 us (2%)
  between operations  17 us (2%)
    reduce_scatter x1, waiting for transfers between devices, scatter_all(): lax.psum_scatter(send, ('seq', 'dp'), scatter_dimension=0, tiled=False)  150 us
    all_gather x1, waiting for transfers between devices, gather_all(): whole = lax.all_gather(local, ('seq', 'dp'), axis=0, tiled=False)  90.7 us
    reduce_scatter x1, waiting for transfers between devices, on_device(): lax.psum_scatter(key_terms.astype(jnp.bfloat16), 'seq', scatter_dimension...  89.9 us
    dot_general x24, matrix products, product(): return jnp.dot(left, right, preferred_element_type=jnp.float32)  88.2 us
    dot_general x12, matrix products, probs_and_grads(): jnp.einsum('qhd,khd->hqk', grad_out, value_block, preferred_element_type=...  62.5 us
    unnamed x306, local copies, waits for them, and re-layouts  59.9 us
    dot_general x18, matrix products, scores_of(): jnp.einsum('qhd,khd->hqk', query, keys, preferred_element_type=jnp.float32)  54.9 us
    all_gather x1, waiting for transfers between devices, on_device(): lax.all_gather(qkv_low[:, 2 * D:], 'seq', axis=0, tiled=True)  51.7 us
  transfers between devices with their start and end apart: 13, of which 6 were waited for; matrix products, arithmetic and copies ran while one was open for 7% of the time, Pallas kernels for 0%

profile of v1, /device:TPU:0, one launch (start us, length us, event | category | flops | bytes accessed | tf_op | source)
XLA Modules:
  0.0 1063.1 jit_solution(7498495313353826023)
XLA Ops:
  7.2 4.2 concatenate.42
  22.1 90.7 %all-gather.9.cloned.1.call-done = bf16[22528,256]{1,0:T(8,128)(2,1)} async-done(((bf16[704,256]{1,0:T(8,128)(2,1)}), bf16[22528,256]{1,0:T(8,128)(2,1)}) %all-gather.9.cloned.1.call-update) | async-done | bytes 11534352 | tf_op jit(solution)/shard_map/all_gather | solution.py:33
  116.7 5.7 fusion.124
  146.3 3.2 multiply_convert_fusion.1
  151.2 4.6 collective-permute-start.2
  162.5 12.6 %add_convert_fusion = bf16[768,2048]{1,0:T(8,128)(2,1)S(1)} fusion(f32[776,2048]{1,0:T(8,128)S(1)} %maximum_convert_fusion, f32[2048]{0:T(1024)S(1)} %get-tuple-element.578, f32[2048]{0:T(1024)S(1)} %get-tuple-element.579, f32[2048]{0:T(1024)S(1)} %get-tuple-element.580, f32[2048]{0:T(1024)S(1)} %get-tuple-element.581, f32[2048]{0:T(1024)S(1)} %get-tuple-element.582, ...), kind=kLoop, calls=%fused_computation.121 | loop fusion | flops 40894464 | bytes 59848704 | tf_op jit(solution)/shard_map/convert_element_type | solution.py:98
  191.7 51.7 %all-gather.5.cloned.1.call-done = bf16[3072,512]{1,0:T(8,128)(2,1)} async-done(((bf16[768,512]{1,0:T(8,128)(2,1)}), bf16[3072,512]{1,0:T(8,128)(2,1)}) %all-gather.5.cloned.1.call-update) | async-done | bytes 3145744 | tf_op jit(solution)/shard_map/all_gather | solution.py:357
  243.4 9.3 reshape.705
  252.7 7.7 copy.142
  260.4 46.7 %all-gather.7.cloned.1.call-done = bf16[3072,512]{1,0:T(8,128)(2,1)} async-done(((bf16[768,512]{1,0:T(8,128)(2,1)}), bf16[3072,512]{1,0:T(8,128)(2,1)}) %all-gather.7.cloned.1.call-update) | async-done | bytes 3145744 | tf_op jit(solution)/shard_map/all_gather | solution.py:356
  307.2 8.9 reshape.706
  316.1 7.6 copy.143
  323.7 36.8 %while.48 = (s32[]{:T(128)}, f32[8,768]{1,0:T(8,128)S(1)}, f32[8,768]{1,0:T(8,128)S(1)}, s32[768]{0:T(1024)S(1)}, s32[6,512]{1,0:T(8,128)S(1)}, /*index=5*/bf16[...) while((s32[]{:T(128)}, f32[8,768]{1,0:T(8,128)S(1)}, ...), condition=%wide.region_11.12_spmd.clone, body=%wide.region_8.11_spmd.clone.sunk | while | flops 425097216 | bytes 27985016 | solution.py:233
  336.2 3.1 fusion.221
  360.5 40.9 %while.49 = (s32[]{:T(128)}, f32[768,8,64]{0,2,1:T(8,128)}, bf16[6,512,8,64]{1,3,2,0:T(8,128)(2,1)}, s32[768]{0:T(1024)S(1)}, s32[6,512]{1,0:T(8,128)S(1)}, /*in...) while((s32[]{:T(128)}, f32[768,8,64]{0,2,1:T(8,128)}, ...), condition=%wide.region_13.14_spmd.clone, body=%wide.region_12.13_spmd.clone.sunk | while | flops 819068928 | bytes 5802618 | solution.py:244
  360.8 6.0 bitcast_add_fusion.4
  367.1 6.6 bitcast_add_fusion.4
  374.0 6.6 bitcast_add_fusion.4
  380.9 6.6 bitcast_add_fusion.4
  387.7 6.6 bitcast_add_fusion.4
  394.6 6.6 bitcast_add_fusion.4
  405.6 4.3 multiply_convert_fusion
  409.9 5.3 fusion.65
  422.5 49.9 %while.50 = (s32[]{:T(128)}, f32[8,768]{1,0:T(8,128)S(1)}, s32[768]{0:T(1024)S(1)}, s32[6,512]{1,0:T(8,128)S(1)}, bf16[6,512,8,64]{1,3,2,0:T(8,128)(2,1)}, /*ind...) while((s32[]{:T(128)}, f32[8,768]{1,0:T(8,128)S(1)}, ...), condition=%wide.region_20.21_spmd.clone, body=%wide.region_18.20_spmd.clone.sunk | while | flops 821434368 | bytes 28705928 | solution.py:265
  425.7 5.1 fusion.233
  434.0 5.1 fusion.233
  442.4 5.1 fusion.233
  450.7 5.1 fusion.233
  459.0 5.1 fusion.233
  467.4 5.1 fusion.233
  472.5 142.2 %while.51 = (s32[]{:T(128)}, f32[768,8,64]{0,2,1:T(8,128)}, bf16[6,512,1024]{2,1,0:T(8,128)(2,1)}, bf16[6,512,8,64]{1,3,2,0:T(8,128)(2,1)}, s32[768]{0:T(1024)S(...) while((s32[]{:T(128)}, f32[768,8,64]{0,2,1:T(8,128)}, ...), condition=%wide.region_22.23_spmd.clone, body=%wide.region_21.22_spmd.clone.sunk | while | flops 2048917504 | bytes 94061864 | solution.py:298
  477.3 4.5 fusion.246
  481.8 5.3 fusion.245
  487.1 3.3 convolution_multiply_fusion.2
  500.9 4.5 fusion.246
  505.5 5.3 fusion.245
  510.8 3.3 convolution_multiply_fusion.2
  524.5 4.5 fusion.246
  529.1 5.3 fusion.245
  534.4 3.3 convolution_multiply_fusion.2
  548.2 4.5 fusion.246
  552.7 5.3 fusion.245
  558.0 3.3 convolution_multiply_fusion.2
  571.8 4.5 fusion.246
  576.3 5.3 fusion.245
  581.6 3.3 convolution_multiply_fusion.2
  595.4 4.5 fusion.246
  599.9 5.3 fusion.245
  605.3 3.3 convolution_multiply_fusion.2
  623.5 3.2 convolution_convert_fusion.1
  634.3 89.9 %reduce-scatter.3.cloned.1.call-done = bf16[768,1024]{1,0:T(8,128)(2,1)} async-done(((bf16[3072,1024]{1,0:T(8,128)(2,1)}), bf16[768,1024]{1,0:T(8,128)(2,1)}) %reduce-scatter.3.cloned.1.call-update) | async-done | bytes 1572880 | tf_op jit(solution)/shard_map/reduce_scatter | solution.py:380
  736.6 36.1 %multiply_reduce_fusion.8 = (f32[2048]{0:T(1024)S(1)}, f32[2048]{0:T(1024)S(1)}, f32[2048]{0:T(1024)S(1)}, f32[2048]{0:T(1024)S(1)}, f32[2048]{0:T(1024)S(1)}, /...) fusion(f32[776,2048]{1,0:T(8,128)} %copy-done, ...), kind=kOutput, calls=%fused_computation.109 | convolution fusion | flops 849328128 | bytes 70735872 | tf_op jit(solution)/shard_map/transpose(jvp())/dot_general | solution.py:135
  772.8 15.4 %multiply_select_fusion.7 = (f32[768,2048]{1,0:T(8,128)S(1)}, f32[768,2048]{1,0:T(8,128)S(1)}, f32[768,2048]{1,0:T(8,128)}, f32[768,2048]{1,0:T(8,128)}, f32[768...) fusion(f32[768,2048]{1,0:T(8,128)} %get-tuple-element.610, ...), kind=kLoop, calls=%fused_computation.119 | loop fusion | flops 23592960 | bytes 56694016 | tf_op jit(solution)/shard_map/transpose(jvp(jit(_where)))/select_n | solution.py:150
  788.3 18.9 %fusion.118 = (bf16[776,2048]{1,0:T(8,128)(2,1)S(1)}, f32[776,2048]{1,0:T(8,128)}) fusion(f32[768,2048]{1,0:T(8,128)} %get-tuple-element.545, f32[768,2048]{1,0:T(8,128)S(1)} %get-tuple-element.547, f32[768,2048]{1,0:T(8,128)} %get-tuple-element.548, f32[768,2048]{1,0:T(8,128)} %get-tuple-element.549, f32[768,2048]{1,0:T(8,128)} %get-tuple-element.550, ...), kind=kLoop, calls=%fused_computation.303 | loop fusion | flops 14303232 | bytes 66158592 | tf_op jit(solution)/shard_map/convert.22
  807.2 3.4 collective-permute-start.4
  812.1 3.3 reshape.660
  817.3 3.3 slice.479
  822.1 5.9 multiply_reduce_fusion.9
  828.0 5.9 fusion.117
  834.0 4.8 fusion.58
  847.1 4.6 collective-permute-start.6
  856.4 3.7 copy.161
  888.1 5.3 fusion.88
  895.2 149.8 %reduce-scatter.5.cloned.1.call-done = bf16[1,704,256]{2,1,0:T(8,128)(2,1)} async-done(((bf16[32,704,256]{2,1,0:T(8,128)(2,1)}), bf16[1,704,256]{2,1,0:T(8,128)(2,1)}) %reduce-scatter.5.cloned.1.call-update) | async-done | bytes 360464 | tf_op jit(solution)/shard_map/reduce_scatter | solution.py:63
  (672 shorter events, 277.0 us)
Async XLA Ops:
  7.2 13.7 %copy-start.13 = (bf16[1,768,512]{2,1,0:T(8,128)(2,1)S(1)}, bf16[1,768,512]{2,1,0:T(8,128)(2,1)}, u32[]{:S(2)}) copy-start(bf16[1,768,512]{2,1,0:T(8,128)(2,1)} %param.25) | copy-start | bytes 2359300
  7.2 105.7 %all-gather.9.cloned.1.call-start = ((), (), s32[]{:S(2)}) async-start(), calls=%async_computation.6 | async-start | bytes 11894784 | tf_op jit(solution)/shard_map/all_gather | solution.py:33
  18.8 224.6 %all-gather.5.cloned.1.call-start = ((), (), s32[]{:S(2)}) async-start(), calls=%async_computation.2 | async-start | bytes 3932160 | tf_op jit(solution)/shard_map/all_gather | solution.py:357
  20.9 101.7 %copy-start.82 = (f32[768]{0:T(1024)}, f32[768]{0:T(1024)S(1)}, u32[]{:S(2)}) copy-start(f32[768]{0:T(1024)S(1)} %broadcast_multiply_fusion.5) | copy-start | bytes 9220
  21.3 92.6 %copy-start.112 = (f32[768]{0:T(1024)}, f32[768]{0:T(1024)S(1)}, u32[]{:S(2)}) copy-start(f32[768]{0:T(1024)S(1)} %fusion.82) | copy-start | bytes 9220
  21.4 116.1 %copy-start.132 = (pred[768]{0:T(1024)(128)(4,1)}, pred[768]{0:T(1024)(128)(4,1)S(1)}, u32[]{:S(2)}) copy-start(pred[768]{0:T(1024)(128)(4,1)S(1)} %get-tuple-element.598) | copy-start | bytes 2308
  21.4 116.1 %copy-start.134 = (pred[768]{0:T(1024)(128)(4,1)}, pred[768]{0:T(1024)(128)(4,1)S(1)}, u32[]{:S(2)}) copy-start(pred[768]{0:T(1024)(128)(4,1)S(1)} %get-tuple-element.599) | copy-start | bytes 2308
  21.4 101.2 %copy-start.104 = (f32[768]{0:T(1024)}, f32[768]{0:T(1024)S(1)}, u32[]{:S(2)}) copy-start(f32[768]{0:T(1024)S(1)} %fusion.106) | copy-start | bytes 9220
  126.3 49.9 %copy-start.7 = (f32[768,512]{1,0:T(8,128)}, f32[768,512]{1,0:T(8,128)S(1)}, u32[]{:S(2)}) copy-start(f32[768,512]{1,0:T(8,128)S(1)} %get-tuple-element.535) | copy-start | bytes 4718596
  126.3 6.2 copy-start.84
  127.3 6.4 copy-start.106
  127.6 12.5 %copy-start.35 = (bf16[768,512]{1,0:T(8,128)(2,1)}, bf16[768,512]{1,0:T(8,128)(2,1)S(1)}, u32[]{:S(2)}) copy-start(bf16[768,512]{1,0:T(8,128)(2,1)S(1)} %multiply_convert_fusion.4) | copy-start | bytes 2359300
  127.7 9.6 collective-permute-start
  130.7 6.6 collective-permute-start.1
  133.9 12.4 %copy-start.80 = (f32[2048]{0:T(1024)}, f32[2048]{0:T(1024)S(1)}, u32[]{:S(2)}) copy-start(f32[2048]{0:T(1024)S(1)} %reshape.698) | copy-start | bytes 24580
  140.2 6.1 copy-start.26
  151.2 9.0 collective-permute-start.2
  155.8 5.6 collective-permute-start.3
  157.3 5.1 copy-start.88
  157.3 5.1 copy-start.90
  157.3 5.1 copy-start.92
  157.3 5.1 copy-start.94
  157.3 5.1 copy-start.96
  157.4 5.1 copy-start.98
  157.4 5.1 copy-start.100
  157.4 5.1 copy-start.102
  157.4 5.1 copy-start.128
  159.0 18.1 %copy-start.130 = (f32[512]{0:T(512)}, f32[512]{0:T(512)S(1)}, u32[]{:S(2)}) copy-start(f32[512]{0:T(512)S(1)} %reshape.700) | copy-start | bytes 6148
  160.3 17.2 %copy-start.65 = (bf16[64,8,6,256]{3,1,2,0:T(8,128)(2,1)}, bf16[64,8,6,256]{3,1,2,0:T(8,128)(2,1)S(1)}, u32[]{:S(2)}) copy-start(bf16[64,8,6,256]{3,1,2,0:T(8,128)(2,1)S(1)} %copy.258) | copy-start | bytes 4718596
  162.4 12.8 %copy-start = (f32[776,2048]{1,0:T(8,128)}, f32[776,2048]{1,0:T(8,128)S(1)}, u32[]{:S(2)}) copy-start(f32[776,2048]{1,0:T(8,128)S(1)} %maximum_convert_fusion) | copy-start | bytes 19070980
  162.5 12.7 %copy-start.68 = (bf16[32,64,256]{2,1,0:T(8,128)(2,1)S(1)}, bf16[32,64,256]{2,1,0:T(8,128)(2,1)}, u32[]{:S(2)}) copy-start(bf16[32,64,256]{2,1,0:T(8,128)(2,1)} %get-tuple-element.541) | copy-start | bytes 3145732
  176.8 226.1 %copy-start.11 = (f32[768,512]{1,0:T(8,128)}, f32[768,512]{1,0:T(8,128)S(1)}, u32[]{:S(2)}) copy-start(f32[768,512]{1,0:T(8,128)S(1)} %get-tuple-element.533) | copy-start | bytes 4718596
  180.4 126.8 %all-gather.7.cloned.1.call-start = ((), (), s32[]{:S(2)}) async-start(), calls=%async_computation.3 | async-start | bytes 3932160 | tf_op jit(solution)/shard_map/all_gather | solution.py:356
  181.2 543.1 %reduce-scatter.3.cloned.1.call-start = ((), (), s32[]{:S(2)}) async-start(), calls=%async_computation.4 | async-start | bytes 7864320 | tf_op jit(solution)/shard_map/reduce_scatter | solution.py:380
  404.9 13.0 %copy-start.15 = (f32[768,512]{1,0:T(8,128)}, f32[768,512]{1,0:T(8,128)S(1)}, u32[]{:S(2)}) copy-start(f32[768,512]{1,0:T(8,128)S(1)} %get-tuple-element.605) | copy-start | bytes 4718596
  614.7 430.3 %reduce-scatter.5.cloned.1.call-start = ((), (), s32[]{:S(2)}) async-start(), calls=%async_computation.5 | async-start | bytes 11894784 | tf_op jit(solution)/shard_map/reduce_scatter | solution.py:63
  634.0 91.9 %copy-start.12 = (f32[768,512]{1,0:T(8,128)S(1)}, f32[768,512]{1,0:T(8,128)}, u32[]{:S(2)}) copy-start(f32[768,512]{1,0:T(8,128)} %copy-done.11) | copy-start | bytes 4718596
  634.0 91.9 %copy-start.109 = (f32[768]{0:T(1024)S(1)}, f32[768]{0:T(1024)}, u32[]{:S(2)}) copy-start(f32[768]{0:T(1024)} %copy-done.108) | copy-start | bytes 9220
  634.0 91.9 %copy-start.121 = (f32[768]{0:T(1024)S(1)}, f32[768]{0:T(1024)}, u32[]{:S(2)}) copy-start(f32[768]{0:T(1024)} %copy-done.120) | copy-start | bytes 9220
  634.0 91.9 %copy-start.131 = (f32[512]{0:T(512)S(1)}, f32[512]{0:T(512)}, u32[]{:S(2)}) copy-start(f32[512]{0:T(512)} %copy-done.130) | copy-start | bytes 6148
  736.6 36.2 %copy-start.89 = (f32[2048]{0:T(1024)S(1)}, f32[2048]{0:T(1024)}, u32[]{:S(2)}) copy-start(f32[2048]{0:T(1024)} %copy-done.88) | copy-start | bytes 24580
  736.6 36.2 %copy-start.91 = (f32[2048]{0:T(1024)S(1)}, f32[2048]{0:T(1024)}, u32[]{:S(2)}) copy-start(f32[2048]{0:T(1024)} %copy-done.90) | copy-start | bytes 24580
  736.6 36.2 %copy-start.93 = (f32[2048]{0:T(1024)S(1)}, f32[2048]{0:T(1024)}, u32[]{:S(2)}) copy-start(f32[2048]{0:T(1024)} %copy-done.92) | copy-start | bytes 24580
  736.6 36.2 %copy-start.95 = (f32[2048]{0:T(1024)S(1)}, f32[2048]{0:T(1024)}, u32[]{:S(2)}) copy-start(f32[2048]{0:T(1024)} %copy-done.94) | copy-start | bytes 24580
  736.6 36.2 %copy-start.97 = (f32[2048]{0:T(1024)S(1)}, f32[2048]{0:T(1024)}, u32[]{:S(2)}) copy-start(f32[2048]{0:T(1024)} %copy-done.96) | copy-start | bytes 24580
  736.6 36.2 %copy-start.99 = (f32[2048]{0:T(1024)S(1)}, f32[2048]{0:T(1024)}, u32[]{:S(2)}) copy-start(f32[2048]{0:T(1024)} %copy-done.98) | copy-start | bytes 24580
  736.6 36.2 %copy-start.101 = (f32[2048]{0:T(1024)S(1)}, f32[2048]{0:T(1024)}, u32[]{:S(2)}) copy-start(f32[2048]{0:T(1024)} %copy-done.100) | copy-start | bytes 24580
  736.6 36.2 %copy-start.103 = (f32[2048]{0:T(1024)S(1)}, f32[2048]{0:T(1024)}, u32[]{:S(2)}) copy-start(f32[2048]{0:T(1024)} %copy-done.102) | copy-start | bytes 24580
  807.2 13.4 %collective-permute-start.4 = (bf16[4,2048]{1,0:T(4,128)(2,1)S(1)}, bf16[4,2048]{1,0:T(4,128)(2,1)S(1)}, u32[]{:S(2)}, u32[]{:S(2)}) collective-permute-start(bf16[4,2048]{1,0:T(4,128)(2,1)S(1)} %get-tuple-element.558), channel_id=1, source_target_pairs={{0,8},{8,16},{16,24},{1,9},{9,17},{17,25},{2,10},{10,18},{18,26},{... | collective-permute-start | bytes 49160 | tf_op jit(solution)/shard_map/ppermute | solution.py:85
  810.6 10.0 collective-permute-start.5
  817.2 4.8 slice-start
  817.2 4.8 slice-start.1
  817.2 4.8 copy-start.27
  817.2 4.8 copy-start.81
  822.1 5.9 copy-start.117
  833.9 4.8 copy-start.71
  833.9 5.4 copy-start.74
  834.0 5.4 copy-start.76
  834.0 5.4 copy-start.78
  846.1 8.5 copy-start.17
  847.1 6.0 collective-permute-start.6
  853.1 7.3 collective-permute-start.7
  888.1 5.4 copy-start.22
  888.1 5.4 copy-start.40
  (114 other events, 278.9 us)
Sparse Core Ops, SparseCore 0:
  19.0 93.8 all-gather.8
  180.5 62.8 all-gather.4
  245.0 62.1 all-gather.6
  614.8 109.3 reduce-scatter.2
  886.9 158.0 reduce-scatter.4

commit v2 on v1

v2 whole, which is shorter than its diff:
```python
import functools
import math

import jax
import jax.numpy as jnp
import numpy as np
from jax import lax
from jax.experimental import pallas as pl
from jax.experimental.pallas import tpu as pltpu
from jax.sharding import PartitionSpec as P

D = 512
HEADS = 8
FF = 2048
KERNEL = 9
HEAD = 64
NARROW = 256
HALF = KERNEL // 2
LANES = 128
PACK = 256
RIM = 16
BLOCKS = 32
F32 = jnp.float32
BF = jnp.bfloat16
LOG2E = math.log2(math.e)
BIG = -1e30
AXES = ("seq", "dp")
VMEM = 58 << 20


def nt(a, b):
    return lax.dot_general(a, b, (((1,), (1,)), ((), ())), preferred_element_type=F32)


def nn(a, b):
    return lax.dot_general(a, b, (((1,), (0,)), ((), ())), preferred_element_type=F32)


def tn(a, b):
    return lax.dot_general(a, b, (((0,), (0,)), ((), ())), preferred_element_type=F32)


def whole_call(kernel, outs, args, scratch=(), scalars=1, flops=0):
    vm = pl.BlockSpec(memory_space=pltpu.VMEM)
    sm = pl.BlockSpec(memory_space=pltpu.SMEM)
    outs = [jax.ShapeDtypeStruct(shape, dtype) for shape, dtype in outs]
    moved = sum(math.prod(a.shape) * a.dtype.itemsize for a in list(args) + outs)
    return pl.pallas_call(
        kernel,
        out_shape=outs,
        in_specs=[sm] * scalars + [vm] * (len(args) - scalars),
        out_specs=[vm] * len(outs),
        scratch_shapes=[pltpu.VMEM(shape, dtype) for shape, dtype in scratch],
        compiler_params=pltpu.CompilerParams(vmem_limit_bytes=VMEM),
        cost_estimate=pl.CostEstimate(flops=flops, bytes_accessed=moved, transcendentals=0),
    )(*args)


def normalise(v):
    mean = jnp.mean(v, axis=1, keepdims=True)
    c = v - mean
    r = lax.rsqrt(jnp.mean(c * c, axis=1, keepdims=True) + 1e-05)
    return c * r, r


def norm_back(grad, hat, r, gain):
    g = grad * gain
    a = jnp.mean(g, axis=1, keepdims=True)
    b = jnp.mean(g * hat, axis=1, keepdims=True)
    return r * (g - a - hat * b)


C0 = math.sqrt(2.0 / math.pi)
C1 = 0.044715


def gelu(x):
    return 0.5 * x * (1.0 + jnp.tanh(x * (C0 + C0 * C1 * (x * x))))


def gelu_and_slope(x):
    xx = x * x
    t = jnp.tanh(x * (C0 + C0 * C1 * xx))
    half = 0.5 * (1.0 + t)
    return x * half, half + (0.5 * x) * (1.0 - t * t) * (C0 + 3.0 * C0 * C1 * xx)


def sigmoid(x):
    return 0.5 * jnp.tanh(0.5 * x) + 0.5


def fold8(v):
    return jnp.sum(v.reshape(v.shape[0] // 8, 8, v.shape[1]), axis=0)


def rows_at(i, tile, start=0):
    return pl.ds(pl.multiple_of(start + i * tile, 16), tile)


def places(base, rows, lanes=LANES):
    return base + lax.broadcasted_iota(jnp.int32, (rows, lanes), 0)


def blocks_of(value):
    return value.astype(BF).reshape(BLOCKS, value.shape[0] // BLOCKS, value.shape[1])


def front1_kernel(tile, x_ref, g1, glu, g2, h1_ref, y2_ref, joined_ref):
    def step(i, carry):
        at = rows_at(i, tile)
        x = x_ref[at, :].astype(F32)
        hat, _ = normalise(x)
        joined = nn((hat * g1[...]).astype(BF), glu[...])
        joined_ref[at, :] = joined
        h1 = x + joined[:, :D] * sigmoid(joined[:, D:])
        h1_ref[at, :] = h1
        hat2, _ = normalise(h1)
        y2_ref[at, :] = (hat2 * g2[...]).astype(BF)
        return carry

    lax.fori_loop(0, x_ref.shape[0] // tile, step, 0)


def front1(x, g1, glu, g2):
    rows = x.shape[0]
    return whole_call(
        functools.partial(front1_kernel, 160),
        [((rows, D), F32), ((rows, D), BF), ((rows, 2 * D), F32)],
        [x, g1, glu, g2],
        scalars=0,
        flops=4 * rows * D * D,
    )


def front2_kernel(tile, group, scal, y2_ref, wide, narrow, g3, left_ref, right_ref, mid_ref, u_ref):
    rows = y2_ref.shape[0]
    base = scal[0] * (rows - 2 * RIM) - RIM
    first = scal[1]
    u_ref[0:RIM, :] = jnp.zeros((RIM, 3 * NARROW), F32)
    u_ref[RIM + rows : 2 * RIM + rows, :] = jnp.zeros((RIM, 3 * NARROW), F32)

    def narrow_step(i, carry):
        y = y2_ref[rows_at(i, tile), :]
        for k in range(3):
            u_ref[rows_at(i, tile, RIM), k * NARROW : (k + 1) * NARROW] = nn(
                y, narrow[k * D : (k + 1) * D, :]
            )
        return carry

    lax.fori_loop(0, rows // tile, narrow_step, 0)

    def step(i, carry):
        at = rows_at(i, tile)
        around = pl.ds(pl.multiple_of(i * tile, 16), tile + 2 * RIM)
        left = nn(y2_ref[at, :], wide[...])
        left_ref[at, :] = left
        pos = places(base + i * tile, tile, NARROW)
        before = pltpu.roll(u_ref[around, 0:NARROW], 1, 0)[RIM : RIM + tile]
        after = pltpu.roll(u_ref[around, 2 * NARROW :], tile + 2 * RIM - 1, 0)[RIM : RIM + tile]
        right = u_ref[rows_at(i, tile, RIM), NARROW : 2 * NARROW]
        right = right + jnp.where((pos == first) | (pos == 0), 0.0, before)
        right = right + jnp.where((pos + 1 == first) | (pos + 1 == group), 0.0, after)
        right_ref[at, :] = right
        left = gelu(left)
        joined = jnp.concatenate([left[:, :NARROW] + gelu(right), left[:, NARROW:]], axis=1)
        hat, _ = normalise(joined)
        row = base + i * tile + lax.broadcasted_iota(jnp.int32, (tile, 1), 0)
        inside = ((row >= 0) & (row < group)).astype(F32)
        mid_ref[at, :] = (hat * inside * g3[...]).astype(BF)
        return carry

    lax.fori_loop(0, rows // tile, step, 0)


def front2(scal, y2, wide, narrow, g3, group):
    rows = y2.shape[0]
    return whole_call(
        functools.partial(front2_kernel, 160, group),
        [((rows, FF), F32), ((rows, NARROW), F32), ((rows, FF), BF)],
        [scal, y2, wide, narrow, g3],
        scratch=[((rows + 2 * RIM, 3 * NARROW), F32)],
        flops=2 * rows * D * (FF + 3 * NARROW),
    )


def crosses(pos, offset, first):
    if offset > 0:
        return (pos < first) & (pos + offset >= first)
    return (pos >= first) & (pos + offset < first)


def conv(win, tile, taps, lanes, pos, first, masked, sign):
    total = None
    for k in range(KERNEL):
        o = sign * (k - HALF)
        v = win[RIM + o : RIM + o + tile, :]
        if masked and o != 0:
            v = jnp.where(crosses(pos, o, first), 0.0, v)
        v = v * taps[k : k + 1, lanes]
        total = v if total is None else total + v
    return total


def front3_kernel(tile, n, share, scal, mid_ref, taps, point, h1_ref, g4, qkv_w, *refs):
    spread_ref, h2_ref, y4_ref = refs[:3]
    outs = refs[3 : 3 + n]
    win, qkv_s = refs[3 + n :]
    rows = h2_ref.shape[0]
    s, first = scal[0], scal[1]
    base = s * rows

    def step(i, carry):
        at = rows_at(i, tile)
        begin = base + i * tile
        near = (first > begin - HALF) & (first < begin + tile + HALF)

        def chunk(c, carry2):
            lanes = pl.ds(pl.multiple_of(c * LANES, LANES), LANES)
            around = pl.ds(pl.multiple_of(i * tile, 16), tile + 2 * RIM)
            win[...] = mid_ref[around, lanes].astype(F32)
            pos = places(begin, tile)
            for masked in (False, True):

                @pl.when(near if masked else jnp.logical_not(near))
                def _():
                    spread_ref[at, lanes] = conv(
                        win, tile, taps, lanes, pos, first, masked, 1
                    ).astype(BF)

            return carry2

        lax.fori_loop(0, FF // LANES, chunk, 0)
        h1 = h1_ref[rows_at(i, tile, RIM), :]
        branch = nn(spread_ref[at, :], point[...])
        h2 = jnp.concatenate([h1[:, :NARROW] + branch, h1[:, NARROW:]], axis=1)
        h2_ref[at, :] = h2
        hat, _ = normalise(h2)
        y4 = (hat * g4[...]).astype(BF)
        y4_ref[at, :] = y4
        qkv_s[...] = nn(y4, qkv_w[...]).astype(BF)
        for k in range(n):
            block = (s ^ k) // share
            for part in range(3):
                outs[k][at, part * LANES : (part + 1) * LANES] = qkv_s[
                    :, pl.ds(pl.multiple_of(part * D + block * LANES, LANES), LANES)
                ]
        return carry

    lax.fori_loop(0, rows // tile, step, 0)


def front3(scal, mid, taps, point, h1, g4, qkv_w, n, share):
    rows = mid.shape[0] - 2 * RIM
    tile = 128
    return whole_call(
        functools.partial(front3_kernel, tile, n, share),
        [((rows, FF), BF), ((rows, D), F32), ((rows, D), BF)] + [((rows, 3 * LANES), BF)] * n,
        [scal, mid, taps, point, h1, g4, qkv_w],
        scratch=[((tile + 2 * RIM, LANES), F32), ((tile, 3 * D), BF)],
        flops=2 * rows * (FF * NARROW + 3 * D * D),
    )


def middle_kernel(tile, n, share, scal, h2_ref, *refs):
    att = refs[:n]
    cot_ref, g5, wa, wup, wdown, mixed_ref, dh3_ref = refs[n : n + 7]
    datt = refs[n + 7 : 2 * n + 7]
    ga_ref, gup_ref, gdown_ref, ln_ref = refs[2 * n + 7 : 2 * n + 11]
    att_s, y5_s, inner_s, du_s, db_s = refs[2 * n + 11 :]
    rows = h2_ref.shape[0]
    s = scal[0]
    for k in range(n):
        block = (s ^ k) // share
        lanes = pl.ds(pl.multiple_of(block * LANES, LANES), LANES)
        if share == 1:
            att_s[:, lanes] = att[k][...]
        else:
            seen = (s ^ k) % share
            before = att_s[:, lanes].astype(F32)
            lane = lax.broadcasted_iota(jnp.int32, (rows, LANES), 1)
            mine = lane // (LANES // share) == seen
            att_s[:, lanes] = jnp.where(mine, att[k][...].astype(F32), before).astype(BF)
    ln_ref[...] = jnp.zeros_like(ln_ref)

    def step(i, carry):
        at = rows_at(i, tile)
        h3 = h2_ref[at, :] + nn(att_s[at, :], wa[...])
        hat, r = normalise(h3)
        y5 = (hat * g5[...]).astype(BF)
        y5_s[at, :] = y5
        value, slope = gelu_and_slope(nn(y5, wup[...]))
        inner = value.astype(BF)
        inner_s[at, :] = inner
        mixed_ref[at, :] = (h3 + nn(inner, wdown[...])).astype(BF)
        cot = cot_ref[at, :]
        du = (nt(cot, wdown[...]) * slope).astype(BF)
        du_s[at, :] = du
        dy5 = nt(du, wup[...])
        ln_ref[...] += fold8(dy5 * hat)
        dh3 = cot.astype(F32) + norm_back(dy5, hat, r, g5[...])
        dh3_ref[at, :] = dh3
        db = dh3.astype(BF)
        db_s[at, :] = db
        da = nt(db, wa[...]).astype(BF)
        for j in range(D // LANES):
            for k in range(n):

                @pl.when((s ^ k) // share == j)
                def _():
                    datt[k][at, :] = da[:, j * LANES : (j + 1) * LANES]

        return carry

    lax.fori_loop(0, rows // tile, step, 0)
    att_t = att_s[...].T
    for j in range(D // PACK):
        ga_ref[:, j * 16 : (j + 1) * 16, :] = blocks_of(
            nn(att_t, db_s[:, j * PACK : (j + 1) * PACK])
        )
    y5_t = y5_s[...].T
    for j in range(FF // PACK):
        cols = slice(j * PACK, (j + 1) * PACK)
        gup_ref[:, j * 16 : (j + 1) * 16, :] = blocks_of(nn(y5_t, du_s[:, cols]))
        down = tn(inner_s[:, cols], cot_ref[...]).astype(BF)
        for m in range(D // PACK):
            gdown_ref[j * 4 : (j + 1) * 4, m * 64 : (m + 1) * 64, :] = down[
                :, m * PACK : (m + 1) * PACK
            ].reshape(4, 64, PACK)


def middle(scal, h2, att, cot, g5, wa, wup, wdown, n, share):
    rows = h2.shape[0]
    return whole_call(
        functools.partial(middle_kernel, 128, n, share),
        [((rows, D), BF), ((rows, D), F32)]
        + [((rows, LANES), BF)] * n
        + [((BLOCKS, 32, PACK), BF), ((BLOCKS, 128, PACK), BF), ((BLOCKS, 128, PACK), BF)]
        + [((8, D), F32)],
        [scal, h2, *att, cot, g5, wa, wup, wdown],
        scratch=[
            ((rows, D), BF),
            ((rows, D), BF),
            ((rows, FF), BF),
            ((rows, FF), BF),
            ((rows, D), BF),
        ],
        flops=6 * rows * (2 * D * FF + D * D),
    )


def back3_kernel(tile, n, share, scal, *refs):
    blocks = refs[:n]
    dh3_ref, h2_ref, y4_ref, spread_ref, g4, qkv_w = refs[n : n + 6]
    dh2_ref, db_ref, gqkv_ref, gpoint_ref, ln_ref = refs[n + 6 : n + 11]
    (dqkv_s,) = refs[n + 11 :]
    rows = h2_ref.shape[0]
    s = scal[0]
    for k in range(n):
        block = (s ^ k) // share
        for part in range(3):
            lanes = pl.ds(pl.multiple_of(part * D + block * LANES, LANES), LANES)
            new = blocks[k][:, part * LANES : (part + 1) * LANES]
            if share > 1:
                lane = lax.broadcasted_iota(jnp.int32, (rows, LANES), 1)
                mine = lane // (LANES // share) == (s ^ k) % share
                new = jnp.where(mine, new.astype(F32), dqkv_s[:, lanes].astype(F32)).astype(BF)
            dqkv_s[:, lanes] = new
    ln_ref[...] = jnp.zeros_like(ln_ref)

    def step(i, carry):
        at = rows_at(i, tile)
        dy4 = nt(dqkv_s[at, :], qkv_w[...])
        hat, r = normalise(h2_ref[at, :])
        ln_ref[...] += fold8(dy4 * hat)
        dh2 = dh3_ref[at, :] + norm_back(dy4, hat, r, g4[...])
        dh2_ref[at, :] = dh2
        db_ref[at, :] = dh2[:, :NARROW].astype(BF)
        return carry

    lax.fori_loop(0, rows // tile, step, 0)
    y4_t = y4_ref[...].T
    for j in range(3 * D // PACK):
        gqkv_ref[:, j * 16 : (j + 1) * 16, :] = blocks_of(
            nn(y4_t, dqkv_s[:, j * PACK : (j + 1) * PACK])
        )
    for j in range(FF // PACK):
        gpoint_ref[j * PACK : (j + 1) * PACK, :] = tn(
            spread_ref[:, j * PACK : (j + 1) * PACK], db_ref[...]
        ).astype(BF)


def back3(scal, blocks, dh3, h2, y4, spread, g4, qkv_w, n, share):
    rows = h2.shape[0]
    return whole_call(
        functools.partial(back3_kernel, 128, n, share),
        [((rows, D), F32), ((rows, NARROW), BF), ((BLOCKS, 96, PACK), BF)]
        + [((FF, PACK), BF), ((8, D), F32)],
        [scal, *blocks, dh3, h2, y4, spread, g4, qkv_w],
        scratch=[((rows, 3 * D), BF)],
        flops=4 * rows * D * 3 * D + 2 * rows * FF * NARROW,
    )


def back2_kernel(tile, group, scal, low_ref, db_ref, high_ref, *refs):
    point, taps, mid_ref, left_ref, right_ref, wide, narrow, y2_ref, g3 = refs[:9]
    dy2_ref, gwide_ref, gnarrow_ref, gdepth_ref, ln_ref = refs[9:14]
    dbx, dsp, win, dmid, dl, dr, st = refs[14:]
    rows = db_ref.shape[0]
    ext = rows + 2 * RIM
    base = scal[0] * rows - RIM
    first = scal[1]
    dbx[0:RIM, :] = low_ref[...]
    dbx[RIM : RIM + rows, :] = db_ref[...]
    dbx[RIM + rows :, :] = high_ref[...]
    dsp[0:RIM, :] = jnp.zeros((RIM, FF), F32)
    dsp[RIM + ext :, :] = jnp.zeros((RIM, FF), F32)
    dr[0:RIM, :] = jnp.zeros((RIM, NARROW), F32)
    dr[RIM + ext :, :] = jnp.zeros((RIM, NARROW), F32)
    gdepth_ref[...] = jnp.zeros_like(gdepth_ref)
    ln_ref[...] = jnp.zeros_like(ln_ref)

    def spread_step(i, carry):
        dsp[rows_at(i, tile, RIM), :] = nt(dbx[rows_at(i, tile), :], point[...])
        return carry

    lax.fori_loop(0, ext // tile, spread_step, 0)

    def step(i, carry):
        at = rows_at(i, tile)
        begin = base + i * tile
        near = (first > begin - HALF) & (first < begin + tile + HALF)
        near = near | (i == 0) | (i == ext // tile - 1)

        def chunk(c, carry2):
            lanes = pl.ds(pl.multiple_of(c * LANES, LANES), LANES)
            around = pl.ds(pl.multiple_of(i * tile, 16), tile + 2 * RIM)
            win[...] = dsp[around, lanes]
            local = i * tile + lax.broadcasted_iota(jnp.int32, (tile, LANES), 0)
            mid = mid_ref[at, lanes].astype(F32)
            pos = places(begin, tile)
            for masked in (False, True):

                @pl.when(near if masked else jnp.logical_not(near))
                def _():
                    total = None
                    for k in range(KERNEL):
                        o = HALF - k
                        v = win[RIM + o : RIM + o + tile, :]
                        if masked and o != 0:
                            v = jnp.where(crosses(pos, o, first), 0.0, v)
                        counted = v
                        if masked:
                            kept = (local + o >= RIM) & (local + o < RIM + rows)
                            counted = jnp.where(kept, v, 0.0)
                        gdepth_ref[k * 8 : (k + 1) * 8, lanes] += fold8(counted * mid)
                        v = v * taps[k : k + 1, lanes]
                        total = v if total is None else total + v
                    dmid[:, lanes] = total

            return carry2

        lax.fori_loop(0, FF // LANES, chunk, 0)
        left, slope = gelu_and_slope(left_ref[at, :])
        right, slope_r = gelu_and_slope(right_ref[at, :])
        joined = jnp.concatenate([left[:, :NARROW] + right, left[:, NARROW:]], axis=1)
        hat, r = normalise(joined)
        local = i * tile + lax.broadcasted_iota(jnp.int32, (tile, 1), 0)
        own = ((local >= RIM) & (local < RIM + rows)).astype(F32)
        pos = base + local
        grad = dmid[...] * ((pos >= 0) & (pos < group)).astype(F32)
        ln_ref[...] += fold8(grad * hat * own)
        dj = norm_back(grad, hat, r, g3[...])
        dl[at, :] = (dj * slope).astype(BF)
        dr[rows_at(i, tile, RIM), :] = (dj[:, :NARROW] * slope_r).astype(BF).astype(F32)
        return carry

    lax.fori_loop(0, ext // tile, step, 0)
    part = 128

    def gather_step(i, carry):
        at = rows_at(i, part)
        around = pl.ds(pl.multiple_of(RIM + i * part, 16), part + 2 * RIM)
        pos = places(base + RIM + i * part, part, NARROW)
        v = dr[around, :]
        after = pltpu.roll(v, part + 2 * RIM - 1, 0)[RIM : RIM + part]
        before = pltpu.roll(v, 1, 0)[RIM : RIM + part]
        after = jnp.where((pos + 1 == first) | (pos + 1 == group), 0.0, after).astype(BF)
        before = jnp.where((pos == first) | (pos == 0), 0.0, before).astype(BF)
        here = v[RIM : RIM + part].astype(BF)
        st[at, 0:NARROW] = after
        st[at, NARROW : 2 * NARROW] = here
        st[at, 2 * NARROW :] = before
        dy2 = nt(dl[rows_at(i, part, RIM), :], wide[...])
        for k, v in enumerate((after, here, before)):
            dy2 = dy2 + nt(v, narrow[k * D : (k + 1) * D, :])
        dy2_ref[at, :] = dy2
        return carry

    lax.fori_loop(0, rows // part, gather_step, 0)
    y2_t = y2_ref[RIM : RIM + rows, :].T
    for j in range(FF // PACK):
        gwide_ref[:, j * 16 : (j + 1) * 16, :] = blocks_of(
            nn(y2_t, dl[RIM : RIM + rows, j * PACK : (j + 1) * PACK])
        )
    for k in range(3):
        gnarrow_ref[k * D : (k + 1) * D, :] = nn(
            y2_t, st[:, k * NARROW : (k + 1) * NARROW]
        ).astype(BF)


def back2(scal, low, db, high, point, taps, mid, left, right, wide, narrow, y2, g3, group):
    rows = db.shape[0]
    ext = rows + 2 * RIM
    tile = 160
    return whole_call(
        functools.partial(back2_kernel, tile, group),
        [((rows, D), F32), ((BLOCKS, 128, PACK), BF), ((3 * D, NARROW), BF)]
        + [((8 * KERNEL, FF), F32), ((8, FF), F32)],
        [scal, low, db, high, point, taps, mid, left, right, wide, narrow, y2, g3],
        scratch=[
            ((ext, NARROW), BF),
            ((ext + 2 * RIM, FF), F32),
            ((tile + 2 * RIM, LANES), F32),
            ((tile, FF), F32),
            ((ext, FF), BF),
            ((ext + 2 * RIM, NARROW), F32),
            ((rows, 3 * NARROW), BF),
        ],
        flops=2 * rows * (FF * NARROW + 2 * FF * D + 6 * D * NARROW),
    )


def back1_kernel(tile, dy2_ref, dh2_ref, h1_ref, joined_ref, x_ref, g1, g2, glu, *refs):
    dx_ref, gglu_ref, ln1_ref, ln2_ref, y1_s, dj_s = refs
    rows = dy2_ref.shape[0]
    ln1_ref[...] = jnp.zeros_like(ln1_ref)
    ln2_ref[...] = jnp.zeros_like(ln2_ref)

    def step(i, carry):
        at = rows_at(i, tile)
        ext = rows_at(i, tile, RIM)
        hat2, r2 = normalise(h1_ref[ext, :])
        dy2 = dy2_ref[at, :]
        ln2_ref[...] += fold8(dy2 * hat2)
        dh1 = dh2_ref[at, :] + norm_back(dy2, hat2, r2, g2[...])
        gate = sigmoid(joined_ref[ext, D:])
        value = joined_ref[ext, :D]
        da = (dh1 * gate).astype(BF)
        db = (dh1 * value * gate * (1.0 - gate)).astype(BF)
        dj_s[at, :D] = da
        dj_s[at, D:] = db
        x = x_ref[ext, :].astype(F32)
        hat1, r1 = normalise(x)
        y1_s[at, :] = (hat1 * g1[...]).astype(BF)
        dy1 = nt(dj_s[at, :], glu[...])
        ln1_ref[...] += fold8(dy1 * hat1)
        dx_ref[at, :] = (dh1 + norm_back(dy1, hat1, r1, g1[...])).astype(dx_ref.dtype)
        return carry

    lax.fori_loop(0, rows // tile, step, 0)
    y1_t = y1_s[...].T
    for j in range(2 * D // PACK):
        gglu_ref[:, j * 16 : (j + 1) * 16, :] = blocks_of(
            nn(y1_t, dj_s[:, j * PACK : (j + 1) * PACK])
        )


def back1(dy2, dh2, h1, joined, x, g1, g2, glu):
    rows = dy2.shape[0]
    return whole_call(
        functools.partial(back1_kernel, 128),
        [((rows, D), BF), ((BLOCKS, 64, PACK), BF), ((8, D), F32), ((8, D), F32)],
        [dy2, dh2, h1, joined, x, g1, g2, glu],
        scratch=[((rows, D), BF), ((rows, 2 * D), BF)],
        scalars=0,
        flops=8 * rows * D * D,
    )


def lane_maps(rows, head):
    lane = lax.broadcasted_iota(jnp.int32,(rows,LANES),1)
    own = (lane >= head*HEAD) & (lane < (head+1)*HEAD)
    rel = lane - (1-head)*HEAD
    return own, rel

def id_column(base, rows, first):
    pos = base + lax.broadcasted_iota(jnp.int32,(rows,LANES),0)
    return pos >= first

def split3(v):
    hi = v.astype(BF).astype(F32)
    mid = (v-hi).astype(BF).astype(F32)
    return hi, mid, v-hi-mid

def tile_ids(start, rows, first):
    return start < first, start+rows > first

def overlap(a_start,a_rows,b_start,b_rows,first):
    a0,a1 = tile_ids(a_start,a_rows,first); b0,b1=tile_ids(b_start,b_rows,first)
    return (a0&b0)|(a1&b1)

def attend_kernel(n, heads, share, tq, tk, scal, *refs):
    qkv = refs[:n]; att = refs[n:2*n]; lse_ref = refs[2*n]
    qa, ka, va, mx_ref, m_ref, q2_ref, acc_ref = refs[2*n+1:]
    s = scal[0]; first = scal[1]
    rows = qkv[0].shape[0]
    for k in range(n):
        base = (s ^ k)*rows
        id1 = id_column(base, rows, first).astype(F32)
        q = qkv[k][:, 0:LANES].astype(F32)*(HEAD**-0.5)
        key = qkv[k][:, LANES:2*LANES].astype(F32)
        v = qkv[k][:, 2*LANES:3*LANES].astype(F32)
        for i in range(heads):
            h = i if share==1 else s % share
            own, rel = lane_maps(rows, h)
            qx = jnp.where(rel==0, 1.0-id1, jnp.where(rel==1, id1, 0.0))
            kx = jnp.where(rel==0, id1*BIG, jnp.where(rel==1, (1.0-id1)*BIG, jnp.where(rel<5,1.0,0.0)))
            qa[i, k*rows:(k+1)*rows,:] = jnp.where(own, q, qx).astype(BF)
            ka[i, k*rows:(k+1)*rows,:] = jnp.where(own, key, kx).astype(BF)
            va[i, k*rows:(k+1)*rows,:] = jnp.where(own, v, 1.0).astype(BF)
    per = rows//tq; per_k = rows//tk
    def fold(sc, best):
        for j in range(tk//LANES):
            best = jnp.maximum(best, sc[:, j*LANES:(j+1)*LANES])
        return best
    def q_step(it, carry):
        kq = it//per
        r0 = pl.multiple_of((it % per)*tq, tq)
        g0 = pl.multiple_of(it*tq, tq)
        own0 = pl.multiple_of((g0//tk)*tk, tk)
        q_start = (s ^ kq)*rows + r0
        for i in range(heads):
            for j in range(max(1,tq//tk)):
                sc = nt(qa[i, pl.ds(g0,tq),:], ka[i, pl.ds(own0+j*tk,tk),:])
                best = fold(sc, sc[:, :LANES] if j==0 else best)
            mx_ref[i] = best
            m_ref[i] = jnp.zeros((tq,LANES),F32)
        def attempt(again):
            for i in range(heads):
                h = i if share==1 else s % share
                own, rel = lane_maps(tq, h)
                m = jnp.max(mx_ref[i], axis=1, keepdims=True)
                mb = m_ref[i] + jnp.broadcast_to(m, (tq,LANES))
                m_ref[i] = mb
                hi,mid,lo = split3(-mb)
                q = qa[i, pl.ds(g0,tq),:].astype(F32)
                q2_ref[i] = jnp.where(rel==2,hi,jnp.where(rel==3,mid,jnp.where(rel==4,lo,q))).astype(BF)
            mx_ref[...] = jnp.full_like(mx_ref, -3e38)
            acc_ref[...] = jnp.zeros_like(acc_ref)
            for kt in range(n*per_k):
                k_start = (s ^ (kt//per_k))*rows + (kt%per_k)*tk
                @pl.when(overlap(q_start,tq,k_start,tk,first))
                def _():
                    for i in range(heads):
                        sc = nt(q2_ref[i], ka[i, kt*tk:(kt+1)*tk,:])
                        mx_ref[i] = fold(sc, mx_ref[i])
                        p = jnp.exp2(sc*LOG2E).astype(BF)
                        acc_ref[i] += nn(p, va[i, kt*tk:(kt+1)*tk,:])
            return (jnp.max(mx_ref[...]) > 40.0).astype(jnp.int32)
        lax.while_loop(lambda again: again > 0, attempt, jnp.int32(1))
        out = jnp.zeros((tq,LANES),F32); lse = jnp.zeros((tq,LANES),F32)
        for i in range(heads):
            h = i if share==1 else s % share
            own,_ = lane_maps(tq,h)
            acc = acc_ref[i]
            total = pltpu.roll(acc, HEAD, 1)
            out = jnp.where(own, acc/total, out)
            lse = jnp.where(own, m_ref[i]+jnp.log(total), lse)
        lse_ref[pl.ds(g0,tq),:] = lse
        for k in range(n):
            @pl.when(kq==k)
            def _():
                att[k][pl.ds(r0,tq),:] = out.astype(BF)
        return carry
    lax.fori_loop(0, n*per, q_step, 0)

def attend(scal, blocks, n, share, tq=768, tk=384):
    rows = blocks[0].shape[0]
    heads = 2 // share
    return whole_call(
        functools.partial(attend_kernel, n, heads, share, tq, tk),
        [((rows, LANES), BF)] * n + [((n * rows, LANES), F32)],
        [scal, *blocks],
        scratch=[((heads, n * rows, LANES), BF)] * 3
        + [((heads, tq, LANES), F32)] * 2
        + [((heads, tq, LANES), BF), ((heads, tq, LANES), F32)],
        flops=4 * n * rows * n * rows * HEAD * heads,
    )


def attend_back_kernel(n, heads, share, tq, tk, scal, *refs):
    qkv = refs[:n]; att = refs[n:2*n]; dat = refs[2*n:3*n]; lse_ref = refs[3*n]
    out = refs[3*n+1:4*n+1]
    qa, ka, va, da, dq_ref, dk_ref, dv_ref = refs[4*n+1:]
    s = scal[0]; first = scal[1]
    rows = qkv[0].shape[0]
    for k in range(n):
        base = (s ^ k)*rows
        sl = slice(k*rows,(k+1)*rows)
        id1 = id_column(base, rows, first).astype(F32)
        q = qkv[k][:, 0:LANES].astype(F32)*(HEAD**-0.5)
        key = qkv[k][:, LANES:2*LANES].astype(F32)
        v = qkv[k][:, 2*LANES:3*LANES].astype(F32)
        do = dat[k][...].astype(F32)
        prod = do*att[k][...].astype(F32)
        for i in range(heads):
            h = i if share==1 else s % share
            own, rel = lane_maps(rows, h)
            lse = pltpu.roll(lse_ref[sl,:], HEAD, 1)
            hi,mid,lo = split3(-lse)
            delta = jnp.sum(jnp.where(own,prod,0.0),axis=1,keepdims=True)
            dhi,dmid,dlo = split3(-delta)
            qx = jnp.where(rel==0, 1.0-id1, jnp.where(rel==1, id1, jnp.where(rel==2,hi,jnp.where(rel==3,mid,jnp.where(rel==4,lo,0.0)))))
            kx = jnp.where(rel==0, id1*BIG, jnp.where(rel==1, (1.0-id1)*BIG, jnp.where(rel<5,1.0,0.0)))
            vx = jnp.where(rel<3,1.0,0.0)
            dx = jnp.where(rel==0,dhi,jnp.where(rel==1,dmid,jnp.where(rel==2,dlo,0.0)))
            qa[i,sl,:] = jnp.where(own,q,qx).astype(BF)
            ka[i,sl,:] = jnp.where(own,key,kx).astype(BF)
            va[i,sl,:] = jnp.where(own,v,vx).astype(BF)
            da[i,sl,:] = jnp.where(own,do,dx).astype(BF)
    dq_ref[...] = jnp.zeros_like(dq_ref)
    per_q = rows//tq; per_k = rows//tk
    def k_step(kt, carry):
        k0 = pl.multiple_of(kt*tk, tk)
        kk = kt//per_k
        k_start = (s ^ kk)*rows + (kt % per_k)*tk
        for i in range(heads):
            dk_ref[i] = jnp.zeros((tk,LANES),F32)
            dv_ref[i] = jnp.zeros((tk,LANES),F32)
        def q_step(qt, c2):
            q0 = pl.multiple_of(qt*tq, tq)
            q_start = (s ^ (qt//per_q))*rows + (qt % per_q)*tq
            @pl.when(overlap(q_start,tq,k_start,tk,first))
            def _():
                for i in range(heads):
                    qq = qa[i,pl.ds(q0,tq),:]; kx = ka[i,pl.ds(k0,tk),:]; dd = da[i,pl.ds(q0,tq),:]
                    st = nt(kx, qq)
                    p = jnp.exp2(st*LOG2E)
                    dp = nt(va[i,pl.ds(k0,tk),:], dd)
                    ds = (p*dp).astype(BF)
                    dv_ref[i] += nn(p.astype(BF), dd)
                    dk_ref[i] += nn(ds, qq)
                    dq_ref[i,pl.ds(q0,tq),:] += tn(ds, kx)
            return c2
        lax.fori_loop(0, n*per_q, q_step, 0)
        dk = jnp.zeros((tk,LANES),F32); dv = jnp.zeros((tk,LANES),F32)
        for i in range(heads):
            h = i if share==1 else s % share
            own,_ = lane_maps(tk,h)
            dk = jnp.where(own, dk_ref[i], dk); dv = jnp.where(own, dv_ref[i], dv)
        r0 = pl.multiple_of((kt % per_k)*tk, tk)
        for k in range(n):
            @pl.when(kk==k)
            def _():
                out[k][pl.ds(r0,tk),LANES:2*LANES] = dk.astype(BF)
                out[k][pl.ds(r0,tk),2*LANES:3*LANES] = dv.astype(BF)
        return carry
    lax.fori_loop(0, n*per_k, k_step, 0)
    for k in range(n):
        sl = slice(k*rows,(k+1)*rows)
        dq = jnp.zeros((rows,LANES),F32)
        for i in range(heads):
            h = i if share==1 else s % share
            own,_ = lane_maps(rows,h)
            dq = jnp.where(own, dq_ref[i,sl,:], dq)
        out[k][:, 0:LANES] = (dq*(HEAD**-0.5)).astype(BF)

def attend_back(scal, blocks, att, datt, lse, n, share, tq=384, tk=384):
    rows = blocks[0].shape[0]
    heads = 2 // share
    return whole_call(
        functools.partial(attend_back_kernel, n, heads, share, tq, tk),
        [((rows, 3 * LANES), BF)] * n,
        [scal, *blocks, *att, *datt, lse],
        scratch=[((heads, n * rows, LANES), BF)] * 4
        + [((heads, n * rows, LANES), F32)]
        + [((heads, tk, LANES), F32)] * 2,
        flops=10 * n * rows * n * rows * HEAD * heads,
    )


def pack_block(block):
    rows, columns = block.shape
    return block.reshape(rows, columns // PACK, PACK).transpose(1, 0, 2).reshape(-1, PACK)


def pack_small(blocks):
    flat = jnp.concatenate(blocks, axis=-1)
    rows = -(-flat.shape[-1] // (16 * PACK)) * 16
    pad = [(0, 0)] * (flat.ndim - 1) + [(0, rows * PACK - flat.shape[-1])]
    return jnp.pad(flat, pad).reshape(flat.shape[:-1] + (rows, PACK))


def gather_all(weights):
    small = [w for w in weights if w.ndim == 1]
    packed = [pack_block(w) for w in weights if w.ndim == 2] + [pack_small(small)]
    local = jnp.concatenate(packed, axis=0)
    whole = lax.all_gather(local, AXES, axis=0, tiled=False)
    count = whole.shape[0]
    tail = whole[:, -packed[-1].shape[0] :].reshape(count, -1)
    result, start, place = [], 0, 0
    for w in weights:
        if w.ndim == 1:
            result.append(tail[:, place : place + w.shape[0]].reshape(-1))
            place += w.shape[0]
        else:
            rows, columns = w.shape
            chunks = columns // PACK
            part = whole[:, start : start + rows * chunks].reshape(count, chunks, rows, PACK)
            result.append(part.transpose(0, 2, 1, 3).reshape(count * rows, columns))
            start += rows * chunks
    return result


def to_owners(grad, w, count):
    if grad.ndim == 2:
        return grad.reshape(count, -1, PACK)
    finer = count // BLOCKS
    if finer == 1:
        return grad
    rows, columns = w.shape
    part = grad.reshape(BLOCKS, columns // PACK, finer, rows, PACK)
    return part.transpose(0, 2, 1, 3, 4).reshape(count, -1, PACK)


def scatter_all(grads, weights):
    count = lax.axis_size("seq") * lax.axis_size("dp")
    small = [g.reshape(count, -1) for g, w in zip(grads, weights) if w.ndim == 1]
    packed = [to_owners(g, w, count) for g, w in zip(grads, weights) if w.ndim == 2]
    packed.append(pack_small(small).astype(BF))
    send = jnp.concatenate(packed, axis=1)
    total = lax.psum_scatter(send, AXES, scatter_dimension=0, tiled=False).astype(F32)
    tail = total[-packed[-1].shape[1] :].reshape(-1)
    result, start, place = [], 0, 0
    for w in weights:
        if w.ndim == 1:
            result.append(tail[place : place + w.shape[0]])
            place += w.shape[0]
        else:
            rows, columns = w.shape
            chunks = columns // PACK
            part = total[start : start + rows * chunks].reshape(chunks, rows, PACK)
            result.append(part.transpose(1, 0, 2).reshape(rows, columns))
            start += rows * chunks
    return result


class Layout:
    def __init__(self, n_seq, n_dp):
        self.n_seq, self.n_dp = n_seq, n_dp
        self.where = {}
        for g in range(n_dp):
            for s in range(n_seq):
                self.where[g, s] = self.place(g, s)
        self.block = np.zeros(n_seq * n_dp, np.int32)
        for (g, s), device in self.where.items():
            self.block[device] = s

    def place(self, g, s):
        if (self.n_seq, self.n_dp) == (4, 8):
            y, x, c = g >> 2, g >> 1 & 1, g & 1
            return (2 * c + y) * 8 + (s & 1) * 4 + x * 2 + (s >> 1)
        return s * self.n_dp + g

    def pairs(self, source, target):
        return [
            (source(g, s), target(g, s))
            for g in range(self.n_dp)
            for s in range(self.n_seq)
            if target(g, s) is not None and source(g, s) is not None
        ]

    def at(self, g, s):
        return self.where.get((g, s))

    def home(self, g, s):
        return s * self.n_dp + g

    def bring(self, value):
        return lax.ppermute(value, AXES, self.pairs(self.home, self.at))

    def bring_to(self, value, step):
        return lax.ppermute(
            value, AXES, self.pairs(self.home, lambda g, s: self.at(g, s + step))
        )

    def send_home(self, value):
        return lax.ppermute(value, AXES, self.pairs(self.at, self.home))

    def to_neighbour(self, value, step):
        return lax.ppermute(value, AXES, self.pairs(self.at, lambda g, s: self.at(g, s + step)))

    def swap(self, values):
        return [values[0]] + [
            lax.ppermute(values[k], AXES, self.pairs(self.at, lambda g, s: self.at(g, s ^ k)))
            for k in range(1, self.n_seq)
        ]


def on_device(tokens, cotangent, first_length, *weights):
    n = lax.axis_size("seq")
    n_dp = lax.axis_size("dp")
    share = n * LANES // D
    layout = Layout(n, n_dp)
    rows = tokens.shape[1]
    group = n * rows
    me = lax.axis_index("seq") * n_dp + lax.axis_index("dp")
    s = jnp.asarray(layout.block)[me]

    tokens = tokens[0]
    x = layout.bring(tokens)
    low = layout.bring_to(tokens[-RIM:], 1)
    high = layout.bring_to(tokens[:RIM], -1)
    first = layout.bring(first_length)[0]
    scal = jnp.stack([s.astype(jnp.int32), first])
    cot = layout.bring(cotangent[0])
    x_ext = jnp.concatenate([low, x, high], axis=0)

    params = gather_all(weights)
    g1, g2, g3, g4, g5 = (p.astype(F32)[None] for p in params[:5])
    glu, wide, narrow, depth, point, qkv_w, wa, wup, wdown = params[5:]
    taps = depth.reshape(KERNEL, FF).astype(F32)

    h1, y2, joined = front1(x_ext, g1, glu, g2)
    left, right, mid = front2(scal, y2, wide, narrow, g3, group)
    spread, h2, y4, *qkv = front3(scal, mid, taps, point, h1, g4, qkv_w, n, share)
    qkv = layout.swap(qkv)
    *att, lse = attend(scal, qkv, n, share)
    mixed, dh3, *rest = middle(
        scal, h2, layout.swap(att), cot, g5, wa, wup, wdown, n, share
    )
    datt, (ga, gup, gdown, ln5) = rest[:n], rest[n:]
    dqkv = attend_back(scal, qkv, att, layout.swap(datt), lse, n, share)
    dh2, db, gqkv, gpoint, ln4 = back3(
        scal, layout.swap(dqkv), dh3, h2, y4, spread, g4, qkv_w, n, share
    )
    dy2, gwide, gnarrow, gdepth, ln3 = back2(
        scal,
        layout.to_neighbour(db[-RIM:], 1),
        db,
        layout.to_neighbour(db[:RIM], -1),
        point,
        taps,
        mid,
        left,
        right,
        wide,
        narrow,
        y2,
        g3,
        group,
    )
    dx, gglu, ln1, ln2 = back1(dy2, dh2, h1, joined, x_ext, g1, g2, glu)
    ln1, ln2, ln3, ln4, ln5 = (jnp.sum(v, axis=0) for v in (ln1, ln2, ln3, ln4, ln5))
    gdepth = jnp.sum(gdepth.reshape(KERNEL, 8, FF), axis=1).reshape(-1)
    grads = [ln1, ln2, ln3, ln4, ln5, gglu, gwide, gnarrow, gdepth, gpoint, gqkv, ga, gup, gdown]
    summed = scatter_all(grads, weights)
    return (
        layout.send_home(mixed)[None],
        layout.send_home(dx).astype(F32)[None],
        *summed,
    )


def solution(mesh):
    token, owner, rows = P("dp", "seq", None), P(AXES), P(AXES, None)
    params = (owner,) * 5 + (rows,) * 3 + (owner,) + (rows,) * 5
    return jax.shard_map(
        on_device,
        mesh=mesh,
        in_specs=(token, token, P("dp")) + params,
        out_specs=(token, token) + params,
        check_vma=False,
    )
```

time: 1070 us -> 708 us (0.66)
  matrix products: 305 us -> 0 us
  Pallas kernels: 0 us -> 242 us
  other arithmetic: 122 us -> 6.97 us
  waiting for transfers between devices: 431 us -> 317 us
  local copies, waits for them, and re-layouts: 164 us -> 81.2 us
  starting transfers between devices: 21.9 us -> 36.8 us
    dot_general x78 -> x0, matrix products: 305 us -> none  [the longest x24 88.2 us: product(): return jnp.dot(left, right, preferred_element_type=jnp.float32)]
    pallas_call x0 -> x9, Pallas kernels: none -> 242 us  [whole_call(): pl.pallas_call(kernel, out_shape=outs, in_specs=[sm] * scalars + [vm] * (...]
    all_gather x3 -> x1, waiting for transfers between devices: 189 us -> 64.5 us  [gather_all(): whole = lax.all_gather(local, AXES, axis=0, tiled=False)]
    ppermute x8 -> x21, waiting for transfers between devices: 1.18 us -> 90.2 us  [the longest x12 66.8 us: swap(): lax.ppermute(values[k], AXES, self.pairs(self.at, lambda g, s: self.at(g,...]
    reduce_scatter x2 -> x1, waiting for transfers between devices: 240 us -> 163 us  [scatter_all(): lax.psum_scatter(send, AXES, scatter_dimension=0, tiled=False).astype(F32)]
    reduce_sum x21 -> x6, other arithmetic: 37.4 us -> 2.56 us  [the longest x5 2.41 us: on_device(): jnp.sum(v, axis=0)]
    unnamed x306 -> x90, local copies, waits for them, and re-layouts: 59.9 us -> 33.2 us
    convert_element_type x18 -> x4, other arithmetic: 26.6 us -> 1.19 us  [the longest x1 1.03 us: scatter_all(): lax.psum_scatter(send, AXES, scatter_dimension=0, tiled=False).astype(F32)]
  transfers between devices with their start and end apart: 13 -> 23, of which waited for: 6 -> 10; matrix products, arithmetic and copies ran while one was open for 7% -> 3% of each run, Pallas kernels for 0% -> 5%
where the time goes in v2:
time: 708 us; the launch traced here: 699 us
  waiting for transfers between devices  317 us (45%)
  Pallas kernels  242 us (34%)
  local copies, waits for them, and re-layouts  81.2 us (11%)
  starting transfers between devices  36.8 us (5%)
  between operations  14.9 us (2%)
    pallas_call x9, Pallas kernels, whole_call(): pl.pallas_call(kernel, out_shape=outs, in_specs=[sm] * scalars + [vm] * (...  242 us
    reduce_scatter x1, waiting for transfers between devices, scatter_all(): lax.psum_scatter(send, AXES, scatter_dimension=0, tiled=False).astype(F32)  163 us
    ppermute x12, waiting for transfers between devices, swap(): lax.ppermute(values[k], AXES, self.pairs(self.at, lambda g, s: self.at(g,...  66.8 us
    all_gather x1, waiting for transfers between devices, gather_all(): whole = lax.all_gather(local, AXES, axis=0, tiled=False)  64.5 us
    unnamed x90, local copies, waits for them, and re-layouts  33.2 us
    ppermute x2, waiting for transfers between devices, bring_to(): lax.ppermute(value, AXES, self.pairs(self.home, lambda g, s: self.at(g, s...  23.1 us
  transfers between devices with their start and end apart: 23, of which 10 were waited for; matrix products, arithmetic and copies ran while one was open for 3% of the time, Pallas kernels for 5%

profile of v2, /device:TPU:0, one launch (start us, length us, event | category | flops | bytes accessed | tf_op | source)
XLA Modules:
  0.0 699.1 jit_solution(4395911576031402848)
XLA Ops:
  7.2 4.1 concatenate.17
  13.8 0.9 reshape.270
  18.8 1.8 collective-permute-start.2
  20.6 1.9 collective-permute-start
  23.2 1.3 collective-permute-start.3
  24.5 8.0 %collective-permute-start.1 = (bf16[16,512]{1,0:T(8,128)(2,1)S(1)}, bf16[16,512]{1,0:T(8,128)(2,1)S(1)}, u32[]{:S(2)}, u32[]{:S(2)}) collective-permute-start(bf16[16,512]{1,0:T(8,128)(2,1)S(1)} %get-tuple-element.114), channel_id=1, source_target_pairs={{0,4},{8,1},{16,5},{1,20},{9,17},{17,21},{2,6},{10,3},{18,7},{3,22... | collective-permute-start | bytes 49160 | tf_op jit(solution)/shard_map/ppermute | solution.py:883
  32.5 1.2 dynamic_slice.3
  33.7 1.9 pad_add_fusion.scal
  36.2 0.9 constant_dynamic-update-slice_fusion.1
  37.1 23.1 %collective-permute-done.3 = bf16[16,512]{1,0:T(8,128)(2,1)S(1)} collective-permute-done((bf16[16,512]{1,0:T(8,128)(2,1)S(1)}, bf16[16,512]{1,0:T(8,128)(2,1)S(1)}, u32[]{:S(2)}, u32[]{:S(2)}) %collective-permute-start.3) | collective-permute-done | bytes 16416 | tf_op jit(solution)/shard_map/ppermute | solution.py:883
  60.8 64.5 %all-gather.3.cloned.1.call-done = bf16[22528,256]{1,0:T(8,128)(2,1)} async-done(((bf16[704,256]{1,0:T(8,128)(2,1)}), bf16[22528,256]{1,0:T(8,128)(2,1)}) %all-gather.3.cloned.1.call-update) | async-done | bytes 11534352 | tf_op jit(solution)/shard_map/all_gather | solution.py:798
  125.3 1.0 slice.159
  126.5 2.1 slice.164
  128.6 2.7 slice.169
  131.2 2.7 fusion.1
  133.9 5.6 fusion
  142.9 2.1 copy.66
  145.1 1.6 copy.86
  147.2 1.2 copy.84
  148.5 0.9 copy.65
  149.4 2.1 copy.85
  151.5 7.3 %shard_map.297 = (f32[800,512]{1,0:T(8,128)}, bf16[800,512]{1,0:T(8,128)(2,1)}, f32[800,1024]{1,0:T(8,128)}) custom-call(bf16[800,512]{1,0:T(8,128)(2,1)} %constant_dynamic-update-slice_fusion.x_ref, f32[1,512]{1,0:T(1,128)} %reshape.313.g1, bf16[512,1024]{1,0:T(8,128)(2,1)} %bitcast.124, f32[1,512]{1,0:T(1,128)} %reshape.314.g2), custom_call_target="tpu_custom_call" | custom-call | flops 838860800 | bytes 7606272 | tf_op jit(solution)/shard_map/pallas_call | solution.py:48
  158.8 12.4 %shard_map.298 = (f32[800,2048]{1,0:T(8,128)}, f32[800,256]{1,0:T(8,128)}, bf16[800,2048]{1,0:T(8,128)(2,1)}) custom-call(s32[2]{0:T(128)} %pad_add_fusion.scal, bf16[800,512]{1,0:T(8,128)(2,1)} %get-tuple-element.62.y2_ref.refs_7_, bf16[512,2048]{1,0:T(8,128)(2,1)} %bitcast.130, bf16[1536,256]{1,0:T(8,128)(2,1)} %bitcast.140, f32[1,2048]{1,0:T(1,128)} %reshape.315.g3.refs_8_), custom_call_target="tpu_custom_call" | custom-call | flops 2306867200 | bytes 14360584 | tf_op jit(solution)/shard_map/pallas_call | solution.py:48
  171.2 20.9 %shard_map.299 = (bf16[768,2048]{1,0:T(8,128)(2,1)}, f32[768,512]{1,0:T(8,128)}, bf16[768,512]{1,0:T(8,128)(2,1)}, bf16[768,384]{1,0:T(8,128)(2,1)}, bf16[768,38...) custom-call(s32[2]{0:T(128)} %pad_add_fusion.scal, ...), custom_call_target="tpu_custom_call" | custom-call | flops 2013265920 | bytes 15476744 | tf_op jit(solution)/shard_map/pallas_call | solution.py:48
  192.2 2.1 collective-permute-start.6
  194.3 7.8 %collective-permute-start.10 = (bf16[768,512]{1,0:T(8,128)(2,1)}, bf16[768,512]{1,0:T(8,128)(2,1)}, u32[]{:S(2)}, u32[]{:S(2)}) collective-permute-start(bf16[768,512]{1,0:T(8,128)(2,1)} %bitcast.24), channel_id=1, source_target_pairs={{0,0},{8,4},{16,1},{24,5},{1,16},{9,20},{17,17},{25,21},{2,2},{10,... | collective-permute-start | bytes 2359304 | tf_op jit(solution)/shard_map/ppermute | solution.py:880
  202.1 11.7 %collective-permute-done.4.refs_1_ = bf16[768,384]{1,0:T(8,128)(2,1)S(1)} collective-permute-done((bf16[768,384]{1,0:T(8,128)(2,1)}, bf16[768,384]{1,0:T(8,128)(2,1)S(1)}, u32[]{:S(2)}, u32[]{:S(2)}) %collective-permute-start.4) | collective-permute-done | bytes 589856 | tf_op jit(solution)/shard_map/ppermute | solution.py:895
  213.8 20.4 %collective-permute-done.6.refs_3_ = bf16[768,384]{1,0:T(8,128)(2,1)S(1)} collective-permute-done((bf16[768,384]{1,0:T(8,128)(2,1)}, bf16[768,384]{1,0:T(8,128)(2,1)S(1)}, u32[]{:S(2)}, u32[]{:S(2)}) %collective-permute-start.6) | collective-permute-done | bytes 589856 | tf_op jit(solution)/shard_map/ppermute | solution.py:895
  235.1 35.8 %shard_map.300 = (bf16[768,128]{1,0:T(8,128)(2,1)}, bf16[768,128]{1,0:T(8,128)(2,1)}, bf16[768,128]{1,0:T(8,128)(2,1)}, bf16[768,128]{1,0:T(8,128)(2,1)}, f32[3072,128]{1,0:T(8,128)}) custom-call(s32[2]{0:T(128)} %pad_add_fusion.scal, bf16[768,384]{1,0:T(8,128)(2,1)} %get-tuple-element.66.refs_0_, bf16[768,384]{1,0:T(8,128)(2,1)} %copy-done.15, ...), custom_call_target="tpu_custom_call" | custom-call | flops 4831838208 | bytes 4718600 | tf_op jit(solution)/shard_map/pallas_call | solution.py:48
  270.8 0.9 collective-permute-start.7
  271.8 1.0 collective-permute-start.8
  273.0 1.1 slice.171
  275.2 0.9 copy.87
  276.3 2.2 copy.69
  278.5 1.9 copy.89
  280.4 0.9 copy.68
  281.3 2.0 copy.88
  284.2 27.7 %shard_map.301 = (bf16[768,512]{1,0:T(8,128)(2,1)}, f32[768,512]{1,0:T(8,128)}, bf16[768,128]{1,0:T(8,128)(2,1)}, bf16[768,128]{1,0:T(8,128)(2,1)}, bf16[768,128...) custom-call(s32[2]{0:T(128)} %pad_add_fusion.scal, ...), custom_call_target="tpu_custom_call" | custom-call | flops 10871635968 | bytes 15747080 | tf_op jit(solution)/shard_map/pallas_call | solution.py:48
  311.9 1.4 collective-permute-start.12
  314.0 5.8 collective-permute-done.12.refs_9_
  319.9 2.8 collective-permute-done.14.refs_11_
  323.3 58.1 %shard_map.302 = (bf16[768,384]{1,0:T(8,128)(2,1)}, bf16[768,384]{1,0:T(8,128)(2,1)}, bf16[768,384]{1,0:T(8,128)(2,1)}, bf16[768,384]{1,0:T(8,128)(2,1)}) custom-call(s32[2]{0:T(128)} %pad_add_fusion.scal, bf16[768,384]{1,0:T(8,128)(2,1)} %get-tuple-element.66.refs_0_, bf16[768,384]{1,0:T(8,128)(2,1)} %copy-done.15, bf16[768,384]{1,0:T(8,128)(2,1)} %copy-done.16, ...), custom_call_target="tpu_custom_call" | custom-call | flops 12079595520 | bytes 7864328 | tf_op jit(solution)/shard_map/pallas_call | solution.py:48
  381.4 2.1 collective-permute-start.15
  383.7 14.1 %collective-permute-done.15.refs_1_ = bf16[768,384]{1,0:T(8,128)(2,1)S(1)} collective-permute-done((bf16[768,384]{1,0:T(8,128)(2,1)}, bf16[768,384]{1,0:T(8,128)(2,1)S(1)}, u32[]{:S(2)}, u32[]{:S(2)}) %collective-permute-start.15) | collective-permute-done | bytes 589856 | tf_op jit(solution)/shard_map/ppermute | solution.py:895
  397.8 11.9 %collective-permute-done.17.refs_3_ = bf16[768,384]{1,0:T(8,128)(2,1)S(1)} collective-permute-done((bf16[768,384]{1,0:T(8,128)(2,1)}, bf16[768,384]{1,0:T(8,128)(2,1)S(1)}, u32[]{:S(2)}, u32[]{:S(2)}) %collective-permute-start.17) | collective-permute-done | bytes 589856 | tf_op jit(solution)/shard_map/ppermute | solution.py:895
  410.5 12.8 %shard_map.303 = (f32[768,512]{1,0:T(8,128)}, bf16[768,256]{1,0:T(8,128)(2,1)}, bf16[32,96,256]{2,1,0:T(8,128)(2,1)}, bf16[2048,256]{1,0:T(8,128)(2,1)}, f32[8,512]{1,0:T(8,128)}) custom-call(s32[2]{0:T(128)} %pad_add_fusion.scal, bf16[768,384]{1,0:T(8,128)(2,1)} %get-tuple-element.80.refs_0_, bf16[768,384]{1,0:T(8,128)(2,1)} %copy-done.18, ...), custom_call_target="tpu_custom_call" | custom-call | flops 3221225472 | bytes 15616008 | tf_op jit(solution)/shard_map/pallas_call | solution.py:48
  424.0 1.3 collective-permute-start.19
  425.3 4.5 collective-permute-start.18
  431.8 55.7 %shard_map.304 = (f32[768,512]{1,0:T(8,128)}, bf16[32,128,256]{2,1,0:T(8,128)(2,1)}, bf16[1536,256]{1,0:T(8,128)(2,1)}, f32[72,2048]{1,0:T(8,128)}, f32[8,2048]{1,0:T(8,128)}) custom-call(s32[2]{0:T(128)} %pad_add_fusion.scal, bf16[16,256]{1,0:T(8,128)(2,1)} %copy-done.28, bf16[768,256]{1,0:T(8,128)(2,1)} %get-tuple-element.87.db_ref, ...), custom_call_target="tpu_custom_call" | custom-call | flops 5234491392 | bytes 21004296 | tf_op jit(solution)/shard_map/pallas_call | solution.py:48
  487.6 11.2 %shard_map.305 = (bf16[768,512]{1,0:T(8,128)(2,1)}, bf16[32,64,256]{2,1,0:T(8,128)(2,1)}, f32[8,512]{1,0:T(8,128)}, f32[8,512]{1,0:T(8,128)}) custom-call(f32[768,512]{1,0:T(8,128)} %get-tuple-element.90.dy2_ref, f32[768,512]{1,0:T(8,128)} %get-tuple-element.91.dh2_ref, f32[800,512]{1,0:T(8,128)} %get-tuple-element.64.h1_ref, ...), custom_call_target="tpu_custom_call" | custom-call | flops 1610612736 | bytes 11800576 | tf_op jit(solution)/shard_map/pallas_call | solution.py:48
  498.8 0.9 reduce_sum.54
  501.2 2.4 constant_dynamic-update-slice_fusion.20
  503.6 1.5 constant_dynamic-update-slice_fusion.19
  505.1 1.0 constant_dynamic-update-slice_fusion.18
  506.1 1.1 constant_dynamic-update-slice_fusion.17
  507.2 1.3 constant_dynamic-update-slice_fusion.16
  509.4 1.5 constant_dynamic-update-slice_fusion.14
  510.9 1.5 constant_dynamic-update-slice_fusion.13
  513.2 1.1 copy-done.13
  515.7 1.4 bitcast_convert_fusion
  517.1 162.6 %reduce-scatter.2.cloned.1.call-done = bf16[1,704,256]{2,1,0:T(8,128)(2,1)} async-done(((bf16[32,704,256]{2,1,0:T(8,128)(2,1)}), bf16[1,704,256]{2,1,0:T(8,128)(2,1)}) %reduce-scatter.2.cloned.1.call-update) | async-done | bytes 360464 | tf_op jit(solution)/shard_map/reduce_scatter | solution.py:832
  679.7 1.0 convert_element_type.96
  688.0 0.9 fusion.3
  690.9 0.9 copy.113
  (154 shorter events, 34.7 us)
Async XLA Ops:
  7.2 118.1 %all-gather.3.cloned.1.call-start = ((), (), s32[]{:S(2)}) async-start(), calls=%async_computation.2 | async-start | bytes 11894784 | tf_op jit(solution)/shard_map/all_gather | solution.py:798
  18.0 0.7 copy-start.10
  18.8 660.9 %reduce-scatter.2.cloned.1.call-start = ((), (), s32[]{:S(2)}) async-start(), calls=%async_computation.1 | async-start | bytes 11894784 | tf_op jit(solution)/shard_map/reduce_scatter | solution.py:832
  18.8 17.4 %collective-permute-start.2 = (bf16[768,512]{1,0:T(8,128)(2,1)}, bf16[768,512]{1,0:T(8,128)(2,1)S(1)}, u32[]{:S(2)}, u32[]{:S(2)}) collective-permute-start(bf16[768,512]{1,0:T(8,128)(2,1)} %bitcast.177), channel_id=1, source_target_pairs={{0,0},{8,4},{16,1},{24,5},{1,16},{9,20},{17,17},{25,21},{2,2},{10,... | collective-permute-start | bytes 2359304 | tf_op jit(solution)/shard_map/ppermute | solution.py:880
  20.6 13.1 %collective-permute-start = (s32[1]{0:T(128)}, s32[1]{0:T(128)}, u32[]{:S(2)}, u32[]{:S(2)}) collective-permute-start(s32[1]{0:T(128)} %param.20), channel_id=1, source_target_pairs={{0,0},{8,4},{16,1},{24,5},{1,16},{9,20},{17,17},{25,21},{2,2},{10,... | collective-permute-start | bytes 20 | tf_op jit(solution)/shard_map/ppermute | solution.py:880
  23.2 37.0 %collective-permute-start.3 = (bf16[16,512]{1,0:T(8,128)(2,1)S(1)}, bf16[16,512]{1,0:T(8,128)(2,1)S(1)}, u32[]{:S(2)}, u32[]{:S(2)}) collective-permute-start(bf16[16,512]{1,0:T(8,128)(2,1)S(1)} %get-tuple-element.113), channel_id=1, source_target_pairs={{8,0},{16,4},{24,1},{9,16},{17,20},{25,17},{10,2},{18,6},{26,3},{1... | collective-permute-start | bytes 49160 | tf_op jit(solution)/shard_map/ppermute | solution.py:883
  24.5 11.1 %collective-permute-start.1 = (bf16[16,512]{1,0:T(8,128)(2,1)S(1)}, bf16[16,512]{1,0:T(8,128)(2,1)S(1)}, u32[]{:S(2)}, u32[]{:S(2)}) collective-permute-start(bf16[16,512]{1,0:T(8,128)(2,1)S(1)} %get-tuple-element.114), channel_id=1, source_target_pairs={{0,4},{8,1},{16,5},{1,20},{9,17},{17,21},{2,6},{10,3},{18,7},{3,22... | collective-permute-start | bytes 49160 | tf_op jit(solution)/shard_map/ppermute | solution.py:883
  145.1 3.4 copy-start.1
  192.1 21.7 %collective-permute-start.4 = (bf16[768,384]{1,0:T(8,128)(2,1)}, bf16[768,384]{1,0:T(8,128)(2,1)S(1)}, u32[]{:S(2)}, u32[]{:S(2)}) collective-permute-start(bf16[768,384]{1,0:T(8,128)(2,1)} %get-tuple-element.67), channel_id=1, source_target_pairs={{0,4},{4,0},{1,5},{5,1},{16,20},{20,16},{17,21},{21,17},{2,6},{6,2... | collective-permute-start | bytes 1769480 | tf_op jit(solution)/shard_map/ppermute | solution.py:895
  192.1 21.7 %collective-permute-start.5 = (bf16[768,384]{1,0:T(8,128)(2,1)}, bf16[768,384]{1,0:T(8,128)(2,1)S(1)}, u32[]{:S(2)}, u32[]{:S(2)}) collective-permute-start(bf16[768,384]{1,0:T(8,128)(2,1)} %get-tuple-element.68), channel_id=1, source_target_pairs={{0,1},{4,5},{1,0},{5,4},{16,17},{20,21},{17,16},{21,20},{2,3},{6,7... | collective-permute-start | bytes 1769480 | tf_op jit(solution)/shard_map/ppermute | solution.py:895
  192.2 42.1 %collective-permute-start.6 = (bf16[768,384]{1,0:T(8,128)(2,1)}, bf16[768,384]{1,0:T(8,128)(2,1)S(1)}, u32[]{:S(2)}, u32[]{:S(2)}) collective-permute-start(bf16[768,384]{1,0:T(8,128)(2,1)} %get-tuple-element.69), channel_id=1, source_target_pairs={{0,5},{4,1},{1,4},{5,0},{16,21},{20,17},{17,20},{21,16},{2,7},{6,3... | collective-permute-start | bytes 1769480 | tf_op jit(solution)/shard_map/ppermute | solution.py:895
  194.3 89.1 %collective-permute-start.10 = (bf16[768,512]{1,0:T(8,128)(2,1)}, bf16[768,512]{1,0:T(8,128)(2,1)}, u32[]{:S(2)}, u32[]{:S(2)}) collective-permute-start(bf16[768,512]{1,0:T(8,128)(2,1)} %bitcast.24), channel_id=1, source_target_pairs={{0,0},{8,4},{16,1},{24,5},{1,16},{9,20},{17,17},{25,21},{2,2},{10,... | collective-permute-start | bytes 2359304 | tf_op jit(solution)/shard_map/ppermute | solution.py:880
  213.8 20.5 %copy-start.15 = (bf16[768,384]{1,0:T(8,128)(2,1)}, bf16[768,384]{1,0:T(8,128)(2,1)S(1)}, u32[]{:S(2)}) copy-start(bf16[768,384]{1,0:T(8,128)(2,1)S(1)} %collective-permute-done.4.refs_1_) | copy-start | bytes 1769476
  213.8 20.4 %copy-start.16 = (bf16[768,384]{1,0:T(8,128)(2,1)}, bf16[768,384]{1,0:T(8,128)(2,1)S(1)}, u32[]{:S(2)}) copy-start(bf16[768,384]{1,0:T(8,128)(2,1)S(1)} %collective-permute-done.5.refs_2_) | copy-start | bytes 1769476
  234.3 0.8 copy-start.17
  270.8 12.5 %collective-permute-start.7 = (bf16[768,128]{1,0:T(8,128)(2,1)}, bf16[768,128]{1,0:T(8,128)(2,1)S(1)}, u32[]{:S(2)}, u32[]{:S(2)}) collective-permute-start(bf16[768,128]{1,0:T(8,128)(2,1)} %get-tuple-element.71.refs_5_), channel_id=1, source_target_pairs={{0,4},{4,0},{1,5},{5,1},{16,20},{20,16},{17,21},{21,17},{2,6},{6,2... | collective-permute-start | bytes 589832 | tf_op jit(solution)/shard_map/ppermute | solution.py:895
  271.8 11.6 %collective-permute-start.8 = (bf16[768,128]{1,0:T(8,128)(2,1)}, bf16[768,128]{1,0:T(8,128)(2,1)S(1)}, u32[]{:S(2)}, u32[]{:S(2)}) collective-permute-start(bf16[768,128]{1,0:T(8,128)(2,1)} %get-tuple-element.72.refs_6_), channel_id=1, source_target_pairs={{0,1},{4,5},{1,0},{5,4},{16,17},{20,21},{17,16},{21,20},{2,3},{6,7... | collective-permute-start | bytes 589832 | tf_op jit(solution)/shard_map/ppermute | solution.py:895
  272.8 10.6 %collective-permute-start.9 = (bf16[768,128]{1,0:T(8,128)(2,1)}, bf16[768,128]{1,0:T(8,128)(2,1)S(1)}, u32[]{:S(2)}, u32[]{:S(2)}) collective-permute-start(bf16[768,128]{1,0:T(8,128)(2,1)} %get-tuple-element.73.refs_7_), channel_id=1, source_target_pairs={{0,5},{4,1},{1,4},{5,0},{16,21},{20,17},{17,20},{21,16},{2,7},{6,3... | collective-permute-start | bytes 589832 | tf_op jit(solution)/shard_map/ppermute | solution.py:895
  274.7 1.6 copy-start
  283.3 0.7 copy-start.21
  283.4 0.7 copy-start.22
  283.4 0.8 copy-start.23
  311.9 8.0 %collective-permute-start.12 = (bf16[768,128]{1,0:T(8,128)(2,1)}, bf16[768,128]{1,0:T(8,128)(2,1)S(1)}, u32[]{:S(2)}, u32[]{:S(2)}) collective-permute-start(bf16[768,128]{1,0:T(8,128)(2,1)} %get-tuple-element.76), channel_id=1, source_target_pairs={{0,4},{4,0},{1,5},{5,1},{16,20},{20,16},{17,21},{21,17},{2,6},{6,2... | collective-permute-start | bytes 589832 | tf_op jit(solution)/shard_map/ppermute | solution.py:895
  313.3 6.6 collective-permute-start.13
  313.5 9.1 %collective-permute-start.14 = (bf16[768,128]{1,0:T(8,128)(2,1)}, bf16[768,128]{1,0:T(8,128)(2,1)S(1)}, u32[]{:S(2)}, u32[]{:S(2)}) collective-permute-start(bf16[768,128]{1,0:T(8,128)(2,1)} %get-tuple-element.78), channel_id=1, source_target_pairs={{0,5},{4,1},{1,4},{5,0},{16,21},{20,17},{17,20},{21,16},{2,7},{6,3... | collective-permute-start | bytes 589832 | tf_op jit(solution)/shard_map/ppermute | solution.py:895
  319.9 2.8 copy-start.24
  319.9 2.8 copy-start.25
  322.7 0.7 copy-start.26
  381.4 16.4 %collective-permute-start.15 = (bf16[768,384]{1,0:T(8,128)(2,1)}, bf16[768,384]{1,0:T(8,128)(2,1)S(1)}, u32[]{:S(2)}, u32[]{:S(2)}) collective-permute-start(bf16[768,384]{1,0:T(8,128)(2,1)} %get-tuple-element.81), channel_id=1, source_target_pairs={{0,4},{4,0},{1,5},{5,1},{16,20},{20,16},{17,21},{21,17},{2,6},{6,2... | collective-permute-start | bytes 1769480 | tf_op jit(solution)/shard_map/ppermute | solution.py:895
  383.5 14.3 %collective-permute-start.16 = (bf16[768,384]{1,0:T(8,128)(2,1)}, bf16[768,384]{1,0:T(8,128)(2,1)S(1)}, u32[]{:S(2)}, u32[]{:S(2)}) collective-permute-start(bf16[768,384]{1,0:T(8,128)(2,1)} %get-tuple-element.82), channel_id=1, source_target_pairs={{0,1},{4,5},{1,0},{5,4},{16,17},{20,21},{17,16},{21,20},{2,3},{6,7... | collective-permute-start | bytes 1769480 | tf_op jit(solution)/shard_map/ppermute | solution.py:895
  383.5 26.2 %collective-permute-start.17 = (bf16[768,384]{1,0:T(8,128)(2,1)}, bf16[768,384]{1,0:T(8,128)(2,1)S(1)}, u32[]{:S(2)}, u32[]{:S(2)}) collective-permute-start(bf16[768,384]{1,0:T(8,128)(2,1)} %get-tuple-element.83), channel_id=1, source_target_pairs={{0,5},{4,1},{1,4},{5,0},{16,21},{20,17},{17,20},{21,16},{2,7},{6,3... | collective-permute-start | bytes 1769480 | tf_op jit(solution)/shard_map/ppermute | solution.py:895
  397.8 11.9 %copy-start.18 = (bf16[768,384]{1,0:T(8,128)(2,1)}, bf16[768,384]{1,0:T(8,128)(2,1)S(1)}, u32[]{:S(2)}) copy-start(bf16[768,384]{1,0:T(8,128)(2,1)S(1)} %collective-permute-done.15.refs_1_) | copy-start | bytes 1769476
  397.8 11.9 %copy-start.19 = (bf16[768,384]{1,0:T(8,128)(2,1)}, bf16[768,384]{1,0:T(8,128)(2,1)S(1)}, u32[]{:S(2)}) copy-start(bf16[768,384]{1,0:T(8,128)(2,1)S(1)} %collective-permute-done.16.refs_2_) | copy-start | bytes 1769476
  409.7 0.8 copy-start.20
  410.5 19.4 %copy-start.12 = (f32[8,512]{1,0:T(8,128)S(1)}, f32[8,512]{1,0:T(8,128)}, u32[]{:S(2)}) copy-start(f32[8,512]{1,0:T(8,128)} %get-tuple-element.106) | copy-start | bytes 49156
  424.0 6.8 collective-permute-start.19
  425.3 5.9 collective-permute-start.18
  430.8 0.6 copy-start.27
  431.2 0.6 copy-start.28
  487.5 12.9 %copy-start.11 = (f32[8,2048]{1,0:T(8,128)S(1)}, f32[8,2048]{1,0:T(8,128)}, u32[]{:S(2)}) copy-start(f32[8,2048]{1,0:T(8,128)} %get-tuple-element.104) | copy-start | bytes 196612
  487.5 13.1 %copy-start.8 = (f32[72,2048]{1,0:T(8,128)S(1)}, f32[72,2048]{1,0:T(8,128)}, u32[]{:S(2)}) copy-start(f32[72,2048]{1,0:T(8,128)} %get-tuple-element.107) | copy-start | bytes 1769476
  498.8 4.8 copy-start.4
  501.2 3.9 copy-start.7
  503.6 2.6 copy-start.6
  503.6 3.7 copy-start.5
  505.1 3.4 copy-start.9
  506.1 3.2 copy-start.3
  508.5 2.4 copy-start.2
  513.1 1.1 copy-start.13
  513.1 1.8 copy-start.14
  514.3 1.4 collective-permute-start.11
  515.0 0.7 collective-permute-start.20
Sparse Core Ops, SparseCore 0:
  18.9 106.3 all-gather.2
  513.3 166.3 reduce-scatter.1

commit v3 on v2

--- a/solution.py
+++ b/solution.py
@@ -40,7 +40,13 @@
     return lax.dot_general(a, b, (((0,), (0,)), ((), ())), preferred_element_type=F32)
 
 
-def whole_call(kernel, outs, args, scratch=(), scalars=1, flops=0):
+def whole_call(kernel, outs, args, scratch=(), scalars=1, micros=0, ties=()):
+    if ties:
+        inner, fixed, count = kernel, len(args), len(ties)
+
+        def kernel(*refs):
+            inner(*refs[:fixed], *refs[fixed + count :])
+
     vm = pl.BlockSpec(memory_space=pltpu.VMEM)
     sm = pl.BlockSpec(memory_space=pltpu.SMEM)
     outs = [jax.ShapeDtypeStruct(shape, dtype) for shape, dtype in outs]
@@ -48,12 +54,15 @@
     return pl.pallas_call(
         kernel,
         out_shape=outs,
-        in_specs=[sm] * scalars + [vm] * (len(args) - scalars),
+        in_specs=[sm] * scalars + [vm] * (len(args) - scalars)
+        + [pl.BlockSpec(memory_space=pl.ANY)] * len(ties),
         out_specs=[vm] * len(outs),
         scratch_shapes=[pltpu.VMEM(shape, dtype) for shape, dtype in scratch],
         compiler_params=pltpu.CompilerParams(vmem_limit_bytes=VMEM),
-        cost_estimate=pl.CostEstimate(flops=flops, bytes_accessed=moved, transcendentals=0),
-    )(*args)
+        cost_estimate=pl.CostEstimate(
+            flops=int(micros * 1.15e9), bytes_accessed=moved, transcendentals=0
+        ),
+    )(*args, *ties)
 
 
 def normalise(v):
@@ -101,11 +110,76 @@
     return base + lax.broadcasted_iota(jnp.int32, (rows, lanes), 0)
 
 
-def blocks_of(value):
-    return value.astype(BF).reshape(BLOCKS, value.shape[0] // BLOCKS, value.shape[1])
-
-
-def front1_kernel(tile, x_ref, g1, glu, g2, h1_ref, y2_ref, joined_ref):
+ROWS = {"glu": 16, "wide": 16, "narrow": 48, "point": 64, "qkv": 16, "attn": 16, "up": 16, "down": 64, "small": 16}
+
+
+def columns_of(name, *chunks):
+    return [(name, j) for j in chunks]
+
+
+WIDE, GLU, QKV, UP = (columns_of(n, *range(k)) for n, k in (("wide", 8), ("glu", 4), ("qkv", 6), ("up", 8)))
+NARROW_0, POINT_0, SMALL_0 = (columns_of(n, 0) for n in ("narrow", "point", "small"))
+ATTN, DOWN = columns_of("attn", 0, 1), columns_of("down", 0, 1)
+LAST = (UP + ATTN[:1], ATTN[1:] + DOWN)
+GATHERS = ((WIDE + QKV[:5], GLU + NARROW_0 + SMALL_0 + QKV[5:] + POINT_0), LAST)
+SUMS = (
+    LAST,
+    (QKV[:5], QKV[5:] + POINT_0),
+    (WIDE[:6], WIDE[6:] + NARROW_0),
+    (GLU[:2], GLU[2:] + SMALL_0),
+)
+
+
+def height(items):
+    return sum(ROWS[name] for name, _ in items)
+
+
+def row_of(items, item):
+    return height(items[: items.index(item)])
+
+
+def slot_bits(half, r):
+    high, low, z = r >> 3, r >> 2 & 1, r & 3
+    x, y = (high, low) if half == 0 else (low, high)
+    return z * 8 + y * 4 + x * 2
+
+
+def slot_of(half, rel):
+    z, y, x, c = rel >> 3, rel >> 2 & 1, rel >> 1 & 1, rel & 1
+    high, low = (x, y) if half == 0 else (y, x)
+    return c * 16 + high * 8 + low * 4 + z
+
+
+def unpack(me, group, pieces, wanted):
+    for half, items in enumerate(GATHERS[group]):
+        for core in range(2):
+            piece = pieces[half * 2 + core]
+            for r in range(BLOCKS // 2):
+                owner = (slot_bits(half, r) + core) ^ me
+                for name, j in items:
+                    if name in wanted:
+                        b, off = ROWS[name], row_of(items, (name, j))
+                        wanted[name][
+                            pl.ds(pl.multiple_of(owner * b, 16), b), j * PACK : (j + 1) * PACK
+                        ] = piece[r, off : off + b, :]
+
+
+def put(me, group, ref, item, value, start=0):
+    half = int(item in SUMS[group][1])
+    off = row_of(SUMS[group][half], item) + half * height(SUMS[group][0])
+    b = ROWS[item[0]]
+    for k in range(value.shape[0] // b):
+        slot = slot_of(half, (start + k) ^ me)
+        ref[slot, off : off + b, :] = value[k * b : (k + 1) * b]
+
+
+def group_grads(group):
+    return [((BLOCKS, height(sum(SUMS[group], [])), PACK), BF)]
+
+
+def front1_kernel(tile, scal, x_ref, g1, g2, p0, p1, p2, p3, h1_ref, y2_ref, joined_ref, glu):
+    unpack(scal[2], 0, (p0, p1, p2, p3), {"glu": glu})
+
     def step(i, carry):
         at = rows_at(i, tile)
         x = x_ref[at, :].astype(F32)
@@ -121,18 +195,21 @@
     lax.fori_loop(0, x_ref.shape[0] // tile, step, 0)
 
 
-def front1(x, g1, glu, g2):
+def front1(scal, x, g1, g2, pieces, ties=()):
     rows = x.shape[0]
     return whole_call(
         functools.partial(front1_kernel, 160),
         [((rows, D), F32), ((rows, D), BF), ((rows, 2 * D), F32)],
-        [x, g1, glu, g2],
-        scalars=0,
-        flops=4 * rows * D * D,
-    )
-
-
-def front2_kernel(tile, group, scal, y2_ref, wide, narrow, g3, left_ref, right_ref, mid_ref, u_ref):
+        [scal, x, g1, g2, *pieces],
+        scratch=[((D, 2 * D), BF)],
+        ties=ties,
+        micros=9,
+    )
+
+
+def front2_kernel(tile, group, scal, y2_ref, g3, p0, p1, p2, p3, *refs):
+    left_ref, right_ref, mid_ref, u_ref, wide, narrow = refs
+    unpack(scal[2], 0, (p0, p1, p2, p3), {"wide": wide, "narrow": narrow})
     rows = y2_ref.shape[0]
     base = scal[0] * (rows - 2 * RIM) - RIM
     first = scal[1]
@@ -172,14 +249,15 @@
     lax.fori_loop(0, rows // tile, step, 0)
 
 
-def front2(scal, y2, wide, narrow, g3, group):
+def front2(scal, y2, g3, pieces, group, ties=()):
     rows = y2.shape[0]
     return whole_call(
         functools.partial(front2_kernel, 160, group),
         [((rows, FF), F32), ((rows, NARROW), F32), ((rows, FF), BF)],
-        [scal, y2, wide, narrow, g3],
-        scratch=[((rows + 2 * RIM, 3 * NARROW), F32)],
-        flops=2 * rows * D * (FF + 3 * NARROW),
+        [scal, y2, g3, *pieces],
+        scratch=[((rows + 2 * RIM, 3 * NARROW), F32), ((D, FF), BF), ((3 * D, NARROW), BF)],
+        ties=ties,
+        micros=14,
     )
 
 
@@ -201,10 +279,11 @@
     return total
 
 
-def front3_kernel(tile, n, share, scal, mid_ref, taps, point, h1_ref, g4, qkv_w, *refs):
+def front3_kernel(tile, n, share, scal, mid_ref, taps, h1_ref, g4, p0, p1, p2, p3, *refs):
     spread_ref, h2_ref, y4_ref = refs[:3]
     outs = refs[3 : 3 + n]
-    win, qkv_s = refs[3 + n :]
+    win, qkv_s, point, qkv_w = refs[3 + n :]
+    unpack(scal[2], 0, (p0, p1, p2, p3), {"point": point, "qkv": qkv_w})
     rows = h2_ref.shape[0]
     s, first = scal[0], scal[1]
     base = s * rows
@@ -249,24 +328,28 @@
     lax.fori_loop(0, rows // tile, step, 0)
 
 
-def front3(scal, mid, taps, point, h1, g4, qkv_w, n, share):
+def front3(scal, mid, taps, h1, g4, pieces, n, share, ties=()):
     rows = mid.shape[0] - 2 * RIM
     tile = 128
     return whole_call(
         functools.partial(front3_kernel, tile, n, share),
         [((rows, FF), BF), ((rows, D), F32), ((rows, D), BF)] + [((rows, 3 * LANES), BF)] * n,
-        [scal, mid, taps, point, h1, g4, qkv_w],
-        scratch=[((tile + 2 * RIM, LANES), F32), ((tile, 3 * D), BF)],
-        flops=2 * rows * (FF * NARROW + 3 * D * D),
+        [scal, mid, taps, h1, g4, *pieces],
+        scratch=[((tile + 2 * RIM, LANES), F32), ((tile, 3 * D), BF)]
+        + [((FF, NARROW), BF), ((D, 3 * D), BF)],
+        ties=ties,
+        micros=22,
     )
 
 
 def middle_kernel(tile, n, share, scal, h2_ref, *refs):
     att = refs[:n]
-    cot_ref, g5, wa, wup, wdown, mixed_ref, dh3_ref = refs[n : n + 7]
-    datt = refs[n + 7 : 2 * n + 7]
-    ga_ref, gup_ref, gdown_ref, ln_ref = refs[2 * n + 7 : 2 * n + 11]
-    att_s, y5_s, inner_s, du_s, db_s = refs[2 * n + 11 :]
+    cot_ref, g5, p0, p1, p2, p3, mixed_ref, dh3_ref = refs[n : n + 8]
+    datt = refs[n + 8 : 2 * n + 8]
+    grads, ln_out = refs[2 * n + 8 : 2 * n + 10]
+    att_s, y5_s, inner_s, du_s, db_s, wa, wup, wdown, ln_ref = refs[2 * n + 10 :]
+    me = scal[2]
+    unpack(me, 1, (p0, p1, p2, p3), {"attn": wa, "up": wup, "down": wdown})
     rows = h2_ref.shape[0]
     s = scal[0]
     for k in range(n):
@@ -312,47 +395,51 @@
         return carry
 
     lax.fori_loop(0, rows // tile, step, 0)
+    ln_out[...] = jnp.sum(ln_ref[...], axis=0, keepdims=True)
     att_t = att_s[...].T
     for j in range(D // PACK):
-        ga_ref[:, j * 16 : (j + 1) * 16, :] = blocks_of(
-            nn(att_t, db_s[:, j * PACK : (j + 1) * PACK])
-        )
+        put(me, 0, grads, ("attn", j), nn(att_t, db_s[:, j * PACK : (j + 1) * PACK]).astype(BF))
     y5_t = y5_s[...].T
     for j in range(FF // PACK):
         cols = slice(j * PACK, (j + 1) * PACK)
-        gup_ref[:, j * 16 : (j + 1) * 16, :] = blocks_of(nn(y5_t, du_s[:, cols]))
+        put(me, 0, grads, ("up", j), nn(y5_t, du_s[:, cols]).astype(BF))
         down = tn(inner_s[:, cols], cot_ref[...]).astype(BF)
         for m in range(D // PACK):
-            gdown_ref[j * 4 : (j + 1) * 4, m * 64 : (m + 1) * 64, :] = down[
-                :, m * PACK : (m + 1) * PACK
-            ].reshape(4, 64, PACK)
-
-
-def middle(scal, h2, att, cot, g5, wa, wup, wdown, n, share):
+            put(me, 0, grads, ("down", m), down[:, m * PACK : (m + 1) * PACK], j * PACK // 64)
+
+
+def middle(scal, h2, att, cot, g5, pieces, n, share, ties=()):
     rows = h2.shape[0]
     return whole_call(
         functools.partial(middle_kernel, 128, n, share),
         [((rows, D), BF), ((rows, D), F32)]
         + [((rows, LANES), BF)] * n
-        + [((BLOCKS, 32, PACK), BF), ((BLOCKS, 128, PACK), BF), ((BLOCKS, 128, PACK), BF)]
-        + [((8, D), F32)],
-        [scal, h2, *att, cot, g5, wa, wup, wdown],
+        + group_grads(0)
+        + [((1, D), F32)],
+        [scal, h2, *att, cot, g5, *pieces],
         scratch=[
             ((rows, D), BF),
             ((rows, D), BF),
             ((rows, FF), BF),
             ((rows, FF), BF),
             ((rows, D), BF),
+            ((D, D), BF),
+            ((D, FF), BF),
+            ((FF, D), BF),
+            ((8, D), F32),
         ],
-        flops=6 * rows * (2 * D * FF + D * D),
+        ties=ties,
+        micros=29,
     )
 
 
 def back3_kernel(tile, n, share, scal, *refs):
     blocks = refs[:n]
-    dh3_ref, h2_ref, y4_ref, spread_ref, g4, qkv_w = refs[n : n + 6]
-    dh2_ref, db_ref, gqkv_ref, gpoint_ref, ln_ref = refs[n + 6 : n + 11]
-    (dqkv_s,) = refs[n + 11 :]
+    dh3_ref, h2_ref, y4_ref, spread_ref, g4, p0, p1, p2, p3 = refs[n : n + 9]
+    dh2_ref, db_ref, grads, ln_out = refs[n + 9 : n + 13]
+    dqkv_s, qkv_w, ln_ref = refs[n + 13 :]
+    me = scal[2]
+    unpack(me, 0, (p0, p1, p2, p3), {"qkv": qkv_w})
     rows = h2_ref.shape[0]
     s = scal[0]
     for k in range(n):
@@ -378,33 +465,32 @@
         return carry
 
     lax.fori_loop(0, rows // tile, step, 0)
+    ln_out[...] = jnp.sum(ln_ref[...], axis=0, keepdims=True)
     y4_t = y4_ref[...].T
     for j in range(3 * D // PACK):
-        gqkv_ref[:, j * 16 : (j + 1) * 16, :] = blocks_of(
-            nn(y4_t, dqkv_s[:, j * PACK : (j + 1) * PACK])
-        )
+        put(me, 1, grads, ("qkv", j), nn(y4_t, dqkv_s[:, j * PACK : (j + 1) * PACK]).astype(BF))
     for j in range(FF // PACK):
-        gpoint_ref[j * PACK : (j + 1) * PACK, :] = tn(
-            spread_ref[:, j * PACK : (j + 1) * PACK], db_ref[...]
-        ).astype(BF)
-
-
-def back3(scal, blocks, dh3, h2, y4, spread, g4, qkv_w, n, share):
+        part = tn(spread_ref[:, j * PACK : (j + 1) * PACK], db_ref[...]).astype(BF)
+        put(me, 1, grads, ("point", 0), part, j * PACK // 64)
+
+
+def back3(scal, blocks, dh3, h2, y4, spread, g4, pieces, n, share, ties=()):
     rows = h2.shape[0]
     return whole_call(
         functools.partial(back3_kernel, 128, n, share),
-        [((rows, D), F32), ((rows, NARROW), BF), ((BLOCKS, 96, PACK), BF)]
-        + [((FF, PACK), BF), ((8, D), F32)],
-        [scal, *blocks, dh3, h2, y4, spread, g4, qkv_w],
-        scratch=[((rows, 3 * D), BF)],
-        flops=4 * rows * D * 3 * D + 2 * rows * FF * NARROW,
+        [((rows, D), F32), ((rows, NARROW), BF)] + group_grads(1) + [((1, D), F32)],
+        [scal, *blocks, dh3, h2, y4, spread, g4, *pieces],
+        scratch=[((rows, 3 * D), BF), ((D, 3 * D), BF), ((8, D), F32)],
+        ties=ties,
+        micros=15,
     )
 
 
 def back2_kernel(tile, group, scal, low_ref, db_ref, high_ref, *refs):
-    point, taps, mid_ref, left_ref, right_ref, wide, narrow, y2_ref, g3 = refs[:9]
-    dy2_ref, gwide_ref, gnarrow_ref, gdepth_ref, ln_ref = refs[9:14]
-    dbx, dsp, win, dmid, dl, dr, st = refs[14:]
+    taps, mid_ref, left_ref, right_ref, g3 = refs[:5]
+    pieces, (dl, st, gdepth_out, ln_out) = refs[5:9], refs[9:13]
+    dbx, dsp, win, dmid, dr, point, gdepth_ref, ln_ref = refs[13:]
+    unpack(scal[2], 0, pieces, {"point": point})
     rows = db_ref.shape[0]
     ext = rows + 2 * RIM
     base = scal[0] * rows - RIM
@@ -475,6 +561,9 @@
         return carry
 
     lax.fori_loop(0, ext // tile, step, 0)
+    for k in range(KERNEL):
+        gdepth_out[k : k + 1, :] = jnp.sum(gdepth_ref[k * 8 : (k + 1) * 8, :], axis=0, keepdims=True)
+    ln_out[...] = jnp.sum(ln_ref[...], axis=0, keepdims=True)
     part = 128
 
     def gather_step(i, carry):
@@ -484,63 +573,80 @@
         v = dr[around, :]
         after = pltpu.roll(v, part + 2 * RIM - 1, 0)[RIM : RIM + part]
         before = pltpu.roll(v, 1, 0)[RIM : RIM + part]
-        after = jnp.where((pos + 1 == first) | (pos + 1 == group), 0.0, after).astype(BF)
-        before = jnp.where((pos == first) | (pos == 0), 0.0, before).astype(BF)
-        here = v[RIM : RIM + part].astype(BF)
-        st[at, 0:NARROW] = after
-        st[at, NARROW : 2 * NARROW] = here
-        st[at, 2 * NARROW :] = before
-        dy2 = nt(dl[rows_at(i, part, RIM), :], wide[...])
-        for k, v in enumerate((after, here, before)):
-            dy2 = dy2 + nt(v, narrow[k * D : (k + 1) * D, :])
-        dy2_ref[at, :] = dy2
+        after = jnp.where((pos + 1 == first) | (pos + 1 == group), 0.0, after)
+        before = jnp.where((pos == first) | (pos == 0), 0.0, before)
+        st[at, 0:NARROW] = after.astype(BF)
+        st[at, NARROW : 2 * NARROW] = v[RIM : RIM + part].astype(BF)
+        st[at, 2 * NARROW :] = before.astype(BF)
         return carry
 
     lax.fori_loop(0, rows // part, gather_step, 0)
-    y2_t = y2_ref[RIM : RIM + rows, :].T
-    for j in range(FF // PACK):
-        gwide_ref[:, j * 16 : (j + 1) * 16, :] = blocks_of(
-            nn(y2_t, dl[RIM : RIM + rows, j * PACK : (j + 1) * PACK])
-        )
-    for k in range(3):
-        gnarrow_ref[k * D : (k + 1) * D, :] = nn(
-            y2_t, st[:, k * NARROW : (k + 1) * NARROW]
-        ).astype(BF)
-
-
-def back2(scal, low, db, high, point, taps, mid, left, right, wide, narrow, y2, g3, group):
+
+
+def back2(scal, low, db, high, taps, mid, left, right, g3, pieces, group, ties=()):
     rows = db.shape[0]
     ext = rows + 2 * RIM
     tile = 160
     return whole_call(
         functools.partial(back2_kernel, tile, group),
-        [((rows, D), F32), ((BLOCKS, 128, PACK), BF), ((3 * D, NARROW), BF)]
-        + [((8 * KERNEL, FF), F32), ((8, FF), F32)],
-        [scal, low, db, high, point, taps, mid, left, right, wide, narrow, y2, g3],
+        [((ext, FF), BF), ((rows, 3 * NARROW), BF), ((KERNEL, FF), F32), ((1, FF), F32)],
+        [scal, low, db, high, taps, mid, left, right, g3, *pieces],
         scratch=[
             ((ext, NARROW), BF),
             ((ext + 2 * RIM, FF), F32),
             ((tile + 2 * RIM, LANES), F32),
             ((tile, FF), F32),
-            ((ext, FF), BF),
             ((ext + 2 * RIM, NARROW), F32),
-            ((rows, 3 * NARROW), BF),
+            ((FF, NARROW), BF),
+            ((8 * KERNEL, FF), F32),
+            ((8, FF), F32),
         ],
-        flops=2 * rows * (FF * NARROW + 2 * FF * D + 6 * D * NARROW),
-    )
-
-
-def back1_kernel(tile, dy2_ref, dh2_ref, h1_ref, joined_ref, x_ref, g1, g2, glu, *refs):
-    dx_ref, gglu_ref, ln1_ref, ln2_ref, y1_s, dj_s = refs
-    rows = dy2_ref.shape[0]
+        ties=ties,
+        micros=49,
+    )
+
+
+def weigh2_kernel(scal, dl, st, y2_ref, grads, gn):
+    me = scal[2]
+    rows = st.shape[0]
+    y2_t = y2_ref[RIM : RIM + rows, :].T
+    for j in range(FF // PACK):
+        part = nn(y2_t, dl[RIM : RIM + rows, j * PACK : (j + 1) * PACK]).astype(BF)
+        put(me, 2, grads, ("wide", j), part)
+    for k in range(3):
+        gn[k * D : (k + 1) * D, :] = nn(y2_t, st[:, k * NARROW : (k + 1) * NARROW]).astype(BF)
+    put(me, 2, grads, ("narrow", 0), gn[...])
+
+
+def weigh2(scal, dl, st, y2, ties=()):
+    return whole_call(
+        weigh2_kernel,
+        group_grads(2),
+        [scal, dl, st, y2],
+        scratch=[((3 * D, NARROW), BF)],
+        ties=ties,
+        micros=7,
+    )
+
+
+def back1_kernel(tile, scal, dl, st, dh2_ref, h1_ref, joined_ref, x_ref, g1, g2, *refs):
+    p0, p1, p2, p3, dx_ref, grads, ln1_out, ln2_out = refs[:8]
+    y1_s, dj_s, glu, wide, narrow, ln1_ref, ln2_ref = refs[8:]
+    rows = st.shape[0]
+    me = scal[2]
+    unpack(me, 0, (p0, p1, p2, p3), {"glu": glu, "wide": wide, "narrow": narrow})
     ln1_ref[...] = jnp.zeros_like(ln1_ref)
     ln2_ref[...] = jnp.zeros_like(ln2_ref)
 
     def step(i, carry):
         at = rows_at(i, tile)
         ext = rows_at(i, tile, RIM)
+        dy2 = nt(dl[ext, :], wide[...])
+        for k in range(3):
+            dy2 = dy2 + nt(
+                st[at, k * NARROW : (k + 1) * NARROW], narrow[k * D : (k + 1) * D, :]
+            )
         hat2, r2 = normalise(h1_ref[ext, :])
-        dy2 = dy2_ref[at, :]
         ln2_ref[...] += fold8(dy2 * hat2)
         dh1 = dh2_ref[at, :] + norm_back(dy2, hat2, r2, g2[...])
         gate = sigmoid(joined_ref[ext, D:])
@@ -558,22 +664,23 @@
         return carry
 
     lax.fori_loop(0, rows // tile, step, 0)
+    ln1_out[...] = jnp.sum(ln1_ref[...], axis=0, keepdims=True)
+    ln2_out[...] = jnp.sum(ln2_ref[...], axis=0, keepdims=True)
     y1_t = y1_s[...].T
     for j in range(2 * D // PACK):
-        gglu_ref[:, j * 16 : (j + 1) * 16, :] = blocks_of(
-            nn(y1_t, dj_s[:, j * PACK : (j + 1) * PACK])
-        )
-
-
-def back1(dy2, dh2, h1, joined, x, g1, g2, glu):
-    rows = dy2.shape[0]
+        put(me, 3, grads, ("glu", j), nn(y1_t, dj_s[:, j * PACK : (j + 1) * PACK]).astype(BF))
+
+
+def back1(scal, dl, st, dh2, h1, joined, x, g1, g2, pieces, ties=()):
+    rows = st.shape[0]
     return whole_call(
         functools.partial(back1_kernel, 128),
-        [((rows, D), BF), ((BLOCKS, 64, PACK), BF), ((8, D), F32), ((8, D), F32)],
-        [dy2, dh2, h1, joined, x, g1, g2, glu],
-        scratch=[((rows, D), BF), ((rows, 2 * D), BF)],
-        scalars=0,
-        flops=8 * rows * D * D,
+        [((rows, D), BF), ((BLOCKS, height(GLU), PACK), BF), ((1, D), F32), ((1, D), F32)],
+        [scal, dl, st, dh2, h1, joined, x, g1, g2, *pieces],
+        scratch=[((rows, D), BF), ((rows, 2 * D), BF), ((D, 2 * D), BF)]
+        + [((D, FF), BF), ((3 * D, NARROW), BF), ((8, D), F32), ((8, D), F32)],
+        ties=ties,
+        micros=20,
     )
 
 
@@ -674,7 +781,7 @@
         return carry
     lax.fori_loop(0, n*per, q_step, 0)
 
-def attend(scal, blocks, n, share, tq=768, tk=384):
+def attend(scal, blocks, n, share, tq=768, tk=384, ties=()):
     rows = blocks[0].shape[0]
     heads = 2 // share
     return whole_call(
@@ -684,7 +791,8 @@
         scratch=[((heads, n * rows, LANES), BF)] * 3
         + [((heads, tq, LANES), F32)] * 2
         + [((heads, tq, LANES), BF), ((heads, tq, LANES), F32)],
-        flops=4 * n * rows * n * rows * HEAD * heads,
+        ties=ties,
+        micros=36,
     )
 
 
@@ -765,7 +873,7 @@
             dq = jnp.where(own, dq_ref[i,sl,:], dq)
         out[k][:, 0:LANES] = (dq*(HEAD**-0.5)).astype(BF)
 
-def attend_back(scal, blocks, att, datt, lse, n, share, tq=384, tk=384):
+def attend_back(scal, blocks, att, datt, lse, n, share, tq=384, tk=384, ties=()):
     rows = blocks[0].shape[0]
     heads = 2 // share
     return whole_call(
@@ -775,74 +883,131 @@
         scratch=[((heads, n * rows, LANES), BF)] * 4
         + [((heads, n * rows, LANES), F32)]
         + [((heads, tk, LANES), F32)] * 2,
-        flops=10 * n * rows * n * rows * HEAD * heads,
-    )
-
-
-def pack_block(block):
-    rows, columns = block.shape
-    return block.reshape(rows, columns // PACK, PACK).transpose(1, 0, 2).reshape(-1, PACK)
-
-
-def pack_small(blocks):
-    flat = jnp.concatenate(blocks, axis=-1)
-    rows = -(-flat.shape[-1] // (16 * PACK)) * 16
-    pad = [(0, 0)] * (flat.ndim - 1) + [(0, rows * PACK - flat.shape[-1])]
-    return jnp.pad(flat, pad).reshape(flat.shape[:-1] + (rows, PACK))
-
-
-def gather_all(weights):
-    small = [w for w in weights if w.ndim == 1]
-    packed = [pack_block(w) for w in weights if w.ndim == 2] + [pack_small(small)]
-    local = jnp.concatenate(packed, axis=0)
-    whole = lax.all_gather(local, AXES, axis=0, tiled=False)
-    count = whole.shape[0]
-    tail = whole[:, -packed[-1].shape[0] :].reshape(count, -1)
-    result, start, place = [], 0, 0
-    for w in weights:
-        if w.ndim == 1:
-            result.append(tail[:, place : place + w.shape[0]].reshape(-1))
-            place += w.shape[0]
-        else:
-            rows, columns = w.shape
-            chunks = columns // PACK
-            part = whole[:, start : start + rows * chunks].reshape(count, chunks, rows, PACK)
-            result.append(part.transpose(0, 2, 1, 3).reshape(count * rows, columns))
-            start += rows * chunks
+        ties=ties,
+        micros=58,
+    )
+
+
+class Links:
+    def __init__(self, n_seq, n_dp):
+        self.count = n_seq * n_dp
+        self.direct = (n_seq, n_dp) == (4, 8)
+
+    def flip(self, value, mask):
+        return lax.ppermute(value, AXES, [(i, i ^ mask) for i in range(self.count)])
+
+    def near(self, group, weights):
+        blocks = [
+            weights[name][:, j * PACK : (j + 1) * PACK] for name, j in sum(GATHERS[group], [])
+        ]
+        block = jnp.concatenate(blocks, axis=0)
+        return jnp.stack([block] + [self.flip(block, k << 3) for k in range(1, 4)])
+
+    def part(self, group, held):
+        low = height(GATHERS[group][0])
+        return [held[:, :low], held[:, low:]]
+
+    def spread(self, held, stage):
+        masks = ((4, 2), (2, 4))[stage]
+        return [jnp.concatenate([h, self.flip(h, m)]) for h, m in zip(held, masks)]
+
+    def across(self, held):
+        return [held[0], self.flip(held[0], 1), held[1], self.flip(held[1], 1)]
+
+    def gather_whole(self, group, weights):
+        whole = {
+            name: lax.all_gather(weights[name], AXES, axis=0, tiled=True)
+            for name in dict(sum(GATHERS[group], []))
+        }
+        pieces = []
+        for half, items in enumerate(GATHERS[group]):
+            blocks = [
+                whole[name][:, j * PACK : (j + 1) * PACK].reshape(BLOCKS, -1, PACK)
+                for name, j in items
+            ]
+            pieces += list(self.by_slot(jnp.concatenate(blocks, axis=1), half))
+        return pieces
+
+    def by_slot(self, blocks, half):
+        shape = blocks.shape[1:]
+        order = ((3, 2, 1, 0), (3, 1, 2, 0))[half]
+        return blocks.reshape(4, 2, 2, 2, *shape).transpose(*order, 4, 5).reshape(2, 16, *shape)
+
+    def by_owner(self, slots, half):
+        shape = slots.shape[1:]
+        order = ((3, 2, 1, 0), (3, 1, 2, 0))[half]
+        return slots.reshape(2, 2, 2, 4, *shape).transpose(*order, 4, 5).reshape(BLOCKS, *shape)
+
+    def add(self, a, b):
+        return (a.astype(F32) + b.astype(F32)).astype(BF)
+
+    def fold(self, slots, mask):
+        middle = slots.shape[0] // 2
+        return self.add(slots[:middle], self.flip(slots[middle:], mask))
+
+    def first(self, group, slots):
+        held = self.fold(slots, 1)
+        low = height(SUMS[group][0])
+        return [held[:, :low], held[:, low:]]
+
+    def next(self, held, stage):
+        masks = ((2, 4), (4, 2))[stage]
+        return [self.fold(h, m) for h, m in zip(held, masks)]
+
+    def finish(self, held):
+        held = jnp.concatenate(held, axis=1)
+        total = held[0].astype(F32)
+        for k in range(1, 4):
+            total = total + self.flip(held[k], k << 3).astype(F32)
+        return total
+
+    def rows_of(self, items, total):
+        parts, at = {}, 0
+        for name, j in items:
+            b = ROWS[name] * BLOCKS // self.count
+            parts.setdefault(name, []).append(total[at : at + b])
+            at += b
+        return {name: jnp.concatenate(p, axis=1) for name, p in parts.items()}
+
+    def scatter_whole(self, group, slots):
+        sent, at = [], 0
+        for half, items in enumerate(SUMS[group]):
+            for name, _ in items:
+                blocks = self.by_owner(slots[:, at : at + ROWS[name]], half)
+                sent.append(blocks.reshape(self.count, -1, PACK))
+                at += ROWS[name]
+        sent = jnp.concatenate(sent, axis=1)
+        return lax.psum_scatter(sent, AXES, scatter_dimension=0, tiled=False).astype(F32)
+
+
+def small_block(arrays, blocks):
+    flat = jnp.concatenate([a.reshape(blocks, -1) for a in arrays], axis=1)
+    flat = jnp.pad(flat, ((0, 0), (0, 16 * PACK - flat.shape[1])))
+    return flat.reshape(blocks * 16, PACK)
+
+
+def slot_matrix(me, half):
+    slots = slot_of(half, lax.iota(jnp.int32, BLOCKS) ^ me)
+    return (slots[:, None] == lax.iota(jnp.int32, BLOCKS)[None, :]).astype(BF)
+
+
+def small_from(pieces, me, sizes):
+    off = row_of(GATHERS[0][1], SMALL_0[0])
+    used = -(-sum(sizes) // PACK)
+    rows = jnp.concatenate([pieces[2][:, off : off + used], pieces[3][:, off : off + used]])
+    rows = nn(slot_matrix(me, 1), rows.reshape(BLOCKS, used * PACK))
+    result, at = [], 0
+    for size in sizes:
+        result.append(rows[:, at : at + size].reshape(-1))
+        at += size
     return result
 
 
-def to_owners(grad, w, count):
-    if grad.ndim == 2:
-        return grad.reshape(count, -1, PACK)
-    finer = count // BLOCKS
-    if finer == 1:
-        return grad
-    rows, columns = w.shape
-    part = grad.reshape(BLOCKS, columns // PACK, finer, rows, PACK)
-    return part.transpose(0, 2, 1, 3, 4).reshape(count, -1, PACK)
-
-
-def scatter_all(grads, weights):
-    count = lax.axis_size("seq") * lax.axis_size("dp")
-    small = [g.reshape(count, -1) for g, w in zip(grads, weights) if w.ndim == 1]
-    packed = [to_owners(g, w, count) for g, w in zip(grads, weights) if w.ndim == 2]
-    packed.append(pack_small(small).astype(BF))
-    send = jnp.concatenate(packed, axis=1)
-    total = lax.psum_scatter(send, AXES, scatter_dimension=0, tiled=False).astype(F32)
-    tail = total[-packed[-1].shape[1] :].reshape(-1)
-    result, start, place = [], 0, 0
-    for w in weights:
-        if w.ndim == 1:
-            result.append(tail[place : place + w.shape[0]])
-            place += w.shape[0]
-        else:
-            rows, columns = w.shape
-            chunks = columns // PACK
-            part = total[start : start + rows * chunks].reshape(chunks, rows, PACK)
-            result.append(part.transpose(1, 0, 2).reshape(rows, columns))
-            start += rows * chunks
-    return result
+def small_to(arrays, me):
+    flat = jnp.concatenate([a.reshape(BLOCKS, -1) for a in arrays], axis=1).astype(BF)
+    flat = tn(slot_matrix(me, 1), flat).astype(BF)
+    flat = jnp.pad(flat, ((0, 0), (0, 16 * PACK - flat.shape[1])))
+    return flat.reshape(BLOCKS, 16, PACK)
 
 
 class Layout:
@@ -897,68 +1062,139 @@
         ]
 
 
+NAMES = ("ln1", "ln2", "ln3", "ln4", "ln5", "glu", "wide", "narrow", "depth", "point", "qkv", "attn", "up", "down")
+SMALL = ("ln1", "ln2", "ln3", "ln4", "ln5", "depth")
+
+
+def after(value, *others):
+    return lax.optimization_barrier((value, *others))[0]
+
+
 def on_device(tokens, cotangent, first_length, *weights):
     n = lax.axis_size("seq")
     n_dp = lax.axis_size("dp")
     share = n * LANES // D
     layout = Layout(n, n_dp)
+    links = Links(n, n_dp)
     rows = tokens.shape[1]
     group = n * rows
     me = lax.axis_index("seq") * n_dp + lax.axis_index("dp")
     s = jnp.asarray(layout.block)[me]
-
+    mine = dict(zip(NAMES, weights))
+    if links.direct:
+        mine["small"] = small_block([mine[k] for k in SMALL], 1)
+    else:
+        me = jnp.zeros_like(me)
+        small = [lax.all_gather(mine[k], AXES, axis=0, tiled=True) for k in SMALL]
+        small = small_block(small, BLOCKS).reshape(links.count, -1, PACK)
+        mine["small"] = small[lax.axis_index("seq") * n_dp + lax.axis_index("dp")]
+
+    direct = links.direct
     tokens = tokens[0]
-    x = layout.bring(tokens)
+    lane = lax.broadcasted_iota(jnp.int32, (RIM, D), 1)
+    digits = jnp.where(lane < LANES, first_length[0] // LANES, first_length[0] % LANES)
+    held = links.near(0, mine) if direct else ()
+    x = layout.bring(jnp.concatenate([tokens, digits.astype(BF)], axis=0))
+    digits = x[rows, 0 : 2 * LANES : LANES].astype(F32).astype(jnp.int32)
+    first = digits[0] * LANES + digits[1]
     low = layout.bring_to(tokens[-RIM:], 1)
     high = layout.bring_to(tokens[:RIM], -1)
-    first = layout.bring(first_length)[0]
-    scal = jnp.stack([s.astype(jnp.int32), first])
-    cot = layout.bring(cotangent[0])
-    x_ext = jnp.concatenate([low, x, high], axis=0)
-
-    params = gather_all(weights)
-    g1, g2, g3, g4, g5 = (p.astype(F32)[None] for p in params[:5])
-    glu, wide, narrow, depth, point, qkv_w, wa, wup, wdown = params[5:]
+    scal = jnp.stack([s.astype(jnp.int32), first, me.astype(jnp.int32)])
+    x_ext = jnp.concatenate([low, x[:rows], high], axis=0)
+    if direct:
+        held = links.spread(links.part(0, held), 0)
+        held = [after(h, x_ext) for h in held]
+        pieces1 = links.across(links.spread(held, 1))
+    else:
+        pieces1, pieces2 = (links.gather_whole(k, mine) for k in range(2))
+    sizes = [mine[k].shape[0] * links.count // BLOCKS for k in SMALL]
+    g1, g2, g3, g4, g5, depth = small_from(pieces1, me, sizes)
+    g1, g2, g3, g4, g5 = (g.astype(F32)[None] for g in (g1, g2, g3, g4, g5))
     taps = depth.reshape(KERNEL, FF).astype(F32)
 
-    h1, y2, joined = front1(x_ext, g1, glu, g2)
-    left, right, mid = front2(scal, y2, wide, narrow, g3, group)
-    spread, h2, y4, *qkv = front3(scal, mid, taps, point, h1, g4, qkv_w, n, share)
+    ties = ()
+    if direct:
+        late = dict(mine)
+        for name in ("attn", "up", "down"):
+            late[name] = after(mine[name], *pieces1)
+        ties = held = (links.near(1, late),)
+    h1, y2, joined = front1(scal, x_ext, g1, g2, pieces1)
+    left, right, mid = front2(scal, y2, g3, pieces1, group)
+    spread, h2, y4, *qkv = front3(scal, mid, taps, h1, g4, pieces1, n, share, ties=ties)
+    cot = layout.bring(after(cotangent, mid)[0])
+    if direct:
+        ties = held = links.spread(links.part(1, held[0]), 0)
     qkv = layout.swap(qkv)
-    *att, lse = attend(scal, qkv, n, share)
-    mixed, dh3, *rest = middle(
-        scal, h2, layout.swap(att), cot, g5, wa, wup, wdown, n, share
-    )
-    datt, (ga, gup, gdown, ln5) = rest[:n], rest[n:]
-    dqkv = attend_back(scal, qkv, att, layout.swap(datt), lse, n, share)
-    dh2, db, gqkv, gpoint, ln4 = back3(
-        scal, layout.swap(dqkv), dh3, h2, y4, spread, g4, qkv_w, n, share
-    )
-    dy2, gwide, gnarrow, gdepth, ln3 = back2(
-        scal,
-        layout.to_neighbour(db[-RIM:], 1),
-        db,
-        layout.to_neighbour(db[:RIM], -1),
-        point,
-        taps,
-        mid,
-        left,
-        right,
-        wide,
-        narrow,
-        y2,
-        g3,
-        group,
-    )
-    dx, gglu, ln1, ln2 = back1(dy2, dh2, h1, joined, x_ext, g1, g2, glu)
-    ln1, ln2, ln3, ln4, ln5 = (jnp.sum(v, axis=0) for v in (ln1, ln2, ln3, ln4, ln5))
-    gdepth = jnp.sum(gdepth.reshape(KERNEL, 8, FF), axis=1).reshape(-1)
-    grads = [ln1, ln2, ln3, ln4, ln5, gglu, gwide, gnarrow, gdepth, gpoint, gqkv, ga, gup, gdown]
-    summed = scatter_all(grads, weights)
+    *att, lse = attend(scal, qkv, n, share, ties=ties)
+    if direct:
+        pieces2 = links.across(links.spread(held, 1))
+    mixed, dh3, *rest = middle(scal, h2, layout.swap(att), cot, g5, pieces2, n, share)
+    datt, sum0, ln5 = rest[:n], rest[n], rest[n + 1]
+    mixed = layout.send_home(mixed)
+    ties = ()
+    if direct:
+        ties = sum0 = links.first(0, sum0)
+    dqkv = attend_back(scal, qkv, att, layout.swap(datt), lse, n, share, ties=ties)
+    if direct:
+        sum0 = links.next(sum0, 0)
+        ties = (mixed, *sum0)
+    dqkv = layout.swap(dqkv)
+    dh2, db, sum1, ln4 = back3(
+        scal, dqkv, dh3, h2, y4, spread, g4, pieces1, n, share, ties=ties
+    )
+    low = layout.to_neighbour(db[-RIM:], 1)
+    high = layout.to_neighbour(db[:RIM], -1)
+    if direct:
+        sum0 = links.next(sum0, 1)
+        sum1 = links.first(1, sum1)
+        ties = (*sum0, *sum1)
+    dl, st, gdepth, ln3 = back2(
+        scal, low, db, high, taps, mid, left, right, g3, pieces1, group, ties=ties
+    )
+    if direct:
+        sum0 = links.finish([after(v, low, high, *sum1) for v in sum0])
+        sum1 = links.next(sum1, 0)
+        ties = (sum0, *sum1)
+    (sum2,) = weigh2(scal, dl, st, y2, ties=ties)
+    if direct:
+        sum1 = links.next(sum1, 1)
+        ties = sum1
+    dx, sum3, ln1, ln2 = back1(scal, dl, st, dh2, h1, joined, x_ext, g1, g2, pieces1, ties=ties)
+    dx = layout.send_home(dx)
+    sum3 = jnp.concatenate([sum3, small_to([ln1, ln2, ln3, ln4, ln5, gdepth], me)], axis=1)
+    if direct:
+        sum1 = links.finish(sum1)
+        sum2 = links.first(2, sum2)
+        sum3 = links.first(3, sum3)
+        held = [jnp.concatenate(v, axis=1) for v in zip(sum2, sum3)]
+        tail = links.finish(links.next(links.next(held, 0), 1))
+        sums = (sum0, sum1, tail)
+        tables = (sum(SUMS[0], []), sum(SUMS[1], []))
+        tables += (SUMS[2][0] + SUMS[3][0] + SUMS[2][1] + SUMS[3][1],)
+    else:
+        sums = [links.scatter_whole(k, v) for k, v in enumerate((sum0, sum1, sum2, sum3))]
+        tables = [sum(items, []) for items in SUMS]
+    out = {}
+    for items, total in zip(tables, sums):
+        out.update(links.rows_of(items, total))
+    flat = out.pop("small")
+    if not links.direct:
+        flat = lax.all_gather(flat, AXES, axis=0, tiled=True).reshape(BLOCKS, -1)
+    else:
+        flat = flat.reshape(1, -1)
+    at = 0
+    for name, size in zip(SMALL, sizes):
+        part = flat[:, at : at + size]
+        at += size
+        if not links.direct:
+            own = mine[name].shape[0]
+            here = lax.axis_index("seq") * n_dp + lax.axis_index("dp")
+            part = lax.dynamic_slice(part.reshape(-1), (here * own,), (own,))
+        out[name] = part.reshape(-1)
     return (
-        layout.send_home(mixed)[None],
-        layout.send_home(dx).astype(F32)[None],
-        *summed,
+        mixed[None],
+        dx.astype(F32)[None],
+        *(out[name] for name in NAMES),
     )
 
 

time: 708 us -> 598 us (0.84)
  waiting for transfers between devices: 317 us -> 155 us
  starting transfers between devices: 36.8 us -> 108 us
  local copies, waits for them, and re-layouts: 81.2 us -> 45.3 us
  Pallas kernels: 242 us -> 259 us
  other arithmetic: 6.97 us -> 19.1 us
  between operations: 14.9 us -> 4.35 us
    reduce_scatter x1 -> x0, waiting for transfers between devices: 163 us -> none  [scatter_all(): lax.psum_scatter(send, AXES, scatter_dimension=0, tiled=False).astype(F32)]
    ppermute x0 -> x43, starting transfers between devices: none -> 83.2 us  [flip(): return lax.ppermute(value, AXES, [(i, i ^ mask) for i in range(self.count)])]
    ppermute x0 -> x43, waiting for transfers between devices: none -> 82.8 us  [flip(): return lax.ppermute(value, AXES, [(i, i ^ mask) for i in range(self.count)])]
    all_gather x1 -> x0, waiting for transfers between devices: 64.5 us -> none  [gather_all(): whole = lax.all_gather(local, AXES, axis=0, tiled=False)]
    ppermute x2, waiting for transfers between devices: 23.1 us -> 0.03 us  [bring_to(): lax.ppermute(value, AXES, self.pairs(self.home, lambda g, s: self.at(g, s...]
    pallas_call x9 -> x10, Pallas kernels: 242 us -> 259 us  [whole_call(): pl.pallas_call(kernel, out_shape=outs, in_specs=[sm] * scalars + [vm] * (...]
    unnamed x90 -> x146, local copies, waits for them, and re-layouts: 33.2 us -> 20.4 us
    reshape x20 -> x10, local copies, waits for them, and re-layouts: 13.6 us -> 2.42 us  [the longest x2 1.17 us: on_device(): out[name] = part.reshape(-1)]
  transfers between devices with their start and end apart: 23 -> 63, of which waited for: 10 -> 23; matrix products, arithmetic and copies ran while one was open for 3% -> 6% of each run, Pallas kernels for 5% -> 36%
where the time goes in v3:
time: 598 us; the launch traced here: 590 us
  Pallas kernels  259 us (43%)
  waiting for transfers between devices  155 us (26%)
  starting transfers between devices  108 us (18%)
  local copies, waits for them, and re-layouts  45.3 us (8%)
  other arithmetic  19.1 us (3%)
    pallas_call x10, Pallas kernels, whole_call(): pl.pallas_call(kernel, out_shape=outs, in_specs=[sm] * scalars + [vm] * (...  259 us
    ppermute x43, starting transfers between devices, flip(): return lax.ppermute(value, AXES, [(i, i ^ mask) for i in range(self.count)])  83.2 us
    ppermute x43, waiting for transfers between devices, flip(): return lax.ppermute(value, AXES, [(i, i ^ mask) for i in range(self.count)])  82.8 us
    ppermute x12, waiting for transfers between devices, swap(): lax.ppermute(values[k], AXES, self.pairs(self.at, lambda g, s: self.at(g,...  72 us
    unnamed x146, local copies, waits for them, and re-layouts  20.4 us
  transfers between devices with their start and end apart: 63, of which 23 were waited for; matrix products, arithmetic and copies ran while one was open for 6% of the time, Pallas kernels for 36%

profile of v3, /device:TPU:0, one launch (start us, length us, event | category | flops | bytes accessed | tf_op | source)
XLA Modules:
  0.0 590.4 jit_solution(6991309785572356963)
XLA Ops:
  16.3 5.0 collective-permute-start.5
  24.5 3.0 collective-permute-done.5
  27.6 14.8 %collective-permute-done.4 = bf16[416,256]{1,0:T(8,128)(2,1)S(1)} collective-permute-done((bf16[416,256]{1,0:T(8,128)(2,1)S(1)}, bf16[416,256]{1,0:T(8,128)(2,1)S(1)}, u32[]{:S(2)}, u32[]{:S(2)}) %collective-permute-start.4) | collective-permute-done | bytes 213024 | tf_op jit(solution)/shard_map/ppermute | solution.py:897
  42.6 7.3 %collective-permute-start.9 = (bf16[4,208,256]{2,1,0:T(8,128)(2,1)S(1)}, bf16[4,208,256]{2,1,0:T(8,128)(2,1)S(1)}, u32[]{:S(2)}, u32[]{:S(2)}) collective-permute-start(bf16[4,208,256]{2,1,0:T(8,128)(2,1)S(1)} %get-tuple-element.128), channel_id=1, source_target_pairs={{0,4},{1,5},{2,6},{3,7},{4,0},{5,1},{6,2},{7,3},{8,12},{9,13},{10,... | collective-permute-start | bytes 1277960 | tf_op jit(solution)/shard_map/ppermute | solution.py:897
  49.8 1.5 collective-permute-start.6
  52.0 2.0 collective-permute-start.1
  55.3 10.0 %collective-permute-done.9 = bf16[4,208,256]{2,1,0:T(8,128)(2,1)S(1)} collective-permute-done((bf16[4,208,256]{2,1,0:T(8,128)(2,1)S(1)}, bf16[4,208,256]{2,1,0:T(8,128)(2,1)S(1)}, u32[]{:S(2)}, u32[]{:S(2)}) %collective-permute-start.9) | collective-permute-done | bytes 426016 | tf_op jit(solution)/shard_map/ppermute | solution.py:897
  66.5 1.6 collective-permute-start.10
  68.1 2.5 collective-permute-start.7
  71.7 14.7 %collective-permute-done.10 = bf16[8,208,256]{2,1,0:T(8,128)(2,1)S(1)} collective-permute-done((bf16[8,208,256]{2,1,0:T(8,128)(2,1)S(1)}, bf16[8,208,256]{2,1,0:T(8,128)(2,1)S(1)}, u32[]{:S(2)}, u32[]{:S(2)}) %collective-permute-start.10) | collective-permute-done | bytes 852000 | tf_op jit(solution)/shard_map/ppermute | solution.py:897
  93.7 4.1 collective-permute-start.14
  97.8 4.0 collective-permute-start.13
  104.4 9.2 %shard_map.297 = (f32[800,512]{1,0:T(8,128)}, bf16[800,512]{1,0:T(8,128)(2,1)}, f32[800,1024]{1,0:T(8,128)}) custom-call(s32[3]{0:T(128)} %pad_add_fusion.scal.refs_0_, bf16[800,512]{1,0:T(8,128)(2,1)} %pad_maximum_fusion.5.x_ref.refs_6_, f32[1,512]{1,0:T(1,128)} %broadcast_in_dim_reshape.15.g1.refs_7_, f32[1,512]{1,0:T(1,128)} %broadcast_in_dim_reshape.16.g2.refs_8_, ...), custom_call_target="tpu_custom_call" | custom-call | flops 10350000128 | bytes 13373452 | tf_op jit(solution)/shard_map/pallas_call | solution.py:54
  114.5 1.6 collective-permute-start.19
  116.0 13.8 %shard_map.298 = (f32[800,2048]{1,0:T(8,128)}, f32[800,256]{1,0:T(8,128)}, bf16[800,2048]{1,0:T(8,128)(2,1)}) custom-call(s32[3]{0:T(128)} %pad_add_fusion.scal.refs_0_, bf16[800,512]{1,0:T(8,128)(2,1)} %get-tuple-element.68.y2_ref.refs_3_, f32[1,2048]{1,0:T(1,128)} %broadcast_in_dim_reshape.17.g3.refs_8_, ...), custom_call_target="tpu_custom_call" | custom-call | flops 16099999744 | bytes 18292748 | tf_op jit(solution)/shard_map/pallas_call | solution.py:54
  131.3 2.1 collective-permute-start.26
  134.1 22.3 %shard_map.299 = (bf16[768,2048]{1,0:T(8,128)(2,1)}, f32[768,512]{1,0:T(8,128)}, bf16[768,512]{1,0:T(8,128)(2,1)}, bf16[768,384]{1,0:T(8,128)(2,1)}, bf16[768,38...) custom-call(s32[3]{0:T(128)} %pad_add_fusion.scal.refs_0_, ...), custom_call_target="tpu_custom_call" | custom-call | flops 25300000768 | bytes 19671052 | tf_op jit(solution)/shard_map/pallas_call | solution.py:54
  156.6 2.0 collective-permute-start.17
  158.7 1.6 collective-permute-start.23
  162.0 18.1 %collective-permute-done.15.refs_2_ = bf16[768,384]{1,0:T(8,128)(2,1)S(1)} collective-permute-done((bf16[768,384]{1,0:T(8,128)(2,1)}, bf16[768,384]{1,0:T(8,128)(2,1)S(1)}, u32[]{:S(2)}, u32[]{:S(2)}) %collective-permute-start.15) | collective-permute-done | bytes 589856 | tf_op jit(solution)/shard_map/ppermute | solution.py:1060
  180.1 15.5 %collective-permute-done.17.refs_4_ = bf16[768,384]{1,0:T(8,128)(2,1)} collective-permute-done((bf16[768,384]{1,0:T(8,128)(2,1)}, bf16[768,384]{1,0:T(8,128)(2,1)}, u32[]{:S(2)}, u32[]{:S(2)}) %collective-permute-start.17) | collective-permute-done | bytes 589856 | tf_op jit(solution)/shard_map/ppermute | solution.py:1060
  195.6 36.2 %shard_map.300 = (bf16[768,128]{1,0:T(8,128)(2,1)}, bf16[768,128]{1,0:T(8,128)(2,1)}, bf16[768,128]{1,0:T(8,128)(2,1)}, bf16[768,128]{1,0:T(8,128)(2,1)}, f32[3072,128]{1,0:T(8,128)}) custom-call(s32[3]{0:T(128)} %pad_add_fusion.scal.refs_0_, bf16[768,384]{1,0:T(8,128)(2,1)} %get-tuple-element.75.refs_1_, bf16[768,384]{1,0:T(8,128)(2,1)} %copy-done.33, ...), custom_call_target="tpu_custom_call" | custom-call | flops 41400000512 | bytes 4718604 | tf_op jit(solution)/shard_map/pallas_call | solution.py:54
  231.9 2.0 collective-permute-start.21
  234.7 5.1 collective-permute-done.20.refs_1_
  239.8 3.6 collective-permute-done.22.refs_3_
  244.5 29.3 %shard_map.301 = (bf16[768,512]{1,0:T(8,128)(2,1)}, f32[768,512]{1,0:T(8,128)}, bf16[768,128]{1,0:T(8,128)(2,1)}, bf16[768,128]{1,0:T(8,128)(2,1)}, bf16[768,128...) custom-call(s32[3]{0:T(128)} %pad_add_fusion.scal.refs_0_, ...), custom_call_target="tpu_custom_call" | custom-call | flops 33350000640 | bytes 15732748 | tf_op jit(solution)/shard_map/pallas_call | solution.py:54
  273.8 2.0 slice.490
  276.7 1.4 collective-permute-start.31
  278.1 1.8 collective-permute-start.28
  281.2 3.3 collective-permute-start.37
  284.5 1.6 fusion.26
  286.2 1.5 collective-permute-start.36
  287.7 4.8 collective-permute-done.31.refs_12_
  293.2 58.2 %shard_map.302 = (bf16[768,384]{1,0:T(8,128)(2,1)}, bf16[768,384]{1,0:T(8,128)(2,1)}, bf16[768,384]{1,0:T(8,128)(2,1)}, bf16[768,384]{1,0:T(8,128)(2,1)}) custom-call(s32[3]{0:T(128)} %pad_add_fusion.scal.refs_0_, bf16[768,384]{1,0:T(8,128)(2,1)} %get-tuple-element.75.refs_1_, bf16[768,384]{1,0:T(8,128)(2,1)} %copy-done.33, ...), custom_call_target="tpu_custom_call" | custom-call | flops 66700001280 | bytes 7864332 | tf_op jit(solution)/shard_map/pallas_call | solution.py:54
  352.6 1.7 collective-permute-start.34
  354.3 1.3 add_convert_fusion.4
  355.6 12.0 %collective-permute-done.33.refs_2_ = bf16[768,384]{1,0:T(8,128)(2,1)} collective-permute-done((bf16[768,384]{1,0:T(8,128)(2,1)}, bf16[768,384]{1,0:T(8,128)(2,1)}, u32[]{:S(2)}, u32[]{:S(2)}) %collective-permute-start.33) | collective-permute-done | bytes 589856 | tf_op jit(solution)/shard_map/ppermute | solution.py:1060
  367.6 12.8 %collective-permute-done.35.refs_4_ = bf16[768,384]{1,0:T(8,128)(2,1)S(1)} collective-permute-done((bf16[768,384]{1,0:T(8,128)(2,1)}, bf16[768,384]{1,0:T(8,128)(2,1)S(1)}, u32[]{:S(2)}, u32[]{:S(2)}) %collective-permute-start.35) | collective-permute-done | bytes 589856 | tf_op jit(solution)/shard_map/ppermute | solution.py:1060
  381.3 15.0 %shard_map.303 = (f32[768,512]{1,0:T(8,128)}, bf16[768,256]{1,0:T(8,128)(2,1)}, bf16[32,160,256]{2,1,0:T(8,128)(2,1)}, f32[1,512]{1,0:T(1,128)}) custom-call(s32[3]{0:T(128)} %pad_add_fusion.scal.refs_0_, bf16[768,384]{1,0:T(8,128)(2,1)} %get-tuple-element.91.refs_1_, bf16[768,384]{1,0:T(8,128)(2,1)} %collective-permute-done.33.refs_2_, ...), custom_call_target="tpu_custom_call" | custom-call | flops 17250000896 | bytes 20844556 | tf_op jit(solution)/shard_map/pallas_call | solution.py:54
  396.4 1.5 slice.504
  403.2 4.5 collective-permute-start.38
  409.2 2.2 add_convert_fusion.2
  415.6 3.0 collective-permute-start.48
  418.6 14.4 %collective-permute-start.50 = (bf16[288,256]{1,0:T(8,128)(2,1)}, bf16[288,256]{1,0:T(8,128)(2,1)}, u32[]{:S(2)}, u32[]{:S(2)}) collective-permute-start(bf16[288,256]{1,0:T(8,128)(2,1)} %get-tuple-element.133), channel_id=1, source_target_pairs={{0,24},{1,25},{2,26},{3,27},{4,28},{5,29},{6,30},{7,31},{8,16},{9,... | collective-permute-start | bytes 442376 | tf_op jit(solution)/shard_map/ppermute | solution.py:897
  433.0 48.4 %shard_map.304 = (bf16[800,2048]{1,0:T(8,128)(2,1)}, bf16[768,768]{1,0:T(8,128)(2,1)}, f32[9,2048]{1,0:T(8,128)}, f32[1,2048]{1,0:T(1,128)}) custom-call(s32[3]{0:T(128)} %pad_add_fusion.scal.refs_0_, bf16[16,256]{1,0:T(8,128)(2,1)} %copy-done.42, bf16[768,256]{1,0:T(8,128)(2,1)} %get-tuple-element.98.refs_2_, bf16[16,256]{1,0:T(8,128)(2,1)} %copy-done.41, ...), custom_call_target="tpu_custom_call" | custom-call | flops 56349999104 | bytes 22495244 | tf_op jit(solution)/shard_map/pallas_call | solution.py:54
  486.8 6.6 %shard_map.306 = bf16[32,176,256]{2,1,0:T(8,128)(2,1)} custom-call(s32[3]{0:T(128)} %pad_add_fusion.scal.refs_0_, bf16[800,2048]{1,0:T(8,128)(2,1)} %get-tuple-element.102.refs_1_, bf16[768,768]{1,0:T(8,128)(2,1)} %get-tuple-element.103.refs_2_, bf16[800,512]{1,0:T(8,128)(2,1)} %get-tuple-element.68.y2_ref.refs_3_, f32[288,256]{1,0:T(8,128)} %copy-done.11, ...), custom_call_target="tpu_custom_call" | custom-call | flops 8049999872 | bytes 8159244 | tf_op jit(solution)/shard_map/pallas_call | solution.py:54
  493.3 1.5 slice.620
  496.4 19.5 %shard_map.305 = (bf16[768,512]{1,0:T(8,128)(2,1)}, bf16[32,64,256]{2,1,0:T(8,128)(2,1)}, f32[1,512]{1,0:T(1,128)}, f32[1,512]{1,0:T(1,128)}) custom-call(s32[3]{0:T(128)} %pad_add_fusion.scal.refs_0_, bf16[800,2048]{1,0:T(8,128)(2,1)} %get-tuple-element.102.refs_1_, bf16[768,768]{1,0:T(8,128)(2,1)} %get-tuple-element.103.refs_2_, ...), custom_call_target="tpu_custom_call" | custom-call | flops 23000000512 | bytes 20422668 | tf_op jit(solution)/shard_map/pallas_call | solution.py:54
  517.4 2.2 collective-permute-start.62
  520.8 2.0 collective-permute-start.47
  523.1 2.0 collective-permute-start.52
  525.0 3.9 collective-permute-done.61
  529.3 1.5 copy-done.1
  531.4 9.5 %collective-permute-start.55 = (bf16[8,128,256]{2,1,0:T(8,128)(2,1)S(1)}, bf16[8,128,256]{2,1,0:T(8,128)(2,1)S(1)}, u32[]{:S(2)}, u32[]{:S(2)}) collective-permute-start(bf16[8,128,256]{2,1,0:T(8,128)(2,1)S(1)} %pad_maximum_fusion.10), channel_id=1, source_target_pairs={{0,4},{1,5},{2,6},{3,7},{4,0},{5,1},{6,2},{7,3},{8,12},{9,13},{10,... | collective-permute-start | bytes 1572872 | tf_op jit(solution)/shard_map/ppermute | solution.py:897
  540.9 2.1 collective-permute-start.53
  543.0 18.4 %collective-permute-done.55 = bf16[8,128,256]{2,1,0:T(8,128)(2,1)S(1)} collective-permute-done((bf16[8,128,256]{2,1,0:T(8,128)(2,1)S(1)}, bf16[8,128,256]{2,1,0:T(8,128)(2,1)S(1)}, u32[]{:S(2)}, u32[]{:S(2)}) %collective-permute-start.55) | collective-permute-done | bytes 524320 | tf_op jit(solution)/shard_map/ppermute | solution.py:897
  561.6 1.8 collective-permute-start.56
  563.6 2.5 collective-permute-start.54
  566.8 3.1 collective-permute-done.56
  570.0 1.9 collective-permute-done.54
  572.2 3.4 collective-permute-start.58
  575.6 1.4 bitcast_convert_fusion
  576.9 1.7 collective-permute-done.57
  579.6 6.2 %collective-permute-done.58 = bf16[256,256]{1,0:T(8,128)(2,1)S(1)} collective-permute-done((bf16[256,256]{1,0:T(8,128)(2,1)S(1)}, bf16[256,256]{1,0:T(8,128)(2,1)S(1)}, u32[]{:S(2)}, u32[]{:S(2)}) %collective-permute-start.58) | collective-permute-done | bytes 131104 | tf_op jit(solution)/shard_map/ppermute | solution.py:897
  (331 shorter events, 70.1 us)
Async XLA Ops:
  16.3 11.3 %collective-permute-start.5 = (bf16[416,256]{1,0:T(8,128)(2,1)S(1)}, bf16[416,256]{1,0:T(8,128)(2,1)S(1)}, u32[]{:S(2)}, u32[]{:S(2)}) collective-permute-start(bf16[416,256]{1,0:T(8,128)(2,1)S(1)} %constant_dynamic-update-slice_fusion), channel_id=1, source_target_pairs={{0,24},{1,25},{2,26},{3,27},{4,28},{5,29},{6,30},{7,31},{8,16},{9,... | collective-permute-start | bytes 638984 | tf_op jit(solution)/shard_map/ppermute | solution.py:897
  21.3 21.0 %collective-permute-start.4 = (bf16[416,256]{1,0:T(8,128)(2,1)S(1)}, bf16[416,256]{1,0:T(8,128)(2,1)S(1)}, u32[]{:S(2)}, u32[]{:S(2)}) collective-permute-start(bf16[416,256]{1,0:T(8,128)(2,1)S(1)} %constant_dynamic-update-slice_fusion), channel_id=1, source_target_pairs={{0,16},{1,17},{2,18},{3,19},{4,20},{5,21},{6,22},{7,23},{8,24},{9,... | collective-permute-start | bytes 638984 | tf_op jit(solution)/shard_map/ppermute | solution.py:897
  21.3 21.0 %collective-permute-start.3 = (bf16[416,256]{1,0:T(8,128)(2,1)S(1)}, bf16[416,256]{1,0:T(8,128)(2,1)S(1)}, u32[]{:S(2)}, u32[]{:S(2)}) collective-permute-start(bf16[416,256]{1,0:T(8,128)(2,1)S(1)} %constant_dynamic-update-slice_fusion), channel_id=1, source_target_pairs={{0,8},{1,9},{2,10},{3,11},{4,12},{5,13},{6,14},{7,15},{8,0},{9,1},... | collective-permute-start | bytes 638984 | tf_op jit(solution)/shard_map/ppermute | solution.py:897
  23.8 41.6 %collective-permute-start = (bf16[784,512]{1,0:T(8,128)(2,1)S(1)}, bf16[784,512]{1,0:T(8,128)(2,1)S(1)}, u32[]{:S(2)}, u32[]{:S(2)}) collective-permute-start(bf16[784,512]{1,0:T(8,128)(2,1)S(1)} %pad_maximum_fusion.6), channel_id=1, source_target_pairs={{0,0},{8,4},{16,1},{24,5},{1,16},{9,20},{17,17},{25,21},{2,2},{10,... | collective-permute-start | bytes 2408456 | tf_op jit(solution)/shard_map/ppermute | solution.py:1045
  42.6 22.8 %collective-permute-start.9 = (bf16[4,208,256]{2,1,0:T(8,128)(2,1)S(1)}, bf16[4,208,256]{2,1,0:T(8,128)(2,1)S(1)}, u32[]{:S(2)}, u32[]{:S(2)}) collective-permute-start(bf16[4,208,256]{2,1,0:T(8,128)(2,1)S(1)} %get-tuple-element.128), channel_id=1, source_target_pairs={{0,4},{1,5},{2,6},{3,7},{4,0},{5,1},{6,2},{7,3},{8,12},{9,13},{10,... | collective-permute-start | bytes 1277960 | tf_op jit(solution)/shard_map/ppermute | solution.py:897
  49.8 18.2 %collective-permute-start.6 = (bf16[4,208,256]{2,1,0:T(8,128)(2,1)S(1)}, bf16[4,208,256]{2,1,0:T(8,128)(2,1)S(1)}, u32[]{:S(2)}, u32[]{:S(2)}) collective-permute-start(bf16[4,208,256]{2,1,0:T(8,128)(2,1)S(1)} %get-tuple-element.129), channel_id=1, source_target_pairs={{0,2},{1,3},{2,0},{3,1},{4,6},{5,7},{6,4},{7,5},{8,10},{9,11},{10,... | collective-permute-start | bytes 1277960 | tf_op jit(solution)/shard_map/ppermute | solution.py:897
  52.0 13.5 %collective-permute-start.1 = (bf16[16,512]{1,0:T(8,128)(2,1)S(1)}, bf16[16,512]{1,0:T(8,128)(2,1)S(1)}, u32[]{:S(2)}, u32[]{:S(2)}) collective-permute-start(bf16[16,512]{1,0:T(8,128)(2,1)S(1)} %get-tuple-element.130), channel_id=1, source_target_pairs={{0,4},{8,1},{16,5},{1,20},{9,17},{17,21},{2,6},{10,3},{18,7},{3,22... | collective-permute-start | bytes 49160 | tf_op jit(solution)/shard_map/ppermute | solution.py:1048
  54.0 11.5 %collective-permute-start.2 = (bf16[16,512]{1,0:T(8,128)(2,1)S(1)}, bf16[16,512]{1,0:T(8,128)(2,1)S(1)}, u32[]{:S(2)}, u32[]{:S(2)}) collective-permute-start(bf16[16,512]{1,0:T(8,128)(2,1)S(1)} %get-tuple-element.131), channel_id=1, source_target_pairs={{8,0},{16,4},{24,1},{9,16},{17,20},{25,17},{10,2},{18,6},{26,3},{1... | collective-permute-start | bytes 49160 | tf_op jit(solution)/shard_map/ppermute | solution.py:1048
  66.5 20.0 %collective-permute-start.10 = (bf16[8,208,256]{2,1,0:T(8,128)(2,1)S(1)}, bf16[8,208,256]{2,1,0:T(8,128)(2,1)S(1)}, u32[]{:S(2)}, u32[]{:S(2)}) collective-permute-start(bf16[8,208,256]{2,1,0:T(8,128)(2,1)S(1)} %pad_maximum_fusion.4), channel_id=1, source_target_pairs={{0,2},{1,3},{2,0},{3,1},{4,6},{5,7},{6,4},{7,5},{8,10},{9,11},{10,... | collective-permute-start | bytes 2555912 | tf_op jit(solution)/shard_map/ppermute | solution.py:897
  68.1 20.5 %collective-permute-start.7 = (bf16[8,208,256]{2,1,0:T(8,128)(2,1)S(1)}, bf16[8,208,256]{2,1,0:T(8,128)(2,1)S(1)}, u32[]{:S(2)}, u32[]{:S(2)}) collective-permute-start(bf16[8,208,256]{2,1,0:T(8,128)(2,1)S(1)} %pad_maximum_fusion.3), channel_id=1, source_target_pairs={{0,4},{1,5},{2,6},{3,7},{4,0},{5,1},{6,2},{7,3},{8,12},{9,13},{10,... | collective-permute-start | bytes 2555912 | tf_op jit(solution)/shard_map/ppermute | solution.py:897
  87.4 5.4 collective-permute-start.11
  88.7 4.9 collective-permute-start.8
  93.7 20.6 %collective-permute-start.14 = (bf16[288,256]{1,0:T(8,128)(2,1)S(1)}, bf16[288,256]{1,0:T(8,128)(2,1)S(1)}, u32[]{:S(2)}, u32[]{:S(2)}) collective-permute-start(bf16[288,256]{1,0:T(8,128)(2,1)S(1)} %constant_dynamic-update-slice_fusion.25), channel_id=1, source_target_pairs={{0,24},{1,25},{2,26},{3,27},{4,28},{5,29},{6,30},{7,31},{8,16},{9,... | collective-permute-start | bytes 442376 | tf_op jit(solution)/shard_map/ppermute | solution.py:897
  97.8 16.5 %collective-permute-start.13 = (bf16[288,256]{1,0:T(8,128)(2,1)S(1)}, bf16[288,256]{1,0:T(8,128)(2,1)S(1)}, u32[]{:S(2)}, u32[]{:S(2)}) collective-permute-start(bf16[288,256]{1,0:T(8,128)(2,1)S(1)} %constant_dynamic-update-slice_fusion.25), channel_id=1, source_target_pairs={{0,16},{1,17},{2,18},{3,19},{4,20},{5,21},{6,22},{7,23},{8,24},{9,... | collective-permute-start | bytes 442376 | tf_op jit(solution)/shard_map/ppermute | solution.py:897
  101.8 12.5 %collective-permute-start.12 = (bf16[288,256]{1,0:T(8,128)(2,1)S(1)}, bf16[288,256]{1,0:T(8,128)(2,1)S(1)}, u32[]{:S(2)}, u32[]{:S(2)}) collective-permute-start(bf16[288,256]{1,0:T(8,128)(2,1)S(1)} %constant_dynamic-update-slice_fusion.25), channel_id=1, source_target_pairs={{0,8},{1,9},{2,10},{3,11},{4,12},{5,13},{6,14},{7,15},{8,0},{9,1},... | collective-permute-start | bytes 442376 | tf_op jit(solution)/shard_map/ppermute | solution.py:897
  114.5 16.8 %collective-permute-start.19 = (bf16[4,144,256]{2,1,0:T(8,128)(2,1)S(1)}, bf16[4,144,256]{2,1,0:T(8,128)(2,1)S(1)}, u32[]{:S(2)}, u32[]{:S(2)}) collective-permute-start(bf16[4,144,256]{2,1,0:T(8,128)(2,1)S(1)} %get-tuple-element.135), channel_id=1, source_target_pairs={{0,2},{1,3},{2,0},{3,1},{4,6},{5,7},{6,4},{7,5},{8,10},{9,11},{10,... | collective-permute-start | bytes 884744 | tf_op jit(solution)/shard_map/ppermute | solution.py:897
  116.0 17.4 %collective-permute-start.18 = (bf16[4,144,256]{2,1,0:T(8,128)(2,1)S(1)}, bf16[4,144,256]{2,1,0:T(8,128)(2,1)S(1)}, u32[]{:S(2)}, u32[]{:S(2)}) collective-permute-start(bf16[4,144,256]{2,1,0:T(8,128)(2,1)S(1)} %get-tuple-element.136), channel_id=1, source_target_pairs={{0,4},{1,5},{2,6},{3,7},{4,0},{5,1},{6,2},{7,3},{8,12},{9,13},{10,... | collective-permute-start | bytes 884744 | tf_op jit(solution)/shard_map/ppermute | solution.py:897
  131.3 29.0 %collective-permute-start.26 = (bf16[8,144,256]{2,1,0:T(8,128)(2,1)S(1)}, bf16[8,144,256]{2,1,0:T(8,128)(2,1)S(1)}, u32[]{:S(2)}, u32[]{:S(2)}) collective-permute-start(bf16[8,144,256]{2,1,0:T(8,128)(2,1)S(1)} %pad_maximum_fusion.9.refs_6_), channel_id=1, source_target_pairs={{0,4},{1,5},{2,6},{3,7},{4,0},{5,1},{6,2},{7,3},{8,12},{9,13},{10,... | collective-permute-start | bytes 1769480 | tf_op jit(solution)/shard_map/ppermute | solution.py:897
  133.5 25.2 %collective-permute-start.24 = (bf16[8,144,256]{2,1,0:T(8,128)(2,1)S(1)}, bf16[8,144,256]{2,1,0:T(8,128)(2,1)S(1)}, u32[]{:S(2)}, u32[]{:S(2)}) collective-permute-start(bf16[8,144,256]{2,1,0:T(8,128)(2,1)S(1)} %pad_maximum_fusion.8.refs_5_), channel_id=1, source_target_pairs={{0,2},{1,3},{2,0},{3,1},{4,6},{5,7},{6,4},{7,5},{8,10},{9,11},{10,... | collective-permute-start | bytes 1769480 | tf_op jit(solution)/shard_map/ppermute | solution.py:897
  156.4 23.7 %collective-permute-start.15 = (bf16[768,384]{1,0:T(8,128)(2,1)}, bf16[768,384]{1,0:T(8,128)(2,1)S(1)}, u32[]{:S(2)}, u32[]{:S(2)}) collective-permute-start(bf16[768,384]{1,0:T(8,128)(2,1)} %get-tuple-element.76), channel_id=1, source_target_pairs={{0,4},{4,0},{1,5},{5,1},{16,20},{20,16},{17,21},{21,17},{2,6},{6,2... | collective-permute-start | bytes 1769480 | tf_op jit(solution)/shard_map/ppermute | solution.py:1060
  156.5 23.6 %collective-permute-start.16 = (bf16[768,384]{1,0:T(8,128)(2,1)}, bf16[768,384]{1,0:T(8,128)(2,1)}, u32[]{:S(2)}, u32[]{:S(2)}) collective-permute-start(bf16[768,384]{1,0:T(8,128)(2,1)} %get-tuple-element.77), channel_id=1, source_target_pairs={{0,1},{4,5},{1,0},{5,4},{16,17},{20,21},{17,16},{21,20},{2,3},{6,7... | collective-permute-start | bytes 1769480 | tf_op jit(solution)/shard_map/ppermute | solution.py:1060
  156.6 39.0 %collective-permute-start.17 = (bf16[768,384]{1,0:T(8,128)(2,1)}, bf16[768,384]{1,0:T(8,128)(2,1)}, u32[]{:S(2)}, u32[]{:S(2)}) collective-permute-start(bf16[768,384]{1,0:T(8,128)(2,1)} %get-tuple-element.78), channel_id=1, source_target_pairs={{0,5},{4,1},{1,4},{5,0},{16,21},{20,17},{17,20},{21,16},{2,7},{6,3... | collective-permute-start | bytes 1769480 | tf_op jit(solution)/shard_map/ppermute | solution.py:1060
  158.7 75.3 %collective-permute-start.23 = (bf16[768,512]{1,0:T(8,128)(2,1)S(1)}, bf16[768,512]{1,0:T(8,128)(2,1)}, u32[]{:S(2)}, u32[]{:S(2)}) collective-permute-start(bf16[768,512]{1,0:T(8,128)(2,1)S(1)} %bitcast.105), channel_id=1, source_target_pairs={{0,0},{8,4},{16,1},{24,5},{1,16},{9,20},{17,17},{25,21},{2,2},{10,... | collective-permute-start | bytes 2359304 | tf_op jit(solution)/shard_map/ppermute | solution.py:1045
  160.3 71.6 %copy-start.14 = (bf16[16,144,256]{2,1,0:T(8,128)(2,1)}, bf16[16,144,256]{2,1,0:T(8,128)(2,1)S(1)}, u32[]{:S(2)}) copy-start(bf16[16,144,256]{2,1,0:T(8,128)(2,1)S(1)} %pad_maximum_fusion.refs_6_) | copy-start | bytes 3538948
  160.3 83.1 %collective-permute-start.25 = (bf16[16,144,256]{2,1,0:T(8,128)(2,1)S(1)}, bf16[16,144,256]{2,1,0:T(8,128)(2,1)}, u32[]{:S(2)}, u32[]{:S(2)}) collective-permute-start(bf16[16,144,256]{2,1,0:T(8,128)(2,1)S(1)} %pad_maximum_fusion.refs_6_), channel_id=1, source_target_pairs={{0,1},{1,0},{2,3},{3,2},{4,5},{5,4},{6,7},{7,6},{8,9},{9,8},{10,11... | collective-permute-start | bytes 3538952 | tf_op jit(solution)/shard_map/ppermute | solution.py:897
  180.1 63.3 %collective-permute-start.27 = (bf16[16,144,256]{2,1,0:T(8,128)(2,1)}, bf16[16,144,256]{2,1,0:T(8,128)(2,1)S(1)}, u32[]{:S(2)}, u32[]{:S(2)}) collective-permute-start(bf16[16,144,256]{2,1,0:T(8,128)(2,1)} %pad_maximum_fusion.1.refs_8_), channel_id=1, source_target_pairs={{0,1},{1,0},{2,3},{3,2},{4,5},{5,4},{6,7},{7,6},{8,9},{9,8},{10,11... | collective-permute-start | bytes 3538952 | tf_op jit(solution)/shard_map/ppermute | solution.py:897
  231.9 7.9 %collective-permute-start.20 = (bf16[768,128]{1,0:T(8,128)(2,1)}, bf16[768,128]{1,0:T(8,128)(2,1)S(1)}, u32[]{:S(2)}, u32[]{:S(2)}) collective-permute-start(bf16[768,128]{1,0:T(8,128)(2,1)} %get-tuple-element.80.refs_6_), channel_id=1, source_target_pairs={{0,4},{4,0},{1,5},{5,1},{16,20},{20,16},{17,21},{21,17},{2,6},{6,2... | collective-permute-start | bytes 589832 | tf_op jit(solution)/shard_map/ppermute | solution.py:1060
  231.9 7.9 %collective-permute-start.21 = (bf16[768,128]{1,0:T(8,128)(2,1)}, bf16[768,128]{1,0:T(8,128)(2,1)S(1)}, u32[]{:S(2)}, u32[]{:S(2)}) collective-permute-start(bf16[768,128]{1,0:T(8,128)(2,1)} %get-tuple-element.81.refs_7_), channel_id=1, source_target_pairs={{0,1},{4,5},{1,0},{5,4},{16,17},{20,21},{17,16},{21,20},{2,3},{6,7... | collective-permute-start | bytes 589832 | tf_op jit(solution)/shard_map/ppermute | solution.py:1060
  233.9 9.5 %collective-permute-start.22 = (bf16[768,128]{1,0:T(8,128)(2,1)}, bf16[768,128]{1,0:T(8,128)(2,1)S(1)}, u32[]{:S(2)}, u32[]{:S(2)}) collective-permute-start(bf16[768,128]{1,0:T(8,128)(2,1)} %get-tuple-element.82.refs_8_), channel_id=1, source_target_pairs={{0,5},{4,1},{1,4},{5,0},{16,21},{20,17},{17,20},{21,16},{2,7},{6,3... | collective-permute-start | bytes 589832 | tf_op jit(solution)/shard_map/ppermute | solution.py:1060
  275.8 4.6 collective-permute-start.32
  275.9 10.2 %collective-permute-start.29 = (bf16[768,128]{1,0:T(8,128)(2,1)}, bf16[768,128]{1,0:T(8,128)(2,1)S(1)}, u32[]{:S(2)}, u32[]{:S(2)}) collective-permute-start(bf16[768,128]{1,0:T(8,128)(2,1)} %get-tuple-element.86), channel_id=1, source_target_pairs={{0,4},{4,0},{1,5},{5,1},{16,20},{20,16},{17,21},{21,17},{2,6},{6,2... | collective-permute-start | bytes 589832 | tf_op jit(solution)/shard_map/ppermute | solution.py:1060
  276.6 11.1 %collective-permute-start.30 = (bf16[768,128]{1,0:T(8,128)(2,1)}, bf16[768,128]{1,0:T(8,128)(2,1)S(1)}, u32[]{:S(2)}, u32[]{:S(2)}) collective-permute-start(bf16[768,128]{1,0:T(8,128)(2,1)} %get-tuple-element.87), channel_id=1, source_target_pairs={{0,1},{4,5},{1,0},{5,4},{16,17},{20,21},{17,16},{21,20},{2,3},{6,7... | collective-permute-start | bytes 589832 | tf_op jit(solution)/shard_map/ppermute | solution.py:1060
  276.7 15.8 %collective-permute-start.31 = (bf16[768,128]{1,0:T(8,128)(2,1)}, bf16[768,128]{1,0:T(8,128)(2,1)S(1)}, u32[]{:S(2)}, u32[]{:S(2)}) collective-permute-start(bf16[768,128]{1,0:T(8,128)(2,1)} %get-tuple-element.88), channel_id=1, source_target_pairs={{0,5},{4,1},{1,4},{5,0},{16,21},{20,17},{17,20},{21,16},{2,7},{6,3... | collective-permute-start | bytes 589832 | tf_op jit(solution)/shard_map/ppermute | solution.py:1060
  278.1 77.5 %collective-permute-start.28 = (bf16[768,512]{1,0:T(8,128)(2,1)}, bf16[768,512]{1,0:T(8,128)(2,1)S(1)}, u32[]{:S(2)}, u32[]{:S(2)}) collective-permute-start(bf16[768,512]{1,0:T(8,128)(2,1)} %get-tuple-element.84), channel_id=1, source_target_pairs={{0,0},{4,8},{1,16},{5,24},{16,1},{20,9},{17,17},{21,25},{2,2},{6,1... | collective-permute-start | bytes 2359304 | tf_op jit(solution)/shard_map/ppermute | solution.py:1053
  281.2 73.0 %collective-permute-start.37 = (bf16[8,144,256]{2,1,0:T(8,128)(2,1)S(1)}, bf16[8,144,256]{2,1,0:T(8,128)(2,1)S(1)}, u32[]{:S(2)}, u32[]{:S(2)}) collective-permute-start(bf16[8,144,256]{2,1,0:T(8,128)(2,1)S(1)} %get-tuple-element.118), channel_id=1, source_target_pairs={{0,4},{1,5},{2,6},{3,7},{4,0},{5,1},{6,2},{7,3},{8,12},{9,13},{10,... | collective-permute-start | bytes 1769480 | tf_op jit(solution)/shard_map/ppermute | solution.py:897
  286.2 68.1 %collective-permute-start.36 = (bf16[8,144,256]{2,1,0:T(8,128)(2,1)S(1)}, bf16[8,144,256]{2,1,0:T(8,128)(2,1)S(1)}, u32[]{:S(2)}, u32[]{:S(2)}) collective-permute-start(bf16[8,144,256]{2,1,0:T(8,128)(2,1)S(1)} %get-tuple-element.119), channel_id=1, source_target_pairs={{0,2},{1,3},{2,0},{3,1},{4,6},{5,7},{6,4},{7,5},{8,10},{9,11},{10,... | collective-permute-start | bytes 1769480 | tf_op jit(solution)/shard_map/ppermute | solution.py:897
  351.4 16.2 %collective-permute-start.33 = (bf16[768,384]{1,0:T(8,128)(2,1)}, bf16[768,384]{1,0:T(8,128)(2,1)}, u32[]{:S(2)}, u32[]{:S(2)}) collective-permute-start(bf16[768,384]{1,0:T(8,128)(2,1)} %get-tuple-element.92), channel_id=1, source_target_pairs={{0,4},{4,0},{1,5},{5,1},{16,20},{20,16},{17,21},{21,17},{2,6},{6,2... | collective-permute-start | bytes 1769480 | tf_op jit(solution)/shard_map/ppermute | solution.py:1060
  352.6 15.1 %collective-permute-start.34 = (bf16[768,384]{1,0:T(8,128)(2,1)}, bf16[768,384]{1,0:T(8,128)(2,1)}, u32[]{:S(2)}, u32[]{:S(2)}) collective-permute-start(bf16[768,384]{1,0:T(8,128)(2,1)} %get-tuple-element.93), channel_id=1, source_target_pairs={{0,1},{4,5},{1,0},{5,4},{16,17},{20,21},{17,16},{21,20},{2,3},{6,7... | collective-permute-start | bytes 1769480 | tf_op jit(solution)/shard_map/ppermute | solution.py:1060
  354.3 26.2 %collective-permute-start.35 = (bf16[768,384]{1,0:T(8,128)(2,1)}, bf16[768,384]{1,0:T(8,128)(2,1)S(1)}, u32[]{:S(2)}, u32[]{:S(2)}) collective-permute-start(bf16[768,384]{1,0:T(8,128)(2,1)} %get-tuple-element.94), channel_id=1, source_target_pairs={{0,5},{4,1},{1,4},{5,0},{16,21},{20,17},{17,20},{21,16},{2,7},{6,3... | collective-permute-start | bytes 1769480 | tf_op jit(solution)/shard_map/ppermute | solution.py:1060
  397.9 11.3 %collective-permute-start.42 = (bf16[16,160,256]{2,1,0:T(8,128)(2,1)S(1)}, bf16[16,160,256]{2,1,0:T(8,128)(2,1)}, u32[]{:S(2)}, u32[]{:S(2)}) collective-permute-start(bf16[16,160,256]{2,1,0:T(8,128)(2,1)S(1)} %slice.504), channel_id=1, source_target_pairs={{0,1},{1,0},{2,3},{3,2},{4,5},{5,4},{6,7},{7,6},{8,9},{9,8},{10,11... | collective-permute-start | bytes 3932168 | tf_op jit(solution)/shard_map/ppermute | solution.py:897
  398.9 9.7 %collective-permute-start.40 = (bf16[4,144,256]{2,1,0:T(8,128)(2,1)}, bf16[4,144,256]{2,1,0:T(8,128)(2,1)S(1)}, u32[]{:S(2)}, u32[]{:S(2)}) collective-permute-start(bf16[4,144,256]{2,1,0:T(8,128)(2,1)} %slice.602), channel_id=1, source_target_pairs={{0,4},{1,5},{2,6},{3,7},{4,0},{5,1},{6,2},{7,3},{8,12},{9,13},{10,... | collective-permute-start | bytes 884744 | tf_op jit(solution)/shard_map/ppermute | solution.py:897
  400.0 9.1 %collective-permute-start.41 = (bf16[4,144,256]{2,1,0:T(8,128)(2,1)S(1)}, bf16[4,144,256]{2,1,0:T(8,128)(2,1)S(1)}, u32[]{:S(2)}, u32[]{:S(2)}) collective-permute-start(bf16[4,144,256]{2,1,0:T(8,128)(2,1)S(1)} %slice.604), channel_id=1, source_target_pairs={{0,2},{1,3},{2,0},{3,1},{4,6},{5,7},{6,4},{7,5},{8,10},{9,11},{10,... | collective-permute-start | bytes 884744 | tf_op jit(solution)/shard_map/ppermute | solution.py:897
  401.9 12.8 %collective-permute-start.39 = (bf16[16,256]{1,0:T(8,128)(2,1)S(1)}, bf16[16,256]{1,0:T(8,128)(2,1)S(1)}, u32[]{:S(2)}, u32[]{:S(2)}) collective-permute-start(bf16[16,256]{1,0:T(8,128)(2,1)S(1)} %get-tuple-element.140), channel_id=1, source_target_pairs={{4,0},{1,4},{5,1},{20,16},{17,20},{21,17},{6,2},{3,6},{7,3},{22,18... | collective-permute-start | bytes 24584 | tf_op jit(solution)/shard_map/ppermute | solution.py:1056
  403.2 11.5 %collective-permute-start.38 = (bf16[16,256]{1,0:T(8,128)(2,1)S(1)}, bf16[16,256]{1,0:T(8,128)(2,1)S(1)}, u32[]{:S(2)}, u32[]{:S(2)}) collective-permute-start(bf16[16,256]{1,0:T(8,128)(2,1)S(1)} %get-tuple-element.141), channel_id=1, source_target_pairs={{0,4},{4,1},{1,5},{16,20},{20,17},{17,21},{2,6},{6,3},{3,7},{18,22... | collective-permute-start | bytes 24584 | tf_op jit(solution)/shard_map/ppermute | solution.py:1056
  412.6 73.1 %collective-permute-start.45 = (bf16[8,80,256]{2,1,0:T(8,128)(2,1)S(1)}, bf16[8,80,256]{2,1,0:T(8,128)(2,1)S(1)}, u32[]{:S(2)}, u32[]{:S(2)}) collective-permute-start(bf16[8,80,256]{2,1,0:T(8,128)(2,1)S(1)} %get-tuple-element.124), channel_id=1, source_target_pairs={{0,4},{1,5},{2,6},{3,7},{4,0},{5,1},{6,2},{7,3},{8,12},{9,13},{10,... | collective-permute-start | bytes 983048 | tf_op jit(solution)/shard_map/ppermute | solution.py:897
  413.6 72.2 %collective-permute-start.43 = (bf16[8,80,256]{2,1,0:T(8,128)(2,1)S(1)}, bf16[8,80,256]{2,1,0:T(8,128)(2,1)S(1)}, u32[]{:S(2)}, u32[]{:S(2)}) collective-permute-start(bf16[8,80,256]{2,1,0:T(8,128)(2,1)S(1)} %get-tuple-element.125), channel_id=1, source_target_pairs={{0,2},{1,3},{2,0},{3,1},{4,6},{5,7},{6,4},{7,5},{8,10},{9,11},{10,... | collective-permute-start | bytes 983048 | tf_op jit(solution)/shard_map/ppermute | solution.py:897
  415.6 67.6 %collective-permute-start.48 = (bf16[288,256]{1,0:T(8,128)(2,1)}, bf16[288,256]{1,0:T(8,128)(2,1)S(1)}, u32[]{:S(2)}, u32[]{:S(2)}) collective-permute-start(bf16[288,256]{1,0:T(8,128)(2,1)} %get-tuple-element.132), channel_id=1, source_target_pairs={{0,8},{1,9},{2,10},{3,11},{4,12},{5,13},{6,14},{7,15},{8,0},{9,1},... | collective-permute-start | bytes 442376 | tf_op jit(solution)/shard_map/ppermute | solution.py:897
  418.6 64.6 %collective-permute-start.50 = (bf16[288,256]{1,0:T(8,128)(2,1)}, bf16[288,256]{1,0:T(8,128)(2,1)}, u32[]{:S(2)}, u32[]{:S(2)}) collective-permute-start(bf16[288,256]{1,0:T(8,128)(2,1)} %get-tuple-element.133), channel_id=1, source_target_pairs={{0,24},{1,25},{2,26},{3,27},{4,28},{5,29},{6,30},{7,31},{8,16},{9,... | collective-permute-start | bytes 442376 | tf_op jit(solution)/shard_map/ppermute | solution.py:897
  433.0 50.3 %collective-permute-start.49 = (bf16[288,256]{1,0:T(8,128)(2,1)}, bf16[288,256]{1,0:T(8,128)(2,1)}, u32[]{:S(2)}, u32[]{:S(2)}) collective-permute-start(bf16[288,256]{1,0:T(8,128)(2,1)} %get-tuple-element.134), channel_id=1, source_target_pairs={{0,16},{1,17},{2,18},{3,19},{4,20},{5,21},{6,22},{7,23},{8,24},{9,... | collective-permute-start | bytes 442376 | tf_op jit(solution)/shard_map/ppermute | solution.py:897
  486.0 8.9 %collective-permute-start.44 = (bf16[4,80,256]{2,1,0:T(8,128)(2,1)S(1)}, bf16[4,80,256]{2,1,0:T(8,128)(2,1)S(1)}, u32[]{:S(2)}, u32[]{:S(2)}) collective-permute-start(bf16[4,80,256]{2,1,0:T(8,128)(2,1)S(1)} %slice.610), channel_id=1, source_target_pairs={{0,4},{1,5},{2,6},{3,7},{4,0},{5,1},{6,2},{7,3},{8,12},{9,13},{10,... | collective-permute-start | bytes 491528 | tf_op jit(solution)/shard_map/ppermute | solution.py:897
  486.1 9.6 %collective-permute-start.46 = (bf16[4,80,256]{2,1,0:T(8,128)(2,1)S(1)}, bf16[4,80,256]{2,1,0:T(8,128)(2,1)S(1)}, u32[]{:S(2)}, u32[]{:S(2)}) collective-permute-start(bf16[4,80,256]{2,1,0:T(8,128)(2,1)S(1)} %slice.614), channel_id=1, source_target_pairs={{0,2},{1,3},{2,0},{3,1},{4,6},{5,7},{6,4},{7,5},{8,10},{9,11},{10,... | collective-permute-start | bytes 491528 | tf_op jit(solution)/shard_map/ppermute | solution.py:897
  494.9 34.5 %collective-permute-start.51 = (bf16[16,176,256]{2,1,0:T(8,128)(2,1)S(1)}, bf16[16,176,256]{2,1,0:T(8,128)(2,1)S(1)}, u32[]{:S(2)}, u32[]{:S(2)}) collective-permute-start(bf16[16,176,256]{2,1,0:T(8,128)(2,1)S(1)} %slice.620), channel_id=1, source_target_pairs={{0,1},{1,0},{2,3},{3,2},{4,5},{5,4},{6,7},{7,6},{8,9},{9,8},{10,11... | collective-permute-start | bytes 4325384 | tf_op jit(solution)/shard_map/ppermute | solution.py:897
  517.3 5.8 collective-permute-start.60
  517.4 7.7 %collective-permute-start.62 = (bf16[160,256]{1,0:T(8,128)(2,1)S(1)}, bf16[160,256]{1,0:T(8,128)(2,1)S(1)}, u32[]{:S(2)}, u32[]{:S(2)}) collective-permute-start(bf16[160,256]{1,0:T(8,128)(2,1)S(1)} %get-tuple-element.143), channel_id=1, source_target_pairs={{0,24},{1,25},{2,26},{3,27},{4,28},{5,29},{6,30},{7,31},{8,16},{9,... | collective-permute-start | bytes 245768 | tf_op jit(solution)/shard_map/ppermute | solution.py:897
  519.5 9.4 %collective-permute-start.61 = (bf16[160,256]{1,0:T(8,128)(2,1)S(1)}, bf16[160,256]{1,0:T(8,128)(2,1)S(1)}, u32[]{:S(2)}, u32[]{:S(2)}) collective-permute-start(bf16[160,256]{1,0:T(8,128)(2,1)S(1)} %get-tuple-element.144), channel_id=1, source_target_pairs={{0,16},{1,17},{2,18},{3,19},{4,20},{5,21},{6,22},{7,23},{8,24},{9,... | collective-permute-start | bytes 245768 | tf_op jit(solution)/shard_map/ppermute | solution.py:897
  520.8 54.7 %collective-permute-start.47 = (bf16[768,512]{1,0:T(8,128)(2,1)}, bf16[768,512]{1,0:T(8,128)(2,1)S(1)}, u32[]{:S(2)}, u32[]{:S(2)}) collective-permute-start(bf16[768,512]{1,0:T(8,128)(2,1)} %get-tuple-element.106), channel_id=1, source_target_pairs={{0,0},{4,8},{1,16},{5,24},{16,1},{20,9},{17,17},{21,25},{2,2},{6,1... | collective-permute-start | bytes 2359304 | tf_op jit(solution)/shard_map/ppermute | solution.py:1053
  523.1 6.0 %collective-permute-start.52 = (bf16[16,80,256]{2,1,0:T(8,128)(2,1)S(1)}, bf16[16,80,256]{2,1,0:T(8,128)(2,1)S(1)}, u32[]{:S(2)}, u32[]{:S(2)}) collective-permute-start(bf16[16,80,256]{2,1,0:T(8,128)(2,1)S(1)} %slice.623), channel_id=1, source_target_pairs={{0,1},{1,0},{2,3},{3,2},{4,5},{5,4},{6,7},{7,6},{8,9},{9,8},{10,11... | collective-permute-start | bytes 1966088 | tf_op jit(solution)/shard_map/ppermute | solution.py:897
  531.4 30.0 %collective-permute-start.55 = (bf16[8,128,256]{2,1,0:T(8,128)(2,1)S(1)}, bf16[8,128,256]{2,1,0:T(8,128)(2,1)S(1)}, u32[]{:S(2)}, u32[]{:S(2)}) collective-permute-start(bf16[8,128,256]{2,1,0:T(8,128)(2,1)S(1)} %pad_maximum_fusion.10), channel_id=1, source_target_pairs={{0,4},{1,5},{2,6},{3,7},{4,0},{5,1},{6,2},{7,3},{8,12},{9,13},{10,... | collective-permute-start | bytes 1572872 | tf_op jit(solution)/shard_map/ppermute | solution.py:897
  540.9 22.4 %collective-permute-start.53 = (bf16[8,128,256]{2,1,0:T(8,128)(2,1)S(1)}, bf16[8,128,256]{2,1,0:T(8,128)(2,1)S(1)}, u32[]{:S(2)}, u32[]{:S(2)}) collective-permute-start(bf16[8,128,256]{2,1,0:T(8,128)(2,1)S(1)} %pad_maximum_fusion.11), channel_id=1, source_target_pairs={{0,2},{1,3},{2,0},{3,1},{4,6},{5,7},{6,4},{7,5},{8,10},{9,11},{10,... | collective-permute-start | bytes 1572872 | tf_op jit(solution)/shard_map/ppermute | solution.py:897
  561.6 8.3 %collective-permute-start.56 = (bf16[4,128,256]{2,1,0:T(8,128)(2,1)S(1)}, bf16[4,128,256]{2,1,0:T(8,128)(2,1)S(1)}, u32[]{:S(2)}, u32[]{:S(2)}) collective-permute-start(bf16[4,128,256]{2,1,0:T(8,128)(2,1)S(1)} %slice.634), channel_id=1, source_target_pairs={{0,2},{1,3},{2,0},{3,1},{4,6},{5,7},{6,4},{7,5},{8,10},{9,11},{10,... | collective-permute-start | bytes 786440 | tf_op jit(solution)/shard_map/ppermute | solution.py:897
  563.6 8.3 %collective-permute-start.54 = (bf16[4,128,256]{2,1,0:T(8,128)(2,1)S(1)}, bf16[4,128,256]{2,1,0:T(8,128)(2,1)S(1)}, u32[]{:S(2)}, u32[]{:S(2)}) collective-permute-start(bf16[4,128,256]{2,1,0:T(8,128)(2,1)S(1)} %slice.628), channel_id=1, source_target_pairs={{0,4},{1,5},{2,6},{3,7},{4,0},{5,1},{6,2},{7,3},{8,12},{9,13},{10,... | collective-permute-start | bytes 786440 | tf_op jit(solution)/shard_map/ppermute | solution.py:897
  572.0 6.7 %collective-permute-start.57 = (bf16[256,256]{1,0:T(8,128)(2,1)S(1)}, bf16[256,256]{1,0:T(8,128)(2,1)S(1)}, u32[]{:S(2)}, u32[]{:S(2)}) collective-permute-start(bf16[256,256]{1,0:T(8,128)(2,1)S(1)} %get-tuple-element.137), channel_id=1, source_target_pairs={{0,8},{1,9},{2,10},{3,11},{4,12},{5,13},{6,14},{7,15},{8,0},{9,1},... | collective-permute-start | bytes 393224 | tf_op jit(solution)/shard_map/ppermute | solution.py:897
  572.1 7.5 %collective-permute-start.59 = (bf16[256,256]{1,0:T(8,128)(2,1)S(1)}, bf16[256,256]{1,0:T(8,128)(2,1)S(1)}, u32[]{:S(2)}, u32[]{:S(2)}) collective-permute-start(bf16[256,256]{1,0:T(8,128)(2,1)S(1)} %get-tuple-element.138), channel_id=1, source_target_pairs={{0,24},{1,25},{2,26},{3,27},{4,28},{5,29},{6,30},{7,31},{8,16},{9,... | collective-permute-start | bytes 393224 | tf_op jit(solution)/shard_map/ppermute | solution.py:897
  572.2 13.6 %collective-permute-start.58 = (bf16[256,256]{1,0:T(8,128)(2,1)S(1)}, bf16[256,256]{1,0:T(8,128)(2,1)S(1)}, u32[]{:S(2)}, u32[]{:S(2)}) collective-permute-start(bf16[256,256]{1,0:T(8,128)(2,1)S(1)} %get-tuple-element.139), channel_id=1, source_target_pairs={{0,16},{1,17},{2,18},{3,19},{4,20},{5,21},{6,22},{7,23},{8,24},{9,... | collective-permute-start | bytes 393224 | tf_op jit(solution)/shard_map/ppermute | solution.py:897
  (43 other events, 446.1 us)

commit v4 on v3

v4 whole, which is shorter than its diff:
```python
import functools
import math

import jax
import jax.numpy as jnp
import numpy as np
from jax import lax
from jax.experimental import pallas as pl
from jax.experimental.pallas import tpu as pltpu
from jax.sharding import PartitionSpec as P

D = 512
HEADS = 8
FF = 2048
KERNEL = 9
HEAD = 64
NARROW = 256
HALF = KERNEL // 2
LANES = 128
PACK = 256
RIM = 16
BLOCKS = 32
F32 = jnp.float32
BF = jnp.bfloat16
LOG2E = math.log2(math.e)
BIG = -1e30
AXES = ("seq", "dp")
VMEM = 58 << 20


def nt(a, b):
    return lax.dot_general(a, b, (((1,), (1,)), ((), ())), preferred_element_type=F32)


def nn(a, b):
    return lax.dot_general(a, b, (((1,), (0,)), ((), ())), preferred_element_type=F32)


def tn(a, b):
    return lax.dot_general(a, b, (((0,), (0,)), ((), ())), preferred_element_type=F32)


def call(kernel, ins, outs, scratch=(), micros=0, ties=(), steps=None):
    if ties:
        inner, fixed, count = kernel, len(ins), len(ties)

        def kernel(*refs):
            inner(*refs[:fixed], *refs[fixed + count :])

    def spec(shape, how, once):
        if how == "s":
            return pl.BlockSpec(memory_space=pltpu.SMEM)
        if steps is None:
            return pl.BlockSpec(memory_space=pltpu.VMEM)
        if how is None:
            zeros = (0,) * len(shape)
            mode = pl.Buffered(1) if once else None
            return pl.BlockSpec(shape, lambda i: zeros, pipeline_mode=mode)
        return pl.BlockSpec((how, *shape[1:]), lambda i: (i, *(0,) * (len(shape) - 1)))

    args = [a for a, _ in ins]
    shapes = [jax.ShapeDtypeStruct(shape, dtype) for shape, dtype, _ in outs]
    moved = sum(math.prod(a.shape) * a.dtype.itemsize for a in args + shapes)
    return pl.pallas_call(
        kernel,
        out_shape=shapes,
        grid=() if steps is None else (steps,),
        in_specs=[spec(a.shape, how, True) for a, how in ins]
        + [pl.BlockSpec(memory_space=pl.ANY)] * len(ties),
        out_specs=[spec(shape, how, False) for shape, _, how in outs],
        scratch_shapes=[pltpu.VMEM(shape, dtype) for shape, dtype in scratch],
        compiler_params=pltpu.CompilerParams(vmem_limit_bytes=VMEM),
        cost_estimate=pl.CostEstimate(
            flops=int(micros * 1.15e9), bytes_accessed=moved, transcendentals=0
        ),
    )(*args, *ties)


def whole_call(kernel, outs, args, scratch=(), micros=0, ties=()):
    ins = [(a, "s" if i == 0 else None) for i, a in enumerate(args)]
    outs = [(shape, dtype, None) for shape, dtype in outs]
    return call(kernel, ins, outs, scratch, micros, ties)


def normalise(v):
    mean = jnp.mean(v, axis=1, keepdims=True)
    c = v - mean
    r = lax.rsqrt(jnp.mean(c * c, axis=1, keepdims=True) + 1e-05)
    return c * r, r


def norm_back(grad, hat, r, gain):
    g = grad * gain
    a = jnp.mean(g, axis=1, keepdims=True)
    b = jnp.mean(g * hat, axis=1, keepdims=True)
    return r * (g - a - hat * b)


C0 = math.sqrt(2.0 / math.pi)
C1 = 0.044715


def gelu(x):
    return 0.5 * x * (1.0 + jnp.tanh(x * (C0 + C0 * C1 * (x * x))))


def gelu_and_slope(x):
    xx = x * x
    t = jnp.tanh(x * (C0 + C0 * C1 * xx))
    half = 0.5 * (1.0 + t)
    return x * half, half + (0.5 * x) * (1.0 - t * t) * (C0 + 3.0 * C0 * C1 * xx)


def sigmoid(x):
    return 0.5 * jnp.tanh(0.5 * x) + 0.5


def fold8(v):
    return jnp.sum(v.reshape(v.shape[0] // 8, 8, v.shape[1]), axis=0)


def rows_at(i, tile, start=0):
    return pl.ds(pl.multiple_of(start + i * tile, 16), tile)


def places(base, rows, lanes=LANES):
    return base + lax.broadcasted_iota(jnp.int32, (rows, lanes), 0)


ROWS = {"glu": 16, "wide": 16, "narrow": 48, "point": 64, "qkv": 16, "attn": 16, "up": 16, "down": 64, "small": 16}


def columns_of(name, *chunks):
    return [(name, j) for j in chunks]


WIDE, GLU, QKV, UP = (columns_of(n, *range(k)) for n, k in (("wide", 8), ("glu", 4), ("qkv", 6), ("up", 8)))
NARROW_0, POINT_0, SMALL_0 = (columns_of(n, 0) for n in ("narrow", "point", "small"))
ATTN, DOWN = columns_of("attn", 0, 1), columns_of("down", 0, 1)
LAST = (UP + ATTN[:1], ATTN[1:] + DOWN)
GATHERS = ((WIDE + QKV[:5], GLU + NARROW_0 + SMALL_0 + QKV[5:] + POINT_0), LAST)
SUMS = (
    LAST,
    (QKV[:5], QKV[5:] + POINT_0),
    (WIDE[:6], WIDE[6:] + NARROW_0),
    (GLU[:2], GLU[2:] + SMALL_0),
)


def height(items):
    return sum(ROWS[name] for name, _ in items)


def row_of(items, item):
    return height(items[: items.index(item)])


def slot_bits(half, r):
    high, low, z = r >> 3, r >> 2 & 1, r & 3
    x, y = (high, low) if half == 0 else (low, high)
    return z * 8 + y * 4 + x * 2


def slot_of(half, rel):
    z, y, x, c = rel >> 3, rel >> 2 & 1, rel >> 1 & 1, rel & 1
    high, low = (x, y) if half == 0 else (y, x)
    return c * 16 + high * 8 + low * 4 + z


def unpack(me, group, pieces, wanted):
    for half, items in enumerate(GATHERS[group]):
        for core in range(2):
            piece = pieces[half * 2 + core]
            for r in range(BLOCKS // 2):
                owner = (slot_bits(half, r) + core) ^ me
                for name, j in items:
                    if name in wanted:
                        b, off = ROWS[name], row_of(items, (name, j))
                        wanted[name][
                            pl.ds(pl.multiple_of(owner * b, 16), b), j * PACK : (j + 1) * PACK
                        ] = piece[r, off : off + b, :]


def put(me, group, ref, item, value, start=0):
    half = int(item in SUMS[group][1])
    off = row_of(SUMS[group][half], item) + half * height(SUMS[group][0])
    b = ROWS[item[0]]
    for k in range(value.shape[0] // b):
        slot = slot_of(half, (start + k) ^ me)
        ref[slot, off : off + b, :] = value[k * b : (k + 1) * b]


def group_grads(group):
    return [((BLOCKS, height(sum(SUMS[group], [])), PACK), BF)]


SHAPES = {"glu": (D, 2 * D), "wide": (D, FF), "narrow": (3 * D, NARROW), "qkv": (D, 3 * D), "point": (FF, NARROW)}

GAINS = ((0, 16), (16, 16), (32, 64), (96, 16), (112, 16))
TAPS = 128
TAP_RUN = KERNEL * FF // BLOCKS
SMALL_ROWS = 3


def iota(shape, dim):
    return lax.broadcasted_iota(jnp.int32, shape, dim)


def owner_slots(me):
    shape = (BLOCKS, BLOCKS)
    return (slot_of(1, iota(shape, 0) ^ me) == iota(shape, 1)).astype(F32).astype(BF)


def gain_maps(offset, width):
    total = BLOCKS * width
    owner = iota((BLOCKS, total), 1) // width == iota((BLOCKS, total), 0)
    value = iota((LANES, total), 0) == offset + iota((LANES, total), 1) % width
    return owner, value.astype(F32).astype(BF)


def tap_runs():
    for b in range(KERNEL * FF // 64):
        f = b * 64
        yield f // FF, f % FF, f // TAP_RUN, TAPS + f % TAP_RUN


def read_small(me, pieces, gains, taps, table):
    off = row_of(GATHERS[0][1], SMALL_0[0])
    for core in range(2):
        for r in range(BLOCKS // 2):
            rows = pieces[2 + core][r, off : off + 16, :].astype(F32)
            slot = core * 16 + r
            for q in range(SMALL_ROWS):
                table[slot : slot + 1, q * PACK : (q + 1) * PACK] = rows[q : q + 1, :]
    table[...] = nn(owner_slots(me), table[...].astype(BF))
    for ref, (offset, width) in zip(gains, GAINS):
        owner, value = gain_maps(offset, width)
        spread = nn(table[:, :LANES].astype(BF), value)
        ref[...] = jnp.sum(jnp.where(owner, spread, 0.0), axis=0, keepdims=True)
    for tap, channel, who, place in tap_runs():
        taps[tap : tap + 1, channel : channel + 64] = table[who : who + 1, place : place + 64]


def write_small(me, gains, taps, table, block, grads):
    table[...] = jnp.zeros_like(table)
    total = jnp.zeros((BLOCKS, LANES), F32)
    for gain, (offset, width) in zip(gains, GAINS):
        owner, value = gain_maps(offset, width)
        total = total + nt(jnp.where(owner, gain[...], 0.0).astype(BF), value)
    table[:, :LANES] = total
    for tap, channel, who, place in tap_runs():
        table[who : who + 1, place : place + 64] = taps[tap : tap + 1, channel : channel + 64]
    table[...] = tn(owner_slots(me), table[...].astype(BF))
    block[...] = jnp.zeros_like(block)
    for slot in range(BLOCKS):
        for q in range(SMALL_ROWS):
            block[slot, q : q + 1, :] = table[slot : slot + 1, q * PACK : (q + 1) * PACK]
    at = height(GLU)
    grads[:, at : at + 16, :] = block[...].astype(BF)


def pack_kernel(names, *refs):
    shards = dict(zip(names, refs))
    for ref, halves in zip(refs[len(names) :], GATHERS):
        at = 0
        for name, j in sum(halves, []):
            b = ROWS[name]
            if name == "small":
                ref[at : at + b, :] = shards[name][...]
            else:
                ref[at : at + b, :] = shards[name][:, j * PACK : (j + 1) * PACK]
            at += b


def pack(shards):
    names = tuple(shards)
    return call(
        functools.partial(pack_kernel, names),
        [(shards[k], None) for k in names],
        [((height(sum(halves, [])), PACK), BF, None) for halves in GATHERS],
        micros=2,
    )


def front1_kernel(scal, x_ref, p0, p1, p2, p3, h1_ref, y2_ref, joined_ref, *refs):
    weights, gains, taps, table = refs[:5], refs[5:10], refs[10], refs[11]
    g1, g2 = gains[:2]

    @pl.when(pl.program_id(0) == 0)
    def _():
        read_small(scal[2], (p0, p1, p2, p3), gains, taps, table)
        unpack(scal[2], 0, (p0, p1, p2, p3), dict(zip(SHAPES, weights)))

    x = x_ref[...].astype(F32)
    hat, _ = normalise(x)
    joined = nn((hat * g1[...]).astype(BF), weights[0][...])
    joined_ref[...] = joined
    h1 = x + joined[:, :D] * sigmoid(joined[:, D:])
    h1_ref[...] = h1
    hat2, _ = normalise(h1)
    y2_ref[...] = (hat2 * g2[...]).astype(BF)


def front1(scal, x, pieces, ties=()):
    rows = x.shape[0]
    tile = 160
    return call(
        front1_kernel,
        [(scal, "s"), (x, tile)] + [(p, None) for p in pieces],
        [((rows, D), F32, tile), ((rows, D), BF, tile), ((rows, 2 * D), F32, tile)]
        + [(shape, BF, None) for shape in SHAPES.values()]
        + [((1, BLOCKS * width), F32, None) for _, width in GAINS]
        + [((KERNEL, FF), F32, None)],
        scratch=[((BLOCKS, SMALL_ROWS * PACK), F32)],
        micros=12,
        ties=ties,
        steps=rows // tile,
    )


def front2_kernel(tile, group, scal, y2_ref, g3, wide, narrow, left_ref, right_ref, mid_ref, u_ref):
    rows = y2_ref.shape[0]
    base = scal[0] * (rows - 2 * RIM) - RIM
    first = scal[1]
    i = pl.program_id(0)

    @pl.when(i == 0)
    def _():
        u_ref[0:RIM, :] = jnp.zeros((RIM, 3 * NARROW), F32)
        u_ref[RIM + rows : 2 * RIM + rows, :] = jnp.zeros((RIM, 3 * NARROW), F32)

        def narrow_step(j, carry):
            y = y2_ref[rows_at(j, tile), :]
            for k in range(3):
                u_ref[rows_at(j, tile, RIM), k * NARROW : (k + 1) * NARROW] = nn(
                    y, narrow[k * D : (k + 1) * D, :]
                )
            return carry

        lax.fori_loop(0, rows // tile, narrow_step, 0)

    around = pl.ds(pl.multiple_of(i * tile, 16), tile + 2 * RIM)
    left = nn(y2_ref[rows_at(i, tile), :], wide[...])
    left_ref[...] = left
    pos = places(base + i * tile, tile, NARROW)
    before = pltpu.roll(u_ref[around, 0:NARROW], 1, 0)[RIM : RIM + tile]
    after = pltpu.roll(u_ref[around, 2 * NARROW :], tile + 2 * RIM - 1, 0)[RIM : RIM + tile]
    right = u_ref[rows_at(i, tile, RIM), NARROW : 2 * NARROW]
    right = right + jnp.where((pos == first) | (pos == 0), 0.0, before)
    right = right + jnp.where((pos + 1 == first) | (pos + 1 == group), 0.0, after)
    right_ref[...] = right
    left = gelu(left)
    joined = jnp.concatenate([left[:, :NARROW] + gelu(right), left[:, NARROW:]], axis=1)
    hat, _ = normalise(joined)
    row = base + i * tile + lax.broadcasted_iota(jnp.int32, (tile, 1), 0)
    inside = ((row >= 0) & (row < group)).astype(F32)
    mid_ref[...] = (hat * inside * g3[...]).astype(BF)


def front2(scal, y2, g3, wide, narrow, group, ties=()):
    rows = y2.shape[0]
    tile = 160
    return call(
        functools.partial(front2_kernel, tile, group),
        [(scal, "s"), (y2, None), (g3, None), (wide, None), (narrow, None)],
        [((rows, FF), F32, tile), ((rows, NARROW), F32, tile), ((rows, FF), BF, tile)],
        scratch=[((rows + 2 * RIM, 3 * NARROW), F32)],
        micros=12,
        ties=ties,
        steps=rows // tile,
    )


def crosses(pos, offset, first):
    if offset > 0:
        return (pos < first) & (pos + offset >= first)
    return (pos >= first) & (pos + offset < first)


def conv(win, tile, taps, lanes, pos, first, masked, sign):
    total = None
    for k in range(KERNEL):
        o = sign * (k - HALF)
        v = win[RIM + o : RIM + o + tile, :]
        if masked and o != 0:
            v = jnp.where(crosses(pos, o, first), 0.0, v)
        v = v * taps[k : k + 1, lanes]
        total = v if total is None else total + v
    return total


def front3_kernel(tile, n, share, scal, mid_ref, taps, h1_ref, g4, point, qkv_w, *refs):
    spread_ref, h2_ref, y4_ref = refs[:3]
    outs = refs[3 : 3 + n]
    win, qkv_s = refs[3 + n :]
    i = pl.program_id(0)
    s, first = scal[0], scal[1]
    begin = s * (mid_ref.shape[0] - 2 * RIM) + i * tile
    near = (first > begin - HALF) & (first < begin + tile + HALF)

    def chunk(c, carry):
        lanes = pl.ds(pl.multiple_of(c * LANES, LANES), LANES)
        around = pl.ds(pl.multiple_of(i * tile, 16), tile + 2 * RIM)
        win[...] = mid_ref[around, lanes].astype(F32)
        pos = places(begin, tile)
        for masked in (False, True):

            @pl.when(near if masked else jnp.logical_not(near))
            def _():
                spread_ref[:, lanes] = conv(win, tile, taps, lanes, pos, first, masked, 1).astype(BF)

        return carry

    lax.fori_loop(0, FF // LANES, chunk, 0)
    h1 = h1_ref[rows_at(i, tile, RIM), :]
    branch = nn(spread_ref[...], point[...])
    h2 = jnp.concatenate([h1[:, :NARROW] + branch, h1[:, NARROW:]], axis=1)
    h2_ref[...] = h2
    hat, _ = normalise(h2)
    y4 = (hat * g4[...]).astype(BF)
    y4_ref[...] = y4
    qkv_s[...] = nn(y4, qkv_w[...]).astype(BF)
    for k in range(n):
        block = (s ^ k) // share
        for part in range(3):
            outs[k][:, part * LANES : (part + 1) * LANES] = qkv_s[
                :, pl.ds(pl.multiple_of(part * D + block * LANES, LANES), LANES)
            ]


def front3(scal, mid, taps, h1, g4, point, qkv_w, n, share, ties=()):
    rows = mid.shape[0] - 2 * RIM
    tile = 128
    return call(
        functools.partial(front3_kernel, tile, n, share),
        [(scal, "s")] + [(a, None) for a in (mid, taps, h1, g4, point, qkv_w)],
        [((rows, FF), BF, tile), ((rows, D), F32, tile), ((rows, D), BF, tile)]
        + [((rows, 3 * LANES), BF, tile)] * n,
        scratch=[((tile + 2 * RIM, LANES), F32), ((tile, 3 * D), BF)],
        micros=20,
        ties=ties,
        steps=rows // tile,
    )


def gather_lanes(wide_ref, n, share, s, blocks, parts):
    rows = wide_ref.shape[0]
    for k in range(n):
        block = (s ^ k) // share
        for part in range(parts):
            lanes = pl.ds(pl.multiple_of(part * D + block * LANES, LANES), LANES)
            new = blocks[k][:, part * LANES : (part + 1) * LANES]
            if share > 1:
                lane = lax.broadcasted_iota(jnp.int32, (rows, LANES), 1)
                mine = lane // (LANES // share) == (s ^ k) % share
                new = jnp.where(mine, new.astype(F32), wide_ref[:, lanes].astype(F32)).astype(BF)
            wide_ref[:, lanes] = new


def middle_kernel(n, share, scal, h2_ref, *refs):
    att = refs[:n]
    cot_ref, g5, p0, p1, p2, p3, mixed_ref, dh3_ref = refs[n : n + 8]
    datt = refs[n + 8 : 2 * n + 8]
    att_s, y5_s, inner_s, du_s, ln_out = refs[2 * n + 8 : 2 * n + 13]
    wa, wup, wdown, ln_ref = refs[2 * n + 13 :]
    s = scal[0]
    i = pl.program_id(0)

    @pl.when(i == 0)
    def _():
        unpack(scal[2], 1, (p0, p1, p2, p3), {"attn": wa, "up": wup, "down": wdown})
        ln_ref[...] = jnp.zeros_like(ln_ref)

    gather_lanes(att_s, n, share, s, att, 1)
    h3 = h2_ref[...] + nn(att_s[...], wa[...])
    hat, r = normalise(h3)
    y5 = (hat * g5[...]).astype(BF)
    y5_s[...] = y5
    value, slope = gelu_and_slope(nn(y5, wup[...]))
    inner = value.astype(BF)
    inner_s[...] = inner
    mixed_ref[...] = (h3 + nn(inner, wdown[...])).astype(BF)
    cot = cot_ref[...]
    du = (nt(cot, wdown[...]) * slope).astype(BF)
    du_s[...] = du
    dy5 = nt(du, wup[...])
    ln_ref[...] += fold8(dy5 * hat)
    dh3 = cot.astype(F32) + norm_back(dy5, hat, r, g5[...])
    dh3_ref[...] = dh3
    da = nt(dh3.astype(BF), wa[...]).astype(BF)
    for j in range(D // LANES):
        for k in range(n):

            @pl.when((s ^ k) // share == j)
            def _():
                datt[k][...] = da[:, j * LANES : (j + 1) * LANES]

    ln_out[...] = jnp.sum(ln_ref[...], axis=0, keepdims=True)


def middle(scal, h2, att, cot, g5, pieces, n, share, ties=()):
    rows = h2.shape[0]
    tile = 128
    return call(
        functools.partial(middle_kernel, n, share),
        [(scal, "s"), (h2, tile)]
        + [(a, tile) for a in (*att, cot)]
        + [(a, None) for a in (g5, *pieces)],
        [((rows, D), BF, tile), ((rows, D), F32, tile)]
        + [((rows, LANES), BF, tile)] * n
        + [((rows, c), BF, tile) for c in (D, D, FF, FF)]
        + [((1, D), F32, None)],
        scratch=[((D, D), BF), ((D, FF), BF), ((FF, D), BF), ((8, D), F32)],
        micros=20,
        ties=ties,
        steps=rows // tile,
    )


def weigh0_kernel(scal, att_s, y5_s, inner_s, du_s, cot_ref, dh3_ref, grads):
    me = scal[2]
    att_t = att_s[...].T
    for j in range(D // PACK):
        part = nn(att_t, dh3_ref[:, j * PACK : (j + 1) * PACK].astype(BF))
        put(me, 0, grads, ("attn", j), part.astype(BF))
    y5_t = y5_s[...].T
    for j in range(FF // PACK):
        cols = slice(j * PACK, (j + 1) * PACK)
        put(me, 0, grads, ("up", j), nn(y5_t, du_s[:, cols]).astype(BF))
        down = tn(inner_s[:, cols], cot_ref[...]).astype(BF)
        for m in range(D // PACK):
            put(me, 0, grads, ("down", m), down[:, m * PACK : (m + 1) * PACK], j * PACK // 64)


def weigh0(scal, att, y5, inner, du, cot, dh3, ties=()):
    return whole_call(
        weigh0_kernel, group_grads(0), [scal, att, y5, inner, du, cot, dh3], micros=10, ties=ties
    )


def back3_kernel(n, share, scal, *refs):
    blocks = refs[:n]
    dh3_ref, h2_ref, g4, qkv_w = refs[n : n + 4]
    dh2_ref, db_ref, dqkv_s, ln_out, ln_ref = refs[n + 4 :]

    @pl.when(pl.program_id(0) == 0)
    def _():
        ln_ref[...] = jnp.zeros_like(ln_ref)

    gather_lanes(dqkv_s, n, share, scal[0], blocks, 3)
    dy4 = nt(dqkv_s[...], qkv_w[...])
    hat, r = normalise(h2_ref[...])
    ln_ref[...] += fold8(dy4 * hat)
    dh2 = dh3_ref[...] + norm_back(dy4, hat, r, g4[...])
    dh2_ref[...] = dh2
    db_ref[...] = dh2[:, :NARROW].astype(BF)
    ln_out[...] = jnp.sum(ln_ref[...], axis=0, keepdims=True)


def back3(scal, blocks, dh3, h2, g4, qkv_w, n, share, ties=()):
    rows = h2.shape[0]
    tile = 128
    return call(
        functools.partial(back3_kernel, n, share),
        [(scal, "s")] + [(a, tile) for a in (*blocks, dh3, h2)] + [(g4, None), (qkv_w, None)],
        [((rows, D), F32, tile), ((rows, NARROW), BF, tile), ((rows, 3 * D), BF, tile)]
        + [((1, D), F32, None)],
        scratch=[((8, D), F32)],
        micros=6,
        ties=ties,
        steps=rows // tile,
    )


def weigh1_kernel(scal, y4_ref, dqkv_s, spread_ref, db_ref, grads):
    me = scal[2]
    y4_t = y4_ref[...].T
    for j in range(3 * D // PACK):
        part = nn(y4_t, dqkv_s[:, j * PACK : (j + 1) * PACK])
        put(me, 1, grads, ("qkv", j), part.astype(BF))
    for j in range(FF // PACK):
        part = tn(spread_ref[:, j * PACK : (j + 1) * PACK], db_ref[...]).astype(BF)
        put(me, 1, grads, ("point", 0), part, j * PACK // 64)


def weigh1(scal, y4, dqkv, spread, db, ties=()):
    return whole_call(
        weigh1_kernel, group_grads(1), [scal, y4, dqkv, spread, db], micros=8, ties=ties
    )


def back2_kernel(tile, group, scal, low_ref, db_ref, high_ref, *refs):
    taps, mid_ref, left_ref, right_ref, g3, point = refs[:6]
    dl, st, gdepth_out, ln_out = refs[6:10]
    dbx, dsp, win, dmid, dr, gdepth_ref, ln_ref = refs[10:]
    rows = db_ref.shape[0]
    ext = rows + 2 * RIM
    base = scal[0] * rows - RIM
    first = scal[1]
    i = pl.program_id(0)
    last = ext // tile - 1

    @pl.when(i == 0)
    def _():
        dbx[0:RIM, :] = low_ref[...]
        dbx[RIM : RIM + rows, :] = db_ref[...]
        dbx[RIM + rows :, :] = high_ref[...]
        dsp[0:RIM, :] = jnp.zeros((RIM, FF), F32)
        dsp[RIM + ext :, :] = jnp.zeros((RIM, FF), F32)
        dr[0:RIM, :] = jnp.zeros((RIM, NARROW), F32)
        dr[RIM + ext :, :] = jnp.zeros((RIM, NARROW), F32)
        gdepth_ref[...] = jnp.zeros_like(gdepth_ref)
        ln_ref[...] = jnp.zeros_like(ln_ref)

        def spread_step(j, carry):
            dsp[rows_at(j, tile, RIM), :] = nt(dbx[rows_at(j, tile), :], point[...])
            return carry

        lax.fori_loop(0, ext // tile, spread_step, 0)

    begin = base + i * tile
    near = (first > begin - HALF) & (first < begin + tile + HALF)
    near = near | (i == 0) | (i == last)

    def chunk(c, carry):
        lanes = pl.ds(pl.multiple_of(c * LANES, LANES), LANES)
        around = pl.ds(pl.multiple_of(i * tile, 16), tile + 2 * RIM)
        win[...] = dsp[around, lanes]
        local = i * tile + lax.broadcasted_iota(jnp.int32, (tile, LANES), 0)
        mid = mid_ref[:, lanes].astype(F32)
        pos = places(begin, tile)
        for masked in (False, True):

            @pl.when(near if masked else jnp.logical_not(near))
            def _():
                total = None
                for k in range(KERNEL):
                    o = HALF - k
                    v = win[RIM + o : RIM + o + tile, :]
                    if masked and o != 0:
                        v = jnp.where(crosses(pos, o, first), 0.0, v)
                    counted = v
                    if masked:
                        kept = (local + o >= RIM) & (local + o < RIM + rows)
                        counted = jnp.where(kept, v, 0.0)
                    gdepth_ref[k * 8 : (k + 1) * 8, lanes] += fold8(counted * mid)
                    v = v * taps[k : k + 1, lanes]
                    total = v if total is None else total + v
                dmid[:, lanes] = total

        return carry

    lax.fori_loop(0, FF // LANES, chunk, 0)
    left, slope = gelu_and_slope(left_ref[...])
    right, slope_r = gelu_and_slope(right_ref[...])
    joined = jnp.concatenate([left[:, :NARROW] + right, left[:, NARROW:]], axis=1)
    hat, r = normalise(joined)
    local = i * tile + lax.broadcasted_iota(jnp.int32, (tile, 1), 0)
    own = ((local >= RIM) & (local < RIM + rows)).astype(F32)
    pos = base + local
    grad = dmid[...] * ((pos >= 0) & (pos < group)).astype(F32)
    ln_ref[...] += fold8(grad * hat * own)
    dj = norm_back(grad, hat, r, g3[...])
    dl[...] = (dj * slope).astype(BF)
    dr[rows_at(i, tile, RIM), :] = (dj[:, :NARROW] * slope_r).astype(BF).astype(F32)

    @pl.when(i == last)
    def _():
        for k in range(KERNEL):
            gdepth_out[k : k + 1, :] = jnp.sum(
                gdepth_ref[k * 8 : (k + 1) * 8, :], axis=0, keepdims=True
            )
        ln_out[...] = jnp.sum(ln_ref[...], axis=0, keepdims=True)
        part = 128

        def gather_step(j, carry):
            at = rows_at(j, part)
            around = pl.ds(pl.multiple_of(RIM + j * part, 16), part + 2 * RIM)
            pos = places(base + RIM + j * part, part, NARROW)
            v = dr[around, :]
            after = pltpu.roll(v, part + 2 * RIM - 1, 0)[RIM : RIM + part]
            before = pltpu.roll(v, 1, 0)[RIM : RIM + part]
            after = jnp.where((pos + 1 == first) | (pos + 1 == group), 0.0, after)
            before = jnp.where((pos == first) | (pos == 0), 0.0, before)
            st[at, 0:NARROW] = after.astype(BF)
            st[at, NARROW : 2 * NARROW] = v[RIM : RIM + part].astype(BF)
            st[at, 2 * NARROW :] = before.astype(BF)
            return carry

        lax.fori_loop(0, rows // part, gather_step, 0)


def back2(scal, low, db, high, taps, mid, left, right, g3, point, group, ties=()):
    rows = db.shape[0]
    ext = rows + 2 * RIM
    tile = 160
    return call(
        functools.partial(back2_kernel, tile, group),
        [(scal, "s")]
        + [(a, None) for a in (low, db, high, taps)]
        + [(a, tile) for a in (mid, left, right)]
        + [(g3, None), (point, None)],
        [((ext, FF), BF, tile), ((rows, 3 * NARROW), BF, None)]
        + [((KERNEL, FF), F32, None), ((1, FF), F32, None)],
        scratch=[
            ((ext, NARROW), BF),
            ((ext + 2 * RIM, FF), F32),
            ((tile + 2 * RIM, LANES), F32),
            ((tile, FF), F32),
            ((ext + 2 * RIM, NARROW), F32),
            ((8 * KERNEL, FF), F32),
            ((8, FF), F32),
        ],
        micros=44,
        ties=ties,
        steps=ext // tile,
    )


def weigh2_kernel(scal, dl, st, y2_ref, grads, gn):
    me = scal[2]
    rows = st.shape[0]
    y2_t = y2_ref[RIM : RIM + rows, :].T
    for j in range(FF // PACK):
        part = nn(y2_t, dl[RIM : RIM + rows, j * PACK : (j + 1) * PACK]).astype(BF)
        put(me, 2, grads, ("wide", j), part)
    for k in range(3):
        gn[k * D : (k + 1) * D, :] = nn(y2_t, st[:, k * NARROW : (k + 1) * NARROW]).astype(BF)
    put(me, 2, grads, ("narrow", 0), gn[...])


def weigh2(scal, dl, st, y2, ties=()):
    return whole_call(
        weigh2_kernel,
        group_grads(2),
        [scal, dl, st, y2],
        scratch=[((3 * D, NARROW), BF)],
        ties=ties,
        micros=7,
    )


def back1_kernel(tile, scal, dl, st, dh2_ref, h1_ref, joined_ref, x_ref, g1, g2, *refs):
    glu, wide, narrow, ln3, ln4, ln5, gdepth, dx_ref, grads = refs[:9]
    y1_s, dj_s, ln1_ref, ln2_ref, ln1, ln2, table, block = refs[9:]
    i = pl.program_id(0)

    @pl.when(i == 0)
    def _():
        ln1_ref[...] = jnp.zeros_like(ln1_ref)
        ln2_ref[...] = jnp.zeros_like(ln2_ref)

    at = rows_at(i, tile)
    ext = rows_at(i, tile, RIM)
    dy2 = nt(dl[ext, :], wide[...])
    for k in range(3):
        dy2 = dy2 + nt(st[:, k * NARROW : (k + 1) * NARROW], narrow[k * D : (k + 1) * D, :])
    hat2, r2 = normalise(h1_ref[ext, :])
    ln2_ref[...] += fold8(dy2 * hat2)
    dh1 = dh2_ref[...] + norm_back(dy2, hat2, r2, g2[...])
    gate = sigmoid(joined_ref[ext, D:])
    value = joined_ref[ext, :D]
    da = (dh1 * gate).astype(BF)
    db = (dh1 * value * gate * (1.0 - gate)).astype(BF)
    dj_s[at, :D] = da
    dj_s[at, D:] = db
    x = x_ref[ext, :].astype(F32)
    hat1, r1 = normalise(x)
    y1_s[at, :] = (hat1 * g1[...]).astype(BF)
    dy1 = nt(dj_s[at, :], glu[...])
    ln1_ref[...] += fold8(dy1 * hat1)
    dx_ref[...] = (dh1 + norm_back(dy1, hat1, r1, g1[...])).astype(dx_ref.dtype)

    @pl.when(i == pl.num_programs(0) - 1)
    def _():
        ln1[...] = jnp.sum(ln1_ref[...], axis=0, keepdims=True)
        ln2[...] = jnp.sum(ln2_ref[...], axis=0, keepdims=True)
        write_small(scal[2], (ln1, ln2, ln3, ln4, ln5), gdepth, table, block, grads)
        y1_t = y1_s[...].T
        for j in range(2 * D // PACK):
            part = nn(y1_t, dj_s[:, j * PACK : (j + 1) * PACK]).astype(BF)
            put(scal[2], 3, grads, ("glu", j), part)


def back1(scal, dl, st, dh2, h1, joined, x, g1, g2, glu, wide, narrow, small, ties=()):
    rows = st.shape[0]
    tile = 128
    return call(
        functools.partial(back1_kernel, tile),
        [(scal, "s"), (dl, None), (st, tile), (dh2, tile)]
        + [(a, None) for a in (h1, joined, x, g1, g2, glu, wide, narrow, *small)],
        [((rows, D), BF, tile), (*group_grads(3)[0], None)],
        scratch=[((rows, D), BF), ((rows, 2 * D), BF), ((8, D), F32), ((8, D), F32)]
        + [((1, D), F32), ((1, D), F32), ((BLOCKS, SMALL_ROWS * PACK), F32), ((BLOCKS, 16, PACK), F32)],
        micros=18,
        ties=ties,
        steps=rows // tile,
    )


def lane_maps(rows, head):
    lane = lax.broadcasted_iota(jnp.int32,(rows,LANES),1)
    own = (lane >= head*HEAD) & (lane < (head+1)*HEAD)
    rel = lane - (1-head)*HEAD
    return own, rel

def id_column(base, rows, first):
    pos = base + lax.broadcasted_iota(jnp.int32,(rows,LANES),0)
    return pos >= first

def split3(v):
    hi = v.astype(BF).astype(F32)
    mid = (v-hi).astype(BF).astype(F32)
    return hi, mid, v-hi-mid

def tile_ids(start, rows, first):
    return start < first, start+rows > first

def overlap(a_start,a_rows,b_start,b_rows,first):
    a0,a1 = tile_ids(a_start,a_rows,first); b0,b1=tile_ids(b_start,b_rows,first)
    return (a0&b0)|(a1&b1)

def attend_kernel(n, heads, share, tq, tk, scal, *refs):
    qkv = refs[:n]; att = refs[n:2*n]; lse_ref = refs[2*n]
    qa, ka, va, mx_ref, m_ref, q2_ref, acc_ref = refs[2*n+1:]
    s = scal[0]; first = scal[1]
    rows = qkv[0].shape[0]
    for k in range(n):
        base = (s ^ k)*rows
        id1 = id_column(base, rows, first).astype(F32)
        q = qkv[k][:, 0:LANES].astype(F32)*(HEAD**-0.5)
        key = qkv[k][:, LANES:2*LANES].astype(F32)
        v = qkv[k][:, 2*LANES:3*LANES].astype(F32)
        for i in range(heads):
            h = i if share==1 else s % share
            own, rel = lane_maps(rows, h)
            qx = jnp.where(rel==0, 1.0-id1, jnp.where(rel==1, id1, 0.0))
            kx = jnp.where(rel==0, id1*BIG, jnp.where(rel==1, (1.0-id1)*BIG, jnp.where(rel<5,1.0,0.0)))
            qa[i, k*rows:(k+1)*rows,:] = jnp.where(own, q, qx).astype(BF)
            ka[i, k*rows:(k+1)*rows,:] = jnp.where(own, key, kx).astype(BF)
            va[i, k*rows:(k+1)*rows,:] = jnp.where(own, v, 1.0).astype(BF)
    per = rows//tq; per_k = rows//tk
    def fold(sc, best):
        for j in range(tk//LANES):
            best = jnp.maximum(best, sc[:, j*LANES:(j+1)*LANES])
        return best
    def q_step(it, carry):
        kq = it//per
        r0 = pl.multiple_of((it % per)*tq, tq)
        g0 = pl.multiple_of(it*tq, tq)
        own0 = pl.multiple_of((g0//tk)*tk, tk)
        q_start = (s ^ kq)*rows + r0
        for i in range(heads):
            for j in range(max(1,tq//tk)):
                sc = nt(qa[i, pl.ds(g0,tq),:], ka[i, pl.ds(own0+j*tk,tk),:])
                best = fold(sc, sc[:, :LANES] if j==0 else best)
            mx_ref[i] = best
            m_ref[i] = jnp.zeros((tq,LANES),F32)
        def attempt(again):
            for i in range(heads):
                h = i if share==1 else s % share
                own, rel = lane_maps(tq, h)
                m = jnp.max(mx_ref[i], axis=1, keepdims=True)
                mb = m_ref[i] + jnp.broadcast_to(m, (tq,LANES))
                m_ref[i] = mb
                hi,mid,lo = split3(-mb)
                q = qa[i, pl.ds(g0,tq),:].astype(F32)
                q2_ref[i] = jnp.where(rel==2,hi,jnp.where(rel==3,mid,jnp.where(rel==4,lo,q))).astype(BF)
            mx_ref[...] = jnp.full_like(mx_ref, -3e38)
            acc_ref[...] = jnp.zeros_like(acc_ref)
            for kt in range(n*per_k):
                k_start = (s ^ (kt//per_k))*rows + (kt%per_k)*tk
                @pl.when(overlap(q_start,tq,k_start,tk,first))
                def _():
                    for i in range(heads):
                        sc = nt(q2_ref[i], ka[i, kt*tk:(kt+1)*tk,:])
                        mx_ref[i] = fold(sc, mx_ref[i])
                        p = jnp.exp2(sc*LOG2E).astype(BF)
                        acc_ref[i] += nn(p, va[i, kt*tk:(kt+1)*tk,:])
            return (jnp.max(mx_ref[...]) > 40.0).astype(jnp.int32)
        lax.while_loop(lambda again: again > 0, attempt, jnp.int32(1))
        out = jnp.zeros((tq,LANES),F32); lse = jnp.zeros((tq,LANES),F32)
        for i in range(heads):
            h = i if share==1 else s % share
            own,_ = lane_maps(tq,h)
            acc = acc_ref[i]
            total = pltpu.roll(acc, HEAD, 1)
            out = jnp.where(own, acc/total, out)
            lse = jnp.where(own, m_ref[i]+jnp.log(total), lse)
        lse_ref[pl.ds(g0,tq),:] = lse
        for k in range(n):
            @pl.when(kq==k)
            def _():
                att[k][pl.ds(r0,tq),:] = out.astype(BF)
        return carry
    lax.fori_loop(0, n*per, q_step, 0)

def attend(scal, blocks, n, share, tq=768, tk=384, ties=()):
    rows = blocks[0].shape[0]
    heads = 2 // share
    return whole_call(
        functools.partial(attend_kernel, n, heads, share, tq, tk),
        [((rows, LANES), BF)] * n + [((n * rows, LANES), F32)],
        [scal, *blocks],
        scratch=[((heads, n * rows, LANES), BF)] * 3
        + [((heads, tq, LANES), F32)] * 2
        + [((heads, tq, LANES), BF), ((heads, tq, LANES), F32)],
        ties=ties,
        micros=36,
    )


def attend_back_kernel(n, heads, share, tq, tk, scal, *refs):
    qkv = refs[:n]; att = refs[n:2*n]; dat = refs[2*n:3*n]; lse_ref = refs[3*n]
    out = refs[3*n+1:4*n+1]
    qa, ka, va, da, dq_ref, dk_ref, dv_ref = refs[4*n+1:]
    s = scal[0]; first = scal[1]
    rows = qkv[0].shape[0]
    for k in range(n):
        base = (s ^ k)*rows
        sl = slice(k*rows,(k+1)*rows)
        id1 = id_column(base, rows, first).astype(F32)
        q = qkv[k][:, 0:LANES].astype(F32)*(HEAD**-0.5)
        key = qkv[k][:, LANES:2*LANES].astype(F32)
        v = qkv[k][:, 2*LANES:3*LANES].astype(F32)
        do = dat[k][...].astype(F32)
        prod = do*att[k][...].astype(F32)
        for i in range(heads):
            h = i if share==1 else s % share
            own, rel = lane_maps(rows, h)
            lse = pltpu.roll(lse_ref[sl,:], HEAD, 1)
            hi,mid,lo = split3(-lse)
            delta = jnp.sum(jnp.where(own,prod,0.0),axis=1,keepdims=True)
            dhi,dmid,dlo = split3(-delta)
            qx = jnp.where(rel==0, 1.0-id1, jnp.where(rel==1, id1, jnp.where(rel==2,hi,jnp.where(rel==3,mid,jnp.where(rel==4,lo,0.0)))))
            kx = jnp.where(rel==0, id1*BIG, jnp.where(rel==1, (1.0-id1)*BIG, jnp.where(rel<5,1.0,0.0)))
            vx = jnp.where(rel<3,1.0,0.0)
            dx = jnp.where(rel==0,dhi,jnp.where(rel==1,dmid,jnp.where(rel==2,dlo,0.0)))
            qa[i,sl,:] = jnp.where(own,q,qx).astype(BF)
            ka[i,sl,:] = jnp.where(own,key,kx).astype(BF)
            va[i,sl,:] = jnp.where(own,v,vx).astype(BF)
            da[i,sl,:] = jnp.where(own,do,dx).astype(BF)
    dq_ref[...] = jnp.zeros_like(dq_ref)
    per_q = rows//tq; per_k = rows//tk
    def k_step(kt, carry):
        k0 = pl.multiple_of(kt*tk, tk)
        kk = kt//per_k
        k_start = (s ^ kk)*rows + (kt % per_k)*tk
        for i in range(heads):
            dk_ref[i] = jnp.zeros((tk,LANES),F32)
            dv_ref[i] = jnp.zeros((tk,LANES),F32)
        def q_step(qt, c2):
            q0 = pl.multiple_of(qt*tq, tq)
            q_start = (s ^ (qt//per_q))*rows + (qt % per_q)*tq
            @pl.when(overlap(q_start,tq,k_start,tk,first))
            def _():
                for i in range(heads):
                    qq = qa[i,pl.ds(q0,tq),:]; kx = ka[i,pl.ds(k0,tk),:]; dd = da[i,pl.ds(q0,tq),:]
                    st = nt(kx, qq)
                    p = jnp.exp2(st*LOG2E)
                    dp = nt(va[i,pl.ds(k0,tk),:], dd)
                    ds = (p*dp).astype(BF)
                    dv_ref[i] += nn(p.astype(BF), dd)
                    dk_ref[i] += nn(ds, qq)
                    dq_ref[i,pl.ds(q0,tq),:] += tn(ds, kx)
            return c2
        lax.fori_loop(0, n*per_q, q_step, 0)
        dk = jnp.zeros((tk,LANES),F32); dv = jnp.zeros((tk,LANES),F32)
        for i in range(heads):
            h = i if share==1 else s % share
            own,_ = lane_maps(tk,h)
            dk = jnp.where(own, dk_ref[i], dk); dv = jnp.where(own, dv_ref[i], dv)
        r0 = pl.multiple_of((kt % per_k)*tk, tk)
        for k in range(n):
            @pl.when(kk==k)
            def _():
                out[k][pl.ds(r0,tk),LANES:2*LANES] = dk.astype(BF)
                out[k][pl.ds(r0,tk),2*LANES:3*LANES] = dv.astype(BF)
        return carry
    lax.fori_loop(0, n*per_k, k_step, 0)
    for k in range(n):
        sl = slice(k*rows,(k+1)*rows)
        dq = jnp.zeros((rows,LANES),F32)
        for i in range(heads):
            h = i if share==1 else s % share
            own,_ = lane_maps(rows,h)
            dq = jnp.where(own, dq_ref[i,sl,:], dq)
        out[k][:, 0:LANES] = (dq*(HEAD**-0.5)).astype(BF)

def attend_back(scal, blocks, att, datt, lse, n, share, tq=384, tk=384, ties=()):
    rows = blocks[0].shape[0]
    heads = 2 // share
    return whole_call(
        functools.partial(attend_back_kernel, n, heads, share, tq, tk),
        [((rows, 3 * LANES), BF)] * n,
        [scal, *blocks, *att, *datt, lse],
        scratch=[((heads, n * rows, LANES), BF)] * 4
        + [((heads, n * rows, LANES), F32)]
        + [((heads, tk, LANES), F32)] * 2,
        ties=ties,
        micros=58,
    )


class Links:
    def __init__(self, n_seq, n_dp):
        self.count = n_seq * n_dp
        self.direct = (n_seq, n_dp) == (4, 8)

    def flip(self, value, mask):
        return lax.ppermute(value, AXES, [(i, i ^ mask) for i in range(self.count)])

    def near(self, block):
        return jnp.stack([block] + [self.flip(block, k << 3) for k in range(1, 4)])

    def part(self, group, held):
        low = height(GATHERS[group][0])
        return [held[:, :low], held[:, low:]]

    def spread(self, held, stage):
        masks = ((4, 2), (2, 4))[stage]
        return [jnp.concatenate([h, self.flip(h, m)]) for h, m in zip(held, masks)]

    def across(self, held):
        return [held[0], self.flip(held[0], 1), held[1], self.flip(held[1], 1)]

    def gather_whole(self, group, weights):
        whole = {
            name: lax.all_gather(weights[name], AXES, axis=0, tiled=True)
            for name in dict(sum(GATHERS[group], []))
        }
        pieces = []
        for half, items in enumerate(GATHERS[group]):
            blocks = [
                whole[name][:, j * PACK : (j + 1) * PACK].reshape(BLOCKS, -1, PACK)
                for name, j in items
            ]
            pieces += list(self.by_slot(jnp.concatenate(blocks, axis=1), half))
        return pieces

    def by_slot(self, blocks, half):
        shape = blocks.shape[1:]
        order = ((3, 2, 1, 0), (3, 1, 2, 0))[half]
        return blocks.reshape(4, 2, 2, 2, *shape).transpose(*order, 4, 5).reshape(2, 16, *shape)

    def by_owner(self, slots, half):
        shape = slots.shape[1:]
        order = ((3, 2, 1, 0), (3, 1, 2, 0))[half]
        return slots.reshape(2, 2, 2, 4, *shape).transpose(*order, 4, 5).reshape(BLOCKS, *shape)

    def add(self, a, b):
        return (a.astype(F32) + b.astype(F32)).astype(BF)

    def fold(self, slots, mask):
        middle = slots.shape[0] // 2
        return self.add(slots[:middle], self.flip(slots[middle:], mask))

    def first(self, group, slots):
        held = self.fold(slots, 1)
        low = height(SUMS[group][0])
        return [held[:, :low], held[:, low:]]

    def next(self, held, stage):
        masks = ((2, 4), (4, 2))[stage]
        return [self.fold(h, m) for h, m in zip(held, masks)]

    def finish(self, held):
        held = jnp.concatenate(held, axis=1)
        total = held[0].astype(F32)
        for k in range(1, 4):
            total = total + self.flip(held[k], k << 3).astype(F32)
        return total

    def rows_of(self, items, total):
        parts, at = {}, 0
        for name, j in items:
            b = ROWS[name] * BLOCKS // self.count
            parts.setdefault(name, []).append(total[at : at + b])
            at += b
        return {name: jnp.concatenate(p, axis=1) for name, p in parts.items()}

    def scatter_whole(self, group, slots):
        sent, at = [], 0
        for half, items in enumerate(SUMS[group]):
            for name, _ in items:
                blocks = self.by_owner(slots[:, at : at + ROWS[name]], half)
                sent.append(blocks.reshape(self.count, -1, PACK))
                at += ROWS[name]
        sent = jnp.concatenate(sent, axis=1)
        return lax.psum_scatter(sent, AXES, scatter_dimension=0, tiled=False).astype(F32)


class Layout:
    def __init__(self, n_seq, n_dp):
        self.n_seq, self.n_dp = n_seq, n_dp
        self.where = {}
        for g in range(n_dp):
            for s in range(n_seq):
                self.where[g, s] = self.place(g, s)
        self.block = np.zeros(n_seq * n_dp, np.int32)
        for (g, s), device in self.where.items():
            self.block[device] = s

    def place(self, g, s):
        if (self.n_seq, self.n_dp) == (4, 8):
            y, x, c = g >> 2, g >> 1 & 1, g & 1
            return (2 * c + y) * 8 + (s & 1) * 4 + x * 2 + (s >> 1)
        return s * self.n_dp + g

    def pairs(self, source, target):
        return [
            (source(g, s), target(g, s))
            for g in range(self.n_dp)
            for s in range(self.n_seq)
            if target(g, s) is not None and source(g, s) is not None
        ]

    def at(self, g, s):
        return self.where.get((g, s))

    def home(self, g, s):
        return s * self.n_dp + g

    def bring(self, value):
        return lax.ppermute(value, AXES, self.pairs(self.home, self.at))

    def bring_to(self, value, step):
        return lax.ppermute(
            value, AXES, self.pairs(self.home, lambda g, s: self.at(g, s + step))
        )

    def send_home(self, value):
        return lax.ppermute(value, AXES, self.pairs(self.at, self.home))

    def to_neighbour(self, value, step):
        return lax.ppermute(value, AXES, self.pairs(self.at, lambda g, s: self.at(g, s + step)))

    def swap(self, values):
        return [values[0]] + [
            lax.ppermute(values[k], AXES, self.pairs(self.at, lambda g, s: self.at(g, s ^ k)))
            for k in range(1, self.n_seq)
        ]


NAMES = ("ln1", "ln2", "ln3", "ln4", "ln5", "glu", "wide", "narrow", "depth", "point", "qkv", "attn", "up", "down")
SMALL = ("ln1", "ln2", "ln3", "ln4", "ln5", "depth")


def sync(*values):
    return lax.optimization_barrier(values)


def small_block(arrays, blocks):
    flat = jnp.concatenate([a.reshape(blocks, -1) for a in arrays], axis=1)
    flat = jnp.pad(flat, ((0, 0), (0, 16 * PACK - flat.shape[1])))
    return flat.reshape(blocks * 16, PACK)


def on_device(tokens, cotangent, first_length, *weights):
    n = lax.axis_size("seq")
    n_dp = lax.axis_size("dp")
    share = n * LANES // D
    layout = Layout(n, n_dp)
    links = Links(n, n_dp)
    direct = links.direct
    rows = tokens.shape[1]
    group = n * rows
    here = lax.axis_index("seq") * n_dp + lax.axis_index("dp")
    me = here if direct else jnp.zeros_like(here)
    s = jnp.asarray(layout.block)[here]
    mine = dict(zip(NAMES, weights))
    if direct:
        mine["small"] = small_block([mine[k] for k in SMALL], 1)
    else:
        small = [lax.all_gather(mine[k], AXES, axis=0, tiled=True) for k in SMALL]
        mine["small"] = small_block(small, BLOCKS).reshape(links.count, -1, PACK)[here]

    tokens = tokens[0]
    digits = jnp.where(
        lax.broadcasted_iota(jnp.int32, (RIM, D), 1) < LANES,
        first_length[0] // LANES,
        first_length[0] % LANES,
    )
    sent = jnp.concatenate([tokens, digits.astype(BF)], axis=0)
    if direct:
        packed, packed_late = pack({k: mine[k] for k in mine if k not in SMALL})
        packed, sent, packed_late = sync(packed, sent, packed_late)
        held = links.near(packed)
    x = layout.bring(sent)
    if direct:
        held, x = sync(held, x)
        held = links.spread(links.part(0, held), 0)
    low = layout.bring_to(tokens[-RIM:], 1)
    high = layout.bring_to(tokens[:RIM], -1)
    if direct:
        held, x, low, high = sync(held, x, low, high)
        held, packed_late = sync(links.spread(held, 1), packed_late)
        pieces1 = links.across(held)
        late = links.near(packed_late)
    else:
        pieces1, pieces2 = (links.gather_whole(k, mine) for k in range(2))
    digits = x[rows, 0 : 2 * LANES : LANES].astype(F32).astype(jnp.int32)
    first = digits[0] * LANES + digits[1]
    scal = jnp.stack([s.astype(jnp.int32), first, me.astype(jnp.int32)])
    x_ext = jnp.concatenate([low, x[:rows], high], axis=0)

    h1, y2, joined, *rest = front1(scal, x_ext, pieces1)
    (glu, wide, narrow, qkv_w, point), (g1, g2, g3, g4, g5, taps) = rest[:5], rest[5:]
    left, right, mid = front2(scal, y2, g3, wide, narrow, group)
    if direct:
        mid, late = sync(mid, late)
        late = links.spread(links.part(1, late), 0)
    spread, h2, y4, *qkv = front3(scal, mid, taps, h1, g4, point, qkv_w, n, share)
    if direct:
        qkv, late = sync(qkv, late)
    qkv = layout.swap(qkv)
    qkv, cot = sync(qkv, cotangent[0])
    cot = layout.bring(cot)
    if direct:
        late, qkv = sync(late, qkv)
        late = links.spread(late, 1)
    *att, lse = attend(scal, qkv, n, share)
    if direct:
        att, late, cot = sync(att, late, cot)
        pieces2 = links.across(late)
    else:
        att, cot = sync(att, cot)
    arrived = layout.swap(att)
    mixed, dh3, *rest = middle(scal, h2, arrived, cot, g5, pieces2, n, share)
    datt, (att_all, y5, inner, du, ln5) = rest[:n], rest[n:]
    datt, du = sync(datt, du)
    datt = layout.swap(datt)
    (sum0,) = weigh0(scal, att_all, y5, inner, du, cot, dh3)
    datt, sum0 = sync(datt, sum0)
    if direct:
        sum0 = links.first(0, sum0)
    dqkv = attend_back(scal, qkv, att, datt, lse, n, share)
    dqkv, sum0 = sync(dqkv, sum0)
    dqkv = layout.swap(dqkv)
    dqkv, sum0 = sync(dqkv, sum0)
    if direct:
        sum0 = links.next(sum0, 0)
    dh2, db, dqkv, ln4 = back3(scal, dqkv, dh3, h2, g4, qkv_w, n, share)
    db, dqkv = sync(db, dqkv)
    low = layout.to_neighbour(db[-RIM:], 1)
    high = layout.to_neighbour(db[:RIM], -1)
    (sum1,) = weigh1(scal, y4, dqkv, spread, db)
    low, high, sum1, sum0 = sync(low, high, sum1, sum0)
    if direct:
        sum1 = links.first(1, sum1)
        low, high, sum1, sum0, mixed = sync(low, high, sum1, sum0, mixed)
        sum0 = links.next(sum0, 1)
        sum1 = links.next(sum1, 0)
    mixed = layout.send_home(mixed)
    dl, st, gdepth, ln3 = back2(scal, low, db, high, taps, mid, left, right, g3, point, group)
    dl, st, sum0, sum1, mixed = sync(dl, st, sum0, sum1, mixed)
    if direct:
        sum1 = links.next(sum1, 1)
    (sum2,) = weigh2(scal, dl, st, y2)
    sum2, sum1, sum0 = sync(sum2, sum1, sum0)
    if direct:
        tail0 = links.finish([*sum0, *sum1])
        sum2 = links.first(2, sum2)
    small = (ln3, ln4, ln5, gdepth)
    dx, sum3 = back1(
        scal, dl, st, dh2, h1, joined, x_ext, g1, g2, glu, wide, narrow, small
    )
    if direct:
        dx, sum3, sum2, tail0 = sync(dx, sum3, sum2, tail0)
        sum3 = links.first(3, sum3)
        held = sync(*(jnp.concatenate(v, axis=1) for v in zip(sum2, sum3)))
        held = sync(*links.next(held, 0))
        held = sync(*links.next(held, 1))
        sums = (tail0, links.finish(held))
        tables = (sum([*SUMS[0], *SUMS[1]], []),)
        tables += (SUMS[2][0] + SUMS[3][0] + SUMS[2][1] + SUMS[3][1],)
    else:
        sums = [links.scatter_whole(k, v) for k, v in enumerate((sum0, sum1, sum2, sum3))]
        tables = [sum(items, []) for items in SUMS]
    dx = layout.send_home(dx)
    out = {}
    for items, total in zip(tables, sums):
        out.update(links.rows_of(items, total))
    flat = out.pop("small")
    if not direct:
        flat = lax.all_gather(flat, AXES, axis=0, tiled=True)
    flat = flat.reshape(-1, 16 * PACK)
    sizes = [width for _, width in GAINS] + [TAP_RUN]
    at = 0
    for name, size in zip(SMALL, sizes):
        part = flat[:, at : at + size].reshape(-1)
        at += size
        if not direct:
            own = mine[name].shape[0]
            part = lax.dynamic_slice(part, (here * own,), (own,))
        out[name] = part
    return (mixed[None], dx.astype(F32)[None], *(out[name] for name in NAMES))


def solution(mesh):
    token, owner, rows = P("dp", "seq", None), P(AXES), P(AXES, None)
    params = (owner,) * 5 + (rows,) * 3 + (owner,) + (rows,) * 5
    return jax.shard_map(
        on_device,
        mesh=mesh,
        in_specs=(token, token, P("dp")) + params,
        out_specs=(token, token) + params,
        check_vma=False,
    )
```

time: 598 us -> 558 us (0.933)
  starting transfers between devices: 108 us -> 77.1 us
  local copies, waits for them, and re-layouts: 45.3 us -> 25.4 us
  waiting for transfers between devices: 155 us -> 173 us
    ppermute x43 -> x40, waiting for transfers between devices: 82.8 us -> 116 us  [flip(): return lax.ppermute(value, AXES, [(i, i ^ mask) for i in range(self.count)])]
    ppermute x43 -> x40, starting transfers between devices: 83.2 us -> 53.3 us  [flip(): return lax.ppermute(value, AXES, [(i, i ^ mask) for i in range(self.count)])]
    ppermute x12, waiting for transfers between devices: 72 us -> 56.3 us  [swap(): lax.ppermute(values[k], AXES, self.pairs(self.at, lambda g, s: self.at(g,...]
    unnamed x146 -> x106, local copies, waits for them, and re-layouts: 20.4 us -> 7.15 us
    pallas_call x10 -> x13, Pallas kernels: 259 us -> 255 us  [call(): pl.pallas_call(kernel, out_shape=shapes, grid=() if steps is None else (s...]
  transfers between devices with their start and end apart: 63 -> 60, of which waited for: 23 -> 25; matrix products, arithmetic and copies ran while one was open for 6% -> 3% of each run, Pallas kernels for 36% -> 36%
where the time goes in v4:
time: 558 us; the launch traced here: 550 us
  Pallas kernels  255 us (46%)
  waiting for transfers between devices  173 us (31%)
  starting transfers between devices  77.1 us (14%)
  local copies, waits for them, and re-layouts  25.4 us (5%)
  other arithmetic  16 us (3%)
    pallas_call x13, Pallas kernels, call(): pl.pallas_call(kernel, out_shape=shapes, grid=() if steps is None else (s...  255 us
    ppermute x40, waiting for transfers between devices, flip(): return lax.ppermute(value, AXES, [(i, i ^ mask) for i in range(self.count)])  116 us
    ppermute x12, waiting for transfers between devices, swap(): lax.ppermute(values[k], AXES, self.pairs(self.at, lambda g, s: self.at(g,...  56.3 us
    ppermute x40, starting transfers between devices, flip(): return lax.ppermute(value, AXES, [(i, i ^ mask) for i in range(self.count)])  53.3 us
  transfers between devices with their start and end apart: 60, of which 25 were waited for; matrix products, arithmetic and copies ran while one was open for 3% of the time, Pallas kernels for 36%

profile of v4, /device:TPU:0, one launch (start us, length us, event | category | flops | bytes accessed | tf_op | source)
XLA Modules:
  0.0 550.3 jit_solution(4082099530826928351)
XLA Ops:
  4.7 1.8 shard_map.297
  6.4 1.6 collective-permute-start.3
  8.0 6.0 %collective-permute-start.2 = (bf16[416,256]{1,0:T(8,128)(2,1)}, bf16[416,256]{1,0:T(8,128)(2,1)S(1)}, u32[]{:S(2)}, u32[]{:S(2)}) collective-permute-start(bf16[416,256]{1,0:T(8,128)(2,1)} %get-tuple-element.172), channel_id=1, source_target_pairs={{0,24},{1,25},{2,26},{3,27},{4,28},{5,29},{6,30},{7,31},{8,16},{9,... | collective-permute-start | bytes 638984 | tf_op jit(solution)/shard_map/ppermute | solution.py:1011
  14.7 22.5 %collective-permute-done.2 = bf16[416,256]{1,0:T(8,128)(2,1)S(1)} collective-permute-done((bf16[416,256]{1,0:T(8,128)(2,1)}, bf16[416,256]{1,0:T(8,128)(2,1)S(1)}, u32[]{:S(2)}, u32[]{:S(2)}) %collective-permute-start.2) | collective-permute-done | bytes 213024 | tf_op jit(solution)/shard_map/ppermute | solution.py:1011
  37.2 12.4 %collective-permute-done.1 = bf16[416,256]{1,0:T(8,128)(2,1)S(1)} collective-permute-done((bf16[416,256]{1,0:T(8,128)(2,1)}, bf16[416,256]{1,0:T(8,128)(2,1)S(1)}, u32[]{:S(2)}, u32[]{:S(2)}) %collective-permute-start.1) | collective-permute-done | bytes 213024 | tf_op jit(solution)/shard_map/ppermute | solution.py:1011
  49.5 3.9 collective-permute-done
  54.5 1.6 collective-permute-start.5
  56.8 1.3 collective-permute-start.7
  58.1 3.9 collective-permute-start.6
  62.8 1.4 collective-permute-done.4
  65.0 1.9 collective-permute-start.9
  66.9 18.2 %collective-permute-done.8 = bf16[8,208,256]{2,1,0:T(8,128)(2,1)S(1)} collective-permute-done((bf16[8,208,256]{2,1,0:T(8,128)(2,1)S(1)}, bf16[8,208,256]{2,1,0:T(8,128)(2,1)S(1)}, u32[]{:S(2)}, u32[]{:S(2)}) %collective-permute-start.8) | collective-permute-done | bytes 852000 | tf_op jit(solution)/shard_map/ppermute | solution.py:1011
  85.2 1.5 collective-permute-done.9
  88.8 1.3 slice.311
  93.9 3.1 collective-permute-start.12
  99.5 1.7 pad_maximum_fusion.9.x_ref
  101.3 5.8 %collective-permute-done.13 = bf16[288,256]{1,0:T(8,128)(2,1)S(1)} collective-permute-done((bf16[288,256]{1,0:T(8,128)(2,1)S(1)}, bf16[288,256]{1,0:T(8,128)(2,1)S(1)}, u32[]{:S(2)}, u32[]{:S(2)}) %collective-permute-start.13) | collective-permute-done | bytes 147488 | tf_op jit(solution)/shard_map/ppermute | solution.py:1011
  107.2 10.9 %shard_map.298 = (f32[800,512]{1,0:T(8,128)}, bf16[800,512]{1,0:T(8,128)(2,1)}, f32[800,1024]{1,0:T(8,128)}, bf16[512,1024]{1,0:T(8,128)(2,1)}, bf16[512,2048]{1...) custom-call(s32[3]{0:T(128)} %pad_add_fusion.scal, ...), custom_call_target="tpu_custom_call" | custom-call | flops 13799999488 | bytes 20013068 | tf_op jit(solution)/shard_map/pallas_call | solution.py:64
  118.1 10.2 %shard_map.299 = (f32[800,2048]{1,0:T(8,128)}, f32[800,256]{1,0:T(8,128)}, bf16[800,2048]{1,0:T(8,128)(2,1)}) custom-call(s32[3]{0:T(128)} %pad_add_fusion.scal, bf16[800,512]{1,0:T(8,128)(2,1)} %get-tuple-element.184.y2_ref, f32[1,2048]{1,0:T(1,128)} %get-tuple-element.185.g3.refs_4_, bf16[512,2048]{1,0:T(8,128)(2,1)} %get-tuple-element.186.wide.refs_1_, ...), custom_call_target="tpu_custom_call" | custom-call | flops 13799999488 | bytes 14360588 | tf_op jit(solution)/shard_map/pallas_call | solution.py:64
  129.1 1.6 collective-permute-start.15
  130.8 19.2 %shard_map.300 = (bf16[768,2048]{1,0:T(8,128)(2,1)}, f32[768,512]{1,0:T(8,128)}, bf16[768,512]{1,0:T(8,128)(2,1)}, bf16[768,384]{1,0:T(8,128)(2,1)}, bf16[768,38...) custom-call(s32[3]{0:T(128)} %pad_add_fusion.scal, ...), custom_call_target="tpu_custom_call" | custom-call | flops 23000000512 | bytes 15476748 | tf_op jit(solution)/shard_map/pallas_call | solution.py:64
  152.4 14.3 %collective-permute-done.17.refs_1_ = bf16[768,384]{1,0:T(8,128)(2,1)S(1)} collective-permute-done((bf16[768,384]{1,0:T(8,128)(2,1)}, bf16[768,384]{1,0:T(8,128)(2,1)S(1)}, u32[]{:S(2)}, u32[]{:S(2)}) %collective-permute-start.17) | collective-permute-done | bytes 589856 | tf_op jit(solution)/shard_map/ppermute | solution.py:1140
  166.7 6.5 %collective-permute-done.19.refs_3_ = bf16[768,384]{1,0:T(8,128)(2,1)S(1)} collective-permute-done((bf16[768,384]{1,0:T(8,128)(2,1)S(1)}, bf16[768,384]{1,0:T(8,128)(2,1)S(1)}, u32[]{:S(2)}, u32[]{:S(2)}) %collective-permute-start.19) | collective-permute-done | bytes 589856 | tf_op jit(solution)/shard_map/ppermute | solution.py:1140
  174.4 1.7 collective-permute-start.21
  176.9 36.0 %shard_map.301 = (bf16[768,128]{1,0:T(8,128)(2,1)}, bf16[768,128]{1,0:T(8,128)(2,1)}, bf16[768,128]{1,0:T(8,128)(2,1)}, bf16[768,128]{1,0:T(8,128)(2,1)}, f32[3072,128]{1,0:T(8,128)}) custom-call(s32[3]{0:T(128)} %pad_add_fusion.scal, bf16[768,384]{1,0:T(8,128)(2,1)} %get-tuple-element.211.refs_0_, bf16[768,384]{1,0:T(8,128)(2,1)} %copy-done.19, ...), custom_call_target="tpu_custom_call" | custom-call | flops 41400000512 | bytes 4718604 | tf_op jit(solution)/shard_map/pallas_call | solution.py:64
  213.1 3.6 collective-permute-start.26
  219.0 5.5 %collective-permute-done.23.refs_1_ = bf16[768,128]{1,0:T(8,128)(2,1)S(1)} collective-permute-done((bf16[768,128]{1,0:T(8,128)(2,1)S(1)}, bf16[768,128]{1,0:T(8,128)(2,1)S(1)}, u32[]{:S(2)}, u32[]{:S(2)}) %collective-permute-start.23) | collective-permute-done | bytes 196640 | tf_op jit(solution)/shard_map/ppermute | solution.py:1140
  224.6 3.9 collective-permute-done.25.refs_3_
  230.0 23.6 %shard_map.302 = (bf16[768,512]{1,0:T(8,128)(2,1)}, f32[768,512]{1,0:T(8,128)}, bf16[768,128]{1,0:T(8,128)(2,1)}, bf16[768,128]{1,0:T(8,128)(2,1)}, bf16[768,128...) custom-call(s32[3]{0:T(128)} %pad_add_fusion.scal, ...), custom_call_target="tpu_custom_call" | custom-call | flops 23000000512 | bytes 18878476 | tf_op jit(solution)/shard_map/pallas_call | solution.py:64
  254.4 1.5 collective-permute-start.30
  255.9 10.3 %shard_map.303 = bf16[32,288,256]{2,1,0:T(8,128)(2,1)} custom-call(s32[3]{0:T(128)} %pad_add_fusion.scal, bf16[768,512]{1,0:T(8,128)(2,1)} %get-tuple-element.240.att_s, bf16[768,512]{1,0:T(8,128)(2,1)} %get-tuple-element.241.y5_s, bf16[768,2048]{1,0:T(8,128)(2,1)} %get-tuple-element.242.inner_s, bf16[768,2048]{1,0:T(8,128)(2,1)} %get-tuple-element.243.du_s, ...), custom_call_target="tpu_custom_call" | custom-call | flops 11500000256 | bytes 14942220 | tf_op jit(solution)/shard_map/pallas_call | solution.py:64
  266.2 3.5 slice.318
  269.9 58.1 %shard_map.304 = (bf16[768,384]{1,0:T(8,128)(2,1)}, bf16[768,384]{1,0:T(8,128)(2,1)}, bf16[768,384]{1,0:T(8,128)(2,1)}, bf16[768,384]{1,0:T(8,128)(2,1)}) custom-call(s32[3]{0:T(128)} %pad_add_fusion.scal, bf16[768,384]{1,0:T(8,128)(2,1)} %get-tuple-element.211.refs_0_, bf16[768,384]{1,0:T(8,128)(2,1)} %copy-done.19, bf16[768,384]{1,0:T(8,128)(2,1)} %copy-done.20, ...), custom_call_target="tpu_custom_call" | custom-call | flops 66700001280 | bytes 7864332 | tf_op jit(solution)/shard_map/pallas_call | solution.py:64
  328.0 2.4 add_convert_fusion
  333.6 14.0 %collective-permute-done.32.refs_1_ = bf16[768,384]{1,0:T(8,128)(2,1)S(1)} collective-permute-done((bf16[768,384]{1,0:T(8,128)(2,1)S(1)}, bf16[768,384]{1,0:T(8,128)(2,1)S(1)}, u32[]{:S(2)}, u32[]{:S(2)}) %collective-permute-start.32) | collective-permute-done | bytes 589856 | tf_op jit(solution)/shard_map/ppermute | solution.py:1140
  347.5 12.0 %collective-permute-done.34.refs_3_ = bf16[768,384]{1,0:T(8,128)(2,1)S(1)} collective-permute-done((bf16[768,384]{1,0:T(8,128)(2,1)S(1)}, bf16[768,384]{1,0:T(8,128)(2,1)S(1)}, u32[]{:S(2)}, u32[]{:S(2)}) %collective-permute-start.34) | collective-permute-done | bytes 589856 | tf_op jit(solution)/shard_map/ppermute | solution.py:1140
  360.4 9.0 %shard_map.305 = (f32[768,512]{1,0:T(8,128)}, bf16[768,256]{1,0:T(8,128)(2,1)}, bf16[768,1536]{1,0:T(8,128)(2,1)}, f32[1,512]{1,0:T(1,128)}) custom-call(s32[3]{0:T(128)} %pad_add_fusion.scal, bf16[768,384]{1,0:T(8,128)(2,1)} %get-tuple-element.261.refs_0_, bf16[768,384]{1,0:T(8,128)(2,1)} %copy-done.27, bf16[768,384]{1,0:T(8,128)(2,1)} %copy-done.28, ...), custom_call_target="tpu_custom_call" | custom-call | flops 6899999744 | bytes 11407372 | tf_op jit(solution)/shard_map/pallas_call | solution.py:64
  371.4 4.5 collective-permute-start.35
  376.4 3.7 collective-permute-start.37
  380.1 6.8 %shard_map.306 = bf16[32,160,256]{2,1,0:T(8,128)(2,1)} custom-call(s32[3]{0:T(128)} %pad_add_fusion.scal, bf16[768,512]{1,0:T(8,128)(2,1)} %get-tuple-element.268.y4_ref, bf16[768,1536]{1,0:T(8,128)(2,1)} %get-tuple-element.269.dqkv_s, bf16[768,2048]{1,0:T(8,128)(2,1)} %get-tuple-element.270.spread_ref, bf16[768,256]{1,0:T(8,128)(2,1)} %get-tuple-element.267.db_ref), custom_call_target="tpu_custom_call" | custom-call | flops 9200000000 | bytes 9306124 | tf_op jit(solution)/shard_map/pallas_call | solution.py:64
  386.8 4.0 collective-permute-done.38
  391.0 2.1 collective-permute-done.37
  393.5 3.0 collective-permute-done.39
  397.9 1.9 collective-permute-start.41
  399.7 1.6 collective-permute-start.40
  402.1 1.9 collective-permute-start.44
  404.0 43.9 %shard_map.307 = (bf16[800,2048]{1,0:T(8,128)(2,1)}, bf16[768,768]{1,0:T(8,128)(2,1)}, f32[9,2048]{1,0:T(8,128)}, f32[1,2048]{1,0:T(1,128)}) custom-call(s32[3]{0:T(128)} %pad_add_fusion.scal, bf16[16,256]{1,0:T(8,128)(2,1)} %copy-done.40, bf16[768,256]{1,0:T(8,128)(2,1)} %get-tuple-element.267.db_ref, bf16[16,256]{1,0:T(8,128)(2,1)} %copy-done.39, ...), custom_call_target="tpu_custom_call" | custom-call | flops 50600001536 | bytes 16728076 | tf_op jit(solution)/shard_map/pallas_call | solution.py:64
  448.5 6.6 %shard_map.309 = bf16[32,176,256]{2,1,0:T(8,128)(2,1)} custom-call(s32[3]{0:T(128)} %pad_add_fusion.scal, bf16[800,2048]{1,0:T(8,128)(2,1)} %get-tuple-element.291.dl, bf16[768,768]{1,0:T(8,128)(2,1)} %get-tuple-element.292.st, bf16[800,512]{1,0:T(8,128)(2,1)} %get-tuple-element.184.y2_ref), custom_call_target="tpu_custom_call" | custom-call | flops 8049999872 | bytes 8159244 | tf_op jit(solution)/shard_map/pallas_call | solution.py:64
  456.2 3.3 collective-permute-start.48
  459.4 2.1 collective-permute-start.50
  463.3 18.9 %shard_map.308 = (bf16[768,512]{1,0:T(8,128)(2,1)}, bf16[32,80,256]{2,1,0:T(8,128)(2,1)}) custom-call(s32[3]{0:T(128)} %pad_add_fusion.scal, bf16[800,2048]{1,0:T(8,128)(2,1)} %get-tuple-element.291.dl, bf16[768,768]{1,0:T(8,128)(2,1)} %get-tuple-element.292.st, f32[768,512]{1,0:T(8,128)} %get-tuple-element.293.dh2_ref, ...), custom_call_target="tpu_custom_call" | custom-call | flops 20700000256 | bytes 17883148 | tf_op jit(solution)/shard_map/pallas_call | solution.py:64
  483.9 1.8 copy-done.5
  488.7 4.5 collective-permute-start.54
  493.2 2.0 collective-permute-start.53
  495.9 26.0 %collective-permute-done.54 = bf16[8,128,256]{2,1,0:T(8,128)(2,1)S(1)} collective-permute-done((bf16[8,128,256]{2,1,0:T(8,128)(2,1)S(1)}, bf16[8,128,256]{2,1,0:T(8,128)(2,1)S(1)}, u32[]{:S(2)}, u32[]{:S(2)}) %collective-permute-start.54) | collective-permute-done | bytes 524320 | tf_op jit(solution)/shard_map/ppermute | solution.py:1011
  523.9 2.5 collective-permute-start.55
  527.0 3.7 collective-permute-done.56
  530.8 1.3 collective-permute-done.55
  532.3 1.3 collective-permute-start.57
  533.8 2.1 collective-permute-start.58
  535.9 1.4 bitcast_convert_fusion
  537.2 2.5 collective-permute-done.57
  539.7 1.4 collective-permute-done.59
  541.1 5.0 collective-permute-done.58
  (262 shorter events, 48.9 us)
Async XLA Ops:
  6.4 48.1 %collective-permute-start.3 = (bf16[784,512]{1,0:T(8,128)(2,1)S(1)}, bf16[784,512]{1,0:T(8,128)(2,1)}, u32[]{:S(2)}, u32[]{:S(2)}) collective-permute-start(bf16[784,512]{1,0:T(8,128)(2,1)S(1)} %pad_maximum_fusion.10), channel_id=1, source_target_pairs={{0,0},{8,4},{16,1},{24,5},{1,16},{9,20},{17,17},{25,21},{2,2},{10,... | collective-permute-start | bytes 2408456 | tf_op jit(solution)/shard_map/ppermute | solution.py:1125
  8.0 29.2 %collective-permute-start.2 = (bf16[416,256]{1,0:T(8,128)(2,1)}, bf16[416,256]{1,0:T(8,128)(2,1)S(1)}, u32[]{:S(2)}, u32[]{:S(2)}) collective-permute-start(bf16[416,256]{1,0:T(8,128)(2,1)} %get-tuple-element.172), channel_id=1, source_target_pairs={{0,24},{1,25},{2,26},{3,27},{4,28},{5,29},{6,30},{7,31},{8,16},{9,... | collective-permute-start | bytes 638984 | tf_op jit(solution)/shard_map/ppermute | solution.py:1011
  14.1 35.5 %collective-permute-start.1 = (bf16[416,256]{1,0:T(8,128)(2,1)}, bf16[416,256]{1,0:T(8,128)(2,1)S(1)}, u32[]{:S(2)}, u32[]{:S(2)}) collective-permute-start(bf16[416,256]{1,0:T(8,128)(2,1)} %get-tuple-element.172), channel_id=1, source_target_pairs={{0,16},{1,17},{2,18},{3,19},{4,20},{5,21},{6,22},{7,23},{8,24},{9,... | collective-permute-start | bytes 638984 | tf_op jit(solution)/shard_map/ppermute | solution.py:1011
  14.3 39.2 %collective-permute-start = (bf16[416,256]{1,0:T(8,128)(2,1)}, bf16[416,256]{1,0:T(8,128)(2,1)S(1)}, u32[]{:S(2)}, u32[]{:S(2)}) collective-permute-start(bf16[416,256]{1,0:T(8,128)(2,1)} %get-tuple-element.172), channel_id=1, source_target_pairs={{0,8},{1,9},{2,10},{3,11},{4,12},{5,13},{6,14},{7,15},{8,0},{9,1},... | collective-permute-start | bytes 638984 | tf_op jit(solution)/shard_map/ppermute | solution.py:1011
  54.5 8.2 %collective-permute-start.5 = (bf16[4,208,256]{2,1,0:T(8,128)(2,1)S(1)}, bf16[4,208,256]{2,1,0:T(8,128)(2,1)S(1)}, u32[]{:S(2)}, u32[]{:S(2)}) collective-permute-start(bf16[4,208,256]{2,1,0:T(8,128)(2,1)S(1)} %get-tuple-element.331), channel_id=1, source_target_pairs={{0,2},{1,3},{2,0},{3,1},{4,6},{5,7},{6,4},{7,5},{8,10},{9,11},{10,... | collective-permute-start | bytes 1277960 | tf_op jit(solution)/shard_map/ppermute | solution.py:1011
  56.1 8.1 %collective-permute-start.4 = (bf16[4,208,256]{2,1,0:T(8,128)(2,1)S(1)}, bf16[4,208,256]{2,1,0:T(8,128)(2,1)S(1)}, u32[]{:S(2)}, u32[]{:S(2)}) collective-permute-start(bf16[4,208,256]{2,1,0:T(8,128)(2,1)S(1)} %get-tuple-element.332), channel_id=1, source_target_pairs={{0,4},{1,5},{2,6},{3,7},{4,0},{5,1},{6,2},{7,3},{8,12},{9,13},{10,... | collective-permute-start | bytes 1277960 | tf_op jit(solution)/shard_map/ppermute | solution.py:1011
  56.8 7.5 %collective-permute-start.7 = (bf16[16,512]{1,0:T(8,128)(2,1)S(1)}, bf16[16,512]{1,0:T(8,128)(2,1)S(1)}, u32[]{:S(2)}, u32[]{:S(2)}) collective-permute-start(bf16[16,512]{1,0:T(8,128)(2,1)S(1)} %get-tuple-element.333), channel_id=1, source_target_pairs={{8,0},{16,4},{24,1},{9,16},{17,20},{25,17},{10,2},{18,6},{26,3},{1... | collective-permute-start | bytes 49160 | tf_op jit(solution)/shard_map/ppermute | solution.py:1128
  58.1 6.2 %collective-permute-start.6 = (bf16[16,512]{1,0:T(8,128)(2,1)S(1)}, bf16[16,512]{1,0:T(8,128)(2,1)S(1)}, u32[]{:S(2)}, u32[]{:S(2)}) collective-permute-start(bf16[16,512]{1,0:T(8,128)(2,1)S(1)} %get-tuple-element.334), channel_id=1, source_target_pairs={{0,4},{8,1},{16,5},{1,20},{9,17},{17,21},{2,6},{10,3},{18,7},{3,22... | collective-permute-start | bytes 49160 | tf_op jit(solution)/shard_map/ppermute | solution.py:1128
  64.4 20.7 %collective-permute-start.8 = (bf16[8,208,256]{2,1,0:T(8,128)(2,1)S(1)}, bf16[8,208,256]{2,1,0:T(8,128)(2,1)S(1)}, u32[]{:S(2)}, u32[]{:S(2)}) collective-permute-start(bf16[8,208,256]{2,1,0:T(8,128)(2,1)S(1)} %pad_maximum_fusion.7), channel_id=1, source_target_pairs={{0,2},{1,3},{2,0},{3,1},{4,6},{5,7},{6,4},{7,5},{8,10},{9,11},{10,... | collective-permute-start | bytes 2555912 | tf_op jit(solution)/shard_map/ppermute | solution.py:1011
  65.0 21.8 %collective-permute-start.9 = (bf16[8,208,256]{2,1,0:T(8,128)(2,1)S(1)}, bf16[8,208,256]{2,1,0:T(8,128)(2,1)S(1)}, u32[]{:S(2)}, u32[]{:S(2)}) collective-permute-start(bf16[8,208,256]{2,1,0:T(8,128)(2,1)S(1)} %pad_maximum_fusion.8), channel_id=1, source_target_pairs={{0,4},{1,5},{2,6},{3,7},{4,0},{5,1},{6,2},{7,3},{8,12},{9,13},{10,... | collective-permute-start | bytes 2555912 | tf_op jit(solution)/shard_map/ppermute | solution.py:1011
  86.9 20.3 %copy-start.4 = (bf16[16,208,256]{2,1,0:T(8,128)(2,1)}, bf16[16,208,256]{2,1,0:T(8,128)(2,1)S(1)}, u32[]{:S(2)}) copy-start(bf16[16,208,256]{2,1,0:T(8,128)(2,1)S(1)} %pad_maximum_fusion.1.p2) | copy-start | bytes 5111812
  86.9 20.3 %collective-permute-start.10 = (bf16[16,208,256]{2,1,0:T(8,128)(2,1)S(1)}, bf16[16,208,256]{2,1,0:T(8,128)(2,1)}, u32[]{:S(2)}, u32[]{:S(2)}) collective-permute-start(bf16[16,208,256]{2,1,0:T(8,128)(2,1)S(1)} %pad_maximum_fusion.p0), channel_id=1, source_target_pairs={{0,1},{1,0},{2,3},{3,2},{4,5},{5,4},{6,7},{7,6},{8,9},{9,8},{10,11... | collective-permute-start | bytes 5111816 | tf_op jit(solution)/shard_map/ppermute | solution.py:1011
  87.1 20.1 %collective-permute-start.11 = (bf16[16,208,256]{2,1,0:T(8,128)(2,1)S(1)}, bf16[16,208,256]{2,1,0:T(8,128)(2,1)}, u32[]{:S(2)}, u32[]{:S(2)}) collective-permute-start(bf16[16,208,256]{2,1,0:T(8,128)(2,1)S(1)} %pad_maximum_fusion.1.p2), channel_id=1, source_target_pairs={{0,1},{1,0},{2,3},{3,2},{4,5},{5,4},{6,7},{7,6},{8,9},{9,8},{10,11... | collective-permute-start | bytes 5111816 | tf_op jit(solution)/shard_map/ppermute | solution.py:1011
  92.6 8.7 %collective-permute-start.14 = (bf16[288,256]{1,0:T(8,128)(2,1)S(1)}, bf16[288,256]{1,0:T(8,128)(2,1)S(1)}, u32[]{:S(2)}, u32[]{:S(2)}) collective-permute-start(bf16[288,256]{1,0:T(8,128)(2,1)S(1)} %copy-done.8), channel_id=1, source_target_pairs={{0,24},{1,25},{2,26},{3,27},{4,28},{5,29},{6,30},{7,31},{8,16},{9,... | collective-permute-start | bytes 442376 | tf_op jit(solution)/shard_map/ppermute | solution.py:1011
  92.7 14.5 %collective-permute-start.13 = (bf16[288,256]{1,0:T(8,128)(2,1)S(1)}, bf16[288,256]{1,0:T(8,128)(2,1)S(1)}, u32[]{:S(2)}, u32[]{:S(2)}) collective-permute-start(bf16[288,256]{1,0:T(8,128)(2,1)S(1)} %copy-done.8), channel_id=1, source_target_pairs={{0,16},{1,17},{2,18},{3,19},{4,20},{5,21},{6,22},{7,23},{8,24},{9,... | collective-permute-start | bytes 442376 | tf_op jit(solution)/shard_map/ppermute | solution.py:1011
  93.9 13.2 %collective-permute-start.12 = (bf16[288,256]{1,0:T(8,128)(2,1)S(1)}, bf16[288,256]{1,0:T(8,128)(2,1)S(1)}, u32[]{:S(2)}, u32[]{:S(2)}) collective-permute-start(bf16[288,256]{1,0:T(8,128)(2,1)S(1)} %copy-done.8), channel_id=1, source_target_pairs={{0,8},{1,9},{2,10},{3,11},{4,12},{5,13},{6,14},{7,15},{8,0},{9,1},... | collective-permute-start | bytes 442376 | tf_op jit(solution)/shard_map/ppermute | solution.py:1011
  128.4 21.7 %collective-permute-start.16 = (bf16[4,144,256]{2,1,0:T(8,128)(2,1)S(1)}, bf16[4,144,256]{2,1,0:T(8,128)(2,1)S(1)}, u32[]{:S(2)}, u32[]{:S(2)}) collective-permute-start(bf16[4,144,256]{2,1,0:T(8,128)(2,1)S(1)} %get-tuple-element.335), channel_id=1, source_target_pairs={{0,2},{1,3},{2,0},{3,1},{4,6},{5,7},{6,4},{7,5},{8,10},{9,11},{10,... | collective-permute-start | bytes 884744 | tf_op jit(solution)/shard_map/ppermute | solution.py:1011
  129.1 21.0 %collective-permute-start.15 = (bf16[4,144,256]{2,1,0:T(8,128)(2,1)S(1)}, bf16[4,144,256]{2,1,0:T(8,128)(2,1)S(1)}, u32[]{:S(2)}, u32[]{:S(2)}) collective-permute-start(bf16[4,144,256]{2,1,0:T(8,128)(2,1)S(1)} %get-tuple-element.336), channel_id=1, source_target_pairs={{0,4},{1,5},{2,6},{3,7},{4,0},{5,1},{6,2},{7,3},{8,12},{9,13},{10,... | collective-permute-start | bytes 884744 | tf_op jit(solution)/shard_map/ppermute | solution.py:1011
  150.0 26.1 %copy-start.16 = (bf16[1,768,512]{2,1,0:T(8,128)(2,1)S(1)}, bf16[1,768,512]{2,1,0:T(8,128)(2,1)}, u32[]{:S(2)}) copy-start(bf16[1,768,512]{2,1,0:T(8,128)(2,1)} %param.19) | copy-start | bytes 2359300
  150.2 16.5 %collective-permute-start.17 = (bf16[768,384]{1,0:T(8,128)(2,1)}, bf16[768,384]{1,0:T(8,128)(2,1)S(1)}, u32[]{:S(2)}, u32[]{:S(2)}) collective-permute-start(bf16[768,384]{1,0:T(8,128)(2,1)} %get-tuple-element.204), channel_id=1, source_target_pairs={{0,4},{4,0},{1,5},{5,1},{16,20},{20,16},{17,21},{21,17},{2,6},{6,2... | collective-permute-start | bytes 1769480 | tf_op jit(solution)/shard_map/ppermute | solution.py:1140
  151.0 15.7 %collective-permute-start.18 = (bf16[768,384]{1,0:T(8,128)(2,1)S(1)}, bf16[768,384]{1,0:T(8,128)(2,1)S(1)}, u32[]{:S(2)}, u32[]{:S(2)}) collective-permute-start(bf16[768,384]{1,0:T(8,128)(2,1)S(1)} %copy-done.26), channel_id=1, source_target_pairs={{0,1},{4,5},{1,0},{5,4},{16,17},{20,21},{17,16},{21,20},{2,3},{6,7... | collective-permute-start | bytes 1769480 | tf_op jit(solution)/shard_map/ppermute | solution.py:1140
  151.2 22.0 %collective-permute-start.19 = (bf16[768,384]{1,0:T(8,128)(2,1)S(1)}, bf16[768,384]{1,0:T(8,128)(2,1)S(1)}, u32[]{:S(2)}, u32[]{:S(2)}) collective-permute-start(bf16[768,384]{1,0:T(8,128)(2,1)S(1)} %copy-done.25), channel_id=1, source_target_pairs={{0,5},{4,1},{1,4},{5,0},{16,21},{20,17},{17,20},{21,16},{2,7},{6,3... | collective-permute-start | bytes 1769480 | tf_op jit(solution)/shard_map/ppermute | solution.py:1140
  173.2 39.6 %collective-permute-start.20 = (bf16[8,144,256]{2,1,0:T(8,128)(2,1)S(1)}, bf16[8,144,256]{2,1,0:T(8,128)(2,1)S(1)}, u32[]{:S(2)}, u32[]{:S(2)}) collective-permute-start(bf16[8,144,256]{2,1,0:T(8,128)(2,1)S(1)} %pad_maximum_fusion.12), channel_id=1, source_target_pairs={{0,2},{1,3},{2,0},{3,1},{4,6},{5,7},{6,4},{7,5},{8,10},{9,11},{10,... | collective-permute-start | bytes 1769480 | tf_op jit(solution)/shard_map/ppermute | solution.py:1011
  174.4 38.6 %collective-permute-start.21 = (bf16[8,144,256]{2,1,0:T(8,128)(2,1)S(1)}, bf16[8,144,256]{2,1,0:T(8,128)(2,1)S(1)}, u32[]{:S(2)}, u32[]{:S(2)}) collective-permute-start(bf16[8,144,256]{2,1,0:T(8,128)(2,1)S(1)} %pad_maximum_fusion.13), channel_id=1, source_target_pairs={{0,4},{1,5},{2,6},{3,7},{4,0},{5,1},{6,2},{7,3},{8,12},{9,13},{10,... | collective-permute-start | bytes 1769480 | tf_op jit(solution)/shard_map/ppermute | solution.py:1011
  176.1 37.0 %collective-permute-start.22 = (bf16[768,512]{1,0:T(8,128)(2,1)S(1)}, bf16[768,512]{1,0:T(8,128)(2,1)S(1)}, u32[]{:S(2)}, u32[]{:S(2)}) collective-permute-start(bf16[768,512]{1,0:T(8,128)(2,1)S(1)} %bitcast.86), channel_id=1, source_target_pairs={{0,0},{8,4},{16,1},{24,5},{1,16},{9,20},{17,17},{25,21},{2,2},{10,... | collective-permute-start | bytes 2359304 | tf_op jit(solution)/shard_map/ppermute | solution.py:1125
  213.1 15.3 %collective-permute-start.26 = (bf16[16,144,256]{2,1,0:T(8,128)(2,1)S(1)}, bf16[16,144,256]{2,1,0:T(8,128)(2,1)S(1)}, u32[]{:S(2)}, u32[]{:S(2)}) collective-permute-start(bf16[16,144,256]{2,1,0:T(8,128)(2,1)S(1)} %pad_maximum_fusion.2.refs_6_), channel_id=1, source_target_pairs={{0,1},{1,0},{2,3},{3,2},{4,5},{5,4},{6,7},{7,6},{8,9},{9,8},{10,11... | collective-permute-start | bytes 3538952 | tf_op jit(solution)/shard_map/ppermute | solution.py:1011
  216.7 11.8 %collective-permute-start.27 = (bf16[16,144,256]{2,1,0:T(8,128)(2,1)S(1)}, bf16[16,144,256]{2,1,0:T(8,128)(2,1)S(1)}, u32[]{:S(2)}, u32[]{:S(2)}) collective-permute-start(bf16[16,144,256]{2,1,0:T(8,128)(2,1)S(1)} %pad_maximum_fusion.3.refs_8_), channel_id=1, source_target_pairs={{0,1},{1,0},{2,3},{3,2},{4,5},{5,4},{6,7},{7,6},{8,9},{9,8},{10,11... | collective-permute-start | bytes 3538952 | tf_op jit(solution)/shard_map/ppermute | solution.py:1011
  216.8 7.8 %collective-permute-start.23 = (bf16[768,128]{1,0:T(8,128)(2,1)S(1)}, bf16[768,128]{1,0:T(8,128)(2,1)S(1)}, u32[]{:S(2)}, u32[]{:S(2)}) collective-permute-start(bf16[768,128]{1,0:T(8,128)(2,1)S(1)} %copy-done.30), channel_id=1, source_target_pairs={{0,4},{4,0},{1,5},{5,1},{16,20},{20,16},{17,21},{21,17},{2,6},{6,2... | collective-permute-start | bytes 589832 | tf_op jit(solution)/shard_map/ppermute | solution.py:1140
  217.4 7.2 %collective-permute-start.24 = (bf16[768,128]{1,0:T(8,128)(2,1)S(1)}, bf16[768,128]{1,0:T(8,128)(2,1)S(1)}, u32[]{:S(2)}, u32[]{:S(2)}) collective-permute-start(bf16[768,128]{1,0:T(8,128)(2,1)S(1)} %copy-done.31), channel_id=1, source_target_pairs={{0,1},{4,5},{1,0},{5,4},{16,17},{20,21},{17,16},{21,20},{2,3},{6,7... | collective-permute-start | bytes 589832 | tf_op jit(solution)/shard_map/ppermute | solution.py:1140
  218.0 10.5 %collective-permute-start.25 = (bf16[768,128]{1,0:T(8,128)(2,1)S(1)}, bf16[768,128]{1,0:T(8,128)(2,1)S(1)}, u32[]{:S(2)}, u32[]{:S(2)}) collective-permute-start(bf16[768,128]{1,0:T(8,128)(2,1)S(1)} %copy-done.32), channel_id=1, source_target_pairs={{0,5},{4,1},{1,4},{5,0},{16,21},{20,17},{17,20},{21,16},{2,7},{6,3... | collective-permute-start | bytes 589832 | tf_op jit(solution)/shard_map/ppermute | solution.py:1140
  253.7 12.5 %collective-permute-start.28 = (bf16[768,128]{1,0:T(8,128)(2,1)}, bf16[768,128]{1,0:T(8,128)(2,1)S(1)}, u32[]{:S(2)}, u32[]{:S(2)}) collective-permute-start(bf16[768,128]{1,0:T(8,128)(2,1)} %get-tuple-element.237), channel_id=1, source_target_pairs={{0,4},{4,0},{1,5},{5,1},{16,20},{20,16},{17,21},{21,17},{2,6},{6,2... | collective-permute-start | bytes 589832 | tf_op jit(solution)/shard_map/ppermute | solution.py:1140
  254.4 11.8 %collective-permute-start.29 = (bf16[768,128]{1,0:T(8,128)(2,1)}, bf16[768,128]{1,0:T(8,128)(2,1)S(1)}, u32[]{:S(2)}, u32[]{:S(2)}) collective-permute-start(bf16[768,128]{1,0:T(8,128)(2,1)} %get-tuple-element.238), channel_id=1, source_target_pairs={{0,1},{4,5},{1,0},{5,4},{16,17},{20,21},{17,16},{21,20},{2,3},{6,7... | collective-permute-start | bytes 589832 | tf_op jit(solution)/shard_map/ppermute | solution.py:1140
  254.4 11.9 %collective-permute-start.30 = (bf16[768,128]{1,0:T(8,128)(2,1)}, bf16[768,128]{1,0:T(8,128)(2,1)S(1)}, u32[]{:S(2)}, u32[]{:S(2)}) collective-permute-start(bf16[768,128]{1,0:T(8,128)(2,1)} %get-tuple-element.239), channel_id=1, source_target_pairs={{0,5},{4,1},{1,4},{5,0},{16,21},{20,17},{17,20},{21,16},{2,7},{6,3... | collective-permute-start | bytes 589832 | tf_op jit(solution)/shard_map/ppermute | solution.py:1140
  266.2 61.7 %slice-start.2 = ((s8[4718592]{0:T(1024)(128)(4,1)}), s8[4194304]{0:T(1024)(128)(4,1)S(1)}, s32[]{:S(2)}) async-start(s8[4718592]{0:T(1024)(128)(4,1)} %bitcast.66), calls=%async_computation.2 | async-start | bytes 8388608
  269.8 58.1 %collective-permute-start.31 = (bf16[16,288,256]{2,1,0:T(8,128)(2,1)}, bf16[16,288,256]{2,1,0:T(8,128)(2,1)}, u32[]{:S(2)}, u32[]{:S(2)}) collective-permute-start(bf16[16,288,256]{2,1,0:T(8,128)(2,1)} %slice.318), channel_id=1, source_target_pairs={{0,1},{1,0},{2,3},{3,2},{4,5},{5,4},{6,7},{7,6},{8,9},{9,8},{10,11... | collective-permute-start | bytes 7077896 | tf_op jit(solution)/shard_map/ppermute | solution.py:1011
  269.9 58.1 %slice-start.3 = ((s8[4718592]{0:T(1024)(128)(4,1)}), s8[524288]{0:T(1024)(128)(4,1)S(1)}, s32[]{:S(2)}) async-start(s8[4718592]{0:T(1024)(128)(4,1)} %bitcast.66), calls=%async_computation.3 | async-start | bytes 1048576
  331.4 16.1 %collective-permute-start.32 = (bf16[768,384]{1,0:T(8,128)(2,1)S(1)}, bf16[768,384]{1,0:T(8,128)(2,1)S(1)}, u32[]{:S(2)}, u32[]{:S(2)}) collective-permute-start(bf16[768,384]{1,0:T(8,128)(2,1)S(1)} %copy-done.24), channel_id=1, source_target_pairs={{0,4},{4,0},{1,5},{5,1},{16,20},{20,16},{17,21},{21,17},{2,6},{6,2... | collective-permute-start | bytes 1769480 | tf_op jit(solution)/shard_map/ppermute | solution.py:1140
  332.1 15.4 %collective-permute-start.33 = (bf16[768,384]{1,0:T(8,128)(2,1)S(1)}, bf16[768,384]{1,0:T(8,128)(2,1)S(1)}, u32[]{:S(2)}, u32[]{:S(2)}) collective-permute-start(bf16[768,384]{1,0:T(8,128)(2,1)S(1)} %copy-done.23), channel_id=1, source_target_pairs={{0,1},{4,5},{1,0},{5,4},{16,17},{20,21},{17,16},{21,20},{2,3},{6,7... | collective-permute-start | bytes 1769480 | tf_op jit(solution)/shard_map/ppermute | solution.py:1140
  332.4 27.2 %collective-permute-start.34 = (bf16[768,384]{1,0:T(8,128)(2,1)S(1)}, bf16[768,384]{1,0:T(8,128)(2,1)S(1)}, u32[]{:S(2)}, u32[]{:S(2)}) collective-permute-start(bf16[768,384]{1,0:T(8,128)(2,1)S(1)} %copy-done.22), channel_id=1, source_target_pairs={{0,5},{4,1},{1,4},{5,0},{16,21},{20,17},{17,20},{21,16},{2,7},{6,3... | collective-permute-start | bytes 1769480 | tf_op jit(solution)/shard_map/ppermute | solution.py:1140
  370.1 23.2 %collective-permute-start.36 = (bf16[16,256]{1,0:T(8,128)(2,1)S(1)}, bf16[16,256]{1,0:T(8,128)(2,1)S(1)}, u32[]{:S(2)}, u32[]{:S(2)}) collective-permute-start(bf16[16,256]{1,0:T(8,128)(2,1)S(1)} %get-tuple-element.357), channel_id=1, source_target_pairs={{4,0},{1,4},{5,1},{20,16},{17,20},{21,17},{6,2},{3,6},{7,3},{22,18... | collective-permute-start | bytes 24584 | tf_op jit(solution)/shard_map/ppermute | solution.py:1136
  371.4 21.9 %collective-permute-start.35 = (bf16[16,256]{1,0:T(8,128)(2,1)S(1)}, bf16[16,256]{1,0:T(8,128)(2,1)S(1)}, u32[]{:S(2)}, u32[]{:S(2)}) collective-permute-start(bf16[16,256]{1,0:T(8,128)(2,1)S(1)} %get-tuple-element.358), channel_id=1, source_target_pairs={{0,4},{4,1},{1,5},{16,20},{20,17},{17,21},{2,6},{6,3},{3,7},{18,22... | collective-permute-start | bytes 24584 | tf_op jit(solution)/shard_map/ppermute | solution.py:1136
  376.0 14.9 %collective-permute-start.38 = (bf16[8,144,256]{2,1,0:T(8,128)(2,1)S(1)}, bf16[8,144,256]{2,1,0:T(8,128)(2,1)S(1)}, u32[]{:S(2)}, u32[]{:S(2)}) collective-permute-start(bf16[8,144,256]{2,1,0:T(8,128)(2,1)S(1)} %slice.326), channel_id=1, source_target_pairs={{0,4},{1,5},{2,6},{3,7},{4,0},{5,1},{6,2},{7,3},{8,12},{9,13},{10,... | collective-permute-start | bytes 1769480 | tf_op jit(solution)/shard_map/ppermute | solution.py:1011
  376.4 16.8 %collective-permute-start.37 = (bf16[8,144,256]{2,1,0:T(8,128)(2,1)S(1)}, bf16[8,144,256]{2,1,0:T(8,128)(2,1)S(1)}, u32[]{:S(2)}, u32[]{:S(2)}) collective-permute-start(bf16[8,144,256]{2,1,0:T(8,128)(2,1)S(1)} %slice.324), channel_id=1, source_target_pairs={{0,2},{1,3},{2,0},{3,1},{4,6},{5,7},{6,4},{7,5},{8,10},{9,11},{10,... | collective-permute-start | bytes 1769480 | tf_op jit(solution)/shard_map/ppermute | solution.py:1011
  393.4 3.1 collective-permute-start.39
  397.9 50.0 %collective-permute-start.41 = (bf16[4,144,256]{2,1,0:T(8,128)(2,1)S(1)}, bf16[4,144,256]{2,1,0:T(8,128)(2,1)S(1)}, u32[]{:S(2)}, u32[]{:S(2)}) collective-permute-start(bf16[4,144,256]{2,1,0:T(8,128)(2,1)S(1)} %slice.334), channel_id=1, source_target_pairs={{0,2},{1,3},{2,0},{3,1},{4,6},{5,7},{6,4},{7,5},{8,10},{9,11},{10,... | collective-permute-start | bytes 884744 | tf_op jit(solution)/shard_map/ppermute | solution.py:1011
  399.7 48.2 %collective-permute-start.40 = (bf16[4,144,256]{2,1,0:T(8,128)(2,1)}, bf16[4,144,256]{2,1,0:T(8,128)(2,1)S(1)}, u32[]{:S(2)}, u32[]{:S(2)}) collective-permute-start(bf16[4,144,256]{2,1,0:T(8,128)(2,1)} %slice.332), channel_id=1, source_target_pairs={{0,4},{1,5},{2,6},{3,7},{4,0},{5,1},{6,2},{7,3},{8,12},{9,13},{10,... | collective-permute-start | bytes 884744 | tf_op jit(solution)/shard_map/ppermute | solution.py:1011
  401.4 46.7 %collective-permute-start.43 = (bf16[8,80,256]{2,1,0:T(8,128)(2,1)S(1)}, bf16[8,80,256]{2,1,0:T(8,128)(2,1)S(1)}, u32[]{:S(2)}, u32[]{:S(2)}) collective-permute-start(bf16[8,80,256]{2,1,0:T(8,128)(2,1)S(1)} %slice.338), channel_id=1, source_target_pairs={{0,4},{1,5},{2,6},{3,7},{4,0},{5,1},{6,2},{7,3},{8,12},{9,13},{10,... | collective-permute-start | bytes 983048 | tf_op jit(solution)/shard_map/ppermute | solution.py:1011
  401.9 46.3 %collective-permute-start.42 = (bf16[8,80,256]{2,1,0:T(8,128)(2,1)S(1)}, bf16[8,80,256]{2,1,0:T(8,128)(2,1)S(1)}, u32[]{:S(2)}, u32[]{:S(2)}) collective-permute-start(bf16[8,80,256]{2,1,0:T(8,128)(2,1)S(1)} %slice.336), channel_id=1, source_target_pairs={{0,2},{1,3},{2,0},{3,1},{4,6},{5,7},{6,4},{7,5},{8,10},{9,11},{10,... | collective-permute-start | bytes 983048 | tf_op jit(solution)/shard_map/ppermute | solution.py:1011
  402.1 46.2 %collective-permute-start.44 = (bf16[768,512]{1,0:T(8,128)(2,1)}, bf16[768,512]{1,0:T(8,128)(2,1)S(1)}, u32[]{:S(2)}, u32[]{:S(2)}) collective-permute-start(bf16[768,512]{1,0:T(8,128)(2,1)} %get-tuple-element.289), channel_id=1, source_target_pairs={{0,0},{4,8},{1,16},{5,24},{16,1},{20,9},{17,17},{21,25},{2,2},{6,1... | collective-permute-start | bytes 2359304 | tf_op jit(solution)/shard_map/ppermute | solution.py:1133
  448.3 6.7 %collective-permute-start.46 = (bf16[4,80,256]{2,1,0:T(8,128)(2,1)S(1)}, bf16[4,80,256]{2,1,0:T(8,128)(2,1)S(1)}, u32[]{:S(2)}, u32[]{:S(2)}) collective-permute-start(bf16[4,80,256]{2,1,0:T(8,128)(2,1)S(1)} %slice.342), channel_id=1, source_target_pairs={{0,2},{1,3},{2,0},{3,1},{4,6},{5,7},{6,4},{7,5},{8,10},{9,11},{10,... | collective-permute-start | bytes 491528 | tf_op jit(solution)/shard_map/ppermute | solution.py:1011
  448.4 6.7 %collective-permute-start.45 = (bf16[4,80,256]{2,1,0:T(8,128)(2,1)S(1)}, bf16[4,80,256]{2,1,0:T(8,128)(2,1)S(1)}, u32[]{:S(2)}, u32[]{:S(2)}) collective-permute-start(bf16[4,80,256]{2,1,0:T(8,128)(2,1)S(1)} %slice.340), channel_id=1, source_target_pairs={{0,4},{1,5},{2,6},{3,7},{4,0},{5,1},{6,2},{7,3},{8,12},{9,13},{10,... | collective-permute-start | bytes 491528 | tf_op jit(solution)/shard_map/ppermute | solution.py:1011
  456.2 26.0 %collective-permute-start.48 = (bf16[448,256]{1,0:T(8,128)(2,1)}, bf16[448,256]{1,0:T(8,128)(2,1)}, u32[]{:S(2)}, u32[]{:S(2)}) collective-permute-start(bf16[448,256]{1,0:T(8,128)(2,1)} %get-tuple-element.328), channel_id=1, source_target_pairs={{0,8},{1,9},{2,10},{3,11},{4,12},{5,13},{6,14},{7,15},{8,0},{9,1},... | collective-permute-start | bytes 688136 | tf_op jit(solution)/shard_map/ppermute | solution.py:1011
  459.4 22.8 %collective-permute-start.50 = (bf16[448,256]{1,0:T(8,128)(2,1)}, bf16[448,256]{1,0:T(8,128)(2,1)}, u32[]{:S(2)}, u32[]{:S(2)}) collective-permute-start(bf16[448,256]{1,0:T(8,128)(2,1)} %get-tuple-element.329), channel_id=1, source_target_pairs={{0,24},{1,25},{2,26},{3,27},{4,28},{5,29},{6,30},{7,31},{8,16},{9,... | collective-permute-start | bytes 688136 | tf_op jit(solution)/shard_map/ppermute | solution.py:1011
  461.5 20.7 %collective-permute-start.49 = (bf16[448,256]{1,0:T(8,128)(2,1)}, bf16[448,256]{1,0:T(8,128)(2,1)}, u32[]{:S(2)}, u32[]{:S(2)}) collective-permute-start(bf16[448,256]{1,0:T(8,128)(2,1)} %get-tuple-element.330), channel_id=1, source_target_pairs={{0,16},{1,17},{2,18},{3,19},{4,20},{5,21},{6,22},{7,23},{8,24},{9,... | collective-permute-start | bytes 688136 | tf_op jit(solution)/shard_map/ppermute | solution.py:1011
  463.3 20.2 %collective-permute-start.47 = (bf16[16,176,256]{2,1,0:T(8,128)(2,1)}, bf16[16,176,256]{2,1,0:T(8,128)(2,1)S(1)}, u32[]{:S(2)}, u32[]{:S(2)}) collective-permute-start(bf16[16,176,256]{2,1,0:T(8,128)(2,1)} %slice.344), channel_id=1, source_target_pairs={{0,1},{1,0},{2,3},{3,2},{4,5},{5,4},{6,7},{7,6},{8,9},{9,8},{10,11... | collective-permute-start | bytes 4325384 | tf_op jit(solution)/shard_map/ppermute | solution.py:1011
  485.8 2.3 collective-permute-start.52
  486.4 49.5 %collective-permute-start.51 = (bf16[768,512]{1,0:T(8,128)(2,1)S(1)}, bf16[768,512]{1,0:T(8,128)(2,1)S(1)}, u32[]{:S(2)}, u32[]{:S(2)}) collective-permute-start(bf16[768,512]{1,0:T(8,128)(2,1)S(1)} %copy-done.17), channel_id=1, source_target_pairs={{0,0},{4,8},{1,16},{5,24},{16,1},{20,9},{17,17},{21,25},{2,2},{6,1... | collective-permute-start | bytes 2359304 | tf_op jit(solution)/shard_map/ppermute | solution.py:1133
  488.7 33.1 %collective-permute-start.54 = (bf16[8,128,256]{2,1,0:T(8,128)(2,1)S(1)}, bf16[8,128,256]{2,1,0:T(8,128)(2,1)S(1)}, u32[]{:S(2)}, u32[]{:S(2)}) collective-permute-start(bf16[8,128,256]{2,1,0:T(8,128)(2,1)S(1)} %slice.358), channel_id=1, source_target_pairs={{0,4},{1,5},{2,6},{3,7},{4,0},{5,1},{6,2},{7,3},{8,12},{9,13},{10,... | collective-permute-start | bytes 1572872 | tf_op jit(solution)/shard_map/ppermute | solution.py:1011
  493.2 28.7 %collective-permute-start.53 = (bf16[8,128,256]{2,1,0:T(8,128)(2,1)S(1)}, bf16[8,128,256]{2,1,0:T(8,128)(2,1)S(1)}, u32[]{:S(2)}, u32[]{:S(2)}) collective-permute-start(bf16[8,128,256]{2,1,0:T(8,128)(2,1)S(1)} %slice.356), channel_id=1, source_target_pairs={{0,2},{1,3},{2,0},{3,1},{4,6},{5,7},{6,4},{7,5},{8,10},{9,11},{10,... | collective-permute-start | bytes 1572872 | tf_op jit(solution)/shard_map/ppermute | solution.py:1011
  522.1 8.6 %collective-permute-start.56 = (bf16[4,128,256]{2,1,0:T(8,128)(2,1)S(1)}, bf16[4,128,256]{2,1,0:T(8,128)(2,1)S(1)}, u32[]{:S(2)}, u32[]{:S(2)}) collective-permute-start(bf16[4,128,256]{2,1,0:T(8,128)(2,1)S(1)} %slice.362), channel_id=1, source_target_pairs={{0,2},{1,3},{2,0},{3,1},{4,6},{5,7},{6,4},{7,5},{8,10},{9,11},{10,... | collective-permute-start | bytes 786440 | tf_op jit(solution)/shard_map/ppermute | solution.py:1011
  523.9 8.3 %collective-permute-start.55 = (bf16[4,128,256]{2,1,0:T(8,128)(2,1)S(1)}, bf16[4,128,256]{2,1,0:T(8,128)(2,1)S(1)}, u32[]{:S(2)}, u32[]{:S(2)}) collective-permute-start(bf16[4,128,256]{2,1,0:T(8,128)(2,1)S(1)} %slice.360), channel_id=1, source_target_pairs={{0,4},{1,5},{2,6},{3,7},{4,0},{5,1},{6,2},{7,3},{8,12},{9,13},{10,... | collective-permute-start | bytes 786440 | tf_op jit(solution)/shard_map/ppermute | solution.py:1011
  532.3 7.4 %collective-permute-start.57 = (bf16[256,256]{1,0:T(8,128)(2,1)S(1)}, bf16[256,256]{1,0:T(8,128)(2,1)S(1)}, u32[]{:S(2)}, u32[]{:S(2)}) collective-permute-start(bf16[256,256]{1,0:T(8,128)(2,1)S(1)} %get-tuple-element.337), channel_id=1, source_target_pairs={{0,8},{1,9},{2,10},{3,11},{4,12},{5,13},{6,14},{7,15},{8,0},{9,1},... | collective-permute-start | bytes 393224 | tf_op jit(solution)/shard_map/ppermute | solution.py:1011
  533.6 7.5 %collective-permute-start.59 = (bf16[256,256]{1,0:T(8,128)(2,1)S(1)}, bf16[256,256]{1,0:T(8,128)(2,1)S(1)}, u32[]{:S(2)}, u32[]{:S(2)}) collective-permute-start(bf16[256,256]{1,0:T(8,128)(2,1)S(1)} %get-tuple-element.338), channel_id=1, source_target_pairs={{0,24},{1,25},{2,26},{3,27},{4,28},{5,29},{6,30},{7,31},{8,16},{9,... | collective-permute-start | bytes 393224 | tf_op jit(solution)/shard_map/ppermute | solution.py:1011
  533.8 12.3 %collective-permute-start.58 = (bf16[256,256]{1,0:T(8,128)(2,1)S(1)}, bf16[256,256]{1,0:T(8,128)(2,1)S(1)}, u32[]{:S(2)}, u32[]{:S(2)}) collective-permute-start(bf16[256,256]{1,0:T(8,128)(2,1)S(1)} %get-tuple-element.339), channel_id=1, source_target_pairs={{0,16},{1,17},{2,18},{3,19},{4,20},{5,21},{6,22},{7,23},{8,24},{9,... | collective-permute-start | bytes 393224 | tf_op jit(solution)/shard_map/ppermute | solution.py:1011
  (41 other events, 205.4 us)

commit v5 on v4

--- a/solution.py
+++ b/solution.py
@@ -52,6 +52,11 @@
             return pl.BlockSpec(memory_space=pltpu.SMEM)
         if steps is None:
             return pl.BlockSpec(memory_space=pltpu.VMEM)
+        if isinstance(how, tuple):
+            tile, start = how
+            block = tuple(pl.Element(b) for b in (tile, *shape[1:]))
+            rest = (0,) * (len(shape) - 1)
+            return pl.BlockSpec(block, lambda i: (pl.multiple_of(start + i * tile, 16), *rest))
         if how is None:
             zeros = (0,) * len(shape)
             mode = pl.Buffered(1) if once else None
@@ -60,7 +65,7 @@
 
     args = [a for a, _ in ins]
     shapes = [jax.ShapeDtypeStruct(shape, dtype) for shape, dtype, _ in outs]
-    moved = sum(math.prod(a.shape) * a.dtype.itemsize for a in args + shapes)
+    moved = sum(math.prod(a.shape) * a.dtype.itemsize for a in args + shapes) if micros else 0
     return pl.pallas_call(
         kernel,
         out_shape=shapes,
@@ -138,13 +143,15 @@
 NARROW_0, POINT_0, SMALL_0 = (columns_of(n, 0) for n in ("narrow", "point", "small"))
 ATTN, DOWN = columns_of("attn", 0, 1), columns_of("down", 0, 1)
 LAST = (UP + ATTN[:1], ATTN[1:] + DOWN)
-GATHERS = ((WIDE + QKV[:5], GLU + NARROW_0 + SMALL_0 + QKV[5:] + POINT_0), LAST)
+GATHERS = ((WIDE, GLU + NARROW_0 + SMALL_0), (QKV[:5], QKV[5:] + POINT_0), LAST)
 SUMS = (
     LAST,
     (QKV[:5], QKV[5:] + POINT_0),
     (WIDE[:6], WIDE[6:] + NARROW_0),
     (GLU[:2], GLU[2:] + SMALL_0),
 )
+
+SPLIT = (1, 2)
 
 
 def height(items):
@@ -186,15 +193,25 @@
     off = row_of(SUMS[group][half], item) + half * height(SUMS[group][0])
     b = ROWS[item[0]]
     for k in range(value.shape[0] // b):
-        slot = slot_of(half, (start + k) ^ me)
+        slot = slot_of(half if group in SPLIT else 0, (start + k) ^ me)
         ref[slot, off : off + b, :] = value[k * b : (k + 1) * b]
 
 
 def group_grads(group):
-    return [((BLOCKS, height(sum(SUMS[group], [])), PACK), BF)]
-
-
-SHAPES = {"glu": (D, 2 * D), "wide": (D, FF), "narrow": (3 * D, NARROW), "qkv": (D, 3 * D), "point": (FF, NARROW)}
+    rows = height(sum(SUMS[group], []))
+    return [((BLOCKS // 2, rows, PACK), BF)] * 2
+
+
+def group_slots(group):
+    return ((BLOCKS, height(sum(SUMS[group], [])), PACK), BF)
+
+
+def part_slots(slots, kept, given):
+    kept[...] = slots[: BLOCKS // 2]
+    given[...] = slots[BLOCKS // 2 :]
+
+
+SHAPES = ({"glu": (D, 2 * D), "wide": (D, FF), "narrow": (3 * D, NARROW)}, {"qkv": (D, 3 * D), "point": (FF, NARROW)})
 
 GAINS = ((0, 16), (16, 16), (32, 64), (96, 16), (112, 16))
 TAPS = 128
@@ -206,9 +223,9 @@
     return lax.broadcasted_iota(jnp.int32, shape, dim)
 
 
-def owner_slots(me):
+def owner_slots(me, half):
     shape = (BLOCKS, BLOCKS)
-    return (slot_of(1, iota(shape, 0) ^ me) == iota(shape, 1)).astype(F32).astype(BF)
+    return (slot_of(half, iota(shape, 0) ^ me) == iota(shape, 1)).astype(F32).astype(BF)
 
 
 def gain_maps(offset, width):
@@ -232,7 +249,7 @@
             slot = core * 16 + r
             for q in range(SMALL_ROWS):
                 table[slot : slot + 1, q * PACK : (q + 1) * PACK] = rows[q : q + 1, :]
-    table[...] = nn(owner_slots(me), table[...].astype(BF))
+    table[...] = nn(owner_slots(me, 1), table[...].astype(BF))
     for ref, (offset, width) in zip(gains, GAINS):
         owner, value = gain_maps(offset, width)
         spread = nn(table[:, :LANES].astype(BF), value)
@@ -250,12 +267,12 @@
     table[:, :LANES] = total
     for tap, channel, who, place in tap_runs():
         table[who : who + 1, place : place + 64] = taps[tap : tap + 1, channel : channel + 64]
-    table[...] = tn(owner_slots(me), table[...].astype(BF))
+    table[...] = tn(owner_slots(me, 0), table[...].astype(BF))
     block[...] = jnp.zeros_like(block)
     for slot in range(BLOCKS):
         for q in range(SMALL_ROWS):
             block[slot, q : q + 1, :] = table[slot : slot + 1, q * PACK : (q + 1) * PACK]
-    at = height(GLU)
+    at = height(sum(SUMS[3], [])) - 16
     grads[:, at : at + 16, :] = block[...].astype(BF)
 
 
@@ -283,13 +300,13 @@
 
 
 def front1_kernel(scal, x_ref, p0, p1, p2, p3, h1_ref, y2_ref, joined_ref, *refs):
-    weights, gains, taps, table = refs[:5], refs[5:10], refs[10], refs[11]
+    weights, gains, taps, table = refs[:3], refs[3:8], refs[8], refs[9]
     g1, g2 = gains[:2]
 
     @pl.when(pl.program_id(0) == 0)
     def _():
         read_small(scal[2], (p0, p1, p2, p3), gains, taps, table)
-        unpack(scal[2], 0, (p0, p1, p2, p3), dict(zip(SHAPES, weights)))
+        unpack(scal[2], 0, (p0, p1, p2, p3), dict(zip(SHAPES[0], weights)))
 
     x = x_ref[...].astype(F32)
     hat, _ = normalise(x)
@@ -308,7 +325,7 @@
         front1_kernel,
         [(scal, "s"), (x, tile)] + [(p, None) for p in pieces],
         [((rows, D), F32, tile), ((rows, D), BF, tile), ((rows, 2 * D), F32, tile)]
-        + [(shape, BF, None) for shape in SHAPES.values()]
+        + [(shape, BF, None) for shape in SHAPES[0].values()]
         + [((1, BLOCKS * width), F32, None) for _, width in GAINS]
         + [((KERNEL, FF), F32, None)],
         scratch=[((BLOCKS, SMALL_ROWS * PACK), F32)],
@@ -389,11 +406,16 @@
     return total
 
 
-def front3_kernel(tile, n, share, scal, mid_ref, taps, h1_ref, g4, point, qkv_w, *refs):
+def front3_kernel(tile, n, share, scal, mid_ref, taps, h1_ref, g4, p0, p1, p2, p3, *refs):
     spread_ref, h2_ref, y4_ref = refs[:3]
     outs = refs[3 : 3 + n]
-    win, qkv_s = refs[3 + n :]
+    qkv_w, point, win, qkv_s = refs[3 + n :]
     i = pl.program_id(0)
+
+    @pl.when(i == 0)
+    def _():
+        unpack(scal[2], 1, (p0, p1, p2, p3), {"qkv": qkv_w, "point": point})
+
     s, first = scal[0], scal[1]
     begin = s * (mid_ref.shape[0] - 2 * RIM) + i * tile
     near = (first > begin - HALF) & (first < begin + tile + HALF)
@@ -428,14 +450,15 @@
             ]
 
 
-def front3(scal, mid, taps, h1, g4, point, qkv_w, n, share, ties=()):
+def front3(scal, mid, taps, h1, g4, pieces, n, share, ties=()):
     rows = mid.shape[0] - 2 * RIM
     tile = 128
     return call(
         functools.partial(front3_kernel, tile, n, share),
-        [(scal, "s")] + [(a, None) for a in (mid, taps, h1, g4, point, qkv_w)],
+        [(scal, "s")] + [(a, None) for a in (mid, taps, h1, g4, *pieces)],
         [((rows, FF), BF, tile), ((rows, D), F32, tile), ((rows, D), BF, tile)]
-        + [((rows, 3 * LANES), BF, tile)] * n,
+        + [((rows, 3 * LANES), BF, tile)] * n
+        + [(shape, BF, None) for shape in SHAPES[1].values()],
         scratch=[((tile + 2 * RIM, LANES), F32), ((tile, 3 * D), BF)],
         micros=20,
         ties=ties,
@@ -468,7 +491,7 @@
 
     @pl.when(i == 0)
     def _():
-        unpack(scal[2], 1, (p0, p1, p2, p3), {"attn": wa, "up": wup, "down": wdown})
+        unpack(scal[2], 2, (p0, p1, p2, p3), {"attn": wa, "up": wup, "down": wdown})
         ln_ref[...] = jnp.zeros_like(ln_ref)
 
     gather_lanes(att_s, n, share, s, att, 1)
@@ -517,7 +540,7 @@
     )
 
 
-def weigh0_kernel(scal, att_s, y5_s, inner_s, du_s, cot_ref, dh3_ref, grads):
+def weigh0_kernel(scal, att_s, y5_s, inner_s, du_s, cot_ref, dh3_ref, kept, given, grads):
     me = scal[2]
     att_t = att_s[...].T
     for j in range(D // PACK):
@@ -530,11 +553,17 @@
         down = tn(inner_s[:, cols], cot_ref[...]).astype(BF)
         for m in range(D // PACK):
             put(me, 0, grads, ("down", m), down[:, m * PACK : (m + 1) * PACK], j * PACK // 64)
+    part_slots(grads, kept, given)
 
 
 def weigh0(scal, att, y5, inner, du, cot, dh3, ties=()):
     return whole_call(
-        weigh0_kernel, group_grads(0), [scal, att, y5, inner, du, cot, dh3], micros=10, ties=ties
+        weigh0_kernel,
+        group_grads(0),
+        [scal, att, y5, inner, du, cot, dh3],
+        scratch=[group_slots(0)],
+        micros=10,
+        ties=ties,
     )
 
 
@@ -572,7 +601,7 @@
     )
 
 
-def weigh1_kernel(scal, y4_ref, dqkv_s, spread_ref, db_ref, grads):
+def weigh1_kernel(scal, y4_ref, dqkv_s, spread_ref, db_ref, kept, given, grads):
     me = scal[2]
     y4_t = y4_ref[...].T
     for j in range(3 * D // PACK):
@@ -581,11 +610,17 @@
     for j in range(FF // PACK):
         part = tn(spread_ref[:, j * PACK : (j + 1) * PACK], db_ref[...]).astype(BF)
         put(me, 1, grads, ("point", 0), part, j * PACK // 64)
+    part_slots(grads, kept, given)
 
 
 def weigh1(scal, y4, dqkv, spread, db, ties=()):
     return whole_call(
-        weigh1_kernel, group_grads(1), [scal, y4, dqkv, spread, db], micros=8, ties=ties
+        weigh1_kernel,
+        group_grads(1),
+        [scal, y4, dqkv, spread, db],
+        scratch=[group_slots(1)],
+        micros=3,
+        ties=ties,
     )
 
 
@@ -717,7 +752,51 @@
     )
 
 
-def weigh2_kernel(scal, dl, st, y2_ref, grads, gn):
+def back1_kernel(scal, dl, st, dh2_ref, h1_ref, joined_ref, x_ref, g1, g2, *refs):
+    glu, wide, narrow, dx_ref, y1_ref, dj_ref, ln1_out, ln2_out, ln1_ref, ln2_ref = refs
+    i = pl.program_id(0)
+
+    @pl.when(i == 0)
+    def _():
+        ln1_ref[...] = jnp.zeros_like(ln1_ref)
+        ln2_ref[...] = jnp.zeros_like(ln2_ref)
+
+    dy2 = nt(dl[...], wide[...])
+    for k in range(3):
+        dy2 = dy2 + nt(st[:, k * NARROW : (k + 1) * NARROW], narrow[k * D : (k + 1) * D, :])
+    hat2, r2 = normalise(h1_ref[...])
+    ln2_ref[...] += fold8(dy2 * hat2)
+    dh1 = dh2_ref[...] + norm_back(dy2, hat2, r2, g2[...])
+    gate = sigmoid(joined_ref[:, D:])
+    value = joined_ref[:, :D]
+    dj_ref[:, :D] = (dh1 * gate).astype(BF)
+    dj_ref[:, D:] = (dh1 * value * gate * (1.0 - gate)).astype(BF)
+    x = x_ref[...].astype(F32)
+    hat1, r1 = normalise(x)
+    y1_ref[...] = (hat1 * g1[...]).astype(BF)
+    dy1 = nt(dj_ref[...], glu[...])
+    ln1_ref[...] += fold8(dy1 * hat1)
+    dx_ref[...] = (dh1 + norm_back(dy1, hat1, r1, g1[...])).astype(dx_ref.dtype)
+    ln1_out[...] = jnp.sum(ln1_ref[...], axis=0, keepdims=True)
+    ln2_out[...] = jnp.sum(ln2_ref[...], axis=0, keepdims=True)
+
+
+def back1(scal, dl, st, dh2, h1, joined, x, g1, g2, glu, wide, narrow, start, rows):
+    tile = 128
+    own, ext = (tile, start), (tile, start + RIM)
+    return call(
+        back1_kernel,
+        [(scal, "s"), (dl, ext), (st, own), (dh2, own), (h1, ext), (joined, ext), (x, ext)]
+        + [(a, None) for a in (g1, g2, glu, wide, narrow)],
+        [((rows, D), BF, tile), ((rows, D), BF, tile), ((rows, 2 * D), BF, tile)]
+        + [((1, D), F32, None)] * 2,
+        scratch=[((8, D), F32), ((8, D), F32)],
+        micros=5,
+        steps=rows // tile,
+    )
+
+
+def weigh2_kernel(scal, dl, st, y2_ref, kept, given, grads, gn):
     me = scal[2]
     rows = st.shape[0]
     y2_t = y2_ref[RIM : RIM + rows, :].T
@@ -727,74 +806,45 @@
     for k in range(3):
         gn[k * D : (k + 1) * D, :] = nn(y2_t, st[:, k * NARROW : (k + 1) * NARROW]).astype(BF)
     put(me, 2, grads, ("narrow", 0), gn[...])
-
-
-def weigh2(scal, dl, st, y2, ties=()):
+    part_slots(grads, kept, given)
+
+
+def weigh2(scal, dl, st, y2):
     return whole_call(
         weigh2_kernel,
         group_grads(2),
         [scal, dl, st, y2],
-        scratch=[((3 * D, NARROW), BF)],
-        ties=ties,
-        micros=7,
-    )
-
-
-def back1_kernel(tile, scal, dl, st, dh2_ref, h1_ref, joined_ref, x_ref, g1, g2, *refs):
-    glu, wide, narrow, ln3, ln4, ln5, gdepth, dx_ref, grads = refs[:9]
-    y1_s, dj_s, ln1_ref, ln2_ref, ln1, ln2, table, block = refs[9:]
-    i = pl.program_id(0)
-
-    @pl.when(i == 0)
-    def _():
-        ln1_ref[...] = jnp.zeros_like(ln1_ref)
-        ln2_ref[...] = jnp.zeros_like(ln2_ref)
-
-    at = rows_at(i, tile)
-    ext = rows_at(i, tile, RIM)
-    dy2 = nt(dl[ext, :], wide[...])
-    for k in range(3):
-        dy2 = dy2 + nt(st[:, k * NARROW : (k + 1) * NARROW], narrow[k * D : (k + 1) * D, :])
-    hat2, r2 = normalise(h1_ref[ext, :])
-    ln2_ref[...] += fold8(dy2 * hat2)
-    dh1 = dh2_ref[...] + norm_back(dy2, hat2, r2, g2[...])
-    gate = sigmoid(joined_ref[ext, D:])
-    value = joined_ref[ext, :D]
-    da = (dh1 * gate).astype(BF)
-    db = (dh1 * value * gate * (1.0 - gate)).astype(BF)
-    dj_s[at, :D] = da
-    dj_s[at, D:] = db
-    x = x_ref[ext, :].astype(F32)
-    hat1, r1 = normalise(x)
-    y1_s[at, :] = (hat1 * g1[...]).astype(BF)
-    dy1 = nt(dj_s[at, :], glu[...])
-    ln1_ref[...] += fold8(dy1 * hat1)
-    dx_ref[...] = (dh1 + norm_back(dy1, hat1, r1, g1[...])).astype(dx_ref.dtype)
-
-    @pl.when(i == pl.num_programs(0) - 1)
-    def _():
-        ln1[...] = jnp.sum(ln1_ref[...], axis=0, keepdims=True)
-        ln2[...] = jnp.sum(ln2_ref[...], axis=0, keepdims=True)
-        write_small(scal[2], (ln1, ln2, ln3, ln4, ln5), gdepth, table, block, grads)
-        y1_t = y1_s[...].T
-        for j in range(2 * D // PACK):
-            part = nn(y1_t, dj_s[:, j * PACK : (j + 1) * PACK]).astype(BF)
-            put(scal[2], 3, grads, ("glu", j), part)
-
-
-def back1(scal, dl, st, dh2, h1, joined, x, g1, g2, glu, wide, narrow, small, ties=()):
-    rows = st.shape[0]
-    tile = 128
-    return call(
-        functools.partial(back1_kernel, tile),
-        [(scal, "s"), (dl, None), (st, tile), (dh2, tile)]
-        + [(a, None) for a in (h1, joined, x, g1, g2, glu, wide, narrow, *small)],
-        [((rows, D), BF, tile), (*group_grads(3)[0], None)],
-        scratch=[((rows, D), BF), ((rows, 2 * D), BF), ((8, D), F32), ((8, D), F32)]
-        + [((1, D), F32), ((1, D), F32), ((BLOCKS, SMALL_ROWS * PACK), F32), ((BLOCKS, 16, PACK), F32)],
-        micros=18,
-        ties=ties,
-        steps=rows // tile,
+        scratch=[group_slots(2), ((3 * D, NARROW), BF)],
+        micros=3,
+    )
+
+
+def weigh3_kernel(halves, scal, *refs):
+    y1, dj, ln1, ln2 = (refs[i * halves : (i + 1) * halves] for i in range(4))
+    gains, taps, kept, given = refs[4 * halves : 4 * halves + 3], *refs[4 * halves + 3 : 4 * halves + 6]
+    grads, table, block, ln1_s, ln2_s = refs[4 * halves + 6 :]
+    me = scal[2]
+    for total, parts in ((ln1_s, ln1), (ln2_s, ln2)):
+        total[...] = sum(p[...] for p in parts[1:]) + parts[0][...]
+    write_small(me, (ln1_s, ln2_s, *gains), taps, table, block, grads)
+    turned = [y[...].T for y in y1]
+    for j in range(2 * D // PACK):
+        part = None
+        for y, d in zip(turned, dj):
+            more = nn(y, d[:, j * PACK : (j + 1) * PACK])
+            part = more if part is None else part + more
+        put(me, 3, grads, ("glu", j), part.astype(BF))
+    part_slots(grads, kept, given)
+
+
+def weigh3(scal, y1, dj, ln1, ln2, gains, taps):
+    return whole_call(
+        functools.partial(weigh3_kernel, len(y1)),
+        group_grads(3),
+        [scal, *y1, *dj, *ln1, *ln2, *gains, taps],
+        scratch=[group_slots(3), ((BLOCKS, SMALL_ROWS * PACK), F32), ((BLOCKS, 16, PACK), F32)]
+        + [((1, D), F32)] * 2,
+        micros=0,
     )
 
 
@@ -1055,10 +1105,43 @@
         middle = slots.shape[0] // 2
         return self.add(slots[:middle], self.flip(slots[middle:], mask))
 
-    def first(self, group, slots):
-        held = self.fold(slots, 1)
+    def cores(self, kept, given):
+        return self.add(kept, self.flip(given, 1))
+
+    def first(self, group, kept, given):
+        held = self.cores(kept, given)
         low = height(SUMS[group][0])
         return [held[:, :low], held[:, low:]]
+
+    def straight(self, held, stage):
+        return self.fold(held, (2, 4)[stage])
+
+    def flips(self, values, mask):
+        flat = self.flip(jnp.concatenate([v.reshape(-1, PACK) for v in values], axis=0), mask)
+        result, at = [], 0
+        for v in values:
+            count = v.size // PACK
+            result.append(flat[at : at + count].reshape(v.shape))
+            at += count
+        return result
+
+    def next_two(self, late, early):
+        a, b = (v.shape[0] // 2 for v in late)
+        c, d = (v.shape[0] // 2 for v in early)
+        got_y = self.flips([late[0][a:], early[1][d:]], 4)
+        got_x = self.flips([late[1][b:], early[0][c:]], 2)
+        late = [self.add(late[0][:a], got_y[0]), self.add(late[1][:b], got_x[0])]
+        early = [self.add(early[0][:c], got_x[1]), self.add(early[1][:d], got_y[1])]
+        return late, early
+
+    def next_and_plane(self, late, held):
+        a, b = (v.shape[0] // 2 for v in late)
+        got_y = self.flips([late[0][a:], held[4:8]], 4)
+        got_x = self.flips([late[1][b:], held[8:12]], 2)
+        total = held[:4].astype(F32) + got_y[1].astype(F32) + got_x[1].astype(F32)
+        total = total + self.flip(held[12:], 6).astype(F32)
+        late = [self.add(late[0][:a], got_y[0]), self.add(late[1][:b], got_x[0])]
+        return late, total.astype(BF)
 
     def next(self, held, stage):
         masks = ((2, 4), (4, 2))[stage]
@@ -1079,11 +1162,12 @@
             at += b
         return {name: jnp.concatenate(p, axis=1) for name, p in parts.items()}
 
-    def scatter_whole(self, group, slots):
+    def scatter_whole(self, group, parts):
+        slots = jnp.concatenate(parts)
         sent, at = [], 0
         for half, items in enumerate(SUMS[group]):
             for name, _ in items:
-                blocks = self.by_owner(slots[:, at : at + ROWS[name]], half)
+                blocks = self.by_owner(slots[:, at : at + ROWS[name]], half if group in SPLIT else 0)
                 sent.append(blocks.reshape(self.count, -1, PACK))
                 at += ROWS[name]
         sent = jnp.concatenate(sent, axis=1)
@@ -1183,101 +1267,117 @@
     )
     sent = jnp.concatenate([tokens, digits.astype(BF)], axis=0)
     if direct:
-        packed, packed_late = pack({k: mine[k] for k in mine if k not in SMALL})
-        packed, sent, packed_late = sync(packed, sent, packed_late)
-        held = links.near(packed)
+        blocks = pack({k: mine[k] for k in mine if k not in SMALL})
+        sent, blocks = sync(sent, blocks)
+        held1 = links.near(blocks[0])
     x = layout.bring(sent)
     if direct:
-        held, x = sync(held, x)
-        held = links.spread(links.part(0, held), 0)
+        held1 = links.spread(links.part(0, *sync(held1)), 0)
     low = layout.bring_to(tokens[-RIM:], 1)
     high = layout.bring_to(tokens[:RIM], -1)
     if direct:
-        held, x, low, high = sync(held, x, low, high)
-        held, packed_late = sync(links.spread(held, 1), packed_late)
-        pieces1 = links.across(held)
-        late = links.near(packed_late)
+        held1, x, low, high, blocks = sync(held1, x, low, high, blocks)
+        held1 = links.spread(held1, 1)
+        held2 = links.near(blocks[1])
+        held1, held2 = sync(held1, held2)
+        pieces1 = links.across(held1)
+        held2 = links.spread(links.part(1, held2), 0)
+        pieces1, held2 = sync(pieces1, held2)
+        held2 = links.spread(held2, 1)
     else:
-        pieces1, pieces2 = (links.gather_whole(k, mine) for k in range(2))
+        pieces1, pieces2, pieces3 = (links.gather_whole(k, mine) for k in range(3))
     digits = x[rows, 0 : 2 * LANES : LANES].astype(F32).astype(jnp.int32)
     first = digits[0] * LANES + digits[1]
     scal = jnp.stack([s.astype(jnp.int32), first, me.astype(jnp.int32)])
     x_ext = jnp.concatenate([low, x[:rows], high], axis=0)
 
     h1, y2, joined, *rest = front1(scal, x_ext, pieces1)
-    (glu, wide, narrow, qkv_w, point), (g1, g2, g3, g4, g5, taps) = rest[:5], rest[5:]
+    (glu, wide, narrow), (g1, g2, g3, g4, g5, taps) = rest[:3], rest[3:]
+    if direct:
+        y2, held2, blocks = sync(y2, held2, blocks)
+        pieces2 = links.across(held2)
+        held3 = links.near(blocks[2])
     left, right, mid = front2(scal, y2, g3, wide, narrow, group)
     if direct:
-        mid, late = sync(mid, late)
-        late = links.spread(links.part(1, late), 0)
-    spread, h2, y4, *qkv = front3(scal, mid, taps, h1, g4, point, qkv_w, n, share)
-    if direct:
-        qkv, late = sync(qkv, late)
+        mid, pieces2, held3 = sync(mid, pieces2, held3)
+        held3 = links.spread(links.part(2, held3), 0)
+    spread, h2, y4, *rest = front3(scal, mid, taps, h1, g4, pieces2, n, share)
+    qkv, (qkv_w, point) = rest[:n], rest[n:]
+    if direct:
+        qkv, held3 = sync(qkv, held3)
     qkv = layout.swap(qkv)
     qkv, cot = sync(qkv, cotangent[0])
     cot = layout.bring(cot)
     if direct:
-        late, qkv = sync(late, qkv)
-        late = links.spread(late, 1)
+        held3, qkv = sync(held3, qkv)
+        held3 = links.spread(held3, 1)
     *att, lse = attend(scal, qkv, n, share)
     if direct:
-        att, late, cot = sync(att, late, cot)
-        pieces2 = links.across(late)
+        att, held3, cot = sync(att, held3, cot)
+        pieces3 = links.across(held3)
     else:
         att, cot = sync(att, cot)
     arrived = layout.swap(att)
-    mixed, dh3, *rest = middle(scal, h2, arrived, cot, g5, pieces2, n, share)
+    mixed, dh3, *rest = middle(scal, h2, arrived, cot, g5, pieces3, n, share)
     datt, (att_all, y5, inner, du, ln5) = rest[:n], rest[n:]
     datt, du = sync(datt, du)
     datt = layout.swap(datt)
-    (sum0,) = weigh0(scal, att_all, y5, inner, du, cot, dh3)
+    sum0 = weigh0(scal, att_all, y5, inner, du, cot, dh3)
     datt, sum0 = sync(datt, sum0)
     if direct:
-        sum0 = links.first(0, sum0)
+        sum0 = links.cores(*sum0)
     dqkv = attend_back(scal, qkv, att, datt, lse, n, share)
     dqkv, sum0 = sync(dqkv, sum0)
     dqkv = layout.swap(dqkv)
-    dqkv, sum0 = sync(dqkv, sum0)
-    if direct:
-        sum0 = links.next(sum0, 0)
+    if direct:
+        sum0 = links.straight(sum0, 0)
+        dqkv, sum0 = sync(dqkv, sum0)
+        sum0 = links.straight(sum0, 1)
     dh2, db, dqkv, ln4 = back3(scal, dqkv, dh3, h2, g4, qkv_w, n, share)
     db, dqkv = sync(db, dqkv)
     low = layout.to_neighbour(db[-RIM:], 1)
     high = layout.to_neighbour(db[:RIM], -1)
-    (sum1,) = weigh1(scal, y4, dqkv, spread, db)
-    low, high, sum1, sum0 = sync(low, high, sum1, sum0)
-    if direct:
-        sum1 = links.first(1, sum1)
-        low, high, sum1, sum0, mixed = sync(low, high, sum1, sum0, mixed)
-        sum0 = links.next(sum0, 1)
-        sum1 = links.next(sum1, 0)
+    sum1 = weigh1(scal, y4, dqkv, spread, db)
+    low, high, sum1, sum0, mixed = sync(low, high, sum1, sum0, mixed)
+    if direct:
+        total0 = links.finish([sum0])
+        sum1 = links.first(1, *sum1)
     mixed = layout.send_home(mixed)
     dl, st, gdepth, ln3 = back2(scal, low, db, high, taps, mid, left, right, g3, point, group)
-    dl, st, sum0, sum1, mixed = sync(dl, st, sum0, sum1, mixed)
-    if direct:
-        sum1 = links.next(sum1, 1)
-    (sum2,) = weigh2(scal, dl, st, y2)
-    sum2, sum1, sum0 = sync(sum2, sum1, sum0)
-    if direct:
-        tail0 = links.finish([*sum0, *sum1])
-        sum2 = links.first(2, sum2)
-    small = (ln3, ln4, ln5, gdepth)
-    dx, sum3 = back1(
-        scal, dl, st, dh2, h1, joined, x_ext, g1, g2, glu, wide, narrow, small
-    )
-    if direct:
-        dx, sum3, sum2, tail0 = sync(dx, sum3, sum2, tail0)
-        sum3 = links.first(3, sum3)
-        held = sync(*(jnp.concatenate(v, axis=1) for v in zip(sum2, sum3)))
-        held = sync(*links.next(held, 0))
-        held = sync(*links.next(held, 1))
-        sums = (tail0, links.finish(held))
-        tables = (sum([*SUMS[0], *SUMS[1]], []),)
-        tables += (SUMS[2][0] + SUMS[3][0] + SUMS[2][1] + SUMS[3][1],)
+    if direct:
+        dl, st, total0, sum1, mixed = sync(dl, st, total0, sum1, mixed)
+        sum1 = links.next(sum1, 0)
+    sum2 = weigh2(scal, dl, st, y2)
+    if direct:
+        (dl, sum2) = sync(dl, sum2)
+        sum2 = links.first(2, *sum2)
+    half = rows // 2
+    fixed = (scal, dl, st, dh2, h1, joined, x_ext, g1, g2, glu, wide, narrow)
+    dx_a, y1_a, dj_a, ln1_a, ln2_a = back1(*fixed, 0, half)
+    if direct:
+        dx_a, dl, sum1, sum2 = sync(dx_a, dl, sum1, sum2)
+        sum1, sum2 = links.next_two(sum1, sum2)
+        fixed = (scal, dl, *fixed[2:])
+    dx_a = layout.send_home(dx_a)
+    dx_b, y1_b, dj_b, ln1_b, ln2_b = back1(*fixed, half, rows - half)
+    if direct:
+        dx_b, dj_b = sync(dx_b, dj_b)
+    dx_b = layout.send_home(dx_b)
+    gains = (ln3, ln4, ln5)
+    sum3 = weigh3(scal, (y1_a, y1_b), (dj_a, dj_b), (ln1_a, ln1_b), (ln2_a, ln2_b), gains, gdepth)
+    if direct:
+        sum3, sum2, sum1, dx_a = sync(sum3, sum2, sum1, dx_a)
+        sum3 = links.cores(*sum3)
+    if direct:
+        sum3, sum2 = sync(sum3, sum2)
+        sum2, sum3 = links.next_and_plane(sum2, sum3)
+        *held, dx_b = sync(*sum2, sum3, dx_b)
+        sums = (total0, links.finish([*sum1, *held]))
+        tables = (sum(SUMS[0], []), sum([*SUMS[1], *SUMS[2], *SUMS[3]], []))
     else:
         sums = [links.scatter_whole(k, v) for k, v in enumerate((sum0, sum1, sum2, sum3))]
         tables = [sum(items, []) for items in SUMS]
-    dx = layout.send_home(dx)
+    dx = jnp.concatenate([dx_a, dx_b], axis=0)
     out = {}
     for items, total in zip(tables, sums):
         out.update(links.rows_of(items, total))

time: 558 us -> 517 us (0.927)
  waiting for transfers between devices: 173 us -> 122 us
  starting transfers between devices: 77.1 us -> 97.8 us
  local copies, waits for them, and re-layouts: 25.4 us -> 15.8 us
    ppermute x40 -> x46, waiting for transfers between devices: 116 us -> 89.9 us  [flip(): return lax.ppermute(value, AXES, [(i, i ^ mask) for i in range(self.count)])]
    ppermute x12, waiting for transfers between devices: 56.3 us -> 31.7 us  [swap(): lax.ppermute(values[k], AXES, self.pairs(self.at, lambda g, s: self.at(g,...]
    ppermute x40 -> x46, starting transfers between devices: 53.3 us -> 73 us  [flip(): return lax.ppermute(value, AXES, [(i, i ^ mask) for i in range(self.count)])]
    slice x16 -> x4, local copies, waits for them, and re-layouts: 5.87 us -> 0.16 us  [fold(): return self.add(slots[:middle], self.flip(slots[middle:], mask))]
    pallas_call x13 -> x15, Pallas kernels: 255 us -> 258 us  [call(): pl.pallas_call(kernel, out_shape=shapes, grid=() if steps is None else (s...]
  transfers between devices with their start and end apart: 60 -> 67, of which waited for: 25 -> 21; matrix products, arithmetic and copies ran while one was open for 3% -> 2% of each run, Pallas kernels for 36% -> 44%
where the time goes in v5:
time: 517 us; the launch traced here: 509 us
  Pallas kernels  258 us (50%)
  waiting for transfers between devices  122 us (24%)
  starting transfers between devices  97.8 us (19%)
  local copies, waits for them, and re-layouts  15.8 us (3%)
  other arithmetic  11.5 us (2%)
    pallas_call x15, Pallas kernels, call(): pl.pallas_call(kernel, out_shape=shapes, grid=() if steps is None else (s...  258 us
    ppermute x46, waiting for transfers between devices, flip(): return lax.ppermute(value, AXES, [(i, i ^ mask) for i in range(self.count)])  89.9 us
    ppermute x46, starting transfers between devices, flip(): return lax.ppermute(value, AXES, [(i, i ^ mask) for i in range(self.count)])  73 us
    ppermute x12, waiting for transfers between devices, swap(): lax.ppermute(values[k], AXES, self.pairs(self.at, lambda g, s: self.at(g,...  31.7 us
  transfers between devices with their start and end apart: 67, of which 21 were waited for; matrix products, arithmetic and copies ran while one was open for 2% of the time, Pallas kernels for 44%

profile of v5, /device:TPU:0, one launch (start us, length us, event | category | flops | bytes accessed | tf_op | source)
XLA Modules:
  0.0 509.1 jit_solution(2374946422192839614)
XLA Ops:
  3.5 1.2 pad_maximum_fusion.5
  4.7 1.7 shard_map.297
  6.4 5.0 collective-permute-start.2
  12.7 3.4 collective-permute-done.2
  16.1 7.9 %collective-permute-done.1 = bf16[256,256]{1,0:T(8,128)(2,1)S(1)} collective-permute-done((bf16[256,256]{1,0:T(8,128)(2,1)}, bf16[256,256]{1,0:T(8,128)(2,1)S(1)}, u32[]{:S(2)}, u32[]{:S(2)}) %collective-permute-start.1) | collective-permute-done | bytes 131104 | tf_op jit(solution)/shard_map/ppermute | solution.py:1061
  25.0 1.4 collective-permute-start.4
  26.4 9.1 %collective-permute-start.3 = (bf16[4,128,256]{2,1,0:T(8,128)(2,1)S(1)}, bf16[4,128,256]{2,1,0:T(8,128)(2,1)S(1)}, u32[]{:S(2)}, u32[]{:S(2)}) collective-permute-start(bf16[4,128,256]{2,1,0:T(8,128)(2,1)S(1)} %get-tuple-element.406), channel_id=1, source_target_pairs={{0,4},{1,5},{2,6},{3,7},{4,0},{5,1},{6,2},{7,3},{8,12},{9,13},{10,... | collective-permute-start | bytes 786440 | tf_op jit(solution)/shard_map/ppermute | solution.py:1061
  36.2 1.3 collective-permute-start.7
  37.5 1.9 collective-permute-start.6
  39.5 9.9 %collective-permute-done.3 = bf16[4,128,256]{2,1,0:T(8,128)(2,1)S(1)} collective-permute-done((bf16[4,128,256]{2,1,0:T(8,128)(2,1)S(1)}, bf16[4,128,256]{2,1,0:T(8,128)(2,1)S(1)}, u32[]{:S(2)}, u32[]{:S(2)}) %collective-permute-start.3) | collective-permute-done | bytes 262176 | tf_op jit(solution)/shard_map/ppermute | solution.py:1061
  50.6 2.5 collective-permute-start.9
  53.9 3.6 collective-permute-start.10
  58.2 1.4 collective-permute-done.12
  59.6 1.6 collective-permute-done.11
  62.5 1.4 collective-permute-done.9
  69.3 1.8 collective-permute-start.15
  71.1 1.2 pad_add_fusion.scal
  72.3 2.3 collective-permute-done.15
  75.8 1.7 collective-permute-start.18
  77.6 9.0 %shard_map.298 = (f32[800,512]{1,0:T(8,128)}, bf16[800,512]{1,0:T(8,128)(2,1)}, f32[800,1024]{1,0:T(8,128)}, bf16[512,1024]{1,0:T(8,128)(2,1)}, bf16[512,2048]{1...) custom-call(s32[3]{0:T(128)} %pad_add_fusion.scal, ...), custom_call_target="tpu_custom_call" | custom-call | flops 13799999488 | bytes 14770188 | tf_op jit(solution)/shard_map/pallas_call | solution.py:69
  87.5 1.8 collective-permute-start.23
  89.4 2.6 collective-permute-start.21
  92.4 10.1 %shard_map.299 = (f32[800,2048]{1,0:T(8,128)}, f32[800,256]{1,0:T(8,128)}, bf16[800,2048]{1,0:T(8,128)(2,1)}) custom-call(s32[3]{0:T(128)} %pad_add_fusion.scal, bf16[800,512]{1,0:T(8,128)(2,1)} %get-tuple-element.227.y2_ref, f32[1,2048]{1,0:T(1,128)} %get-tuple-element.228.g3.refs_4_, bf16[512,2048]{1,0:T(8,128)(2,1)} %get-tuple-element.229.wide.refs_1_, ...), custom_call_target="tpu_custom_call" | custom-call | flops 13799999488 | bytes 14360588 | tf_op jit(solution)/shard_map/pallas_call | solution.py:69
  104.1 19.9 %shard_map.300 = (bf16[768,2048]{1,0:T(8,128)(2,1)}, f32[768,512]{1,0:T(8,128)}, bf16[768,512]{1,0:T(8,128)(2,1)}, bf16[768,384]{1,0:T(8,128)(2,1)}, bf16[768,38...) custom-call(s32[3]{0:T(128)} %pad_add_fusion.scal, ...), custom_call_target="tpu_custom_call" | custom-call | flops 23000000512 | bytes 18098188 | tf_op jit(solution)/shard_map/pallas_call | solution.py:69
  125.2 1.1 collective-permute-start.28
  126.4 14.3 %collective-permute-done.26.refs_1_ = bf16[768,384]{1,0:T(8,128)(2,1)S(1)} collective-permute-done((bf16[768,384]{1,0:T(8,128)(2,1)}, bf16[768,384]{1,0:T(8,128)(2,1)S(1)}, u32[]{:S(2)}, u32[]{:S(2)}) %collective-permute-start.26) | collective-permute-done | bytes 589856 | tf_op jit(solution)/shard_map/ppermute | solution.py:1224
  140.7 8.1 %collective-permute-done.28.refs_3_ = bf16[768,384]{1,0:T(8,128)(2,1)S(1)} collective-permute-done((bf16[768,384]{1,0:T(8,128)(2,1)S(1)}, bf16[768,384]{1,0:T(8,128)(2,1)S(1)}, u32[]{:S(2)}, u32[]{:S(2)}) %collective-permute-start.28) | collective-permute-done | bytes 589856 | tf_op jit(solution)/shard_map/ppermute | solution.py:1224
  151.5 35.9 %shard_map.301 = (bf16[768,128]{1,0:T(8,128)(2,1)}, bf16[768,128]{1,0:T(8,128)(2,1)}, bf16[768,128]{1,0:T(8,128)(2,1)}, bf16[768,128]{1,0:T(8,128)(2,1)}, f32[3072,128]{1,0:T(8,128)}) custom-call(s32[3]{0:T(128)} %pad_add_fusion.scal, bf16[768,384]{1,0:T(8,128)(2,1)} %get-tuple-element.258.refs_0_, bf16[768,384]{1,0:T(8,128)(2,1)} %copy-done.27, ...), custom_call_target="tpu_custom_call" | custom-call | flops 41400000512 | bytes 4718604 | tf_op jit(solution)/shard_map/pallas_call | solution.py:69
  187.8 3.6 collective-permute-start.35
  191.5 3.4 collective-permute-start.32
  195.9 4.6 collective-permute-done.32.refs_1_
  200.5 4.3 collective-permute-done.34.refs_3_
  206.3 23.6 %shard_map.302 = (bf16[768,512]{1,0:T(8,128)(2,1)}, f32[768,512]{1,0:T(8,128)}, bf16[768,128]{1,0:T(8,128)(2,1)}, bf16[768,128]{1,0:T(8,128)(2,1)}, bf16[768,128...) custom-call(s32[3]{0:T(128)} %pad_add_fusion.scal, ...), custom_call_target="tpu_custom_call" | custom-call | flops 23000000512 | bytes 18878476 | tf_op jit(solution)/shard_map/pallas_call | solution.py:69
  229.9 1.8 collective-permute-start.37
  232.1 10.3 %shard_map.303 = (bf16[16,288,256]{2,1,0:T(8,128)(2,1)}, bf16[16,288,256]{2,1,0:T(8,128)(2,1)}) custom-call(s32[3]{0:T(128)} %pad_add_fusion.scal, bf16[768,512]{1,0:T(8,128)(2,1)} %get-tuple-element.287.att_s, bf16[768,512]{1,0:T(8,128)(2,1)} %get-tuple-element.288.y5_s, bf16[768,2048]{1,0:T(8,128)(2,1)} %get-tuple-element.289.inner_s, ...), custom_call_target="tpu_custom_call" | custom-call | flops 11500000256 | bytes 14942220 | tf_op jit(solution)/shard_map/pallas_call | solution.py:69
  243.3 58.1 %shard_map.304 = (bf16[768,384]{1,0:T(8,128)(2,1)}, bf16[768,384]{1,0:T(8,128)(2,1)}, bf16[768,384]{1,0:T(8,128)(2,1)}, bf16[768,384]{1,0:T(8,128)(2,1)}) custom-call(s32[3]{0:T(128)} %pad_add_fusion.scal, bf16[768,384]{1,0:T(8,128)(2,1)} %get-tuple-element.258.refs_0_, bf16[768,384]{1,0:T(8,128)(2,1)} %copy-done.27, bf16[768,384]{1,0:T(8,128)(2,1)} %copy-done.28, ...), custom_call_target="tpu_custom_call" | custom-call | flops 66700001280 | bytes 7864332 | tf_op jit(solution)/shard_map/pallas_call | solution.py:69
  302.2 2.8 collective-permute-start.44
  305.0 1.9 collective-permute-start.41
  307.1 24.1 %collective-permute-done.44 = bf16[8,288,256]{2,1,0:T(8,128)(2,1)S(1)} collective-permute-done((bf16[8,288,256]{2,1,0:T(8,128)(2,1)S(1)}, bf16[8,288,256]{2,1,0:T(8,128)(2,1)S(1)}, u32[]{:S(2)}, u32[]{:S(2)}) %collective-permute-start.44) | collective-permute-done | bytes 1179680 | tf_op jit(solution)/shard_map/ppermute | solution.py:1061
  332.0 1.5 collective-permute-start.47
  333.5 9.1 %shard_map.305 = (f32[768,512]{1,0:T(8,128)}, bf16[768,256]{1,0:T(8,128)(2,1)}, bf16[768,1536]{1,0:T(8,128)(2,1)}, f32[1,512]{1,0:T(1,128)}) custom-call(s32[3]{0:T(128)} %pad_add_fusion.scal, bf16[768,384]{1,0:T(8,128)(2,1)} %get-tuple-element.310.refs_0_, bf16[768,384]{1,0:T(8,128)(2,1)} %copy-done.34, bf16[768,384]{1,0:T(8,128)(2,1)} %copy-done.36, ...), custom_call_target="tpu_custom_call" | custom-call | flops 6899999744 | bytes 11407372 | tf_op jit(solution)/shard_map/pallas_call | solution.py:69
  343.3 1.3 collective-permute-start.46
  344.6 4.5 collective-permute-start.45
  349.1 6.8 %shard_map.306 = (bf16[16,160,256]{2,1,0:T(8,128)(2,1)}, bf16[16,160,256]{2,1,0:T(8,128)(2,1)}) custom-call(s32[3]{0:T(128)} %pad_add_fusion.scal, bf16[768,512]{1,0:T(8,128)(2,1)} %get-tuple-element.318.y4_ref, bf16[768,1536]{1,0:T(8,128)(2,1)} %get-tuple-element.319.dqkv_s, bf16[768,2048]{1,0:T(8,128)(2,1)} %get-tuple-element.320.spread_ref, ...), custom_call_target="tpu_custom_call" | custom-call | flops 3449999872 | bytes 9306124 | tf_op jit(solution)/shard_map/pallas_call | solution.py:69
  356.2 1.2 collective-permute-start.50
  357.4 2.2 collective-permute-start.49
  359.7 1.8 collective-permute-start.52
  362.5 43.9 %shard_map.307 = (bf16[800,2048]{1,0:T(8,128)(2,1)}, bf16[768,768]{1,0:T(8,128)(2,1)}, f32[9,2048]{1,0:T(8,128)}, f32[1,2048]{1,0:T(1,128)}) custom-call(s32[3]{0:T(128)} %pad_add_fusion.scal, bf16[16,256]{1,0:T(8,128)(2,1)} %copy-done.49, bf16[768,256]{1,0:T(8,128)(2,1)} %get-tuple-element.317.db_ref, bf16[16,256]{1,0:T(8,128)(2,1)} %copy-done.48, ...), custom_call_target="tpu_custom_call" | custom-call | flops 50600001536 | bytes 16728076 | tf_op jit(solution)/shard_map/pallas_call | solution.py:69
  407.1 6.7 %shard_map.308 = (bf16[16,176,256]{2,1,0:T(8,128)(2,1)}, bf16[16,176,256]{2,1,0:T(8,128)(2,1)}) custom-call(s32[3]{0:T(128)} %pad_add_fusion.scal, bf16[800,2048]{1,0:T(8,128)(2,1)} %get-tuple-element.353.dl, bf16[768,768]{1,0:T(8,128)(2,1)} %get-tuple-element.338.st, bf16[800,512]{1,0:T(8,128)(2,1)} %get-tuple-element.227.y2_ref), custom_call_target="tpu_custom_call" | custom-call | flops 3449999872 | bytes 8159244 | tf_op jit(solution)/shard_map/pallas_call | solution.py:69
  414.0 1.8 collective-permute-start.53
  415.8 9.0 %shard_map.309 = (bf16[384,512]{1,0:T(8,128)(2,1)}, bf16[384,512]{1,0:T(8,128)(2,1)}, bf16[384,1024]{1,0:T(8,128)(2,1)}, f32[1,512]{1,0:T(1,128)}, f32[1,512]{1,0:T(1,128)}) custom-call(s32[3]{0:T(128)} %pad_add_fusion.scal, bf16[800,2048]{1,0:T(8,128)(2,1)} %get-tuple-element.353.dl, bf16[768,768]{1,0:T(8,128)(2,1)} %get-tuple-element.338.st, ...), custom_call_target="tpu_custom_call" | custom-call | flops 5750000128 | bytes 17276940 | tf_op jit(solution)/shard_map/pallas_call | solution.py:69
  426.9 2.0 collective-permute-start.57
  429.3 9.0 %shard_map.310 = (bf16[384,512]{1,0:T(8,128)(2,1)}, bf16[384,512]{1,0:T(8,128)(2,1)}, bf16[384,1024]{1,0:T(8,128)(2,1)}, f32[1,512]{1,0:T(1,128)}, f32[1,512]{1,0:T(1,128)}) custom-call(s32[3]{0:T(128)} %pad_add_fusion.scal, bf16[800,2048]{1,0:T(8,128)(2,1)} %get-tuple-element.353.dl, bf16[768,768]{1,0:T(8,128)(2,1)} %get-tuple-element.338.st, ...), custom_call_target="tpu_custom_call" | custom-call | flops 5750000128 | bytes 17276940 | tf_op jit(solution)/shard_map/pallas_call | solution.py:69
  438.3 1.8 collective-permute-start.58
  440.2 4.8 shard_map.311
  446.2 6.1 %collective-permute-start.59 = (bf16[16,80,256]{2,1,0:T(8,128)(2,1)S(1)}, bf16[16,80,256]{2,1,0:T(8,128)(2,1)S(1)}, u32[]{:S(2)}, u32[]{:S(2)}) collective-permute-start(bf16[16,80,256]{2,1,0:T(8,128)(2,1)S(1)} %copy-done.24), channel_id=1, source_target_pairs={{0,1},{1,0},{2,3},{3,2},{4,5},{5,4},{6,7},{7,6},{8,9},{9,8},{10,11... | collective-permute-start | bytes 1966088 | tf_op jit(solution)/shard_map/ppermute | solution.py:1061
  454.3 1.8 collective-permute-start.61
  456.1 5.9 %collective-permute-start.62 = (bf16[4,80,256]{2,1,0:T(8,128)(2,1)S(1)}, bf16[4,80,256]{2,1,0:T(8,128)(2,1)S(1)}, u32[]{:S(2)}, u32[]{:S(2)}) collective-permute-start(bf16[4,80,256]{2,1,0:T(8,128)(2,1)S(1)} %get-tuple-element.397), channel_id=1, source_target_pairs={{0,6},{1,7},{2,4},{3,5},{4,2},{5,3},{6,0},{7,1},{8,14},{9,15},{10,... | collective-permute-start | bytes 491528 | tf_op jit(solution)/shard_map/ppermute | solution.py:1061
  462.4 1.9 collective-permute-done.61
  464.4 17.2 %collective-permute-done.60 = bf16[704,256]{1,0:T(8,128)(2,1)S(1)} collective-permute-done((bf16[704,256]{1,0:T(8,128)(2,1)S(1)}, bf16[704,256]{1,0:T(8,128)(2,1)S(1)}, u32[]{:S(2)}, u32[]{:S(2)}) %collective-permute-start.60) | collective-permute-done | bytes 360480 | tf_op jit(solution)/shard_map/ppermute | solution.py:1061
  483.3 2.2 collective-permute-start.65
  486.1 1.4 maximum_convert_fusion
  487.5 6.1 %collective-permute-done.64 = bf16[416,256]{1,0:T(8,128)(2,1)S(1)} collective-permute-done((bf16[416,256]{1,0:T(8,128)(2,1)S(1)}, bf16[416,256]{1,0:T(8,128)(2,1)S(1)}, u32[]{:S(2)}, u32[]{:S(2)}) %collective-permute-start.64) | collective-permute-done | bytes 213024 | tf_op jit(solution)/shard_map/ppermute | solution.py:1061
  494.0 10.1 %collective-permute-done.65 = bf16[416,256]{1,0:T(8,128)(2,1)S(1)} collective-permute-done((bf16[416,256]{1,0:T(8,128)(2,1)S(1)}, bf16[416,256]{1,0:T(8,128)(2,1)S(1)}, u32[]{:S(2)}, u32[]{:S(2)}) %collective-permute-start.65) | collective-permute-done | bytes 213024 | tf_op jit(solution)/shard_map/ppermute | solution.py:1061
  (299 shorter events, 42.9 us)
Async XLA Ops:
  6.4 9.7 %collective-permute-start.2 = (bf16[256,256]{1,0:T(8,128)(2,1)}, bf16[256,256]{1,0:T(8,128)(2,1)S(1)}, u32[]{:S(2)}, u32[]{:S(2)}) collective-permute-start(bf16[256,256]{1,0:T(8,128)(2,1)} %get-tuple-element.206), channel_id=1, source_target_pairs={{0,24},{1,25},{2,26},{3,27},{4,28},{5,29},{6,30},{7,31},{8,16},{9,... | collective-permute-start | bytes 393224 | tf_op jit(solution)/shard_map/ppermute | solution.py:1061
  11.4 12.5 %collective-permute-start.1 = (bf16[256,256]{1,0:T(8,128)(2,1)}, bf16[256,256]{1,0:T(8,128)(2,1)S(1)}, u32[]{:S(2)}, u32[]{:S(2)}) collective-permute-start(bf16[256,256]{1,0:T(8,128)(2,1)} %get-tuple-element.206), channel_id=1, source_target_pairs={{0,16},{1,17},{2,18},{3,19},{4,20},{5,21},{6,22},{7,23},{8,24},{9,... | collective-permute-start | bytes 393224 | tf_op jit(solution)/shard_map/ppermute | solution.py:1061
  11.4 12.5 %collective-permute-start = (bf16[256,256]{1,0:T(8,128)(2,1)}, bf16[256,256]{1,0:T(8,128)(2,1)S(1)}, u32[]{:S(2)}, u32[]{:S(2)}) collective-permute-start(bf16[256,256]{1,0:T(8,128)(2,1)} %get-tuple-element.206), channel_id=1, source_target_pairs={{0,8},{1,9},{2,10},{3,11},{4,12},{5,13},{6,14},{7,15},{8,0},{9,1},... | collective-permute-start | bytes 393224 | tf_op jit(solution)/shard_map/ppermute | solution.py:1061
  12.0 37.5 %collective-permute-start.5 = (bf16[784,512]{1,0:T(8,128)(2,1)S(1)}, bf16[784,512]{1,0:T(8,128)(2,1)S(1)}, u32[]{:S(2)}, u32[]{:S(2)}) collective-permute-start(bf16[784,512]{1,0:T(8,128)(2,1)S(1)} %pad_maximum_fusion.5), channel_id=1, source_target_pairs={{0,0},{8,4},{16,1},{24,5},{1,16},{9,20},{17,17},{25,21},{2,2},{10,... | collective-permute-start | bytes 2408456 | tf_op jit(solution)/shard_map/ppermute | solution.py:1209
  25.0 14.4 %collective-permute-start.4 = (bf16[4,128,256]{2,1,0:T(8,128)(2,1)S(1)}, bf16[4,128,256]{2,1,0:T(8,128)(2,1)S(1)}, u32[]{:S(2)}, u32[]{:S(2)}) collective-permute-start(bf16[4,128,256]{2,1,0:T(8,128)(2,1)S(1)} %get-tuple-element.405), channel_id=1, source_target_pairs={{0,2},{1,3},{2,0},{3,1},{4,6},{5,7},{6,4},{7,5},{8,10},{9,11},{10,... | collective-permute-start | bytes 786440 | tf_op jit(solution)/shard_map/ppermute | solution.py:1061
  26.4 23.0 %collective-permute-start.3 = (bf16[4,128,256]{2,1,0:T(8,128)(2,1)S(1)}, bf16[4,128,256]{2,1,0:T(8,128)(2,1)S(1)}, u32[]{:S(2)}, u32[]{:S(2)}) collective-permute-start(bf16[4,128,256]{2,1,0:T(8,128)(2,1)S(1)} %get-tuple-element.406), channel_id=1, source_target_pairs={{0,4},{1,5},{2,6},{3,7},{4,0},{5,1},{6,2},{7,3},{8,12},{9,13},{10,... | collective-permute-start | bytes 786440 | tf_op jit(solution)/shard_map/ppermute | solution.py:1061
  36.2 13.2 %collective-permute-start.7 = (bf16[16,512]{1,0:T(8,128)(2,1)S(1)}, bf16[16,512]{1,0:T(8,128)(2,1)S(1)}, u32[]{:S(2)}, u32[]{:S(2)}) collective-permute-start(bf16[16,512]{1,0:T(8,128)(2,1)S(1)} %get-tuple-element.395), channel_id=1, source_target_pairs={{8,0},{16,4},{24,1},{9,16},{17,20},{25,17},{10,2},{18,6},{26,3},{1... | collective-permute-start | bytes 49160 | tf_op jit(solution)/shard_map/ppermute | solution.py:1212
  37.5 12.0 %collective-permute-start.6 = (bf16[16,512]{1,0:T(8,128)(2,1)S(1)}, bf16[16,512]{1,0:T(8,128)(2,1)S(1)}, u32[]{:S(2)}, u32[]{:S(2)}) collective-permute-start(bf16[16,512]{1,0:T(8,128)(2,1)S(1)} %get-tuple-element.396), channel_id=1, source_target_pairs={{0,4},{8,1},{16,5},{1,20},{9,17},{17,21},{2,6},{10,3},{18,7},{3,22... | collective-permute-start | bytes 49160 | tf_op jit(solution)/shard_map/ppermute | solution.py:1212
  49.5 12.9 %collective-permute-start.8 = (bf16[8,128,256]{2,1,0:T(8,128)(2,1)S(1)}, bf16[8,128,256]{2,1,0:T(8,128)(2,1)S(1)}, u32[]{:S(2)}, u32[]{:S(2)}) collective-permute-start(bf16[8,128,256]{2,1,0:T(8,128)(2,1)S(1)} %pad_maximum_fusion.13), channel_id=1, source_target_pairs={{0,2},{1,3},{2,0},{3,1},{4,6},{5,7},{6,4},{7,5},{8,10},{9,11},{10,... | collective-permute-start | bytes 1572872 | tf_op jit(solution)/shard_map/ppermute | solution.py:1061
  50.6 13.3 %collective-permute-start.9 = (bf16[8,128,256]{2,1,0:T(8,128)(2,1)S(1)}, bf16[8,128,256]{2,1,0:T(8,128)(2,1)S(1)}, u32[]{:S(2)}, u32[]{:S(2)}) collective-permute-start(bf16[8,128,256]{2,1,0:T(8,128)(2,1)S(1)} %pad_maximum_fusion.14), channel_id=1, source_target_pairs={{0,4},{1,5},{2,6},{3,7},{4,0},{5,1},{6,2},{7,3},{8,12},{9,13},{10,... | collective-permute-start | bytes 1572872 | tf_op jit(solution)/shard_map/ppermute | solution.py:1061
  53.1 6.4 %collective-permute-start.12 = (bf16[160,256]{1,0:T(8,128)(2,1)S(1)}, bf16[160,256]{1,0:T(8,128)(2,1)S(1)}, u32[]{:S(2)}, u32[]{:S(2)}) collective-permute-start(bf16[160,256]{1,0:T(8,128)(2,1)S(1)} %copy-done.14), channel_id=1, source_target_pairs={{0,24},{1,25},{2,26},{3,27},{4,28},{5,29},{6,30},{7,31},{8,16},{9,... | collective-permute-start | bytes 245768 | tf_op jit(solution)/shard_map/ppermute | solution.py:1061
  53.9 7.3 %collective-permute-start.11 = (bf16[160,256]{1,0:T(8,128)(2,1)S(1)}, bf16[160,256]{1,0:T(8,128)(2,1)S(1)}, u32[]{:S(2)}, u32[]{:S(2)}) collective-permute-start(bf16[160,256]{1,0:T(8,128)(2,1)S(1)} %copy-done.14), channel_id=1, source_target_pairs={{0,16},{1,17},{2,18},{3,19},{4,20},{5,21},{6,22},{7,23},{8,24},{9,... | collective-permute-start | bytes 245768 | tf_op jit(solution)/shard_map/ppermute | solution.py:1061
  53.9 7.3 %collective-permute-start.10 = (bf16[160,256]{1,0:T(8,128)(2,1)S(1)}, bf16[160,256]{1,0:T(8,128)(2,1)S(1)}, u32[]{:S(2)}, u32[]{:S(2)}) collective-permute-start(bf16[160,256]{1,0:T(8,128)(2,1)S(1)} %copy-done.14), channel_id=1, source_target_pairs={{0,8},{1,9},{2,10},{3,11},{4,12},{5,13},{6,14},{7,15},{8,0},{9,1},... | collective-permute-start | bytes 245768 | tf_op jit(solution)/shard_map/ppermute | solution.py:1061
  64.0 10.7 %collective-permute-start.13 = (bf16[16,128,256]{2,1,0:T(8,128)(2,1)S(1)}, bf16[16,128,256]{2,1,0:T(8,128)(2,1)S(1)}, u32[]{:S(2)}, u32[]{:S(2)}) collective-permute-start(bf16[16,128,256]{2,1,0:T(8,128)(2,1)S(1)} %pad_maximum_fusion.2.p0), channel_id=1, source_target_pairs={{0,1},{1,0},{2,3},{3,2},{4,5},{5,4},{6,7},{7,6},{8,9},{9,8},{10,11... | collective-permute-start | bytes 3145736 | tf_op jit(solution)/shard_map/ppermute | solution.py:1061
  64.1 10.6 %collective-permute-start.14 = (bf16[16,128,256]{2,1,0:T(8,128)(2,1)S(1)}, bf16[16,128,256]{2,1,0:T(8,128)(2,1)S(1)}, u32[]{:S(2)}, u32[]{:S(2)}) collective-permute-start(bf16[16,128,256]{2,1,0:T(8,128)(2,1)S(1)} %pad_maximum_fusion.3.p2), channel_id=1, source_target_pairs={{0,1},{1,0},{2,3},{3,2},{4,5},{5,4},{6,7},{7,6},{8,9},{9,8},{10,11... | collective-permute-start | bytes 3145736 | tf_op jit(solution)/shard_map/ppermute | solution.py:1061
  74.7 11.9 %collective-permute-start.17 = (bf16[8,80,256]{2,1,0:T(8,128)(2,1)S(1)}, bf16[8,80,256]{2,1,0:T(8,128)(2,1)S(1)}, u32[]{:S(2)}, u32[]{:S(2)}) collective-permute-start(bf16[8,80,256]{2,1,0:T(8,128)(2,1)S(1)} %pad_maximum_fusion.18), channel_id=1, source_target_pairs={{0,2},{1,3},{2,0},{3,1},{4,6},{5,7},{6,4},{7,5},{8,10},{9,11},{10,... | collective-permute-start | bytes 983048 | tf_op jit(solution)/shard_map/ppermute | solution.py:1061
  75.8 10.9 %collective-permute-start.18 = (bf16[8,80,256]{2,1,0:T(8,128)(2,1)S(1)}, bf16[8,80,256]{2,1,0:T(8,128)(2,1)S(1)}, u32[]{:S(2)}, u32[]{:S(2)}) collective-permute-start(bf16[8,80,256]{2,1,0:T(8,128)(2,1)S(1)} %pad_maximum_fusion.19), channel_id=1, source_target_pairs={{0,4},{1,5},{2,6},{3,7},{4,0},{5,1},{6,2},{7,3},{8,12},{9,13},{10,... | collective-permute-start | bytes 983048 | tf_op jit(solution)/shard_map/ppermute | solution.py:1061
  87.5 15.0 %collective-permute-start.23 = (bf16[288,256]{1,0:T(8,128)(2,1)S(1)}, bf16[288,256]{1,0:T(8,128)(2,1)S(1)}, u32[]{:S(2)}, u32[]{:S(2)}) collective-permute-start(bf16[288,256]{1,0:T(8,128)(2,1)S(1)} %copy-done.13), channel_id=1, source_target_pairs={{0,24},{1,25},{2,26},{3,27},{4,28},{5,29},{6,30},{7,31},{8,16},{9,... | collective-permute-start | bytes 442376 | tf_op jit(solution)/shard_map/ppermute | solution.py:1061
  89.4 13.2 %collective-permute-start.22 = (bf16[288,256]{1,0:T(8,128)(2,1)S(1)}, bf16[288,256]{1,0:T(8,128)(2,1)S(1)}, u32[]{:S(2)}, u32[]{:S(2)}) collective-permute-start(bf16[288,256]{1,0:T(8,128)(2,1)S(1)} %copy-done.13), channel_id=1, source_target_pairs={{0,16},{1,17},{2,18},{3,19},{4,20},{5,21},{6,22},{7,23},{8,24},{9,... | collective-permute-start | bytes 442376 | tf_op jit(solution)/shard_map/ppermute | solution.py:1061
  89.4 13.2 %collective-permute-start.21 = (bf16[288,256]{1,0:T(8,128)(2,1)S(1)}, bf16[288,256]{1,0:T(8,128)(2,1)S(1)}, u32[]{:S(2)}, u32[]{:S(2)}) collective-permute-start(bf16[288,256]{1,0:T(8,128)(2,1)S(1)} %copy-done.13), channel_id=1, source_target_pairs={{0,8},{1,9},{2,10},{3,11},{4,12},{5,13},{6,14},{7,15},{8,0},{9,1},... | collective-permute-start | bytes 442376 | tf_op jit(solution)/shard_map/ppermute | solution.py:1061
  91.9 10.7 %collective-permute-start.19 = (bf16[16,80,256]{2,1,0:T(8,128)(2,1)S(1)}, bf16[16,80,256]{2,1,0:T(8,128)(2,1)S(1)}, u32[]{:S(2)}, u32[]{:S(2)}) collective-permute-start(bf16[16,80,256]{2,1,0:T(8,128)(2,1)S(1)} %pad_maximum_fusion.6.p0), channel_id=1, source_target_pairs={{0,1},{1,0},{2,3},{3,2},{4,5},{5,4},{6,7},{7,6},{8,9},{9,8},{10,11... | collective-permute-start | bytes 1966088 | tf_op jit(solution)/shard_map/ppermute | solution.py:1061
  91.9 10.7 %collective-permute-start.20 = (bf16[16,80,256]{2,1,0:T(8,128)(2,1)S(1)}, bf16[16,80,256]{2,1,0:T(8,128)(2,1)S(1)}, u32[]{:S(2)}, u32[]{:S(2)}) collective-permute-start(bf16[16,80,256]{2,1,0:T(8,128)(2,1)S(1)} %pad_maximum_fusion.7.p2), channel_id=1, source_target_pairs={{0,1},{1,0},{2,3},{3,2},{4,5},{5,4},{6,7},{7,6},{8,9},{9,8},{10,11... | collective-permute-start | bytes 1966088 | tf_op jit(solution)/shard_map/ppermute | solution.py:1061
  102.7 21.3 %collective-permute-start.25 = (bf16[4,144,256]{2,1,0:T(8,128)(2,1)S(1)}, bf16[4,144,256]{2,1,0:T(8,128)(2,1)S(1)}, u32[]{:S(2)}, u32[]{:S(2)}) collective-permute-start(bf16[4,144,256]{2,1,0:T(8,128)(2,1)S(1)} %get-tuple-element.403), channel_id=1, source_target_pairs={{0,2},{1,3},{2,0},{3,1},{4,6},{5,7},{6,4},{7,5},{8,10},{9,11},{10,... | collective-permute-start | bytes 884744 | tf_op jit(solution)/shard_map/ppermute | solution.py:1061
  103.8 20.3 %collective-permute-start.24 = (bf16[4,144,256]{2,1,0:T(8,128)(2,1)S(1)}, bf16[4,144,256]{2,1,0:T(8,128)(2,1)S(1)}, u32[]{:S(2)}, u32[]{:S(2)}) collective-permute-start(bf16[4,144,256]{2,1,0:T(8,128)(2,1)S(1)} %get-tuple-element.404), channel_id=1, source_target_pairs={{0,4},{1,5},{2,6},{3,7},{4,0},{5,1},{6,2},{7,3},{8,12},{9,13},{10,... | collective-permute-start | bytes 884744 | tf_op jit(solution)/shard_map/ppermute | solution.py:1061
  124.1 16.5 %collective-permute-start.26 = (bf16[768,384]{1,0:T(8,128)(2,1)}, bf16[768,384]{1,0:T(8,128)(2,1)S(1)}, u32[]{:S(2)}, u32[]{:S(2)}) collective-permute-start(bf16[768,384]{1,0:T(8,128)(2,1)} %get-tuple-element.251), channel_id=1, source_target_pairs={{0,4},{4,0},{1,5},{5,1},{16,20},{20,16},{17,21},{21,17},{2,6},{6,2... | collective-permute-start | bytes 1769480 | tf_op jit(solution)/shard_map/ppermute | solution.py:1224
  125.0 15.7 %collective-permute-start.27 = (bf16[768,384]{1,0:T(8,128)(2,1)S(1)}, bf16[768,384]{1,0:T(8,128)(2,1)S(1)}, u32[]{:S(2)}, u32[]{:S(2)}) collective-permute-start(bf16[768,384]{1,0:T(8,128)(2,1)S(1)} %copy-done.35), channel_id=1, source_target_pairs={{0,1},{4,5},{1,0},{5,4},{16,17},{20,21},{17,16},{21,20},{2,3},{6,7... | collective-permute-start | bytes 1769480 | tf_op jit(solution)/shard_map/ppermute | solution.py:1224
  125.2 23.6 %collective-permute-start.28 = (bf16[768,384]{1,0:T(8,128)(2,1)S(1)}, bf16[768,384]{1,0:T(8,128)(2,1)S(1)}, u32[]{:S(2)}, u32[]{:S(2)}) collective-permute-start(bf16[768,384]{1,0:T(8,128)(2,1)S(1)} %copy-done.33), channel_id=1, source_target_pairs={{0,5},{4,1},{1,4},{5,0},{16,21},{20,17},{17,20},{21,16},{2,7},{6,3... | collective-permute-start | bytes 1769480 | tf_op jit(solution)/shard_map/ppermute | solution.py:1224
  148.8 38.6 %collective-permute-start.29 = (bf16[8,144,256]{2,1,0:T(8,128)(2,1)S(1)}, bf16[8,144,256]{2,1,0:T(8,128)(2,1)S(1)}, u32[]{:S(2)}, u32[]{:S(2)}) collective-permute-start(bf16[8,144,256]{2,1,0:T(8,128)(2,1)S(1)} %pad_maximum_fusion.9), channel_id=1, source_target_pairs={{0,2},{1,3},{2,0},{3,1},{4,6},{5,7},{6,4},{7,5},{8,10},{9,11},{10,... | collective-permute-start | bytes 1769480 | tf_op jit(solution)/shard_map/ppermute | solution.py:1061
  149.9 37.7 %collective-permute-start.30 = (bf16[8,144,256]{2,1,0:T(8,128)(2,1)S(1)}, bf16[8,144,256]{2,1,0:T(8,128)(2,1)S(1)}, u32[]{:S(2)}, u32[]{:S(2)}) collective-permute-start(bf16[8,144,256]{2,1,0:T(8,128)(2,1)S(1)} %pad_maximum_fusion.10), channel_id=1, source_target_pairs={{0,4},{1,5},{2,6},{3,7},{4,0},{5,1},{6,2},{7,3},{8,12},{9,13},{10,... | collective-permute-start | bytes 1769480 | tf_op jit(solution)/shard_map/ppermute | solution.py:1061
  150.8 37.0 %collective-permute-start.31 = (bf16[768,512]{1,0:T(8,128)(2,1)S(1)}, bf16[768,512]{1,0:T(8,128)(2,1)S(1)}, u32[]{:S(2)}, u32[]{:S(2)}) collective-permute-start(bf16[768,512]{1,0:T(8,128)(2,1)S(1)} %bitcast.131), channel_id=1, source_target_pairs={{0,0},{8,4},{16,1},{24,5},{1,16},{9,20},{17,17},{25,21},{2,2},{10,... | collective-permute-start | bytes 2359304 | tf_op jit(solution)/shard_map/ppermute | solution.py:1209
  187.8 17.1 %collective-permute-start.35 = (bf16[16,144,256]{2,1,0:T(8,128)(2,1)S(1)}, bf16[16,144,256]{2,1,0:T(8,128)(2,1)S(1)}, u32[]{:S(2)}, u32[]{:S(2)}) collective-permute-start(bf16[16,144,256]{2,1,0:T(8,128)(2,1)S(1)} %pad_maximum_fusion.refs_6_), channel_id=1, source_target_pairs={{0,1},{1,0},{2,3},{3,2},{4,5},{5,4},{6,7},{7,6},{8,9},{9,8},{10,11... | collective-permute-start | bytes 3538952 | tf_op jit(solution)/shard_map/ppermute | solution.py:1061
  191.4 13.4 %collective-permute-start.36 = (bf16[16,144,256]{2,1,0:T(8,128)(2,1)S(1)}, bf16[16,144,256]{2,1,0:T(8,128)(2,1)S(1)}, u32[]{:S(2)}, u32[]{:S(2)}) collective-permute-start(bf16[16,144,256]{2,1,0:T(8,128)(2,1)S(1)} %pad_maximum_fusion.1.refs_8_), channel_id=1, source_target_pairs={{0,1},{1,0},{2,3},{3,2},{4,5},{5,4},{6,7},{7,6},{8,9},{9,8},{10,11... | collective-permute-start | bytes 3538952 | tf_op jit(solution)/shard_map/ppermute | solution.py:1061
  191.5 9.0 %collective-permute-start.32 = (bf16[768,128]{1,0:T(8,128)(2,1)S(1)}, bf16[768,128]{1,0:T(8,128)(2,1)S(1)}, u32[]{:S(2)}, u32[]{:S(2)}) collective-permute-start(bf16[768,128]{1,0:T(8,128)(2,1)S(1)} %copy-done.39), channel_id=1, source_target_pairs={{0,4},{4,0},{1,5},{5,1},{16,20},{20,16},{17,21},{21,17},{2,6},{6,2... | collective-permute-start | bytes 589832 | tf_op jit(solution)/shard_map/ppermute | solution.py:1224
  195.4 9.4 %collective-permute-start.34 = (bf16[768,128]{1,0:T(8,128)(2,1)S(1)}, bf16[768,128]{1,0:T(8,128)(2,1)S(1)}, u32[]{:S(2)}, u32[]{:S(2)}) collective-permute-start(bf16[768,128]{1,0:T(8,128)(2,1)S(1)} %copy-done.41), channel_id=1, source_target_pairs={{0,5},{4,1},{1,4},{5,0},{16,21},{20,17},{17,20},{21,16},{2,7},{6,3... | collective-permute-start | bytes 589832 | tf_op jit(solution)/shard_map/ppermute | solution.py:1224
  229.9 12.5 %collective-permute-start.37 = (bf16[768,128]{1,0:T(8,128)(2,1)}, bf16[768,128]{1,0:T(8,128)(2,1)S(1)}, u32[]{:S(2)}, u32[]{:S(2)}) collective-permute-start(bf16[768,128]{1,0:T(8,128)(2,1)} %get-tuple-element.284), channel_id=1, source_target_pairs={{0,4},{4,0},{1,5},{5,1},{16,20},{20,16},{17,21},{21,17},{2,6},{6,2... | collective-permute-start | bytes 589832 | tf_op jit(solution)/shard_map/ppermute | solution.py:1224
  231.7 10.8 %collective-permute-start.38 = (bf16[768,128]{1,0:T(8,128)(2,1)}, bf16[768,128]{1,0:T(8,128)(2,1)S(1)}, u32[]{:S(2)}, u32[]{:S(2)}) collective-permute-start(bf16[768,128]{1,0:T(8,128)(2,1)} %get-tuple-element.285), channel_id=1, source_target_pairs={{0,1},{4,5},{1,0},{5,4},{16,17},{20,21},{17,16},{21,20},{2,3},{6,7... | collective-permute-start | bytes 589832 | tf_op jit(solution)/shard_map/ppermute | solution.py:1224
  231.7 10.8 %collective-permute-start.39 = (bf16[768,128]{1,0:T(8,128)(2,1)}, bf16[768,128]{1,0:T(8,128)(2,1)S(1)}, u32[]{:S(2)}, u32[]{:S(2)}) collective-permute-start(bf16[768,128]{1,0:T(8,128)(2,1)} %get-tuple-element.286), channel_id=1, source_target_pairs={{0,5},{4,1},{1,4},{5,0},{16,21},{20,17},{17,20},{21,16},{2,7},{6,3... | collective-permute-start | bytes 589832 | tf_op jit(solution)/shard_map/ppermute | solution.py:1224
  242.5 58.9 %collective-permute-start.40 = (bf16[16,288,256]{2,1,0:T(8,128)(2,1)}, bf16[16,288,256]{2,1,0:T(8,128)(2,1)S(1)}, u32[]{:S(2)}, u32[]{:S(2)}) collective-permute-start(bf16[16,288,256]{2,1,0:T(8,128)(2,1)} %get-tuple-element.304), channel_id=1, source_target_pairs={{0,1},{1,0},{2,3},{3,2},{4,5},{5,4},{6,7},{7,6},{8,9},{9,8},{10,11... | collective-permute-start | bytes 7077896 | tf_op jit(solution)/shard_map/ppermute | solution.py:1061
  302.2 29.0 %collective-permute-start.44 = (bf16[8,288,256]{2,1,0:T(8,128)(2,1)S(1)}, bf16[8,288,256]{2,1,0:T(8,128)(2,1)S(1)}, u32[]{:S(2)}, u32[]{:S(2)}) collective-permute-start(bf16[8,288,256]{2,1,0:T(8,128)(2,1)S(1)} %slice.314), channel_id=1, source_target_pairs={{0,2},{1,3},{2,0},{3,1},{4,6},{5,7},{6,4},{7,5},{8,10},{9,11},{10,... | collective-permute-start | bytes 3538952 | tf_op jit(solution)/shard_map/ppermute | solution.py:1061
  305.0 26.6 %collective-permute-start.41 = (bf16[768,384]{1,0:T(8,128)(2,1)S(1)}, bf16[768,384]{1,0:T(8,128)(2,1)S(1)}, u32[]{:S(2)}, u32[]{:S(2)}) collective-permute-start(bf16[768,384]{1,0:T(8,128)(2,1)S(1)} %copy-done.32), channel_id=1, source_target_pairs={{0,4},{4,0},{1,5},{5,1},{16,20},{20,16},{17,21},{21,17},{2,6},{6,2... | collective-permute-start | bytes 1769480 | tf_op jit(solution)/shard_map/ppermute | solution.py:1224
  306.9 24.7 %collective-permute-start.42 = (bf16[768,384]{1,0:T(8,128)(2,1)S(1)}, bf16[768,384]{1,0:T(8,128)(2,1)S(1)}, u32[]{:S(2)}, u32[]{:S(2)}) collective-permute-start(bf16[768,384]{1,0:T(8,128)(2,1)S(1)} %copy-done.31), channel_id=1, source_target_pairs={{0,1},{4,5},{1,0},{5,4},{16,17},{20,21},{17,16},{21,20},{2,3},{6,7... | collective-permute-start | bytes 1769480 | tf_op jit(solution)/shard_map/ppermute | solution.py:1224
  306.9 25.1 %collective-permute-start.43 = (bf16[768,384]{1,0:T(8,128)(2,1)S(1)}, bf16[768,384]{1,0:T(8,128)(2,1)S(1)}, u32[]{:S(2)}, u32[]{:S(2)}) collective-permute-start(bf16[768,384]{1,0:T(8,128)(2,1)S(1)} %copy-done.30), channel_id=1, source_target_pairs={{0,5},{4,1},{1,4},{5,0},{16,21},{20,17},{17,20},{21,16},{2,7},{6,3... | collective-permute-start | bytes 1769480 | tf_op jit(solution)/shard_map/ppermute | solution.py:1224
  332.0 23.9 %collective-permute-start.47 = (bf16[4,288,256]{2,1,0:T(8,128)(2,1)S(1)}, bf16[4,288,256]{2,1,0:T(8,128)(2,1)S(1)}, u32[]{:S(2)}, u32[]{:S(2)}) collective-permute-start(bf16[4,288,256]{2,1,0:T(8,128)(2,1)S(1)} %slice.318), channel_id=1, source_target_pairs={{0,4},{1,5},{2,6},{3,7},{4,0},{5,1},{6,2},{7,3},{8,12},{9,13},{10,... | collective-permute-start | bytes 1769480 | tf_op jit(solution)/shard_map/ppermute | solution.py:1061
  343.3 12.8 %collective-permute-start.46 = (bf16[16,256]{1,0:T(8,128)(2,1)S(1)}, bf16[16,256]{1,0:T(8,128)(2,1)S(1)}, u32[]{:S(2)}, u32[]{:S(2)}) collective-permute-start(bf16[16,256]{1,0:T(8,128)(2,1)S(1)} %get-tuple-element.424), channel_id=1, source_target_pairs={{4,0},{1,4},{5,1},{20,16},{17,20},{21,17},{6,2},{3,6},{7,3},{22,18... | collective-permute-start | bytes 24584 | tf_op jit(solution)/shard_map/ppermute | solution.py:1220
  344.6 11.5 %collective-permute-start.45 = (bf16[16,256]{1,0:T(8,128)(2,1)S(1)}, bf16[16,256]{1,0:T(8,128)(2,1)S(1)}, u32[]{:S(2)}, u32[]{:S(2)}) collective-permute-start(bf16[16,256]{1,0:T(8,128)(2,1)S(1)} %get-tuple-element.425), channel_id=1, source_target_pairs={{0,4},{4,1},{1,5},{16,20},{20,17},{17,21},{2,6},{6,3},{3,7},{18,22... | collective-permute-start | bytes 24584 | tf_op jit(solution)/shard_map/ppermute | solution.py:1220
  356.1 50.3 %collective-permute-start.48 = (bf16[288,256]{1,0:T(8,128)(2,1)S(1)}, bf16[288,256]{1,0:T(8,128)(2,1)S(1)}, u32[]{:S(2)}, u32[]{:S(2)}) collective-permute-start(bf16[288,256]{1,0:T(8,128)(2,1)S(1)} %get-tuple-element.400), channel_id=1, source_target_pairs={{0,8},{1,9},{2,10},{3,11},{4,12},{5,13},{6,14},{7,15},{8,0},{9,1},... | collective-permute-start | bytes 442376 | tf_op jit(solution)/shard_map/ppermute | solution.py:1061
  356.2 50.2 %collective-permute-start.50 = (bf16[288,256]{1,0:T(8,128)(2,1)S(1)}, bf16[288,256]{1,0:T(8,128)(2,1)S(1)}, u32[]{:S(2)}, u32[]{:S(2)}) collective-permute-start(bf16[288,256]{1,0:T(8,128)(2,1)S(1)} %get-tuple-element.401), channel_id=1, source_target_pairs={{0,24},{1,25},{2,26},{3,27},{4,28},{5,29},{6,30},{7,31},{8,16},{9,... | collective-permute-start | bytes 442376 | tf_op jit(solution)/shard_map/ppermute | solution.py:1061
  357.4 49.0 %collective-permute-start.49 = (bf16[288,256]{1,0:T(8,128)(2,1)S(1)}, bf16[288,256]{1,0:T(8,128)(2,1)S(1)}, u32[]{:S(2)}, u32[]{:S(2)}) collective-permute-start(bf16[288,256]{1,0:T(8,128)(2,1)S(1)} %get-tuple-element.402), channel_id=1, source_target_pairs={{0,16},{1,17},{2,18},{3,19},{4,20},{5,21},{6,22},{7,23},{8,24},{9,... | collective-permute-start | bytes 442376 | tf_op jit(solution)/shard_map/ppermute | solution.py:1061
  359.7 47.3 %collective-permute-start.52 = (bf16[768,512]{1,0:T(8,128)(2,1)}, bf16[768,512]{1,0:T(8,128)(2,1)S(1)}, u32[]{:S(2)}, u32[]{:S(2)}) collective-permute-start(bf16[768,512]{1,0:T(8,128)(2,1)} %get-tuple-element.335), channel_id=1, source_target_pairs={{0,0},{4,8},{1,16},{5,24},{16,1},{20,9},{17,17},{21,25},{2,2},{6,1... | collective-permute-start | bytes 2359304 | tf_op jit(solution)/shard_map/ppermute | solution.py:1217
  361.5 45.1 %collective-permute-start.51 = (bf16[16,160,256]{2,1,0:T(8,128)(2,1)}, bf16[16,160,256]{2,1,0:T(8,128)(2,1)S(1)}, u32[]{:S(2)}, u32[]{:S(2)}) collective-permute-start(bf16[16,160,256]{2,1,0:T(8,128)(2,1)} %get-tuple-element.334), channel_id=1, source_target_pairs={{0,1},{1,0},{2,3},{3,2},{4,5},{5,4},{6,7},{7,6},{8,9},{9,8},{10,11... | collective-permute-start | bytes 3932168 | tf_op jit(solution)/shard_map/ppermute | solution.py:1061
  413.8 11.9 %collective-permute-start.55 = (bf16[16,176,256]{2,1,0:T(8,128)(2,1)}, bf16[16,176,256]{2,1,0:T(8,128)(2,1)S(1)}, u32[]{:S(2)}, u32[]{:S(2)}) collective-permute-start(bf16[16,176,256]{2,1,0:T(8,128)(2,1)} %get-tuple-element.352), channel_id=1, source_target_pairs={{0,1},{1,0},{2,3},{3,2},{4,5},{5,4},{6,7},{7,6},{8,9},{9,8},{10,11... | collective-permute-start | bytes 4325384 | tf_op jit(solution)/shard_map/ppermute | solution.py:1061
  413.9 11.6 %collective-permute-start.54 = (bf16[8,80,256]{2,1,0:T(8,128)(2,1)S(1)}, bf16[8,80,256]{2,1,0:T(8,128)(2,1)S(1)}, u32[]{:S(2)}, u32[]{:S(2)}) collective-permute-start(bf16[8,80,256]{2,1,0:T(8,128)(2,1)S(1)} %slice.328), channel_id=1, source_target_pairs={{0,4},{1,5},{2,6},{3,7},{4,0},{5,1},{6,2},{7,3},{8,12},{9,13},{10,... | collective-permute-start | bytes 983048 | tf_op jit(solution)/shard_map/ppermute | solution.py:1061
  414.0 11.6 %collective-permute-start.53 = (bf16[8,80,256]{2,1,0:T(8,128)(2,1)S(1)}, bf16[8,80,256]{2,1,0:T(8,128)(2,1)S(1)}, u32[]{:S(2)}, u32[]{:S(2)}) collective-permute-start(bf16[8,80,256]{2,1,0:T(8,128)(2,1)S(1)} %slice.326), channel_id=1, source_target_pairs={{0,2},{1,3},{2,0},{3,1},{4,6},{5,7},{6,4},{7,5},{8,10},{9,11},{10,... | collective-permute-start | bytes 983048 | tf_op jit(solution)/shard_map/ppermute | solution.py:1061
  426.9 18.1 %collective-permute-start.57 = (bf16[960,256]{1,0:T(8,128)(2,1)S(1)}, bf16[960,256]{1,0:T(8,128)(2,1)S(1)}, u32[]{:S(2)}, u32[]{:S(2)}) collective-permute-start(bf16[960,256]{1,0:T(8,128)(2,1)S(1)} %pad_maximum_fusion.15), channel_id=1, source_target_pairs={{0,4},{1,5},{2,6},{3,7},{4,0},{5,1},{6,2},{7,3},{8,12},{9,13},{10,... | collective-permute-start | bytes 1474568 | tf_op jit(solution)/shard_map/ppermute | solution.py:1061
  428.9 16.2 %collective-permute-start.56 = (bf16[1088,256]{1,0:T(8,128)(2,1)S(1)}, bf16[1088,256]{1,0:T(8,128)(2,1)S(1)}, u32[]{:S(2)}, u32[]{:S(2)}) collective-permute-start(bf16[1088,256]{1,0:T(8,128)(2,1)S(1)} %pad_maximum_fusion.11), channel_id=1, source_target_pairs={{0,2},{1,3},{2,0},{3,1},{4,6},{5,7},{6,4},{7,5},{8,10},{9,11},{10,... | collective-permute-start | bytes 1671176 | tf_op jit(solution)/shard_map/ppermute | solution.py:1061
  438.3 7.8 %collective-permute-start.58 = (bf16[384,512]{1,0:T(8,128)(2,1)}, bf16[384,512]{1,0:T(8,128)(2,1)S(1)}, u32[]{:S(2)}, u32[]{:S(2)}) collective-permute-start(bf16[384,512]{1,0:T(8,128)(2,1)} %get-tuple-element.373), channel_id=1, source_target_pairs={{0,0},{4,8},{1,16},{5,24},{16,1},{20,9},{17,17},{21,25},{2,2},{6,1... | collective-permute-start | bytes 1179656 | tf_op jit(solution)/shard_map/ppermute | solution.py:1217
  446.2 7.8 %collective-permute-start.59 = (bf16[16,80,256]{2,1,0:T(8,128)(2,1)S(1)}, bf16[16,80,256]{2,1,0:T(8,128)(2,1)S(1)}, u32[]{:S(2)}, u32[]{:S(2)}) collective-permute-start(bf16[16,80,256]{2,1,0:T(8,128)(2,1)S(1)} %copy-done.24), channel_id=1, source_target_pairs={{0,1},{1,0},{2,3},{3,2},{4,5},{5,4},{6,7},{7,6},{8,9},{9,8},{10,11... | collective-permute-start | bytes 1966088 | tf_op jit(solution)/shard_map/ppermute | solution.py:1061
  452.3 29.5 %collective-permute-start.63 = (bf16[384,512]{1,0:T(8,128)(2,1)S(1)}, bf16[384,512]{1,0:T(8,128)(2,1)S(1)}, u32[]{:S(2)}, u32[]{:S(2)}) collective-permute-start(bf16[384,512]{1,0:T(8,128)(2,1)S(1)} %copy-done.38), channel_id=1, source_target_pairs={{0,0},{4,8},{1,16},{5,24},{16,1},{20,9},{17,17},{21,25},{2,2},{6,1... | collective-permute-start | bytes 1179656 | tf_op jit(solution)/shard_map/ppermute | solution.py:1217
  454.3 10.1 %collective-permute-start.61 = (bf16[640,256]{1,0:T(8,128)(2,1)S(1)}, bf16[640,256]{1,0:T(8,128)(2,1)S(1)}, u32[]{:S(2)}, u32[]{:S(2)}) collective-permute-start(bf16[640,256]{1,0:T(8,128)(2,1)S(1)} %pad_maximum_fusion.20), channel_id=1, source_target_pairs={{0,2},{1,3},{2,0},{3,1},{4,6},{5,7},{6,4},{7,5},{8,10},{9,11},{10,... | collective-permute-start | bytes 983048 | tf_op jit(solution)/shard_map/ppermute | solution.py:1061
  456.1 25.6 %collective-permute-start.62 = (bf16[4,80,256]{2,1,0:T(8,128)(2,1)S(1)}, bf16[4,80,256]{2,1,0:T(8,128)(2,1)S(1)}, u32[]{:S(2)}, u32[]{:S(2)}) collective-permute-start(bf16[4,80,256]{2,1,0:T(8,128)(2,1)S(1)} %get-tuple-element.397), channel_id=1, source_target_pairs={{0,6},{1,7},{2,4},{3,5},{4,2},{5,3},{6,0},{7,1},{8,14},{9,15},{10,... | collective-permute-start | bytes 491528 | tf_op jit(solution)/shard_map/ppermute | solution.py:1061
  462.1 19.6 %collective-permute-start.60 = (bf16[704,256]{1,0:T(8,128)(2,1)S(1)}, bf16[704,256]{1,0:T(8,128)(2,1)S(1)}, u32[]{:S(2)}, u32[]{:S(2)}) collective-permute-start(bf16[704,256]{1,0:T(8,128)(2,1)S(1)} %pad_maximum_fusion.16), channel_id=1, source_target_pairs={{0,4},{1,5},{2,6},{3,7},{4,0},{5,1},{6,2},{7,3},{8,12},{9,13},{10,... | collective-permute-start | bytes 1081352 | tf_op jit(solution)/shard_map/ppermute | solution.py:1061
  482.0 11.6 %collective-permute-start.64 = (bf16[416,256]{1,0:T(8,128)(2,1)S(1)}, bf16[416,256]{1,0:T(8,128)(2,1)S(1)}, u32[]{:S(2)}, u32[]{:S(2)}) collective-permute-start(bf16[416,256]{1,0:T(8,128)(2,1)S(1)} %get-tuple-element.392), channel_id=1, source_target_pairs={{0,8},{1,9},{2,10},{3,11},{4,12},{5,13},{6,14},{7,15},{8,0},{9,1},... | collective-permute-start | bytes 638984 | tf_op jit(solution)/shard_map/ppermute | solution.py:1061
  482.8 11.2 %collective-permute-start.66 = (bf16[416,256]{1,0:T(8,128)(2,1)S(1)}, bf16[416,256]{1,0:T(8,128)(2,1)S(1)}, u32[]{:S(2)}, u32[]{:S(2)}) collective-permute-start(bf16[416,256]{1,0:T(8,128)(2,1)S(1)} %get-tuple-element.393), channel_id=1, source_target_pairs={{0,24},{1,25},{2,26},{3,27},{4,28},{5,29},{6,30},{7,31},{8,16},{9,... | collective-permute-start | bytes 638984 | tf_op jit(solution)/shard_map/ppermute | solution.py:1061
  483.3 20.8 %collective-permute-start.65 = (bf16[416,256]{1,0:T(8,128)(2,1)S(1)}, bf16[416,256]{1,0:T(8,128)(2,1)S(1)}, u32[]{:S(2)}, u32[]{:S(2)}) collective-permute-start(bf16[416,256]{1,0:T(8,128)(2,1)S(1)} %get-tuple-element.394), channel_id=1, source_target_pairs={{0,16},{1,17},{2,18},{3,19},{4,20},{5,21},{6,22},{7,23},{8,24},{9,... | collective-permute-start | bytes 638984 | tf_op jit(solution)/shard_map/ppermute | solution.py:1061
  (56 other events, 452.4 us)

commit v6 on v5

--- a/solution.py
+++ b/solution.py
@@ -124,8 +124,8 @@
     return jnp.sum(v.reshape(v.shape[0] // 8, 8, v.shape[1]), axis=0)
 
 
-def rows_at(i, tile, start=0):
-    return pl.ds(pl.multiple_of(start + i * tile, 16), tile)
+def rows_at(i, tile, start=0, count=None):
+    return pl.ds(pl.multiple_of(start + i * tile, 16), count or tile)
 
 
 def places(base, rows, lanes=LANES):
@@ -366,12 +366,14 @@
     right = right + jnp.where((pos == first) | (pos == 0), 0.0, before)
     right = right + jnp.where((pos + 1 == first) | (pos + 1 == group), 0.0, after)
     right_ref[...] = right
-    left = gelu(left)
-    joined = jnp.concatenate([left[:, :NARROW] + gelu(right), left[:, NARROW:]], axis=1)
-    hat, _ = normalise(joined)
-    row = base + i * tile + lax.broadcasted_iota(jnp.int32, (tile, 1), 0)
-    inside = ((row >= 0) & (row < group)).astype(F32)
-    mid_ref[...] = (hat * inside * g3[...]).astype(BF)
+    for q in range(0, tile, STEP):
+        at = slice(q, q + STEP)
+        left = gelu(left_ref[at, :])
+        joined = jnp.concatenate([left[:, :NARROW] + gelu(right_ref[at, :]), left[:, NARROW:]], axis=1)
+        hat, _ = normalise(joined)
+        row = base + i * tile + q + iota((STEP, 1), 0)
+        inside = ((row >= 0) & (row < group)).astype(F32)
+        mid_ref[at, :] = (hat * inside * g3[...]).astype(BF)
 
 
 def front2(scal, y2, g3, wide, narrow, group, ties=()):
@@ -394,16 +396,8 @@
     return (pos >= first) & (pos + offset < first)
 
 
-def conv(win, tile, taps, lanes, pos, first, masked, sign):
-    total = None
-    for k in range(KERNEL):
-        o = sign * (k - HALF)
-        v = win[RIM + o : RIM + o + tile, :]
-        if masked and o != 0:
-            v = jnp.where(crosses(pos, o, first), 0.0, v)
-        v = v * taps[k : k + 1, lanes]
-        total = v if total is None else total + v
-    return total
+WIDTH = 4
+STEP = 16
 
 
 def front3_kernel(tile, n, share, scal, mid_ref, taps, h1_ref, g4, p0, p1, p2, p3, *refs):
@@ -421,19 +415,30 @@
     near = (first > begin - HALF) & (first < begin + tile + HALF)
 
     def chunk(c, carry):
-        lanes = pl.ds(pl.multiple_of(c * LANES, LANES), LANES)
         around = pl.ds(pl.multiple_of(i * tile, 16), tile + 2 * RIM)
-        win[...] = mid_ref[around, lanes].astype(F32)
-        pos = places(begin, tile)
+        lanes = [pl.ds(pl.multiple_of((c * WIDTH + w) * LANES, LANES), LANES) for w in range(WIDTH)]
+        for w in range(WIDTH):
+            win[w] = mid_ref[around, lanes[w]].astype(F32)
         for masked in (False, True):
 
             @pl.when(near if masked else jnp.logical_not(near))
             def _():
-                spread_ref[:, lanes] = conv(win, tile, taps, lanes, pos, first, masked, 1).astype(BF)
+                for w in range(WIDTH):
+                    tap = [taps[k : k + 1, lanes[w]] for k in range(KERNEL)]
+                    for r in range(0, tile, STEP):
+                        pos = places(begin + r, STEP)
+                        total = None
+                        for k in range(KERNEL):
+                            o = k - HALF
+                            v = win[w, RIM + o + r : RIM + o + r + STEP, :]
+                            if masked and o != 0:
+                                v = jnp.where(crosses(pos, o, first), 0.0, v)
+                            total = v * tap[k] if total is None else total + v * tap[k]
+                        spread_ref[r : r + STEP, lanes[w]] = total.astype(BF)
 
         return carry
 
-    lax.fori_loop(0, FF // LANES, chunk, 0)
+    lax.fori_loop(0, FF // (WIDTH * LANES), chunk, 0)
     h1 = h1_ref[rows_at(i, tile, RIM), :]
     branch = nn(spread_ref[...], point[...])
     h2 = jnp.concatenate([h1[:, :NARROW] + branch, h1[:, NARROW:]], axis=1)
@@ -459,7 +464,7 @@
         [((rows, FF), BF, tile), ((rows, D), F32, tile), ((rows, D), BF, tile)]
         + [((rows, 3 * LANES), BF, tile)] * n
         + [(shape, BF, None) for shape in SHAPES[1].values()],
-        scratch=[((tile + 2 * RIM, LANES), F32), ((tile, 3 * D), BF)],
+        scratch=[((WIDTH, tile + 2 * RIM, LANES), F32), ((tile, 3 * D), BF)],
         micros=20,
         ties=ties,
         steps=rows // tile,
@@ -658,46 +663,56 @@
     near = near | (i == 0) | (i == last)
 
     def chunk(c, carry):
-        lanes = pl.ds(pl.multiple_of(c * LANES, LANES), LANES)
         around = pl.ds(pl.multiple_of(i * tile, 16), tile + 2 * RIM)
-        win[...] = dsp[around, lanes]
-        local = i * tile + lax.broadcasted_iota(jnp.int32, (tile, LANES), 0)
-        mid = mid_ref[:, lanes].astype(F32)
-        pos = places(begin, tile)
+        lanes = [pl.ds(pl.multiple_of((c * WIDTH + w) * LANES, LANES), LANES) for w in range(WIDTH)]
+        for w in range(WIDTH):
+            win[w] = dsp[around, lanes[w]]
         for masked in (False, True):
 
             @pl.when(near if masked else jnp.logical_not(near))
             def _():
-                total = None
-                for k in range(KERNEL):
-                    o = HALF - k
-                    v = win[RIM + o : RIM + o + tile, :]
-                    if masked and o != 0:
-                        v = jnp.where(crosses(pos, o, first), 0.0, v)
-                    counted = v
-                    if masked:
-                        kept = (local + o >= RIM) & (local + o < RIM + rows)
-                        counted = jnp.where(kept, v, 0.0)
-                    gdepth_ref[k * 8 : (k + 1) * 8, lanes] += fold8(counted * mid)
-                    v = v * taps[k : k + 1, lanes]
-                    total = v if total is None else total + v
-                dmid[:, lanes] = total
+                for w in range(WIDTH):
+                    tap = [taps[k : k + 1, lanes[w]] for k in range(KERNEL)]
+                    pairs = [None] * KERNEL
+                    for r in range(0, tile, STEP):
+                        pos = places(begin + r, STEP)
+                        local = i * tile + r + iota((STEP, LANES), 0)
+                        mid = mid_ref[r : r + STEP, lanes[w]].astype(F32)
+                        total = None
+                        for k in range(KERNEL):
+                            o = HALF - k
+                            v = win[w, RIM + o + r : RIM + o + r + STEP, :]
+                            if masked and o != 0:
+                                v = jnp.where(crosses(pos, o, first), 0.0, v)
+                            counted = v
+                            if masked:
+                                kept = (local + o >= RIM) & (local + o < RIM + rows)
+                                counted = jnp.where(kept, v, 0.0)
+                            counted = counted * mid
+                            counted = counted[:8] + counted[8:]
+                            pairs[k] = counted if pairs[k] is None else pairs[k] + counted
+                            total = v * tap[k] if total is None else total + v * tap[k]
+                        dmid[r : r + STEP, lanes[w]] = total
+                    for k in range(KERNEL):
+                        gdepth_ref[k * 8 : (k + 1) * 8, lanes[w]] += pairs[k]
 
         return carry
 
-    lax.fori_loop(0, FF // LANES, chunk, 0)
-    left, slope = gelu_and_slope(left_ref[...])
-    right, slope_r = gelu_and_slope(right_ref[...])
-    joined = jnp.concatenate([left[:, :NARROW] + right, left[:, NARROW:]], axis=1)
-    hat, r = normalise(joined)
-    local = i * tile + lax.broadcasted_iota(jnp.int32, (tile, 1), 0)
-    own = ((local >= RIM) & (local < RIM + rows)).astype(F32)
-    pos = base + local
-    grad = dmid[...] * ((pos >= 0) & (pos < group)).astype(F32)
-    ln_ref[...] += fold8(grad * hat * own)
-    dj = norm_back(grad, hat, r, g3[...])
-    dl[...] = (dj * slope).astype(BF)
-    dr[rows_at(i, tile, RIM), :] = (dj[:, :NARROW] * slope_r).astype(BF).astype(F32)
+    lax.fori_loop(0, FF // (WIDTH * LANES), chunk, 0)
+    for q in range(0, tile, STEP):
+        at = slice(q, q + STEP)
+        left, slope = gelu_and_slope(left_ref[at, :])
+        right, slope_r = gelu_and_slope(right_ref[at, :])
+        joined = jnp.concatenate([left[:, :NARROW] + right, left[:, NARROW:]], axis=1)
+        hat, r = normalise(joined)
+        local = i * tile + q + iota((STEP, 1), 0)
+        own = ((local >= RIM) & (local < RIM + rows)).astype(F32)
+        pos = base + local
+        grad = dmid[at, :] * ((pos >= 0) & (pos < group)).astype(F32)
+        ln_ref[...] += fold8(grad * hat * own)
+        dj = norm_back(grad, hat, r, g3[...])
+        dl[at, :] = (dj * slope).astype(BF)
+        dr[rows_at(i, tile, RIM + q, STEP), :] = (dj[:, :NARROW] * slope_r).astype(BF).astype(F32)
 
     @pl.when(i == last)
     def _():
@@ -740,7 +755,7 @@
         scratch=[
             ((ext, NARROW), BF),
             ((ext + 2 * RIM, FF), F32),
-            ((tile + 2 * RIM, LANES), F32),
+            ((WIDTH, tile + 2 * RIM, LANES), F32),
             ((tile, FF), F32),
             ((ext + 2 * RIM, NARROW), F32),
             ((8 * KERNEL, FF), F32),
@@ -945,7 +960,7 @@
         return carry
     lax.fori_loop(0, n*per, q_step, 0)
 
-def attend(scal, blocks, n, share, tq=768, tk=384, ties=()):
+def attend(scal, blocks, n, share, tq=768, tk=768, ties=()):
     rows = blocks[0].shape[0]
     heads = 2 // share
     return whole_call(
@@ -1279,18 +1294,18 @@
         held1, x, low, high, blocks = sync(held1, x, low, high, blocks)
         held1 = links.spread(held1, 1)
         held2 = links.near(blocks[1])
-        held1, held2 = sync(held1, held2)
+    digits = x[rows, 0 : 2 * LANES : LANES].astype(F32).astype(jnp.int32)
+    first = digits[0] * LANES + digits[1]
+    scal = jnp.stack([s.astype(jnp.int32), first, me.astype(jnp.int32)])
+    x_ext = jnp.concatenate([low, x[:rows], high], axis=0)
+    if direct:
+        held1, held2, scal, x_ext = sync(held1, held2, scal, x_ext)
         pieces1 = links.across(held1)
         held2 = links.spread(links.part(1, held2), 0)
         pieces1, held2 = sync(pieces1, held2)
         held2 = links.spread(held2, 1)
     else:
         pieces1, pieces2, pieces3 = (links.gather_whole(k, mine) for k in range(3))
-    digits = x[rows, 0 : 2 * LANES : LANES].astype(F32).astype(jnp.int32)
-    first = digits[0] * LANES + digits[1]
-    scal = jnp.stack([s.astype(jnp.int32), first, me.astype(jnp.int32)])
-    x_ext = jnp.concatenate([low, x[:rows], high], axis=0)
-
     h1, y2, joined, *rest = front1(scal, x_ext, pieces1)
     (glu, wide, narrow), (g1, g2, g3, g4, g5, taps) = rest[:3], rest[3:]
     if direct:

time: 517 us -> 504 us (0.975)
  Pallas kernels: 258 us -> 244 us
    pallas_call x15, Pallas kernels: 258 us -> 244 us  [call(): pl.pallas_call(kernel, out_shape=shapes, grid=() if steps is None else (s...]
  transfers between devices with their start and end apart: 67 -> 67, of which waited for: 21 -> 18; matrix products, arithmetic and copies ran while one was open for 2% -> 2% of each run, Pallas kernels for 44% -> 43%
where the time goes in v6:
time: 504 us; the launch traced here: 496 us
  Pallas kernels  244 us (48%)
  waiting for transfers between devices  124 us (25%)
  starting transfers between devices  97.7 us (19%)
  local copies, waits for them, and re-layouts  14.5 us (3%)
  other arithmetic  11.5 us (2%)
    pallas_call x15, Pallas kernels, call(): pl.pallas_call(kernel, out_shape=shapes, grid=() if steps is None else (s...  244 us
    ppermute x46, waiting for transfers between devices, flip(): return lax.ppermute(value, AXES, [(i, i ^ mask) for i in range(self.count)])  91.4 us
    ppermute x46, starting transfers between devices, flip(): return lax.ppermute(value, AXES, [(i, i ^ mask) for i in range(self.count)])  72.4 us
    ppermute x12, waiting for transfers between devices, swap(): lax.ppermute(values[k], AXES, self.pairs(self.at, lambda g, s: self.at(g,...  32.5 us
    ppermute x12, starting transfers between devices, swap(): lax.ppermute(values[k], AXES, self.pairs(self.at, lambda g, s: self.at(g,...  10.5 us
  transfers between devices with their start and end apart: 67, of which 18 were waited for; matrix products, arithmetic and copies ran while one was open for 2% of the time, Pallas kernels for 43%

profile of v6, /device:TPU:0, one launch (start us, length us, event | category | flops | bytes accessed | tf_op | source)
XLA Modules:
  0.0 495.5 jit_solution(2920610421967699470)
XLA Ops:
  3.5 1.2 pad_maximum_fusion.5
  4.7 1.7 shard_map.297
  6.4 5.0 %collective-permute-start.2 = (bf16[256,256]{1,0:T(8,128)(2,1)}, bf16[256,256]{1,0:T(8,128)(2,1)S(1)}, u32[]{:S(2)}, u32[]{:S(2)}) collective-permute-start(bf16[256,256]{1,0:T(8,128)(2,1)} %get-tuple-element.208), channel_id=1, source_target_pairs={{0,24},{1,25},{2,26},{3,27},{4,28},{5,29},{6,30},{7,31},{8,16},{9,... | collective-permute-start | bytes 393224 | tf_op jit(solution)/shard_map/ppermute | solution.py:1076
  12.8 3.3 collective-permute-done.2
  16.1 7.9 %collective-permute-done.1 = bf16[256,256]{1,0:T(8,128)(2,1)S(1)} collective-permute-done((bf16[256,256]{1,0:T(8,128)(2,1)}, bf16[256,256]{1,0:T(8,128)(2,1)S(1)}, u32[]{:S(2)}, u32[]{:S(2)}) %collective-permute-start.1) | collective-permute-done | bytes 131104 | tf_op jit(solution)/shard_map/ppermute | solution.py:1076
  25.0 1.4 collective-permute-start.4
  26.3 9.1 %collective-permute-start.3 = (bf16[4,128,256]{2,1,0:T(8,128)(2,1)S(1)}, bf16[4,128,256]{2,1,0:T(8,128)(2,1)S(1)}, u32[]{:S(2)}, u32[]{:S(2)}) collective-permute-start(bf16[4,128,256]{2,1,0:T(8,128)(2,1)S(1)} %get-tuple-element.410), channel_id=1, source_target_pairs={{0,4},{1,5},{2,6},{3,7},{4,0},{5,1},{6,2},{7,3},{8,12},{9,13},{10,... | collective-permute-start | bytes 786440 | tf_op jit(solution)/shard_map/ppermute | solution.py:1076
  36.2 1.3 collective-permute-start.7
  37.5 1.9 collective-permute-start.6
  40.0 9.3 %collective-permute-done.3 = bf16[4,128,256]{2,1,0:T(8,128)(2,1)S(1)} collective-permute-done((bf16[4,128,256]{2,1,0:T(8,128)(2,1)S(1)}, bf16[4,128,256]{2,1,0:T(8,128)(2,1)S(1)}, u32[]{:S(2)}, u32[]{:S(2)}) %collective-permute-start.3) | collective-permute-done | bytes 262176 | tf_op jit(solution)/shard_map/ppermute | solution.py:1076
  49.7 2.7 collective-permute-start.12
  52.4 1.8 collective-permute-start.10
  55.2 2.5 collective-permute-start.9
  60.5 1.2 pad_add_fusion.scal
  61.8 4.2 collective-permute-done.8
  66.2 1.4 collective-permute-done.9
  69.3 1.7 collective-permute-start.15
  71.1 3.5 collective-permute-done.16
  76.4 1.7 collective-permute-start.18
  78.2 9.0 %shard_map.298 = (f32[800,512]{1,0:T(8,128)}, bf16[800,512]{1,0:T(8,128)(2,1)}, f32[800,1024]{1,0:T(8,128)}, bf16[512,1024]{1,0:T(8,128)(2,1)}, bf16[512,2048]{1...) custom-call(s32[3]{0:T(128)} %pad_add_fusion.scal, ...), custom_call_target="tpu_custom_call" | custom-call | flops 13799999488 | bytes 14770188 | tf_op jit(solution)/shard_map/pallas_call | solution.py:69
  88.1 1.9 collective-permute-start.23
  90.0 2.5 collective-permute-start.21
  93.0 10.5 %shard_map.299 = (f32[800,2048]{1,0:T(8,128)}, f32[800,256]{1,0:T(8,128)}, bf16[800,2048]{1,0:T(8,128)(2,1)}) custom-call(s32[3]{0:T(128)} %pad_add_fusion.scal, bf16[800,512]{1,0:T(8,128)(2,1)} %get-tuple-element.231.y2_ref, f32[1,2048]{1,0:T(1,128)} %get-tuple-element.232.g3.refs_4_, bf16[512,2048]{1,0:T(8,128)(2,1)} %get-tuple-element.233.wide.refs_1_, ...), custom_call_target="tpu_custom_call" | custom-call | flops 13799999488 | bytes 14360588 | tf_op jit(solution)/shard_map/pallas_call | solution.py:69
  105.0 17.8 %shard_map.300 = (bf16[768,2048]{1,0:T(8,128)(2,1)}, f32[768,512]{1,0:T(8,128)}, bf16[768,512]{1,0:T(8,128)(2,1)}, bf16[768,384]{1,0:T(8,128)(2,1)}, bf16[768,38...) custom-call(s32[3]{0:T(128)} %pad_add_fusion.scal, ...), custom_call_target="tpu_custom_call" | custom-call | flops 23000000512 | bytes 18098188 | tf_op jit(solution)/shard_map/pallas_call | solution.py:69
  124.0 1.1 collective-permute-start.28
  125.2 14.3 %collective-permute-done.26.refs_1_ = bf16[768,384]{1,0:T(8,128)(2,1)S(1)} collective-permute-done((bf16[768,384]{1,0:T(8,128)(2,1)}, bf16[768,384]{1,0:T(8,128)(2,1)S(1)}, u32[]{:S(2)}, u32[]{:S(2)}) %collective-permute-start.26) | collective-permute-done | bytes 589856 | tf_op jit(solution)/shard_map/ppermute | solution.py:1239
  139.5 9.2 %collective-permute-done.28.refs_3_ = bf16[768,384]{1,0:T(8,128)(2,1)S(1)} collective-permute-done((bf16[768,384]{1,0:T(8,128)(2,1)S(1)}, bf16[768,384]{1,0:T(8,128)(2,1)S(1)}, u32[]{:S(2)}, u32[]{:S(2)}) %collective-permute-start.28) | collective-permute-done | bytes 589856 | tf_op jit(solution)/shard_map/ppermute | solution.py:1239
  151.4 34.7 %shard_map.301 = (bf16[768,128]{1,0:T(8,128)(2,1)}, bf16[768,128]{1,0:T(8,128)(2,1)}, bf16[768,128]{1,0:T(8,128)(2,1)}, bf16[768,128]{1,0:T(8,128)(2,1)}, f32[3072,128]{1,0:T(8,128)}) custom-call(s32[3]{0:T(128)} %pad_add_fusion.scal, bf16[768,384]{1,0:T(8,128)(2,1)} %get-tuple-element.262.refs_0_, bf16[768,384]{1,0:T(8,128)(2,1)} %copy-done.25, ...), custom_call_target="tpu_custom_call" | custom-call | flops 41400000512 | bytes 4718604 | tf_op jit(solution)/shard_map/pallas_call | solution.py:69
  186.4 2.7 collective-permute-start.35
  189.1 3.3 collective-permute-start.32
  193.5 4.6 collective-permute-done.32.refs_1_
  198.0 4.3 collective-permute-done.34.refs_3_
  203.8 23.6 %shard_map.302 = (bf16[768,512]{1,0:T(8,128)(2,1)}, f32[768,512]{1,0:T(8,128)}, bf16[768,128]{1,0:T(8,128)(2,1)}, bf16[768,128]{1,0:T(8,128)(2,1)}, bf16[768,128...) custom-call(s32[3]{0:T(128)} %pad_add_fusion.scal, ...), custom_call_target="tpu_custom_call" | custom-call | flops 23000000512 | bytes 18878476 | tf_op jit(solution)/shard_map/pallas_call | solution.py:69
  227.4 1.8 collective-permute-start.37
  229.6 10.3 %shard_map.303 = (bf16[16,288,256]{2,1,0:T(8,128)(2,1)}, bf16[16,288,256]{2,1,0:T(8,128)(2,1)}) custom-call(s32[3]{0:T(128)} %pad_add_fusion.scal, bf16[768,512]{1,0:T(8,128)(2,1)} %get-tuple-element.291.att_s, bf16[768,512]{1,0:T(8,128)(2,1)} %get-tuple-element.292.y5_s, bf16[768,2048]{1,0:T(8,128)(2,1)} %get-tuple-element.293.inner_s, ...), custom_call_target="tpu_custom_call" | custom-call | flops 11500000256 | bytes 14942220 | tf_op jit(solution)/shard_map/pallas_call | solution.py:69
  240.8 58.2 %shard_map.304 = (bf16[768,384]{1,0:T(8,128)(2,1)}, bf16[768,384]{1,0:T(8,128)(2,1)}, bf16[768,384]{1,0:T(8,128)(2,1)}, bf16[768,384]{1,0:T(8,128)(2,1)}) custom-call(s32[3]{0:T(128)} %pad_add_fusion.scal, bf16[768,384]{1,0:T(8,128)(2,1)} %get-tuple-element.262.refs_0_, bf16[768,384]{1,0:T(8,128)(2,1)} %copy-done.25, bf16[768,384]{1,0:T(8,128)(2,1)} %copy-done.26, ...), custom_call_target="tpu_custom_call" | custom-call | flops 66700001280 | bytes 7864332 | tf_op jit(solution)/shard_map/pallas_call | solution.py:69
  299.8 2.3 collective-permute-start.44
  302.7 1.5 collective-permute-start.43
  304.2 24.1 %collective-permute-done.44 = bf16[8,288,256]{2,1,0:T(8,128)(2,1)S(1)} collective-permute-done((bf16[8,288,256]{2,1,0:T(8,128)(2,1)S(1)}, bf16[8,288,256]{2,1,0:T(8,128)(2,1)S(1)}, u32[]{:S(2)}, u32[]{:S(2)}) %collective-permute-start.44) | collective-permute-done | bytes 1179680 | tf_op jit(solution)/shard_map/ppermute | solution.py:1076
  328.8 1.6 collective-permute-start.47
  330.4 9.2 %shard_map.305 = (f32[768,512]{1,0:T(8,128)}, bf16[768,256]{1,0:T(8,128)(2,1)}, bf16[768,1536]{1,0:T(8,128)(2,1)}, f32[1,512]{1,0:T(1,128)}) custom-call(s32[3]{0:T(128)} %pad_add_fusion.scal, bf16[768,384]{1,0:T(8,128)(2,1)} %get-tuple-element.314.refs_0_, bf16[768,384]{1,0:T(8,128)(2,1)} %copy-done.32, bf16[768,384]{1,0:T(8,128)(2,1)} %copy-done.34, ...), custom_call_target="tpu_custom_call" | custom-call | flops 6899999744 | bytes 11407372 | tf_op jit(solution)/shard_map/pallas_call | solution.py:69
  340.3 1.3 collective-permute-start.46
  341.5 4.5 collective-permute-start.45
  346.1 6.8 %shard_map.306 = (bf16[16,160,256]{2,1,0:T(8,128)(2,1)}, bf16[16,160,256]{2,1,0:T(8,128)(2,1)}) custom-call(s32[3]{0:T(128)} %pad_add_fusion.scal, bf16[768,512]{1,0:T(8,128)(2,1)} %get-tuple-element.322.y4_ref, bf16[768,1536]{1,0:T(8,128)(2,1)} %get-tuple-element.323.dqkv_s, bf16[768,2048]{1,0:T(8,128)(2,1)} %get-tuple-element.324.spread_ref, ...), custom_call_target="tpu_custom_call" | custom-call | flops 3449999872 | bytes 9306124 | tf_op jit(solution)/shard_map/pallas_call | solution.py:69
  353.1 1.3 collective-permute-start.48
  355.3 1.3 collective-permute-start.49
  356.7 1.8 collective-permute-start.52
  358.4 1.9 collective-permute-start.51
  360.3 32.5 %shard_map.307 = (bf16[800,2048]{1,0:T(8,128)(2,1)}, bf16[768,768]{1,0:T(8,128)(2,1)}, f32[9,2048]{1,0:T(8,128)}, f32[1,2048]{1,0:T(1,128)}) custom-call(s32[3]{0:T(128)} %pad_add_fusion.scal, bf16[16,256]{1,0:T(8,128)(2,1)} %copy-done.47, bf16[768,256]{1,0:T(8,128)(2,1)} %get-tuple-element.321.db_ref, bf16[16,256]{1,0:T(8,128)(2,1)} %copy-done.46, ...), custom_call_target="tpu_custom_call" | custom-call | flops 50600001536 | bytes 16728076 | tf_op jit(solution)/shard_map/pallas_call | solution.py:69
  393.6 6.7 %shard_map.308 = (bf16[16,176,256]{2,1,0:T(8,128)(2,1)}, bf16[16,176,256]{2,1,0:T(8,128)(2,1)}) custom-call(s32[3]{0:T(128)} %pad_add_fusion.scal, bf16[800,2048]{1,0:T(8,128)(2,1)} %get-tuple-element.357.dl, bf16[768,768]{1,0:T(8,128)(2,1)} %get-tuple-element.342.st, bf16[800,512]{1,0:T(8,128)(2,1)} %get-tuple-element.231.y2_ref), custom_call_target="tpu_custom_call" | custom-call | flops 3449999872 | bytes 8159244 | tf_op jit(solution)/shard_map/pallas_call | solution.py:69
  400.9 9.0 %shard_map.309 = (bf16[384,512]{1,0:T(8,128)(2,1)}, bf16[384,512]{1,0:T(8,128)(2,1)}, bf16[384,1024]{1,0:T(8,128)(2,1)}, f32[1,512]{1,0:T(1,128)}, f32[1,512]{1,0:T(1,128)}) custom-call(s32[3]{0:T(128)} %pad_add_fusion.scal, bf16[800,2048]{1,0:T(8,128)(2,1)} %get-tuple-element.357.dl, bf16[768,768]{1,0:T(8,128)(2,1)} %get-tuple-element.342.st, ...), custom_call_target="tpu_custom_call" | custom-call | flops 5750000128 | bytes 17276940 | tf_op jit(solution)/shard_map/pallas_call | solution.py:69
  412.0 1.6 collective-permute-start.57
  413.6 2.1 collective-permute-start.56
  415.7 9.0 %shard_map.310 = (bf16[384,512]{1,0:T(8,128)(2,1)}, bf16[384,512]{1,0:T(8,128)(2,1)}, bf16[384,1024]{1,0:T(8,128)(2,1)}, f32[1,512]{1,0:T(1,128)}, f32[1,512]{1,0:T(1,128)}) custom-call(s32[3]{0:T(128)} %pad_add_fusion.scal, bf16[800,2048]{1,0:T(8,128)(2,1)} %get-tuple-element.357.dl, bf16[768,768]{1,0:T(8,128)(2,1)} %get-tuple-element.342.st, ...), custom_call_target="tpu_custom_call" | custom-call | flops 5750000128 | bytes 17276940 | tf_op jit(solution)/shard_map/pallas_call | solution.py:69
  424.8 1.8 collective-permute-start.58
  426.6 4.7 shard_map.311
  432.6 6.0 %collective-permute-start.59 = (bf16[16,80,256]{2,1,0:T(8,128)(2,1)S(1)}, bf16[16,80,256]{2,1,0:T(8,128)(2,1)S(1)}, u32[]{:S(2)}, u32[]{:S(2)}) collective-permute-start(bf16[16,80,256]{2,1,0:T(8,128)(2,1)S(1)} %copy-done.22), channel_id=1, source_target_pairs={{0,1},{1,0},{2,3},{3,2},{4,5},{5,4},{6,7},{7,6},{8,9},{9,8},{10,11... | collective-permute-start | bytes 1966088 | tf_op jit(solution)/shard_map/ppermute | solution.py:1076
  441.1 7.3 %collective-permute-start.62 = (bf16[4,80,256]{2,1,0:T(8,128)(2,1)S(1)}, bf16[4,80,256]{2,1,0:T(8,128)(2,1)S(1)}, u32[]{:S(2)}, u32[]{:S(2)}) collective-permute-start(bf16[4,80,256]{2,1,0:T(8,128)(2,1)S(1)} %get-tuple-element.401), channel_id=1, source_target_pairs={{0,6},{1,7},{2,4},{3,5},{4,2},{5,3},{6,0},{7,1},{8,14},{9,15},{10,... | collective-permute-start | bytes 491528 | tf_op jit(solution)/shard_map/ppermute | solution.py:1076
  448.6 2.7 collective-permute-done.61
  451.4 16.7 %collective-permute-done.60 = bf16[704,256]{1,0:T(8,128)(2,1)S(1)} collective-permute-done((bf16[704,256]{1,0:T(8,128)(2,1)S(1)}, bf16[704,256]{1,0:T(8,128)(2,1)S(1)}, u32[]{:S(2)}, u32[]{:S(2)}) %collective-permute-start.60) | collective-permute-done | bytes 360480 | tf_op jit(solution)/shard_map/ppermute | solution.py:1076
  469.2 2.8 collective-permute-start.65
  472.5 1.4 maximum_convert_fusion
  473.9 6.3 %collective-permute-done.64 = bf16[416,256]{1,0:T(8,128)(2,1)S(1)} collective-permute-done((bf16[416,256]{1,0:T(8,128)(2,1)S(1)}, bf16[416,256]{1,0:T(8,128)(2,1)S(1)}, u32[]{:S(2)}, u32[]{:S(2)}) %collective-permute-start.64) | collective-permute-done | bytes 213024 | tf_op jit(solution)/shard_map/ppermute | solution.py:1076
  480.2 10.3 %collective-permute-done.65 = bf16[416,256]{1,0:T(8,128)(2,1)S(1)} collective-permute-done((bf16[416,256]{1,0:T(8,128)(2,1)S(1)}, bf16[416,256]{1,0:T(8,128)(2,1)S(1)}, u32[]{:S(2)}, u32[]{:S(2)}) %collective-permute-start.65) | collective-permute-done | bytes 213024 | tf_op jit(solution)/shard_map/ppermute | solution.py:1076
  (294 shorter events, 40.2 us)
Async XLA Ops:
  6.4 9.7 %collective-permute-start.2 = (bf16[256,256]{1,0:T(8,128)(2,1)}, bf16[256,256]{1,0:T(8,128)(2,1)S(1)}, u32[]{:S(2)}, u32[]{:S(2)}) collective-permute-start(bf16[256,256]{1,0:T(8,128)(2,1)} %get-tuple-element.208), channel_id=1, source_target_pairs={{0,24},{1,25},{2,26},{3,27},{4,28},{5,29},{6,30},{7,31},{8,16},{9,... | collective-permute-start | bytes 393224 | tf_op jit(solution)/shard_map/ppermute | solution.py:1076
  11.4 12.5 %collective-permute-start.1 = (bf16[256,256]{1,0:T(8,128)(2,1)}, bf16[256,256]{1,0:T(8,128)(2,1)S(1)}, u32[]{:S(2)}, u32[]{:S(2)}) collective-permute-start(bf16[256,256]{1,0:T(8,128)(2,1)} %get-tuple-element.208), channel_id=1, source_target_pairs={{0,16},{1,17},{2,18},{3,19},{4,20},{5,21},{6,22},{7,23},{8,24},{9,... | collective-permute-start | bytes 393224 | tf_op jit(solution)/shard_map/ppermute | solution.py:1076
  11.4 12.5 %collective-permute-start = (bf16[256,256]{1,0:T(8,128)(2,1)}, bf16[256,256]{1,0:T(8,128)(2,1)S(1)}, u32[]{:S(2)}, u32[]{:S(2)}) collective-permute-start(bf16[256,256]{1,0:T(8,128)(2,1)} %get-tuple-element.208), channel_id=1, source_target_pairs={{0,8},{1,9},{2,10},{3,11},{4,12},{5,13},{6,14},{7,15},{8,0},{9,1},... | collective-permute-start | bytes 393224 | tf_op jit(solution)/shard_map/ppermute | solution.py:1076
  12.1 37.4 %collective-permute-start.5 = (bf16[784,512]{1,0:T(8,128)(2,1)S(1)}, bf16[784,512]{1,0:T(8,128)(2,1)S(1)}, u32[]{:S(2)}, u32[]{:S(2)}) collective-permute-start(bf16[784,512]{1,0:T(8,128)(2,1)S(1)} %pad_maximum_fusion.5), channel_id=1, source_target_pairs={{0,0},{8,4},{16,1},{24,5},{1,16},{9,20},{17,17},{25,21},{2,2},{10,... | collective-permute-start | bytes 2408456 | tf_op jit(solution)/shard_map/ppermute | solution.py:1224
  25.0 15.0 %collective-permute-start.4 = (bf16[4,128,256]{2,1,0:T(8,128)(2,1)S(1)}, bf16[4,128,256]{2,1,0:T(8,128)(2,1)S(1)}, u32[]{:S(2)}, u32[]{:S(2)}) collective-permute-start(bf16[4,128,256]{2,1,0:T(8,128)(2,1)S(1)} %get-tuple-element.409), channel_id=1, source_target_pairs={{0,2},{1,3},{2,0},{3,1},{4,6},{5,7},{6,4},{7,5},{8,10},{9,11},{10,... | collective-permute-start | bytes 786440 | tf_op jit(solution)/shard_map/ppermute | solution.py:1076
  26.3 23.0 %collective-permute-start.3 = (bf16[4,128,256]{2,1,0:T(8,128)(2,1)S(1)}, bf16[4,128,256]{2,1,0:T(8,128)(2,1)S(1)}, u32[]{:S(2)}, u32[]{:S(2)}) collective-permute-start(bf16[4,128,256]{2,1,0:T(8,128)(2,1)S(1)} %get-tuple-element.410), channel_id=1, source_target_pairs={{0,4},{1,5},{2,6},{3,7},{4,0},{5,1},{6,2},{7,3},{8,12},{9,13},{10,... | collective-permute-start | bytes 786440 | tf_op jit(solution)/shard_map/ppermute | solution.py:1076
  36.2 13.2 %collective-permute-start.7 = (bf16[16,512]{1,0:T(8,128)(2,1)S(1)}, bf16[16,512]{1,0:T(8,128)(2,1)S(1)}, u32[]{:S(2)}, u32[]{:S(2)}) collective-permute-start(bf16[16,512]{1,0:T(8,128)(2,1)S(1)} %get-tuple-element.399), channel_id=1, source_target_pairs={{8,0},{16,4},{24,1},{9,16},{17,20},{25,17},{10,2},{18,6},{26,3},{1... | collective-permute-start | bytes 49160 | tf_op jit(solution)/shard_map/ppermute | solution.py:1227
  37.5 12.1 %collective-permute-start.6 = (bf16[16,512]{1,0:T(8,128)(2,1)S(1)}, bf16[16,512]{1,0:T(8,128)(2,1)S(1)}, u32[]{:S(2)}, u32[]{:S(2)}) collective-permute-start(bf16[16,512]{1,0:T(8,128)(2,1)S(1)} %get-tuple-element.400), channel_id=1, source_target_pairs={{0,4},{8,1},{16,5},{1,20},{9,17},{17,21},{2,6},{10,3},{18,7},{3,22... | collective-permute-start | bytes 49160 | tf_op jit(solution)/shard_map/ppermute | solution.py:1227
  49.7 12.1 %collective-permute-start.12 = (bf16[160,256]{1,0:T(8,128)(2,1)S(1)}, bf16[160,256]{1,0:T(8,128)(2,1)S(1)}, u32[]{:S(2)}, u32[]{:S(2)}) collective-permute-start(bf16[160,256]{1,0:T(8,128)(2,1)S(1)} %copy-done.13), channel_id=1, source_target_pairs={{0,24},{1,25},{2,26},{3,27},{4,28},{5,29},{6,30},{7,31},{8,16},{9,... | collective-permute-start | bytes 245768 | tf_op jit(solution)/shard_map/ppermute | solution.py:1076
  52.3 9.4 %collective-permute-start.11 = (bf16[160,256]{1,0:T(8,128)(2,1)S(1)}, bf16[160,256]{1,0:T(8,128)(2,1)S(1)}, u32[]{:S(2)}, u32[]{:S(2)}) collective-permute-start(bf16[160,256]{1,0:T(8,128)(2,1)S(1)} %copy-done.13), channel_id=1, source_target_pairs={{0,16},{1,17},{2,18},{3,19},{4,20},{5,21},{6,22},{7,23},{8,24},{9,... | collective-permute-start | bytes 245768 | tf_op jit(solution)/shard_map/ppermute | solution.py:1076
  52.4 9.4 %collective-permute-start.10 = (bf16[160,256]{1,0:T(8,128)(2,1)S(1)}, bf16[160,256]{1,0:T(8,128)(2,1)S(1)}, u32[]{:S(2)}, u32[]{:S(2)}) collective-permute-start(bf16[160,256]{1,0:T(8,128)(2,1)S(1)} %copy-done.13), channel_id=1, source_target_pairs={{0,8},{1,9},{2,10},{3,11},{4,12},{5,13},{6,14},{7,15},{8,0},{9,1},... | collective-permute-start | bytes 245768 | tf_op jit(solution)/shard_map/ppermute | solution.py:1076
  54.1 11.9 %collective-permute-start.8 = (bf16[8,128,256]{2,1,0:T(8,128)(2,1)S(1)}, bf16[8,128,256]{2,1,0:T(8,128)(2,1)S(1)}, u32[]{:S(2)}, u32[]{:S(2)}) collective-permute-start(bf16[8,128,256]{2,1,0:T(8,128)(2,1)S(1)} %pad_maximum_fusion.13), channel_id=1, source_target_pairs={{0,2},{1,3},{2,0},{3,1},{4,6},{5,7},{6,4},{7,5},{8,10},{9,11},{10,... | collective-permute-start | bytes 1572872 | tf_op jit(solution)/shard_map/ppermute | solution.py:1076
  55.2 12.3 %collective-permute-start.9 = (bf16[8,128,256]{2,1,0:T(8,128)(2,1)S(1)}, bf16[8,128,256]{2,1,0:T(8,128)(2,1)S(1)}, u32[]{:S(2)}, u32[]{:S(2)}) collective-permute-start(bf16[8,128,256]{2,1,0:T(8,128)(2,1)S(1)} %pad_maximum_fusion.14), channel_id=1, source_target_pairs={{0,4},{1,5},{2,6},{3,7},{4,0},{5,1},{6,2},{7,3},{8,12},{9,13},{10,... | collective-permute-start | bytes 1572872 | tf_op jit(solution)/shard_map/ppermute | solution.py:1076
  67.7 7.6 %collective-permute-start.13 = (bf16[16,128,256]{2,1,0:T(8,128)(2,1)S(1)}, bf16[16,128,256]{2,1,0:T(8,128)(2,1)S(1)}, u32[]{:S(2)}, u32[]{:S(2)}) collective-permute-start(bf16[16,128,256]{2,1,0:T(8,128)(2,1)S(1)} %pad_maximum_fusion.2.p0), channel_id=1, source_target_pairs={{0,1},{1,0},{2,3},{3,2},{4,5},{5,4},{6,7},{7,6},{8,9},{9,8},{10,11... | collective-permute-start | bytes 3145736 | tf_op jit(solution)/shard_map/ppermute | solution.py:1076
  67.8 7.5 %collective-permute-start.14 = (bf16[16,128,256]{2,1,0:T(8,128)(2,1)S(1)}, bf16[16,128,256]{2,1,0:T(8,128)(2,1)}, u32[]{:S(2)}, u32[]{:S(2)}) collective-permute-start(bf16[16,128,256]{2,1,0:T(8,128)(2,1)S(1)} %pad_maximum_fusion.3.p2), channel_id=1, source_target_pairs={{0,1},{1,0},{2,3},{3,2},{4,5},{5,4},{6,7},{7,6},{8,9},{9,8},{10,11... | collective-permute-start | bytes 3145736 | tf_op jit(solution)/shard_map/ppermute | solution.py:1076
  75.3 11.9 %collective-permute-start.17 = (bf16[8,80,256]{2,1,0:T(8,128)(2,1)S(1)}, bf16[8,80,256]{2,1,0:T(8,128)(2,1)S(1)}, u32[]{:S(2)}, u32[]{:S(2)}) collective-permute-start(bf16[8,80,256]{2,1,0:T(8,128)(2,1)S(1)} %pad_maximum_fusion.18), channel_id=1, source_target_pairs={{0,2},{1,3},{2,0},{3,1},{4,6},{5,7},{6,4},{7,5},{8,10},{9,11},{10,... | collective-permute-start | bytes 983048 | tf_op jit(solution)/shard_map/ppermute | solution.py:1076
  76.4 10.9 %collective-permute-start.18 = (bf16[8,80,256]{2,1,0:T(8,128)(2,1)S(1)}, bf16[8,80,256]{2,1,0:T(8,128)(2,1)S(1)}, u32[]{:S(2)}, u32[]{:S(2)}) collective-permute-start(bf16[8,80,256]{2,1,0:T(8,128)(2,1)S(1)} %pad_maximum_fusion.19), channel_id=1, source_target_pairs={{0,4},{1,5},{2,6},{3,7},{4,0},{5,1},{6,2},{7,3},{8,12},{9,13},{10,... | collective-permute-start | bytes 983048 | tf_op jit(solution)/shard_map/ppermute | solution.py:1076
  88.1 15.4 %collective-permute-start.23 = (bf16[288,256]{1,0:T(8,128)(2,1)S(1)}, bf16[288,256]{1,0:T(8,128)(2,1)S(1)}, u32[]{:S(2)}, u32[]{:S(2)}) collective-permute-start(bf16[288,256]{1,0:T(8,128)(2,1)S(1)} %copy-done.12), channel_id=1, source_target_pairs={{0,24},{1,25},{2,26},{3,27},{4,28},{5,29},{6,30},{7,31},{8,16},{9,... | collective-permute-start | bytes 442376 | tf_op jit(solution)/shard_map/ppermute | solution.py:1076
  90.0 13.5 %collective-permute-start.22 = (bf16[288,256]{1,0:T(8,128)(2,1)S(1)}, bf16[288,256]{1,0:T(8,128)(2,1)S(1)}, u32[]{:S(2)}, u32[]{:S(2)}) collective-permute-start(bf16[288,256]{1,0:T(8,128)(2,1)S(1)} %copy-done.12), channel_id=1, source_target_pairs={{0,16},{1,17},{2,18},{3,19},{4,20},{5,21},{6,22},{7,23},{8,24},{9,... | collective-permute-start | bytes 442376 | tf_op jit(solution)/shard_map/ppermute | solution.py:1076
  90.0 13.5 %collective-permute-start.21 = (bf16[288,256]{1,0:T(8,128)(2,1)S(1)}, bf16[288,256]{1,0:T(8,128)(2,1)S(1)}, u32[]{:S(2)}, u32[]{:S(2)}) collective-permute-start(bf16[288,256]{1,0:T(8,128)(2,1)S(1)} %copy-done.12), channel_id=1, source_target_pairs={{0,8},{1,9},{2,10},{3,11},{4,12},{5,13},{6,14},{7,15},{8,0},{9,1},... | collective-permute-start | bytes 442376 | tf_op jit(solution)/shard_map/ppermute | solution.py:1076
  92.5 11.2 %collective-permute-start.19 = (bf16[16,80,256]{2,1,0:T(8,128)(2,1)S(1)}, bf16[16,80,256]{2,1,0:T(8,128)(2,1)S(1)}, u32[]{:S(2)}, u32[]{:S(2)}) collective-permute-start(bf16[16,80,256]{2,1,0:T(8,128)(2,1)S(1)} %pad_maximum_fusion.6.p0), channel_id=1, source_target_pairs={{0,1},{1,0},{2,3},{3,2},{4,5},{5,4},{6,7},{7,6},{8,9},{9,8},{10,11... | collective-permute-start | bytes 1966088 | tf_op jit(solution)/shard_map/ppermute | solution.py:1076
  92.5 11.2 %collective-permute-start.20 = (bf16[16,80,256]{2,1,0:T(8,128)(2,1)S(1)}, bf16[16,80,256]{2,1,0:T(8,128)(2,1)S(1)}, u32[]{:S(2)}, u32[]{:S(2)}) collective-permute-start(bf16[16,80,256]{2,1,0:T(8,128)(2,1)S(1)} %pad_maximum_fusion.7.p2), channel_id=1, source_target_pairs={{0,1},{1,0},{2,3},{3,2},{4,5},{5,4},{6,7},{7,6},{8,9},{9,8},{10,11... | collective-permute-start | bytes 1966088 | tf_op jit(solution)/shard_map/ppermute | solution.py:1076
  103.7 19.1 %collective-permute-start.25 = (bf16[4,144,256]{2,1,0:T(8,128)(2,1)S(1)}, bf16[4,144,256]{2,1,0:T(8,128)(2,1)S(1)}, u32[]{:S(2)}, u32[]{:S(2)}) collective-permute-start(bf16[4,144,256]{2,1,0:T(8,128)(2,1)S(1)} %get-tuple-element.407), channel_id=1, source_target_pairs={{0,2},{1,3},{2,0},{3,1},{4,6},{5,7},{6,4},{7,5},{8,10},{9,11},{10,... | collective-permute-start | bytes 884744 | tf_op jit(solution)/shard_map/ppermute | solution.py:1076
  104.8 18.1 %collective-permute-start.24 = (bf16[4,144,256]{2,1,0:T(8,128)(2,1)S(1)}, bf16[4,144,256]{2,1,0:T(8,128)(2,1)S(1)}, u32[]{:S(2)}, u32[]{:S(2)}) collective-permute-start(bf16[4,144,256]{2,1,0:T(8,128)(2,1)S(1)} %get-tuple-element.408), channel_id=1, source_target_pairs={{0,4},{1,5},{2,6},{3,7},{4,0},{5,1},{6,2},{7,3},{8,12},{9,13},{10,... | collective-permute-start | bytes 884744 | tf_op jit(solution)/shard_map/ppermute | solution.py:1076
  123.0 16.5 %collective-permute-start.26 = (bf16[768,384]{1,0:T(8,128)(2,1)}, bf16[768,384]{1,0:T(8,128)(2,1)S(1)}, u32[]{:S(2)}, u32[]{:S(2)}) collective-permute-start(bf16[768,384]{1,0:T(8,128)(2,1)} %get-tuple-element.255), channel_id=1, source_target_pairs={{0,4},{4,0},{1,5},{5,1},{16,20},{20,16},{17,21},{21,17},{2,6},{6,2... | collective-permute-start | bytes 1769480 | tf_op jit(solution)/shard_map/ppermute | solution.py:1239
  123.9 15.7 %collective-permute-start.27 = (bf16[768,384]{1,0:T(8,128)(2,1)S(1)}, bf16[768,384]{1,0:T(8,128)(2,1)S(1)}, u32[]{:S(2)}, u32[]{:S(2)}) collective-permute-start(bf16[768,384]{1,0:T(8,128)(2,1)S(1)} %copy-done.33), channel_id=1, source_target_pairs={{0,1},{4,5},{1,0},{5,4},{16,17},{20,21},{17,16},{21,20},{2,3},{6,7... | collective-permute-start | bytes 1769480 | tf_op jit(solution)/shard_map/ppermute | solution.py:1239
  124.0 24.7 %collective-permute-start.28 = (bf16[768,384]{1,0:T(8,128)(2,1)S(1)}, bf16[768,384]{1,0:T(8,128)(2,1)S(1)}, u32[]{:S(2)}, u32[]{:S(2)}) collective-permute-start(bf16[768,384]{1,0:T(8,128)(2,1)S(1)} %copy-done.31), channel_id=1, source_target_pairs={{0,5},{4,1},{1,4},{5,0},{16,21},{20,17},{17,20},{21,16},{2,7},{6,3... | collective-permute-start | bytes 1769480 | tf_op jit(solution)/shard_map/ppermute | solution.py:1239
  148.8 37.3 %collective-permute-start.29 = (bf16[8,144,256]{2,1,0:T(8,128)(2,1)S(1)}, bf16[8,144,256]{2,1,0:T(8,128)(2,1)S(1)}, u32[]{:S(2)}, u32[]{:S(2)}) collective-permute-start(bf16[8,144,256]{2,1,0:T(8,128)(2,1)S(1)} %pad_maximum_fusion.9), channel_id=1, source_target_pairs={{0,2},{1,3},{2,0},{3,1},{4,6},{5,7},{6,4},{7,5},{8,10},{9,11},{10,... | collective-permute-start | bytes 1769480 | tf_op jit(solution)/shard_map/ppermute | solution.py:1076
  149.8 36.4 %collective-permute-start.30 = (bf16[8,144,256]{2,1,0:T(8,128)(2,1)S(1)}, bf16[8,144,256]{2,1,0:T(8,128)(2,1)S(1)}, u32[]{:S(2)}, u32[]{:S(2)}) collective-permute-start(bf16[8,144,256]{2,1,0:T(8,128)(2,1)S(1)} %pad_maximum_fusion.10), channel_id=1, source_target_pairs={{0,4},{1,5},{2,6},{3,7},{4,0},{5,1},{6,2},{7,3},{8,12},{9,13},{10,... | collective-permute-start | bytes 1769480 | tf_op jit(solution)/shard_map/ppermute | solution.py:1076
  150.7 35.7 %collective-permute-start.31 = (bf16[768,512]{1,0:T(8,128)(2,1)S(1)}, bf16[768,512]{1,0:T(8,128)(2,1)S(1)}, u32[]{:S(2)}, u32[]{:S(2)}) collective-permute-start(bf16[768,512]{1,0:T(8,128)(2,1)S(1)} %bitcast.131), channel_id=1, source_target_pairs={{0,0},{8,4},{16,1},{24,5},{1,16},{9,20},{17,17},{25,21},{2,2},{10,... | collective-permute-start | bytes 2359304 | tf_op jit(solution)/shard_map/ppermute | solution.py:1224
  186.4 16.0 %collective-permute-start.35 = (bf16[16,144,256]{2,1,0:T(8,128)(2,1)S(1)}, bf16[16,144,256]{2,1,0:T(8,128)(2,1)S(1)}, u32[]{:S(2)}, u32[]{:S(2)}) collective-permute-start(bf16[16,144,256]{2,1,0:T(8,128)(2,1)S(1)} %pad_maximum_fusion.refs_6_), channel_id=1, source_target_pairs={{0,1},{1,0},{2,3},{3,2},{4,5},{5,4},{6,7},{7,6},{8,9},{9,8},{10,11... | collective-permute-start | bytes 3538952 | tf_op jit(solution)/shard_map/ppermute | solution.py:1076
  189.1 13.3 %collective-permute-start.36 = (bf16[16,144,256]{2,1,0:T(8,128)(2,1)S(1)}, bf16[16,144,256]{2,1,0:T(8,128)(2,1)S(1)}, u32[]{:S(2)}, u32[]{:S(2)}) collective-permute-start(bf16[16,144,256]{2,1,0:T(8,128)(2,1)S(1)} %pad_maximum_fusion.1.refs_8_), channel_id=1, source_target_pairs={{0,1},{1,0},{2,3},{3,2},{4,5},{5,4},{6,7},{7,6},{8,9},{9,8},{10,11... | collective-permute-start | bytes 3538952 | tf_op jit(solution)/shard_map/ppermute | solution.py:1076
  189.1 8.9 %collective-permute-start.32 = (bf16[768,128]{1,0:T(8,128)(2,1)S(1)}, bf16[768,128]{1,0:T(8,128)(2,1)S(1)}, u32[]{:S(2)}, u32[]{:S(2)}) collective-permute-start(bf16[768,128]{1,0:T(8,128)(2,1)S(1)} %copy-done.37), channel_id=1, source_target_pairs={{0,4},{4,0},{1,5},{5,1},{16,20},{20,16},{17,21},{21,17},{2,6},{6,2... | collective-permute-start | bytes 589832 | tf_op jit(solution)/shard_map/ppermute | solution.py:1239
  192.9 9.4 %collective-permute-start.34 = (bf16[768,128]{1,0:T(8,128)(2,1)S(1)}, bf16[768,128]{1,0:T(8,128)(2,1)S(1)}, u32[]{:S(2)}, u32[]{:S(2)}) collective-permute-start(bf16[768,128]{1,0:T(8,128)(2,1)S(1)} %copy-done.39), channel_id=1, source_target_pairs={{0,5},{4,1},{1,4},{5,0},{16,21},{20,17},{17,20},{21,16},{2,7},{6,3... | collective-permute-start | bytes 589832 | tf_op jit(solution)/shard_map/ppermute | solution.py:1239
  227.4 12.5 %collective-permute-start.37 = (bf16[768,128]{1,0:T(8,128)(2,1)}, bf16[768,128]{1,0:T(8,128)(2,1)S(1)}, u32[]{:S(2)}, u32[]{:S(2)}) collective-permute-start(bf16[768,128]{1,0:T(8,128)(2,1)} %get-tuple-element.288), channel_id=1, source_target_pairs={{0,4},{4,0},{1,5},{5,1},{16,20},{20,16},{17,21},{21,17},{2,6},{6,2... | collective-permute-start | bytes 589832 | tf_op jit(solution)/shard_map/ppermute | solution.py:1239
  229.2 10.7 %collective-permute-start.38 = (bf16[768,128]{1,0:T(8,128)(2,1)}, bf16[768,128]{1,0:T(8,128)(2,1)S(1)}, u32[]{:S(2)}, u32[]{:S(2)}) collective-permute-start(bf16[768,128]{1,0:T(8,128)(2,1)} %get-tuple-element.289), channel_id=1, source_target_pairs={{0,1},{4,5},{1,0},{5,4},{16,17},{20,21},{17,16},{21,20},{2,3},{6,7... | collective-permute-start | bytes 589832 | tf_op jit(solution)/shard_map/ppermute | solution.py:1239
  229.2 10.8 %collective-permute-start.39 = (bf16[768,128]{1,0:T(8,128)(2,1)}, bf16[768,128]{1,0:T(8,128)(2,1)S(1)}, u32[]{:S(2)}, u32[]{:S(2)}) collective-permute-start(bf16[768,128]{1,0:T(8,128)(2,1)} %get-tuple-element.290), channel_id=1, source_target_pairs={{0,5},{4,1},{1,4},{5,0},{16,21},{20,17},{17,20},{21,16},{2,7},{6,3... | collective-permute-start | bytes 589832 | tf_op jit(solution)/shard_map/ppermute | solution.py:1239
  240.0 59.0 %collective-permute-start.40 = (bf16[16,288,256]{2,1,0:T(8,128)(2,1)}, bf16[16,288,256]{2,1,0:T(8,128)(2,1)S(1)}, u32[]{:S(2)}, u32[]{:S(2)}) collective-permute-start(bf16[16,288,256]{2,1,0:T(8,128)(2,1)} %get-tuple-element.308), channel_id=1, source_target_pairs={{0,1},{1,0},{2,3},{3,2},{4,5},{5,4},{6,7},{7,6},{8,9},{9,8},{10,11... | collective-permute-start | bytes 7077896 | tf_op jit(solution)/shard_map/ppermute | solution.py:1076
  299.8 28.5 %collective-permute-start.44 = (bf16[8,288,256]{2,1,0:T(8,128)(2,1)S(1)}, bf16[8,288,256]{2,1,0:T(8,128)(2,1)S(1)}, u32[]{:S(2)}, u32[]{:S(2)}) collective-permute-start(bf16[8,288,256]{2,1,0:T(8,128)(2,1)S(1)} %slice.314), channel_id=1, source_target_pairs={{0,2},{1,3},{2,0},{3,1},{4,6},{5,7},{6,4},{7,5},{8,10},{9,11},{10,... | collective-permute-start | bytes 3538952 | tf_op jit(solution)/shard_map/ppermute | solution.py:1076
  302.0 26.6 %collective-permute-start.41 = (bf16[768,384]{1,0:T(8,128)(2,1)S(1)}, bf16[768,384]{1,0:T(8,128)(2,1)S(1)}, u32[]{:S(2)}, u32[]{:S(2)}) collective-permute-start(bf16[768,384]{1,0:T(8,128)(2,1)S(1)} %copy-done.30), channel_id=1, source_target_pairs={{0,4},{4,0},{1,5},{5,1},{16,20},{20,16},{17,21},{21,17},{2,6},{6,2... | collective-permute-start | bytes 1769480 | tf_op jit(solution)/shard_map/ppermute | solution.py:1239
  302.7 26.0 %collective-permute-start.42 = (bf16[768,384]{1,0:T(8,128)(2,1)S(1)}, bf16[768,384]{1,0:T(8,128)(2,1)S(1)}, u32[]{:S(2)}, u32[]{:S(2)}) collective-permute-start(bf16[768,384]{1,0:T(8,128)(2,1)S(1)} %copy-done.29), channel_id=1, source_target_pairs={{0,1},{4,5},{1,0},{5,4},{16,17},{20,21},{17,16},{21,20},{2,3},{6,7... | collective-permute-start | bytes 1769480 | tf_op jit(solution)/shard_map/ppermute | solution.py:1239
  302.7 26.0 %collective-permute-start.43 = (bf16[768,384]{1,0:T(8,128)(2,1)S(1)}, bf16[768,384]{1,0:T(8,128)(2,1)S(1)}, u32[]{:S(2)}, u32[]{:S(2)}) collective-permute-start(bf16[768,384]{1,0:T(8,128)(2,1)S(1)} %copy-done.28), channel_id=1, source_target_pairs={{0,5},{4,1},{1,4},{5,0},{16,21},{20,17},{17,20},{21,16},{2,7},{6,3... | collective-permute-start | bytes 1769480 | tf_op jit(solution)/shard_map/ppermute | solution.py:1239
  328.8 24.1 %collective-permute-start.47 = (bf16[4,288,256]{2,1,0:T(8,128)(2,1)S(1)}, bf16[4,288,256]{2,1,0:T(8,128)(2,1)S(1)}, u32[]{:S(2)}, u32[]{:S(2)}) collective-permute-start(bf16[4,288,256]{2,1,0:T(8,128)(2,1)S(1)} %slice.318), channel_id=1, source_target_pairs={{0,4},{1,5},{2,6},{3,7},{4,0},{5,1},{6,2},{7,3},{8,12},{9,13},{10,... | collective-permute-start | bytes 1769480 | tf_op jit(solution)/shard_map/ppermute | solution.py:1076
  340.3 12.8 %collective-permute-start.46 = (bf16[16,256]{1,0:T(8,128)(2,1)S(1)}, bf16[16,256]{1,0:T(8,128)(2,1)S(1)}, u32[]{:S(2)}, u32[]{:S(2)}) collective-permute-start(bf16[16,256]{1,0:T(8,128)(2,1)S(1)} %get-tuple-element.428), channel_id=1, source_target_pairs={{4,0},{1,4},{5,1},{20,16},{17,20},{21,17},{6,2},{3,6},{7,3},{22,18... | collective-permute-start | bytes 24584 | tf_op jit(solution)/shard_map/ppermute | solution.py:1235
  341.5 11.5 %collective-permute-start.45 = (bf16[16,256]{1,0:T(8,128)(2,1)S(1)}, bf16[16,256]{1,0:T(8,128)(2,1)S(1)}, u32[]{:S(2)}, u32[]{:S(2)}) collective-permute-start(bf16[16,256]{1,0:T(8,128)(2,1)S(1)} %get-tuple-element.429), channel_id=1, source_target_pairs={{0,4},{4,1},{1,5},{16,20},{20,17},{17,21},{2,6},{6,3},{3,7},{18,22... | collective-permute-start | bytes 24584 | tf_op jit(solution)/shard_map/ppermute | solution.py:1235
  353.1 39.8 %collective-permute-start.48 = (bf16[288,256]{1,0:T(8,128)(2,1)S(1)}, bf16[288,256]{1,0:T(8,128)(2,1)S(1)}, u32[]{:S(2)}, u32[]{:S(2)}) collective-permute-start(bf16[288,256]{1,0:T(8,128)(2,1)S(1)} %get-tuple-element.404), channel_id=1, source_target_pairs={{0,8},{1,9},{2,10},{3,11},{4,12},{5,13},{6,14},{7,15},{8,0},{9,1},... | collective-permute-start | bytes 442376 | tf_op jit(solution)/shard_map/ppermute | solution.py:1076
  354.4 38.5 %collective-permute-start.50 = (bf16[288,256]{1,0:T(8,128)(2,1)S(1)}, bf16[288,256]{1,0:T(8,128)(2,1)S(1)}, u32[]{:S(2)}, u32[]{:S(2)}) collective-permute-start(bf16[288,256]{1,0:T(8,128)(2,1)S(1)} %get-tuple-element.405), channel_id=1, source_target_pairs={{0,24},{1,25},{2,26},{3,27},{4,28},{5,29},{6,30},{7,31},{8,16},{9,... | collective-permute-start | bytes 442376 | tf_op jit(solution)/shard_map/ppermute | solution.py:1076
  355.3 37.6 %collective-permute-start.49 = (bf16[288,256]{1,0:T(8,128)(2,1)S(1)}, bf16[288,256]{1,0:T(8,128)(2,1)S(1)}, u32[]{:S(2)}, u32[]{:S(2)}) collective-permute-start(bf16[288,256]{1,0:T(8,128)(2,1)S(1)} %get-tuple-element.406), channel_id=1, source_target_pairs={{0,16},{1,17},{2,18},{3,19},{4,20},{5,21},{6,22},{7,23},{8,24},{9,... | collective-permute-start | bytes 442376 | tf_op jit(solution)/shard_map/ppermute | solution.py:1076
  356.7 36.9 %collective-permute-start.52 = (bf16[768,512]{1,0:T(8,128)(2,1)}, bf16[768,512]{1,0:T(8,128)(2,1)S(1)}, u32[]{:S(2)}, u32[]{:S(2)}) collective-permute-start(bf16[768,512]{1,0:T(8,128)(2,1)} %get-tuple-element.339), channel_id=1, source_target_pairs={{0,0},{4,8},{1,16},{5,24},{16,1},{20,9},{17,17},{21,25},{2,2},{6,1... | collective-permute-start | bytes 2359304 | tf_op jit(solution)/shard_map/ppermute | solution.py:1232
  358.4 34.6 %collective-permute-start.51 = (bf16[16,160,256]{2,1,0:T(8,128)(2,1)}, bf16[16,160,256]{2,1,0:T(8,128)(2,1)S(1)}, u32[]{:S(2)}, u32[]{:S(2)}) collective-permute-start(bf16[16,160,256]{2,1,0:T(8,128)(2,1)} %get-tuple-element.338), channel_id=1, source_target_pairs={{0,1},{1,0},{2,3},{3,2},{4,5},{5,4},{6,7},{7,6},{8,9},{9,8},{10,11... | collective-permute-start | bytes 3932168 | tf_op jit(solution)/shard_map/ppermute | solution.py:1076
  400.3 10.6 %collective-permute-start.55 = (bf16[16,176,256]{2,1,0:T(8,128)(2,1)}, bf16[16,176,256]{2,1,0:T(8,128)(2,1)S(1)}, u32[]{:S(2)}, u32[]{:S(2)}) collective-permute-start(bf16[16,176,256]{2,1,0:T(8,128)(2,1)} %get-tuple-element.356), channel_id=1, source_target_pairs={{0,1},{1,0},{2,3},{3,2},{4,5},{5,4},{6,7},{7,6},{8,9},{9,8},{10,11... | collective-permute-start | bytes 4325384 | tf_op jit(solution)/shard_map/ppermute | solution.py:1076
  400.3 10.3 %collective-permute-start.54 = (bf16[8,80,256]{2,1,0:T(8,128)(2,1)S(1)}, bf16[8,80,256]{2,1,0:T(8,128)(2,1)S(1)}, u32[]{:S(2)}, u32[]{:S(2)}) collective-permute-start(bf16[8,80,256]{2,1,0:T(8,128)(2,1)S(1)} %slice.328), channel_id=1, source_target_pairs={{0,4},{1,5},{2,6},{3,7},{4,0},{5,1},{6,2},{7,3},{8,12},{9,13},{10,... | collective-permute-start | bytes 983048 | tf_op jit(solution)/shard_map/ppermute | solution.py:1076
  400.6 10.1 %collective-permute-start.53 = (bf16[8,80,256]{2,1,0:T(8,128)(2,1)S(1)}, bf16[8,80,256]{2,1,0:T(8,128)(2,1)S(1)}, u32[]{:S(2)}, u32[]{:S(2)}) collective-permute-start(bf16[8,80,256]{2,1,0:T(8,128)(2,1)S(1)} %slice.326), channel_id=1, source_target_pairs={{0,2},{1,3},{2,0},{3,1},{4,6},{5,7},{6,4},{7,5},{8,10},{9,11},{10,... | collective-permute-start | bytes 983048 | tf_op jit(solution)/shard_map/ppermute | solution.py:1076
  412.0 19.4 %collective-permute-start.57 = (bf16[960,256]{1,0:T(8,128)(2,1)S(1)}, bf16[960,256]{1,0:T(8,128)(2,1)S(1)}, u32[]{:S(2)}, u32[]{:S(2)}) collective-permute-start(bf16[960,256]{1,0:T(8,128)(2,1)S(1)} %pad_maximum_fusion.15), channel_id=1, source_target_pairs={{0,4},{1,5},{2,6},{3,7},{4,0},{5,1},{6,2},{7,3},{8,12},{9,13},{10,... | collective-permute-start | bytes 1474568 | tf_op jit(solution)/shard_map/ppermute | solution.py:1076
  413.6 17.9 %collective-permute-start.56 = (bf16[1088,256]{1,0:T(8,128)(2,1)S(1)}, bf16[1088,256]{1,0:T(8,128)(2,1)S(1)}, u32[]{:S(2)}, u32[]{:S(2)}) collective-permute-start(bf16[1088,256]{1,0:T(8,128)(2,1)S(1)} %pad_maximum_fusion.11), channel_id=1, source_target_pairs={{0,2},{1,3},{2,0},{3,1},{4,6},{5,7},{6,4},{7,5},{8,10},{9,11},{10,... | collective-permute-start | bytes 1671176 | tf_op jit(solution)/shard_map/ppermute | solution.py:1076
  424.8 7.8 %collective-permute-start.58 = (bf16[384,512]{1,0:T(8,128)(2,1)}, bf16[384,512]{1,0:T(8,128)(2,1)S(1)}, u32[]{:S(2)}, u32[]{:S(2)}) collective-permute-start(bf16[384,512]{1,0:T(8,128)(2,1)} %get-tuple-element.377), channel_id=1, source_target_pairs={{0,0},{4,8},{1,16},{5,24},{16,1},{20,9},{17,17},{21,25},{2,2},{6,1... | collective-permute-start | bytes 1179656 | tf_op jit(solution)/shard_map/ppermute | solution.py:1232
  432.6 7.8 %collective-permute-start.59 = (bf16[16,80,256]{2,1,0:T(8,128)(2,1)S(1)}, bf16[16,80,256]{2,1,0:T(8,128)(2,1)S(1)}, u32[]{:S(2)}, u32[]{:S(2)}) collective-permute-start(bf16[16,80,256]{2,1,0:T(8,128)(2,1)S(1)} %copy-done.22), channel_id=1, source_target_pairs={{0,1},{1,0},{2,3},{3,2},{4,5},{5,4},{6,7},{7,6},{8,9},{9,8},{10,11... | collective-permute-start | bytes 1966088 | tf_op jit(solution)/shard_map/ppermute | solution.py:1076
  438.7 29.5 %collective-permute-start.63 = (bf16[384,512]{1,0:T(8,128)(2,1)S(1)}, bf16[384,512]{1,0:T(8,128)(2,1)S(1)}, u32[]{:S(2)}, u32[]{:S(2)}) collective-permute-start(bf16[384,512]{1,0:T(8,128)(2,1)S(1)} %copy-done.36), channel_id=1, source_target_pairs={{0,0},{4,8},{1,16},{5,24},{16,1},{20,9},{17,17},{21,25},{2,2},{6,1... | collective-permute-start | bytes 1179656 | tf_op jit(solution)/shard_map/ppermute | solution.py:1232
  440.7 10.6 %collective-permute-start.61 = (bf16[640,256]{1,0:T(8,128)(2,1)S(1)}, bf16[640,256]{1,0:T(8,128)(2,1)S(1)}, u32[]{:S(2)}, u32[]{:S(2)}) collective-permute-start(bf16[640,256]{1,0:T(8,128)(2,1)S(1)} %pad_maximum_fusion.20), channel_id=1, source_target_pairs={{0,2},{1,3},{2,0},{3,1},{4,6},{5,7},{6,4},{7,5},{8,10},{9,11},{10,... | collective-permute-start | bytes 983048 | tf_op jit(solution)/shard_map/ppermute | solution.py:1076
  441.1 27.0 %collective-permute-start.62 = (bf16[4,80,256]{2,1,0:T(8,128)(2,1)S(1)}, bf16[4,80,256]{2,1,0:T(8,128)(2,1)S(1)}, u32[]{:S(2)}, u32[]{:S(2)}) collective-permute-start(bf16[4,80,256]{2,1,0:T(8,128)(2,1)S(1)} %get-tuple-element.401), channel_id=1, source_target_pairs={{0,6},{1,7},{2,4},{3,5},{4,2},{5,3},{6,0},{7,1},{8,14},{9,15},{10,... | collective-permute-start | bytes 491528 | tf_op jit(solution)/shard_map/ppermute | solution.py:1076
  448.5 19.6 %collective-permute-start.60 = (bf16[704,256]{1,0:T(8,128)(2,1)S(1)}, bf16[704,256]{1,0:T(8,128)(2,1)S(1)}, u32[]{:S(2)}, u32[]{:S(2)}) collective-permute-start(bf16[704,256]{1,0:T(8,128)(2,1)S(1)} %pad_maximum_fusion.16), channel_id=1, source_target_pairs={{0,4},{1,5},{2,6},{3,7},{4,0},{5,1},{6,2},{7,3},{8,12},{9,13},{10,... | collective-permute-start | bytes 1081352 | tf_op jit(solution)/shard_map/ppermute | solution.py:1076
  468.4 11.8 %collective-permute-start.64 = (bf16[416,256]{1,0:T(8,128)(2,1)S(1)}, bf16[416,256]{1,0:T(8,128)(2,1)S(1)}, u32[]{:S(2)}, u32[]{:S(2)}) collective-permute-start(bf16[416,256]{1,0:T(8,128)(2,1)S(1)} %get-tuple-element.396), channel_id=1, source_target_pairs={{0,8},{1,9},{2,10},{3,11},{4,12},{5,13},{6,14},{7,15},{8,0},{9,1},... | collective-permute-start | bytes 638984 | tf_op jit(solution)/shard_map/ppermute | solution.py:1076
  469.2 11.0 %collective-permute-start.66 = (bf16[416,256]{1,0:T(8,128)(2,1)S(1)}, bf16[416,256]{1,0:T(8,128)(2,1)S(1)}, u32[]{:S(2)}, u32[]{:S(2)}) collective-permute-start(bf16[416,256]{1,0:T(8,128)(2,1)S(1)} %get-tuple-element.397), channel_id=1, source_target_pairs={{0,24},{1,25},{2,26},{3,27},{4,28},{5,29},{6,30},{7,31},{8,16},{9,... | collective-permute-start | bytes 638984 | tf_op jit(solution)/shard_map/ppermute | solution.py:1076
  469.2 21.3 %collective-permute-start.65 = (bf16[416,256]{1,0:T(8,128)(2,1)S(1)}, bf16[416,256]{1,0:T(8,128)(2,1)S(1)}, u32[]{:S(2)}, u32[]{:S(2)}) collective-permute-start(bf16[416,256]{1,0:T(8,128)(2,1)S(1)} %get-tuple-element.398), channel_id=1, source_target_pairs={{0,16},{1,17},{2,18},{3,19},{4,20},{5,21},{6,22},{7,23},{8,24},{9,... | collective-permute-start | bytes 638984 | tf_op jit(solution)/shard_map/ppermute | solution.py:1076
  (53 other events, 405.7 us)

commit v7 on v6

--- a/solution.py
+++ b/solution.py
@@ -320,7 +320,7 @@
 
 def front1(scal, x, pieces, ties=()):
     rows = x.shape[0]
-    tile = 160
+    tile = 400
     return call(
         front1_kernel,
         [(scal, "s"), (x, tile)] + [(p, None) for p in pieces],
@@ -378,7 +378,7 @@
 
 def front2(scal, y2, g3, wide, narrow, group, ties=()):
     rows = y2.shape[0]
-    tile = 160
+    tile = 400
     return call(
         functools.partial(front2_kernel, tile, group),
         [(scal, "s"), (y2, None), (g3, None), (wide, None), (narrow, None)],
@@ -457,7 +457,7 @@
 
 def front3(scal, mid, taps, h1, g4, pieces, n, share, ties=()):
     rows = mid.shape[0] - 2 * RIM
-    tile = 128
+    tile = 256
     return call(
         functools.partial(front3_kernel, tile, n, share),
         [(scal, "s")] + [(a, None) for a in (mid, taps, h1, g4, *pieces)],
@@ -528,7 +528,7 @@
 
 def middle(scal, h2, att, cot, g5, pieces, n, share, ties=()):
     rows = h2.shape[0]
-    tile = 128
+    tile = 384
     return call(
         functools.partial(middle_kernel, n, share),
         [(scal, "s"), (h2, tile)]
@@ -593,7 +593,7 @@
 
 def back3(scal, blocks, dh3, h2, g4, qkv_w, n, share, ties=()):
     rows = h2.shape[0]
-    tile = 128
+    tile = 384
     return call(
         functools.partial(back3_kernel, n, share),
         [(scal, "s")] + [(a, tile) for a in (*blocks, dh3, h2)] + [(g4, None), (qkv_w, None)],
@@ -797,7 +797,7 @@
 
 
 def back1(scal, dl, st, dh2, h1, joined, x, g1, g2, glu, wide, narrow, start, rows):
-    tile = 128
+    tile = 384
     own, ext = (tile, start), (tile, start + RIM)
     return call(
         back1_kernel,

time: 504 us -> 497 us (0.986)
  Pallas kernels: 244 us -> 236 us
    pallas_call x15, Pallas kernels: 244 us -> 236 us  [call(): pl.pallas_call(kernel, out_shape=shapes, grid=() if steps is None else (s...]
  transfers between devices with their start and end apart: 67 -> 67, of which waited for: 18 -> 19; matrix products, arithmetic and copies ran while one was open for 2% -> 2% of each run, Pallas kernels for 43% -> 42%
where the time goes in v7:
time: 497 us; the launch traced here: 488 us
  Pallas kernels  236 us (47%)
  waiting for transfers between devices  126 us (25%)
  starting transfers between devices  95.7 us (19%)
  local copies, waits for them, and re-layouts  14.6 us (3%)
  other arithmetic  11.5 us (2%)
    pallas_call x15, Pallas kernels, call(): pl.pallas_call(kernel, out_shape=shapes, grid=() if steps is None else (s...  236 us
    ppermute x46, waiting for transfers between devices, flip(): return lax.ppermute(value, AXES, [(i, i ^ mask) for i in range(self.count)])  92.7 us
    ppermute x46, starting transfers between devices, flip(): return lax.ppermute(value, AXES, [(i, i ^ mask) for i in range(self.count)])  72.5 us
    ppermute x12, waiting for transfers between devices, swap(): lax.ppermute(values[k], AXES, self.pairs(self.at, lambda g, s: self.at(g,...  32.9 us
  transfers between devices with their start and end apart: 67, of which 19 were waited for; matrix products, arithmetic and copies ran while one was open for 2% of the time, Pallas kernels for 42%

profile of v7, /device:TPU:0, one launch (start us, length us, event | category | flops | bytes accessed | tf_op | source)
XLA Modules:
  0.0 487.6 jit_solution(15845316856822907958)
XLA Ops:
  3.5 1.2 pad_maximum_fusion.5
  4.7 1.7 shard_map.297
  6.4 5.0 %collective-permute-start.2 = (bf16[256,256]{1,0:T(8,128)(2,1)}, bf16[256,256]{1,0:T(8,128)(2,1)S(1)}, u32[]{:S(2)}, u32[]{:S(2)}) collective-permute-start(bf16[256,256]{1,0:T(8,128)(2,1)} %get-tuple-element.208), channel_id=1, source_target_pairs={{0,24},{1,25},{2,26},{3,27},{4,28},{5,29},{6,30},{7,31},{8,16},{9,... | collective-permute-start | bytes 393224 | tf_op jit(solution)/shard_map/ppermute | solution.py:1076
  12.8 3.3 collective-permute-done.2
  16.1 7.9 %collective-permute-done.1 = bf16[256,256]{1,0:T(8,128)(2,1)S(1)} collective-permute-done((bf16[256,256]{1,0:T(8,128)(2,1)}, bf16[256,256]{1,0:T(8,128)(2,1)S(1)}, u32[]{:S(2)}, u32[]{:S(2)}) %collective-permute-start.1) | collective-permute-done | bytes 131104 | tf_op jit(solution)/shard_map/ppermute | solution.py:1076
  25.0 1.4 collective-permute-start.4
  26.3 9.1 %collective-permute-start.3 = (bf16[4,128,256]{2,1,0:T(8,128)(2,1)S(1)}, bf16[4,128,256]{2,1,0:T(8,128)(2,1)S(1)}, u32[]{:S(2)}, u32[]{:S(2)}) collective-permute-start(bf16[4,128,256]{2,1,0:T(8,128)(2,1)S(1)} %get-tuple-element.410), channel_id=1, source_target_pairs={{0,4},{1,5},{2,6},{3,7},{4,0},{5,1},{6,2},{7,3},{8,12},{9,13},{10,... | collective-permute-start | bytes 786440 | tf_op jit(solution)/shard_map/ppermute | solution.py:1076
  36.2 1.3 collective-permute-start.7
  37.5 1.9 collective-permute-start.6
  40.0 9.3 %collective-permute-done.3 = bf16[4,128,256]{2,1,0:T(8,128)(2,1)S(1)} collective-permute-done((bf16[4,128,256]{2,1,0:T(8,128)(2,1)S(1)}, bf16[4,128,256]{2,1,0:T(8,128)(2,1)S(1)}, u32[]{:S(2)}, u32[]{:S(2)}) %collective-permute-start.3) | collective-permute-done | bytes 262176 | tf_op jit(solution)/shard_map/ppermute | solution.py:1076
  49.7 2.7 collective-permute-start.12
  52.4 1.8 collective-permute-start.10
  54.1 1.1 collective-permute-start.8
  55.2 2.5 collective-permute-start.9
  60.5 1.2 pad_add_fusion.scal
  61.8 4.2 collective-permute-done.8
  66.2 1.4 collective-permute-done.9
  69.3 1.7 collective-permute-start.15
  71.1 3.5 collective-permute-done.16
  75.3 1.1 collective-permute-start.17
  76.4 1.7 collective-permute-start.18
  78.2 7.9 %shard_map.298 = (f32[800,512]{1,0:T(8,128)}, bf16[800,512]{1,0:T(8,128)(2,1)}, f32[800,1024]{1,0:T(8,128)}, bf16[512,1024]{1,0:T(8,128)(2,1)}, bf16[512,2048]{1...) custom-call(s32[3]{0:T(128)} %pad_add_fusion.scal, ...), custom_call_target="tpu_custom_call" | custom-call | flops 13799999488 | bytes 14770188 | tf_op jit(solution)/shard_map/pallas_call | solution.py:69
  86.9 1.9 collective-permute-start.23
  88.8 2.5 collective-permute-start.21
  91.8 10.0 %shard_map.299 = (f32[800,2048]{1,0:T(8,128)}, f32[800,256]{1,0:T(8,128)}, bf16[800,2048]{1,0:T(8,128)(2,1)}) custom-call(s32[3]{0:T(128)} %pad_add_fusion.scal, bf16[800,512]{1,0:T(8,128)(2,1)} %get-tuple-element.231.y2_ref, f32[1,2048]{1,0:T(1,128)} %get-tuple-element.232.g3.refs_4_, bf16[512,2048]{1,0:T(8,128)(2,1)} %get-tuple-element.233.wide.refs_1_, ...), custom_call_target="tpu_custom_call" | custom-call | flops 13799999488 | bytes 14360588 | tf_op jit(solution)/shard_map/pallas_call | solution.py:69
  103.4 16.6 %shard_map.300 = (bf16[768,2048]{1,0:T(8,128)(2,1)}, f32[768,512]{1,0:T(8,128)}, bf16[768,512]{1,0:T(8,128)(2,1)}, bf16[768,384]{1,0:T(8,128)(2,1)}, bf16[768,38...) custom-call(s32[3]{0:T(128)} %pad_add_fusion.scal, ...), custom_call_target="tpu_custom_call" | custom-call | flops 23000000512 | bytes 18098188 | tf_op jit(solution)/shard_map/pallas_call | solution.py:69
  121.2 1.1 collective-permute-start.28
  122.4 14.3 %collective-permute-done.26.refs_1_ = bf16[768,384]{1,0:T(8,128)(2,1)S(1)} collective-permute-done((bf16[768,384]{1,0:T(8,128)(2,1)}, bf16[768,384]{1,0:T(8,128)(2,1)S(1)}, u32[]{:S(2)}, u32[]{:S(2)}) %collective-permute-start.26) | collective-permute-done | bytes 589856 | tf_op jit(solution)/shard_map/ppermute | solution.py:1239
  136.7 9.2 %collective-permute-done.28.refs_3_ = bf16[768,384]{1,0:T(8,128)(2,1)S(1)} collective-permute-done((bf16[768,384]{1,0:T(8,128)(2,1)S(1)}, bf16[768,384]{1,0:T(8,128)(2,1)S(1)}, u32[]{:S(2)}, u32[]{:S(2)}) %collective-permute-start.28) | collective-permute-done | bytes 589856 | tf_op jit(solution)/shard_map/ppermute | solution.py:1239
  148.8 34.5 %shard_map.301 = (bf16[768,128]{1,0:T(8,128)(2,1)}, bf16[768,128]{1,0:T(8,128)(2,1)}, bf16[768,128]{1,0:T(8,128)(2,1)}, bf16[768,128]{1,0:T(8,128)(2,1)}, f32[3072,128]{1,0:T(8,128)}) custom-call(s32[3]{0:T(128)} %pad_add_fusion.scal, bf16[768,384]{1,0:T(8,128)(2,1)} %get-tuple-element.262.refs_0_, bf16[768,384]{1,0:T(8,128)(2,1)} %copy-done.25, ...), custom_call_target="tpu_custom_call" | custom-call | flops 41400000512 | bytes 4718604 | tf_op jit(solution)/shard_map/pallas_call | solution.py:69
  183.6 4.2 collective-permute-start.35
  190.2 5.5 %collective-permute-done.32.refs_1_ = bf16[768,128]{1,0:T(8,128)(2,1)S(1)} collective-permute-done((bf16[768,128]{1,0:T(8,128)(2,1)S(1)}, bf16[768,128]{1,0:T(8,128)(2,1)S(1)}, u32[]{:S(2)}, u32[]{:S(2)}) %collective-permute-start.32) | collective-permute-done | bytes 196640 | tf_op jit(solution)/shard_map/ppermute | solution.py:1239
  195.7 3.9 collective-permute-done.34.refs_3_
  201.1 24.3 %shard_map.302 = (bf16[768,512]{1,0:T(8,128)(2,1)}, f32[768,512]{1,0:T(8,128)}, bf16[768,128]{1,0:T(8,128)(2,1)}, bf16[768,128]{1,0:T(8,128)(2,1)}, bf16[768,128...) custom-call(s32[3]{0:T(128)} %pad_add_fusion.scal, ...), custom_call_target="tpu_custom_call" | custom-call | flops 23000000512 | bytes 18878476 | tf_op jit(solution)/shard_map/pallas_call | solution.py:69
  226.0 1.5 collective-permute-start.39
  227.6 10.3 %shard_map.303 = (bf16[16,288,256]{2,1,0:T(8,128)(2,1)}, bf16[16,288,256]{2,1,0:T(8,128)(2,1)}) custom-call(s32[3]{0:T(128)} %pad_add_fusion.scal, bf16[768,512]{1,0:T(8,128)(2,1)} %get-tuple-element.291.att_s, bf16[768,512]{1,0:T(8,128)(2,1)} %get-tuple-element.292.y5_s, bf16[768,2048]{1,0:T(8,128)(2,1)} %get-tuple-element.293.inner_s, ...), custom_call_target="tpu_custom_call" | custom-call | flops 11500000256 | bytes 14942220 | tf_op jit(solution)/shard_map/pallas_call | solution.py:69
  238.7 58.2 %shard_map.304 = (bf16[768,384]{1,0:T(8,128)(2,1)}, bf16[768,384]{1,0:T(8,128)(2,1)}, bf16[768,384]{1,0:T(8,128)(2,1)}, bf16[768,384]{1,0:T(8,128)(2,1)}) custom-call(s32[3]{0:T(128)} %pad_add_fusion.scal, bf16[768,384]{1,0:T(8,128)(2,1)} %get-tuple-element.262.refs_0_, bf16[768,384]{1,0:T(8,128)(2,1)} %copy-done.25, bf16[768,384]{1,0:T(8,128)(2,1)} %copy-done.26, ...), custom_call_target="tpu_custom_call" | custom-call | flops 66700001280 | bytes 7864332 | tf_op jit(solution)/shard_map/pallas_call | solution.py:69
  297.8 2.5 collective-permute-start.44
  301.0 1.4 collective-permute-start.43
  302.4 24.0 %collective-permute-done.44 = bf16[8,288,256]{2,1,0:T(8,128)(2,1)S(1)} collective-permute-done((bf16[8,288,256]{2,1,0:T(8,128)(2,1)S(1)}, bf16[8,288,256]{2,1,0:T(8,128)(2,1)S(1)}, u32[]{:S(2)}, u32[]{:S(2)}) %collective-permute-start.44) | collective-permute-done | bytes 1179680 | tf_op jit(solution)/shard_map/ppermute | solution.py:1076
  328.0 6.5 %shard_map.305 = (f32[768,512]{1,0:T(8,128)}, bf16[768,256]{1,0:T(8,128)(2,1)}, bf16[768,1536]{1,0:T(8,128)(2,1)}, f32[1,512]{1,0:T(1,128)}) custom-call(s32[3]{0:T(128)} %pad_add_fusion.scal, bf16[768,384]{1,0:T(8,128)(2,1)} %get-tuple-element.314.refs_0_, bf16[768,384]{1,0:T(8,128)(2,1)} %copy-done.32, bf16[768,384]{1,0:T(8,128)(2,1)} %copy-done.34, ...), custom_call_target="tpu_custom_call" | custom-call | flops 6899999744 | bytes 11407372 | tf_op jit(solution)/shard_map/pallas_call | solution.py:69
  335.2 1.3 collective-permute-start.46
  336.5 4.5 collective-permute-start.45
  341.1 6.8 %shard_map.306 = (bf16[16,160,256]{2,1,0:T(8,128)(2,1)}, bf16[16,160,256]{2,1,0:T(8,128)(2,1)}) custom-call(s32[3]{0:T(128)} %pad_add_fusion.scal, bf16[768,512]{1,0:T(8,128)(2,1)} %get-tuple-element.322.y4_ref, bf16[768,1536]{1,0:T(8,128)(2,1)} %get-tuple-element.323.dqkv_s, bf16[768,2048]{1,0:T(8,128)(2,1)} %get-tuple-element.324.spread_ref, ...), custom_call_target="tpu_custom_call" | custom-call | flops 3449999872 | bytes 9306124 | tf_op jit(solution)/shard_map/pallas_call | solution.py:69
  349.1 1.2 collective-permute-start.50
  350.3 1.3 collective-permute-start.49
  351.6 1.8 collective-permute-start.52
  353.4 1.9 collective-permute-start.51
  355.3 32.8 %shard_map.307 = (bf16[800,2048]{1,0:T(8,128)(2,1)}, bf16[768,768]{1,0:T(8,128)(2,1)}, f32[9,2048]{1,0:T(8,128)}, f32[1,2048]{1,0:T(1,128)}) custom-call(s32[3]{0:T(128)} %pad_add_fusion.scal, bf16[16,256]{1,0:T(8,128)(2,1)} %copy-done.47, bf16[768,256]{1,0:T(8,128)(2,1)} %get-tuple-element.321.db_ref, bf16[16,256]{1,0:T(8,128)(2,1)} %copy-done.46, ...), custom_call_target="tpu_custom_call" | custom-call | flops 50600001536 | bytes 16728076 | tf_op jit(solution)/shard_map/pallas_call | solution.py:69
  388.8 6.7 %shard_map.308 = (bf16[16,176,256]{2,1,0:T(8,128)(2,1)}, bf16[16,176,256]{2,1,0:T(8,128)(2,1)}) custom-call(s32[3]{0:T(128)} %pad_add_fusion.scal, bf16[800,2048]{1,0:T(8,128)(2,1)} %get-tuple-element.357.dl, bf16[768,768]{1,0:T(8,128)(2,1)} %get-tuple-element.342.st, bf16[800,512]{1,0:T(8,128)(2,1)} %get-tuple-element.231.y2_ref), custom_call_target="tpu_custom_call" | custom-call | flops 3449999872 | bytes 8159244 | tf_op jit(solution)/shard_map/pallas_call | solution.py:69
  396.4 7.4 %shard_map.309 = (bf16[384,512]{1,0:T(8,128)(2,1)}, bf16[384,512]{1,0:T(8,128)(2,1)}, bf16[384,1024]{1,0:T(8,128)(2,1)}, f32[1,512]{1,0:T(1,128)}, f32[1,512]{1,0:T(1,128)}) custom-call(s32[3]{0:T(128)} %pad_add_fusion.scal, bf16[800,2048]{1,0:T(8,128)(2,1)} %get-tuple-element.357.dl, bf16[768,768]{1,0:T(8,128)(2,1)} %get-tuple-element.342.st, ...), custom_call_target="tpu_custom_call" | custom-call | flops 5750000128 | bytes 17276940 | tf_op jit(solution)/shard_map/pallas_call | solution.py:69
  404.4 1.3 collective-permute-done.54
  406.7 1.6 collective-permute-start.57
  409.3 7.3 %shard_map.310 = (bf16[384,512]{1,0:T(8,128)(2,1)}, bf16[384,512]{1,0:T(8,128)(2,1)}, bf16[384,1024]{1,0:T(8,128)(2,1)}, f32[1,512]{1,0:T(1,128)}, f32[1,512]{1,0:T(1,128)}) custom-call(s32[3]{0:T(128)} %pad_add_fusion.scal, bf16[800,2048]{1,0:T(8,128)(2,1)} %get-tuple-element.357.dl, bf16[768,768]{1,0:T(8,128)(2,1)} %get-tuple-element.342.st, ...), custom_call_target="tpu_custom_call" | custom-call | flops 5750000128 | bytes 17276940 | tf_op jit(solution)/shard_map/pallas_call | solution.py:69
  416.6 1.6 collective-permute-start.58
  418.2 4.7 shard_map.311
  424.2 6.3 %collective-permute-start.59 = (bf16[16,80,256]{2,1,0:T(8,128)(2,1)S(1)}, bf16[16,80,256]{2,1,0:T(8,128)(2,1)S(1)}, u32[]{:S(2)}, u32[]{:S(2)}) collective-permute-start(bf16[16,80,256]{2,1,0:T(8,128)(2,1)S(1)} %copy-done.22), channel_id=1, source_target_pairs={{0,1},{1,0},{2,3},{3,2},{4,5},{5,4},{6,7},{7,6},{8,9},{9,8},{10,11... | collective-permute-start | bytes 1966088 | tf_op jit(solution)/shard_map/ppermute | solution.py:1076
  433.3 7.0 %collective-permute-start.62 = (bf16[4,80,256]{2,1,0:T(8,128)(2,1)S(1)}, bf16[4,80,256]{2,1,0:T(8,128)(2,1)S(1)}, u32[]{:S(2)}, u32[]{:S(2)}) collective-permute-start(bf16[4,80,256]{2,1,0:T(8,128)(2,1)S(1)} %get-tuple-element.401), channel_id=1, source_target_pairs={{0,6},{1,7},{2,4},{3,5},{4,2},{5,3},{6,0},{7,1},{8,14},{9,15},{10,... | collective-permute-start | bytes 491528 | tf_op jit(solution)/shard_map/ppermute | solution.py:1076
  440.4 2.7 collective-permute-done.61
  443.2 16.7 %collective-permute-done.60 = bf16[704,256]{1,0:T(8,128)(2,1)S(1)} collective-permute-done((bf16[704,256]{1,0:T(8,128)(2,1)S(1)}, bf16[704,256]{1,0:T(8,128)(2,1)S(1)}, u32[]{:S(2)}, u32[]{:S(2)}) %collective-permute-start.60) | collective-permute-done | bytes 360480 | tf_op jit(solution)/shard_map/ppermute | solution.py:1076
  461.0 2.7 collective-permute-start.65
  464.4 1.4 maximum_convert_fusion
  465.7 6.3 %collective-permute-done.64 = bf16[416,256]{1,0:T(8,128)(2,1)S(1)} collective-permute-done((bf16[416,256]{1,0:T(8,128)(2,1)S(1)}, bf16[416,256]{1,0:T(8,128)(2,1)S(1)}, u32[]{:S(2)}, u32[]{:S(2)}) %collective-permute-start.64) | collective-permute-done | bytes 213024 | tf_op jit(solution)/shard_map/ppermute | solution.py:1076
  472.0 10.3 %collective-permute-done.65 = bf16[416,256]{1,0:T(8,128)(2,1)S(1)} collective-permute-done((bf16[416,256]{1,0:T(8,128)(2,1)S(1)}, bf16[416,256]{1,0:T(8,128)(2,1)S(1)}, u32[]{:S(2)}, u32[]{:S(2)}) %collective-permute-start.65) | collective-permute-done | bytes 213024 | tf_op jit(solution)/shard_map/ppermute | solution.py:1076
  (294 shorter events, 42.0 us)
Async XLA Ops:
  6.4 9.7 %collective-permute-start.2 = (bf16[256,256]{1,0:T(8,128)(2,1)}, bf16[256,256]{1,0:T(8,128)(2,1)S(1)}, u32[]{:S(2)}, u32[]{:S(2)}) collective-permute-start(bf16[256,256]{1,0:T(8,128)(2,1)} %get-tuple-element.208), channel_id=1, source_target_pairs={{0,24},{1,25},{2,26},{3,27},{4,28},{5,29},{6,30},{7,31},{8,16},{9,... | collective-permute-start | bytes 393224 | tf_op jit(solution)/shard_map/ppermute | solution.py:1076
  11.4 12.5 %collective-permute-start.1 = (bf16[256,256]{1,0:T(8,128)(2,1)}, bf16[256,256]{1,0:T(8,128)(2,1)S(1)}, u32[]{:S(2)}, u32[]{:S(2)}) collective-permute-start(bf16[256,256]{1,0:T(8,128)(2,1)} %get-tuple-element.208), channel_id=1, source_target_pairs={{0,16},{1,17},{2,18},{3,19},{4,20},{5,21},{6,22},{7,23},{8,24},{9,... | collective-permute-start | bytes 393224 | tf_op jit(solution)/shard_map/ppermute | solution.py:1076
  11.4 12.5 %collective-permute-start = (bf16[256,256]{1,0:T(8,128)(2,1)}, bf16[256,256]{1,0:T(8,128)(2,1)S(1)}, u32[]{:S(2)}, u32[]{:S(2)}) collective-permute-start(bf16[256,256]{1,0:T(8,128)(2,1)} %get-tuple-element.208), channel_id=1, source_target_pairs={{0,8},{1,9},{2,10},{3,11},{4,12},{5,13},{6,14},{7,15},{8,0},{9,1},... | collective-permute-start | bytes 393224 | tf_op jit(solution)/shard_map/ppermute | solution.py:1076
  12.1 37.4 %collective-permute-start.5 = (bf16[784,512]{1,0:T(8,128)(2,1)S(1)}, bf16[784,512]{1,0:T(8,128)(2,1)S(1)}, u32[]{:S(2)}, u32[]{:S(2)}) collective-permute-start(bf16[784,512]{1,0:T(8,128)(2,1)S(1)} %pad_maximum_fusion.5), channel_id=1, source_target_pairs={{0,0},{8,4},{16,1},{24,5},{1,16},{9,20},{17,17},{25,21},{2,2},{10,... | collective-permute-start | bytes 2408456 | tf_op jit(solution)/shard_map/ppermute | solution.py:1224
  25.0 15.0 %collective-permute-start.4 = (bf16[4,128,256]{2,1,0:T(8,128)(2,1)S(1)}, bf16[4,128,256]{2,1,0:T(8,128)(2,1)S(1)}, u32[]{:S(2)}, u32[]{:S(2)}) collective-permute-start(bf16[4,128,256]{2,1,0:T(8,128)(2,1)S(1)} %get-tuple-element.409), channel_id=1, source_target_pairs={{0,2},{1,3},{2,0},{3,1},{4,6},{5,7},{6,4},{7,5},{8,10},{9,11},{10,... | collective-permute-start | bytes 786440 | tf_op jit(solution)/shard_map/ppermute | solution.py:1076
  26.3 23.0 %collective-permute-start.3 = (bf16[4,128,256]{2,1,0:T(8,128)(2,1)S(1)}, bf16[4,128,256]{2,1,0:T(8,128)(2,1)S(1)}, u32[]{:S(2)}, u32[]{:S(2)}) collective-permute-start(bf16[4,128,256]{2,1,0:T(8,128)(2,1)S(1)} %get-tuple-element.410), channel_id=1, source_target_pairs={{0,4},{1,5},{2,6},{3,7},{4,0},{5,1},{6,2},{7,3},{8,12},{9,13},{10,... | collective-permute-start | bytes 786440 | tf_op jit(solution)/shard_map/ppermute | solution.py:1076
  36.2 13.2 %collective-permute-start.7 = (bf16[16,512]{1,0:T(8,128)(2,1)S(1)}, bf16[16,512]{1,0:T(8,128)(2,1)S(1)}, u32[]{:S(2)}, u32[]{:S(2)}) collective-permute-start(bf16[16,512]{1,0:T(8,128)(2,1)S(1)} %get-tuple-element.399), channel_id=1, source_target_pairs={{8,0},{16,4},{24,1},{9,16},{17,20},{25,17},{10,2},{18,6},{26,3},{1... | collective-permute-start | bytes 49160 | tf_op jit(solution)/shard_map/ppermute | solution.py:1227
  37.5 12.1 %collective-permute-start.6 = (bf16[16,512]{1,0:T(8,128)(2,1)S(1)}, bf16[16,512]{1,0:T(8,128)(2,1)S(1)}, u32[]{:S(2)}, u32[]{:S(2)}) collective-permute-start(bf16[16,512]{1,0:T(8,128)(2,1)S(1)} %get-tuple-element.400), channel_id=1, source_target_pairs={{0,4},{8,1},{16,5},{1,20},{9,17},{17,21},{2,6},{10,3},{18,7},{3,22... | collective-permute-start | bytes 49160 | tf_op jit(solution)/shard_map/ppermute | solution.py:1227
  49.7 12.1 %collective-permute-start.12 = (bf16[160,256]{1,0:T(8,128)(2,1)S(1)}, bf16[160,256]{1,0:T(8,128)(2,1)S(1)}, u32[]{:S(2)}, u32[]{:S(2)}) collective-permute-start(bf16[160,256]{1,0:T(8,128)(2,1)S(1)} %copy-done.13), channel_id=1, source_target_pairs={{0,24},{1,25},{2,26},{3,27},{4,28},{5,29},{6,30},{7,31},{8,16},{9,... | collective-permute-start | bytes 245768 | tf_op jit(solution)/shard_map/ppermute | solution.py:1076
  52.3 9.4 %collective-permute-start.11 = (bf16[160,256]{1,0:T(8,128)(2,1)S(1)}, bf16[160,256]{1,0:T(8,128)(2,1)S(1)}, u32[]{:S(2)}, u32[]{:S(2)}) collective-permute-start(bf16[160,256]{1,0:T(8,128)(2,1)S(1)} %copy-done.13), channel_id=1, source_target_pairs={{0,16},{1,17},{2,18},{3,19},{4,20},{5,21},{6,22},{7,23},{8,24},{9,... | collective-permute-start | bytes 245768 | tf_op jit(solution)/shard_map/ppermute | solution.py:1076
  52.4 9.4 %collective-permute-start.10 = (bf16[160,256]{1,0:T(8,128)(2,1)S(1)}, bf16[160,256]{1,0:T(8,128)(2,1)S(1)}, u32[]{:S(2)}, u32[]{:S(2)}) collective-permute-start(bf16[160,256]{1,0:T(8,128)(2,1)S(1)} %copy-done.13), channel_id=1, source_target_pairs={{0,8},{1,9},{2,10},{3,11},{4,12},{5,13},{6,14},{7,15},{8,0},{9,1},... | collective-permute-start | bytes 245768 | tf_op jit(solution)/shard_map/ppermute | solution.py:1076
  54.1 11.9 %collective-permute-start.8 = (bf16[8,128,256]{2,1,0:T(8,128)(2,1)S(1)}, bf16[8,128,256]{2,1,0:T(8,128)(2,1)S(1)}, u32[]{:S(2)}, u32[]{:S(2)}) collective-permute-start(bf16[8,128,256]{2,1,0:T(8,128)(2,1)S(1)} %pad_maximum_fusion.13), channel_id=1, source_target_pairs={{0,2},{1,3},{2,0},{3,1},{4,6},{5,7},{6,4},{7,5},{8,10},{9,11},{10,... | collective-permute-start | bytes 1572872 | tf_op jit(solution)/shard_map/ppermute | solution.py:1076
  55.2 12.3 %collective-permute-start.9 = (bf16[8,128,256]{2,1,0:T(8,128)(2,1)S(1)}, bf16[8,128,256]{2,1,0:T(8,128)(2,1)S(1)}, u32[]{:S(2)}, u32[]{:S(2)}) collective-permute-start(bf16[8,128,256]{2,1,0:T(8,128)(2,1)S(1)} %pad_maximum_fusion.14), channel_id=1, source_target_pairs={{0,4},{1,5},{2,6},{3,7},{4,0},{5,1},{6,2},{7,3},{8,12},{9,13},{10,... | collective-permute-start | bytes 1572872 | tf_op jit(solution)/shard_map/ppermute | solution.py:1076
  67.7 7.6 %collective-permute-start.13 = (bf16[16,128,256]{2,1,0:T(8,128)(2,1)S(1)}, bf16[16,128,256]{2,1,0:T(8,128)(2,1)S(1)}, u32[]{:S(2)}, u32[]{:S(2)}) collective-permute-start(bf16[16,128,256]{2,1,0:T(8,128)(2,1)S(1)} %pad_maximum_fusion.2.p0), channel_id=1, source_target_pairs={{0,1},{1,0},{2,3},{3,2},{4,5},{5,4},{6,7},{7,6},{8,9},{9,8},{10,11... | collective-permute-start | bytes 3145736 | tf_op jit(solution)/shard_map/ppermute | solution.py:1076
  67.8 7.5 %collective-permute-start.14 = (bf16[16,128,256]{2,1,0:T(8,128)(2,1)S(1)}, bf16[16,128,256]{2,1,0:T(8,128)(2,1)}, u32[]{:S(2)}, u32[]{:S(2)}) collective-permute-start(bf16[16,128,256]{2,1,0:T(8,128)(2,1)S(1)} %pad_maximum_fusion.3.p2), channel_id=1, source_target_pairs={{0,1},{1,0},{2,3},{3,2},{4,5},{5,4},{6,7},{7,6},{8,9},{9,8},{10,11... | collective-permute-start | bytes 3145736 | tf_op jit(solution)/shard_map/ppermute | solution.py:1076
  75.3 10.7 %collective-permute-start.17 = (bf16[8,80,256]{2,1,0:T(8,128)(2,1)S(1)}, bf16[8,80,256]{2,1,0:T(8,128)(2,1)S(1)}, u32[]{:S(2)}, u32[]{:S(2)}) collective-permute-start(bf16[8,80,256]{2,1,0:T(8,128)(2,1)S(1)} %pad_maximum_fusion.18), channel_id=1, source_target_pairs={{0,2},{1,3},{2,0},{3,1},{4,6},{5,7},{6,4},{7,5},{8,10},{9,11},{10,... | collective-permute-start | bytes 983048 | tf_op jit(solution)/shard_map/ppermute | solution.py:1076
  76.4 9.7 %collective-permute-start.18 = (bf16[8,80,256]{2,1,0:T(8,128)(2,1)S(1)}, bf16[8,80,256]{2,1,0:T(8,128)(2,1)S(1)}, u32[]{:S(2)}, u32[]{:S(2)}) collective-permute-start(bf16[8,80,256]{2,1,0:T(8,128)(2,1)S(1)} %pad_maximum_fusion.19), channel_id=1, source_target_pairs={{0,4},{1,5},{2,6},{3,7},{4,0},{5,1},{6,2},{7,3},{8,12},{9,13},{10,... | collective-permute-start | bytes 983048 | tf_op jit(solution)/shard_map/ppermute | solution.py:1076
  86.9 14.9 %collective-permute-start.23 = (bf16[288,256]{1,0:T(8,128)(2,1)S(1)}, bf16[288,256]{1,0:T(8,128)(2,1)S(1)}, u32[]{:S(2)}, u32[]{:S(2)}) collective-permute-start(bf16[288,256]{1,0:T(8,128)(2,1)S(1)} %copy-done.12), channel_id=1, source_target_pairs={{0,24},{1,25},{2,26},{3,27},{4,28},{5,29},{6,30},{7,31},{8,16},{9,... | collective-permute-start | bytes 442376 | tf_op jit(solution)/shard_map/ppermute | solution.py:1076
  88.8 13.0 %collective-permute-start.22 = (bf16[288,256]{1,0:T(8,128)(2,1)S(1)}, bf16[288,256]{1,0:T(8,128)(2,1)S(1)}, u32[]{:S(2)}, u32[]{:S(2)}) collective-permute-start(bf16[288,256]{1,0:T(8,128)(2,1)S(1)} %copy-done.12), channel_id=1, source_target_pairs={{0,16},{1,17},{2,18},{3,19},{4,20},{5,21},{6,22},{7,23},{8,24},{9,... | collective-permute-start | bytes 442376 | tf_op jit(solution)/shard_map/ppermute | solution.py:1076
  88.8 13.0 %collective-permute-start.21 = (bf16[288,256]{1,0:T(8,128)(2,1)S(1)}, bf16[288,256]{1,0:T(8,128)(2,1)S(1)}, u32[]{:S(2)}, u32[]{:S(2)}) collective-permute-start(bf16[288,256]{1,0:T(8,128)(2,1)S(1)} %copy-done.12), channel_id=1, source_target_pairs={{0,8},{1,9},{2,10},{3,11},{4,12},{5,13},{6,14},{7,15},{8,0},{9,1},... | collective-permute-start | bytes 442376 | tf_op jit(solution)/shard_map/ppermute | solution.py:1076
  91.3 10.6 %collective-permute-start.19 = (bf16[16,80,256]{2,1,0:T(8,128)(2,1)S(1)}, bf16[16,80,256]{2,1,0:T(8,128)(2,1)S(1)}, u32[]{:S(2)}, u32[]{:S(2)}) collective-permute-start(bf16[16,80,256]{2,1,0:T(8,128)(2,1)S(1)} %pad_maximum_fusion.6.p0), channel_id=1, source_target_pairs={{0,1},{1,0},{2,3},{3,2},{4,5},{5,4},{6,7},{7,6},{8,9},{9,8},{10,11... | collective-permute-start | bytes 1966088 | tf_op jit(solution)/shard_map/ppermute | solution.py:1076
  91.3 10.6 %collective-permute-start.20 = (bf16[16,80,256]{2,1,0:T(8,128)(2,1)S(1)}, bf16[16,80,256]{2,1,0:T(8,128)(2,1)S(1)}, u32[]{:S(2)}, u32[]{:S(2)}) collective-permute-start(bf16[16,80,256]{2,1,0:T(8,128)(2,1)S(1)} %pad_maximum_fusion.7.p2), channel_id=1, source_target_pairs={{0,1},{1,0},{2,3},{3,2},{4,5},{5,4},{6,7},{7,6},{8,9},{9,8},{10,11... | collective-permute-start | bytes 1966088 | tf_op jit(solution)/shard_map/ppermute | solution.py:1076
  102.0 18.0 %collective-permute-start.25 = (bf16[4,144,256]{2,1,0:T(8,128)(2,1)S(1)}, bf16[4,144,256]{2,1,0:T(8,128)(2,1)S(1)}, u32[]{:S(2)}, u32[]{:S(2)}) collective-permute-start(bf16[4,144,256]{2,1,0:T(8,128)(2,1)S(1)} %get-tuple-element.407), channel_id=1, source_target_pairs={{0,2},{1,3},{2,0},{3,1},{4,6},{5,7},{6,4},{7,5},{8,10},{9,11},{10,... | collective-permute-start | bytes 884744 | tf_op jit(solution)/shard_map/ppermute | solution.py:1076
  103.1 17.0 %collective-permute-start.24 = (bf16[4,144,256]{2,1,0:T(8,128)(2,1)S(1)}, bf16[4,144,256]{2,1,0:T(8,128)(2,1)S(1)}, u32[]{:S(2)}, u32[]{:S(2)}) collective-permute-start(bf16[4,144,256]{2,1,0:T(8,128)(2,1)S(1)} %get-tuple-element.408), channel_id=1, source_target_pairs={{0,4},{1,5},{2,6},{3,7},{4,0},{5,1},{6,2},{7,3},{8,12},{9,13},{10,... | collective-permute-start | bytes 884744 | tf_op jit(solution)/shard_map/ppermute | solution.py:1076
  120.2 16.5 %collective-permute-start.26 = (bf16[768,384]{1,0:T(8,128)(2,1)}, bf16[768,384]{1,0:T(8,128)(2,1)S(1)}, u32[]{:S(2)}, u32[]{:S(2)}) collective-permute-start(bf16[768,384]{1,0:T(8,128)(2,1)} %get-tuple-element.255), channel_id=1, source_target_pairs={{0,4},{4,0},{1,5},{5,1},{16,20},{20,16},{17,21},{21,17},{2,6},{6,2... | collective-permute-start | bytes 1769480 | tf_op jit(solution)/shard_map/ppermute | solution.py:1239
  121.1 15.7 %collective-permute-start.27 = (bf16[768,384]{1,0:T(8,128)(2,1)S(1)}, bf16[768,384]{1,0:T(8,128)(2,1)S(1)}, u32[]{:S(2)}, u32[]{:S(2)}) collective-permute-start(bf16[768,384]{1,0:T(8,128)(2,1)S(1)} %copy-done.33), channel_id=1, source_target_pairs={{0,1},{4,5},{1,0},{5,4},{16,17},{20,21},{17,16},{21,20},{2,3},{6,7... | collective-permute-start | bytes 1769480 | tf_op jit(solution)/shard_map/ppermute | solution.py:1239
  121.2 24.7 %collective-permute-start.28 = (bf16[768,384]{1,0:T(8,128)(2,1)S(1)}, bf16[768,384]{1,0:T(8,128)(2,1)S(1)}, u32[]{:S(2)}, u32[]{:S(2)}) collective-permute-start(bf16[768,384]{1,0:T(8,128)(2,1)S(1)} %copy-done.31), channel_id=1, source_target_pairs={{0,5},{4,1},{1,4},{5,0},{16,21},{20,17},{17,20},{21,16},{2,7},{6,3... | collective-permute-start | bytes 1769480 | tf_op jit(solution)/shard_map/ppermute | solution.py:1239
  145.9 37.4 %collective-permute-start.29 = (bf16[8,144,256]{2,1,0:T(8,128)(2,1)S(1)}, bf16[8,144,256]{2,1,0:T(8,128)(2,1)S(1)}, u32[]{:S(2)}, u32[]{:S(2)}) collective-permute-start(bf16[8,144,256]{2,1,0:T(8,128)(2,1)S(1)} %pad_maximum_fusion.9), channel_id=1, source_target_pairs={{0,2},{1,3},{2,0},{3,1},{4,6},{5,7},{6,4},{7,5},{8,10},{9,11},{10,... | collective-permute-start | bytes 1769480 | tf_op jit(solution)/shard_map/ppermute | solution.py:1076
  147.0 36.5 %collective-permute-start.30 = (bf16[8,144,256]{2,1,0:T(8,128)(2,1)S(1)}, bf16[8,144,256]{2,1,0:T(8,128)(2,1)S(1)}, u32[]{:S(2)}, u32[]{:S(2)}) collective-permute-start(bf16[8,144,256]{2,1,0:T(8,128)(2,1)S(1)} %pad_maximum_fusion.10), channel_id=1, source_target_pairs={{0,4},{1,5},{2,6},{3,7},{4,0},{5,1},{6,2},{7,3},{8,12},{9,13},{10,... | collective-permute-start | bytes 1769480 | tf_op jit(solution)/shard_map/ppermute | solution.py:1076
  147.8 35.8 %collective-permute-start.31 = (bf16[768,512]{1,0:T(8,128)(2,1)S(1)}, bf16[768,512]{1,0:T(8,128)(2,1)S(1)}, u32[]{:S(2)}, u32[]{:S(2)}) collective-permute-start(bf16[768,512]{1,0:T(8,128)(2,1)S(1)} %bitcast.131), channel_id=1, source_target_pairs={{0,0},{8,4},{16,1},{24,5},{1,16},{9,20},{17,17},{25,21},{2,2},{10,... | collective-permute-start | bytes 2359304 | tf_op jit(solution)/shard_map/ppermute | solution.py:1224
  183.6 16.0 %collective-permute-start.35 = (bf16[16,144,256]{2,1,0:T(8,128)(2,1)S(1)}, bf16[16,144,256]{2,1,0:T(8,128)(2,1)S(1)}, u32[]{:S(2)}, u32[]{:S(2)}) collective-permute-start(bf16[16,144,256]{2,1,0:T(8,128)(2,1)S(1)} %pad_maximum_fusion.refs_6_), channel_id=1, source_target_pairs={{0,1},{1,0},{2,3},{3,2},{4,5},{5,4},{6,7},{7,6},{8,9},{9,8},{10,11... | collective-permute-start | bytes 3538952 | tf_op jit(solution)/shard_map/ppermute | solution.py:1076
  187.9 11.8 %collective-permute-start.36 = (bf16[16,144,256]{2,1,0:T(8,128)(2,1)S(1)}, bf16[16,144,256]{2,1,0:T(8,128)(2,1)S(1)}, u32[]{:S(2)}, u32[]{:S(2)}) collective-permute-start(bf16[16,144,256]{2,1,0:T(8,128)(2,1)S(1)} %pad_maximum_fusion.1.refs_8_), channel_id=1, source_target_pairs={{0,1},{1,0},{2,3},{3,2},{4,5},{5,4},{6,7},{7,6},{8,9},{9,8},{10,11... | collective-permute-start | bytes 3538952 | tf_op jit(solution)/shard_map/ppermute | solution.py:1076
  187.9 7.8 %collective-permute-start.32 = (bf16[768,128]{1,0:T(8,128)(2,1)S(1)}, bf16[768,128]{1,0:T(8,128)(2,1)S(1)}, u32[]{:S(2)}, u32[]{:S(2)}) collective-permute-start(bf16[768,128]{1,0:T(8,128)(2,1)S(1)} %copy-done.37), channel_id=1, source_target_pairs={{0,4},{4,0},{1,5},{5,1},{16,20},{20,16},{17,21},{21,17},{2,6},{6,2... | collective-permute-start | bytes 589832 | tf_op jit(solution)/shard_map/ppermute | solution.py:1239
  189.1 10.5 %collective-permute-start.34 = (bf16[768,128]{1,0:T(8,128)(2,1)S(1)}, bf16[768,128]{1,0:T(8,128)(2,1)S(1)}, u32[]{:S(2)}, u32[]{:S(2)}) collective-permute-start(bf16[768,128]{1,0:T(8,128)(2,1)S(1)} %copy-done.39), channel_id=1, source_target_pairs={{0,5},{4,1},{1,4},{5,0},{16,21},{20,17},{17,20},{21,16},{2,7},{6,3... | collective-permute-start | bytes 589832 | tf_op jit(solution)/shard_map/ppermute | solution.py:1239
  225.4 12.5 %collective-permute-start.37 = (bf16[768,128]{1,0:T(8,128)(2,1)}, bf16[768,128]{1,0:T(8,128)(2,1)S(1)}, u32[]{:S(2)}, u32[]{:S(2)}) collective-permute-start(bf16[768,128]{1,0:T(8,128)(2,1)} %get-tuple-element.288), channel_id=1, source_target_pairs={{0,4},{4,0},{1,5},{5,1},{16,20},{20,16},{17,21},{21,17},{2,6},{6,2... | collective-permute-start | bytes 589832 | tf_op jit(solution)/shard_map/ppermute | solution.py:1239
  226.0 11.8 %collective-permute-start.38 = (bf16[768,128]{1,0:T(8,128)(2,1)}, bf16[768,128]{1,0:T(8,128)(2,1)S(1)}, u32[]{:S(2)}, u32[]{:S(2)}) collective-permute-start(bf16[768,128]{1,0:T(8,128)(2,1)} %get-tuple-element.289), channel_id=1, source_target_pairs={{0,1},{4,5},{1,0},{5,4},{16,17},{20,21},{17,16},{21,20},{2,3},{6,7... | collective-permute-start | bytes 589832 | tf_op jit(solution)/shard_map/ppermute | solution.py:1239
  226.0 11.8 %collective-permute-start.39 = (bf16[768,128]{1,0:T(8,128)(2,1)}, bf16[768,128]{1,0:T(8,128)(2,1)S(1)}, u32[]{:S(2)}, u32[]{:S(2)}) collective-permute-start(bf16[768,128]{1,0:T(8,128)(2,1)} %get-tuple-element.290), channel_id=1, source_target_pairs={{0,5},{4,1},{1,4},{5,0},{16,21},{20,17},{17,20},{21,16},{2,7},{6,3... | collective-permute-start | bytes 589832 | tf_op jit(solution)/shard_map/ppermute | solution.py:1239
  237.9 59.0 %collective-permute-start.40 = (bf16[16,288,256]{2,1,0:T(8,128)(2,1)}, bf16[16,288,256]{2,1,0:T(8,128)(2,1)S(1)}, u32[]{:S(2)}, u32[]{:S(2)}) collective-permute-start(bf16[16,288,256]{2,1,0:T(8,128)(2,1)} %get-tuple-element.308), channel_id=1, source_target_pairs={{0,1},{1,0},{2,3},{3,2},{4,5},{5,4},{6,7},{7,6},{8,9},{9,8},{10,11... | collective-permute-start | bytes 7077896 | tf_op jit(solution)/shard_map/ppermute | solution.py:1076
  297.8 28.7 %collective-permute-start.44 = (bf16[8,288,256]{2,1,0:T(8,128)(2,1)S(1)}, bf16[8,288,256]{2,1,0:T(8,128)(2,1)S(1)}, u32[]{:S(2)}, u32[]{:S(2)}) collective-permute-start(bf16[8,288,256]{2,1,0:T(8,128)(2,1)S(1)} %slice.314), channel_id=1, source_target_pairs={{0,2},{1,3},{2,0},{3,1},{4,6},{5,7},{6,4},{7,5},{8,10},{9,11},{10,... | collective-permute-start | bytes 3538952 | tf_op jit(solution)/shard_map/ppermute | solution.py:1076
  300.3 26.5 %collective-permute-start.41 = (bf16[768,384]{1,0:T(8,128)(2,1)S(1)}, bf16[768,384]{1,0:T(8,128)(2,1)S(1)}, u32[]{:S(2)}, u32[]{:S(2)}) collective-permute-start(bf16[768,384]{1,0:T(8,128)(2,1)S(1)} %copy-done.30), channel_id=1, source_target_pairs={{0,4},{4,0},{1,5},{5,1},{16,20},{20,16},{17,21},{21,17},{2,6},{6,2... | collective-permute-start | bytes 1769480 | tf_op jit(solution)/shard_map/ppermute | solution.py:1239
  301.0 25.8 %collective-permute-start.42 = (bf16[768,384]{1,0:T(8,128)(2,1)S(1)}, bf16[768,384]{1,0:T(8,128)(2,1)S(1)}, u32[]{:S(2)}, u32[]{:S(2)}) collective-permute-start(bf16[768,384]{1,0:T(8,128)(2,1)S(1)} %copy-done.29), channel_id=1, source_target_pairs={{0,1},{4,5},{1,0},{5,4},{16,17},{20,21},{17,16},{21,20},{2,3},{6,7... | collective-permute-start | bytes 1769480 | tf_op jit(solution)/shard_map/ppermute | solution.py:1239
  301.0 25.9 %collective-permute-start.43 = (bf16[768,384]{1,0:T(8,128)(2,1)S(1)}, bf16[768,384]{1,0:T(8,128)(2,1)S(1)}, u32[]{:S(2)}, u32[]{:S(2)}) collective-permute-start(bf16[768,384]{1,0:T(8,128)(2,1)S(1)} %copy-done.28), channel_id=1, source_target_pairs={{0,5},{4,1},{1,4},{5,0},{16,21},{20,17},{17,20},{21,16},{2,7},{6,3... | collective-permute-start | bytes 1769480 | tf_op jit(solution)/shard_map/ppermute | solution.py:1239
  326.9 20.9 %collective-permute-start.47 = (bf16[4,288,256]{2,1,0:T(8,128)(2,1)S(1)}, bf16[4,288,256]{2,1,0:T(8,128)(2,1)S(1)}, u32[]{:S(2)}, u32[]{:S(2)}) collective-permute-start(bf16[4,288,256]{2,1,0:T(8,128)(2,1)S(1)} %slice.318), channel_id=1, source_target_pairs={{0,4},{1,5},{2,6},{3,7},{4,0},{5,1},{6,2},{7,3},{8,12},{9,13},{10,... | collective-permute-start | bytes 1769480 | tf_op jit(solution)/shard_map/ppermute | solution.py:1076
  335.2 12.8 %collective-permute-start.46 = (bf16[16,256]{1,0:T(8,128)(2,1)S(1)}, bf16[16,256]{1,0:T(8,128)(2,1)S(1)}, u32[]{:S(2)}, u32[]{:S(2)}) collective-permute-start(bf16[16,256]{1,0:T(8,128)(2,1)S(1)} %get-tuple-element.428), channel_id=1, source_target_pairs={{4,0},{1,4},{5,1},{20,16},{17,20},{21,17},{6,2},{3,6},{7,3},{22,18... | collective-permute-start | bytes 24584 | tf_op jit(solution)/shard_map/ppermute | solution.py:1235
  336.5 11.5 %collective-permute-start.45 = (bf16[16,256]{1,0:T(8,128)(2,1)S(1)}, bf16[16,256]{1,0:T(8,128)(2,1)S(1)}, u32[]{:S(2)}, u32[]{:S(2)}) collective-permute-start(bf16[16,256]{1,0:T(8,128)(2,1)S(1)} %get-tuple-element.429), channel_id=1, source_target_pairs={{0,4},{4,1},{1,5},{16,20},{20,17},{17,21},{2,6},{6,3},{3,7},{18,22... | collective-permute-start | bytes 24584 | tf_op jit(solution)/shard_map/ppermute | solution.py:1235
  348.1 40.0 %collective-permute-start.48 = (bf16[288,256]{1,0:T(8,128)(2,1)S(1)}, bf16[288,256]{1,0:T(8,128)(2,1)S(1)}, u32[]{:S(2)}, u32[]{:S(2)}) collective-permute-start(bf16[288,256]{1,0:T(8,128)(2,1)S(1)} %get-tuple-element.404), channel_id=1, source_target_pairs={{0,8},{1,9},{2,10},{3,11},{4,12},{5,13},{6,14},{7,15},{8,0},{9,1},... | collective-permute-start | bytes 442376 | tf_op jit(solution)/shard_map/ppermute | solution.py:1076
  349.1 39.0 %collective-permute-start.50 = (bf16[288,256]{1,0:T(8,128)(2,1)S(1)}, bf16[288,256]{1,0:T(8,128)(2,1)S(1)}, u32[]{:S(2)}, u32[]{:S(2)}) collective-permute-start(bf16[288,256]{1,0:T(8,128)(2,1)S(1)} %get-tuple-element.405), channel_id=1, source_target_pairs={{0,24},{1,25},{2,26},{3,27},{4,28},{5,29},{6,30},{7,31},{8,16},{9,... | collective-permute-start | bytes 442376 | tf_op jit(solution)/shard_map/ppermute | solution.py:1076
  350.3 37.8 %collective-permute-start.49 = (bf16[288,256]{1,0:T(8,128)(2,1)S(1)}, bf16[288,256]{1,0:T(8,128)(2,1)S(1)}, u32[]{:S(2)}, u32[]{:S(2)}) collective-permute-start(bf16[288,256]{1,0:T(8,128)(2,1)S(1)} %get-tuple-element.406), channel_id=1, source_target_pairs={{0,16},{1,17},{2,18},{3,19},{4,20},{5,21},{6,22},{7,23},{8,24},{9,... | collective-permute-start | bytes 442376 | tf_op jit(solution)/shard_map/ppermute | solution.py:1076
  351.6 37.1 %collective-permute-start.52 = (bf16[768,512]{1,0:T(8,128)(2,1)}, bf16[768,512]{1,0:T(8,128)(2,1)S(1)}, u32[]{:S(2)}, u32[]{:S(2)}) collective-permute-start(bf16[768,512]{1,0:T(8,128)(2,1)} %get-tuple-element.339), channel_id=1, source_target_pairs={{0,0},{4,8},{1,16},{5,24},{16,1},{20,9},{17,17},{21,25},{2,2},{6,1... | collective-permute-start | bytes 2359304 | tf_op jit(solution)/shard_map/ppermute | solution.py:1232
  353.4 34.8 %collective-permute-start.51 = (bf16[16,160,256]{2,1,0:T(8,128)(2,1)}, bf16[16,160,256]{2,1,0:T(8,128)(2,1)S(1)}, u32[]{:S(2)}, u32[]{:S(2)}) collective-permute-start(bf16[16,160,256]{2,1,0:T(8,128)(2,1)} %get-tuple-element.338), channel_id=1, source_target_pairs={{0,1},{1,0},{2,3},{3,2},{4,5},{5,4},{6,7},{7,6},{8,9},{9,8},{10,11... | collective-permute-start | bytes 3932168 | tf_op jit(solution)/shard_map/ppermute | solution.py:1076
  395.5 10.4 %collective-permute-start.55 = (bf16[16,176,256]{2,1,0:T(8,128)(2,1)}, bf16[16,176,256]{2,1,0:T(8,128)(2,1)S(1)}, u32[]{:S(2)}, u32[]{:S(2)}) collective-permute-start(bf16[16,176,256]{2,1,0:T(8,128)(2,1)} %get-tuple-element.356), channel_id=1, source_target_pairs={{0,1},{1,0},{2,3},{3,2},{4,5},{5,4},{6,7},{7,6},{8,9},{9,8},{10,11... | collective-permute-start | bytes 4325384 | tf_op jit(solution)/shard_map/ppermute | solution.py:1076
  395.6 10.2 %collective-permute-start.54 = (bf16[8,80,256]{2,1,0:T(8,128)(2,1)S(1)}, bf16[8,80,256]{2,1,0:T(8,128)(2,1)S(1)}, u32[]{:S(2)}, u32[]{:S(2)}) collective-permute-start(bf16[8,80,256]{2,1,0:T(8,128)(2,1)S(1)} %slice.328), channel_id=1, source_target_pairs={{0,4},{1,5},{2,6},{3,7},{4,0},{5,1},{6,2},{7,3},{8,12},{9,13},{10,... | collective-permute-start | bytes 983048 | tf_op jit(solution)/shard_map/ppermute | solution.py:1076
  395.6 10.2 %collective-permute-start.53 = (bf16[8,80,256]{2,1,0:T(8,128)(2,1)S(1)}, bf16[8,80,256]{2,1,0:T(8,128)(2,1)S(1)}, u32[]{:S(2)}, u32[]{:S(2)}) collective-permute-start(bf16[8,80,256]{2,1,0:T(8,128)(2,1)S(1)} %slice.326), channel_id=1, source_target_pairs={{0,2},{1,3},{2,0},{3,1},{4,6},{5,7},{6,4},{7,5},{8,10},{9,11},{10,... | collective-permute-start | bytes 983048 | tf_op jit(solution)/shard_map/ppermute | solution.py:1076
  406.7 16.3 %collective-permute-start.57 = (bf16[960,256]{1,0:T(8,128)(2,1)S(1)}, bf16[960,256]{1,0:T(8,128)(2,1)S(1)}, u32[]{:S(2)}, u32[]{:S(2)}) collective-permute-start(bf16[960,256]{1,0:T(8,128)(2,1)S(1)} %pad_maximum_fusion.15), channel_id=1, source_target_pairs={{0,4},{1,5},{2,6},{3,7},{4,0},{5,1},{6,2},{7,3},{8,12},{9,13},{10,... | collective-permute-start | bytes 1474568 | tf_op jit(solution)/shard_map/ppermute | solution.py:1076
  408.4 14.8 %collective-permute-start.56 = (bf16[1088,256]{1,0:T(8,128)(2,1)S(1)}, bf16[1088,256]{1,0:T(8,128)(2,1)S(1)}, u32[]{:S(2)}, u32[]{:S(2)}) collective-permute-start(bf16[1088,256]{1,0:T(8,128)(2,1)S(1)} %pad_maximum_fusion.11), channel_id=1, source_target_pairs={{0,2},{1,3},{2,0},{3,1},{4,6},{5,7},{6,4},{7,5},{8,10},{9,11},{10,... | collective-permute-start | bytes 1671176 | tf_op jit(solution)/shard_map/ppermute | solution.py:1076
  416.6 7.6 %collective-permute-start.58 = (bf16[384,512]{1,0:T(8,128)(2,1)}, bf16[384,512]{1,0:T(8,128)(2,1)S(1)}, u32[]{:S(2)}, u32[]{:S(2)}) collective-permute-start(bf16[384,512]{1,0:T(8,128)(2,1)} %get-tuple-element.377), channel_id=1, source_target_pairs={{0,0},{4,8},{1,16},{5,24},{16,1},{20,9},{17,17},{21,25},{2,2},{6,1... | collective-permute-start | bytes 1179656 | tf_op jit(solution)/shard_map/ppermute | solution.py:1232
  424.2 8.0 %collective-permute-start.59 = (bf16[16,80,256]{2,1,0:T(8,128)(2,1)S(1)}, bf16[16,80,256]{2,1,0:T(8,128)(2,1)S(1)}, u32[]{:S(2)}, u32[]{:S(2)}) collective-permute-start(bf16[16,80,256]{2,1,0:T(8,128)(2,1)S(1)} %copy-done.22), channel_id=1, source_target_pairs={{0,1},{1,0},{2,3},{3,2},{4,5},{5,4},{6,7},{7,6},{8,9},{9,8},{10,11... | collective-permute-start | bytes 1966088 | tf_op jit(solution)/shard_map/ppermute | solution.py:1076
  430.5 29.5 %collective-permute-start.63 = (bf16[384,512]{1,0:T(8,128)(2,1)S(1)}, bf16[384,512]{1,0:T(8,128)(2,1)S(1)}, u32[]{:S(2)}, u32[]{:S(2)}) collective-permute-start(bf16[384,512]{1,0:T(8,128)(2,1)S(1)} %copy-done.36), channel_id=1, source_target_pairs={{0,0},{4,8},{1,16},{5,24},{16,1},{20,9},{17,17},{21,25},{2,2},{6,1... | collective-permute-start | bytes 1179656 | tf_op jit(solution)/shard_map/ppermute | solution.py:1232
  432.5 10.6 %collective-permute-start.61 = (bf16[640,256]{1,0:T(8,128)(2,1)S(1)}, bf16[640,256]{1,0:T(8,128)(2,1)S(1)}, u32[]{:S(2)}, u32[]{:S(2)}) collective-permute-start(bf16[640,256]{1,0:T(8,128)(2,1)S(1)} %pad_maximum_fusion.20), channel_id=1, source_target_pairs={{0,2},{1,3},{2,0},{3,1},{4,6},{5,7},{6,4},{7,5},{8,10},{9,11},{10,... | collective-permute-start | bytes 983048 | tf_op jit(solution)/shard_map/ppermute | solution.py:1076
  433.3 26.7 %collective-permute-start.62 = (bf16[4,80,256]{2,1,0:T(8,128)(2,1)S(1)}, bf16[4,80,256]{2,1,0:T(8,128)(2,1)S(1)}, u32[]{:S(2)}, u32[]{:S(2)}) collective-permute-start(bf16[4,80,256]{2,1,0:T(8,128)(2,1)S(1)} %get-tuple-element.401), channel_id=1, source_target_pairs={{0,6},{1,7},{2,4},{3,5},{4,2},{5,3},{6,0},{7,1},{8,14},{9,15},{10,... | collective-permute-start | bytes 491528 | tf_op jit(solution)/shard_map/ppermute | solution.py:1076
  440.3 19.6 %collective-permute-start.60 = (bf16[704,256]{1,0:T(8,128)(2,1)S(1)}, bf16[704,256]{1,0:T(8,128)(2,1)S(1)}, u32[]{:S(2)}, u32[]{:S(2)}) collective-permute-start(bf16[704,256]{1,0:T(8,128)(2,1)S(1)} %pad_maximum_fusion.16), channel_id=1, source_target_pairs={{0,4},{1,5},{2,6},{3,7},{4,0},{5,1},{6,2},{7,3},{8,12},{9,13},{10,... | collective-permute-start | bytes 1081352 | tf_op jit(solution)/shard_map/ppermute | solution.py:1076
  460.2 11.8 %collective-permute-start.64 = (bf16[416,256]{1,0:T(8,128)(2,1)S(1)}, bf16[416,256]{1,0:T(8,128)(2,1)S(1)}, u32[]{:S(2)}, u32[]{:S(2)}) collective-permute-start(bf16[416,256]{1,0:T(8,128)(2,1)S(1)} %get-tuple-element.396), channel_id=1, source_target_pairs={{0,8},{1,9},{2,10},{3,11},{4,12},{5,13},{6,14},{7,15},{8,0},{9,1},... | collective-permute-start | bytes 638984 | tf_op jit(solution)/shard_map/ppermute | solution.py:1076
  461.0 11.0 %collective-permute-start.66 = (bf16[416,256]{1,0:T(8,128)(2,1)S(1)}, bf16[416,256]{1,0:T(8,128)(2,1)S(1)}, u32[]{:S(2)}, u32[]{:S(2)}) collective-permute-start(bf16[416,256]{1,0:T(8,128)(2,1)S(1)} %get-tuple-element.397), channel_id=1, source_target_pairs={{0,24},{1,25},{2,26},{3,27},{4,28},{5,29},{6,30},{7,31},{8,16},{9,... | collective-permute-start | bytes 638984 | tf_op jit(solution)/shard_map/ppermute | solution.py:1076
  461.0 21.3 %collective-permute-start.65 = (bf16[416,256]{1,0:T(8,128)(2,1)S(1)}, bf16[416,256]{1,0:T(8,128)(2,1)S(1)}, u32[]{:S(2)}, u32[]{:S(2)}) collective-permute-start(bf16[416,256]{1,0:T(8,128)(2,1)S(1)} %get-tuple-element.398), channel_id=1, source_target_pairs={{0,16},{1,17},{2,18},{3,19},{4,20},{5,21},{6,22},{7,23},{8,24},{9,... | collective-permute-start | bytes 638984 | tf_op jit(solution)/shard_map/ppermute | solution.py:1076
  (53 other events, 405.3 us)

commit v8 on v7

--- a/solution.py
+++ b/solution.py
@@ -743,7 +743,7 @@
 def back2(scal, low, db, high, taps, mid, left, right, g3, point, group, ties=()):
     rows = db.shape[0]
     ext = rows + 2 * RIM
-    tile = 160
+    tile = 80
     return call(
         functools.partial(back2_kernel, tile, group),
         [(scal, "s")]

time: 497 us -> 497 us (level)
  transfers between devices with their start and end apart: 67 -> 67, of which waited for: 19 -> 20; matrix products, arithmetic and copies ran while one was open for 2% -> 2% of each run, Pallas kernels for 42% -> 42%
where the time goes in v8:
time: 497 us; the launch traced here: 488 us
  Pallas kernels  235 us (47%)
  waiting for transfers between devices  124 us (25%)
  starting transfers between devices  97.8 us (20%)
  local copies, waits for them, and re-layouts  14.9 us (3%)
  other arithmetic  11.5 us (2%)
    pallas_call x15, Pallas kernels, call(): pl.pallas_call(kernel, out_shape=shapes, grid=() if steps is None else (s...  235 us
    ppermute x46, waiting for transfers between devices, flip(): return lax.ppermute(value, AXES, [(i, i ^ mask) for i in range(self.count)])  91.4 us
    ppermute x46, starting transfers between devices, flip(): return lax.ppermute(value, AXES, [(i, i ^ mask) for i in range(self.count)])  73.2 us
    ppermute x12, waiting for transfers between devices, swap(): lax.ppermute(values[k], AXES, self.pairs(self.at, lambda g, s: self.at(g,...  32.6 us
  transfers between devices with their start and end apart: 67, of which 20 were waited for; matrix products, arithmetic and copies ran while one was open for 2% of the time, Pallas kernels for 42%

profile of v8, /device:TPU:0, one launch (start us, length us, event | category | flops | bytes accessed | tf_op | source)
XLA Modules:
  0.0 488.2 jit_solution(15285825212494735719)
XLA Ops:
  3.5 1.2 pad_maximum_fusion.5
  4.7 1.7 shard_map.297
  6.4 5.0 %collective-permute-start.2 = (bf16[256,256]{1,0:T(8,128)(2,1)}, bf16[256,256]{1,0:T(8,128)(2,1)S(1)}, u32[]{:S(2)}, u32[]{:S(2)}) collective-permute-start(bf16[256,256]{1,0:T(8,128)(2,1)} %get-tuple-element.208), channel_id=1, source_target_pairs={{0,24},{1,25},{2,26},{3,27},{4,28},{5,29},{6,30},{7,31},{8,16},{9,... | collective-permute-start | bytes 393224 | tf_op jit(solution)/shard_map/ppermute | solution.py:1076
  12.8 3.3 collective-permute-done.2
  16.1 7.9 %collective-permute-done.1 = bf16[256,256]{1,0:T(8,128)(2,1)S(1)} collective-permute-done((bf16[256,256]{1,0:T(8,128)(2,1)}, bf16[256,256]{1,0:T(8,128)(2,1)S(1)}, u32[]{:S(2)}, u32[]{:S(2)}) %collective-permute-start.1) | collective-permute-done | bytes 131104 | tf_op jit(solution)/shard_map/ppermute | solution.py:1076
  25.0 1.4 collective-permute-start.4
  26.3 9.1 %collective-permute-start.3 = (bf16[4,128,256]{2,1,0:T(8,128)(2,1)S(1)}, bf16[4,128,256]{2,1,0:T(8,128)(2,1)S(1)}, u32[]{:S(2)}, u32[]{:S(2)}) collective-permute-start(bf16[4,128,256]{2,1,0:T(8,128)(2,1)S(1)} %get-tuple-element.410), channel_id=1, source_target_pairs={{0,4},{1,5},{2,6},{3,7},{4,0},{5,1},{6,2},{7,3},{8,12},{9,13},{10,... | collective-permute-start | bytes 786440 | tf_op jit(solution)/shard_map/ppermute | solution.py:1076
  36.2 1.3 collective-permute-start.7
  37.5 1.9 collective-permute-start.6
  40.0 9.3 %collective-permute-done.3 = bf16[4,128,256]{2,1,0:T(8,128)(2,1)S(1)} collective-permute-done((bf16[4,128,256]{2,1,0:T(8,128)(2,1)S(1)}, bf16[4,128,256]{2,1,0:T(8,128)(2,1)S(1)}, u32[]{:S(2)}, u32[]{:S(2)}) %collective-permute-start.3) | collective-permute-done | bytes 262176 | tf_op jit(solution)/shard_map/ppermute | solution.py:1076
  49.7 2.7 collective-permute-start.12
  52.4 1.8 collective-permute-start.10
  55.2 2.5 collective-permute-start.9
  60.5 1.2 pad_add_fusion.scal
  61.8 4.2 collective-permute-done.8
  66.2 1.4 collective-permute-done.9
  69.3 1.7 collective-permute-start.15
  71.1 3.5 collective-permute-done.16
  76.4 1.7 collective-permute-start.18
  78.2 7.9 %shard_map.298 = (f32[800,512]{1,0:T(8,128)}, bf16[800,512]{1,0:T(8,128)(2,1)}, f32[800,1024]{1,0:T(8,128)}, bf16[512,1024]{1,0:T(8,128)(2,1)}, bf16[512,2048]{1...) custom-call(s32[3]{0:T(128)} %pad_add_fusion.scal, ...), custom_call_target="tpu_custom_call" | custom-call | flops 13799999488 | bytes 14770188 | tf_op jit(solution)/shard_map/pallas_call | solution.py:69
  86.9 1.9 collective-permute-start.23
  88.8 2.5 collective-permute-start.21
  91.8 10.0 %shard_map.299 = (f32[800,2048]{1,0:T(8,128)}, f32[800,256]{1,0:T(8,128)}, bf16[800,2048]{1,0:T(8,128)(2,1)}) custom-call(s32[3]{0:T(128)} %pad_add_fusion.scal, bf16[800,512]{1,0:T(8,128)(2,1)} %get-tuple-element.231.y2_ref, f32[1,2048]{1,0:T(1,128)} %get-tuple-element.232.g3.refs_4_, bf16[512,2048]{1,0:T(8,128)(2,1)} %get-tuple-element.233.wide.refs_1_, ...), custom_call_target="tpu_custom_call" | custom-call | flops 13799999488 | bytes 14360588 | tf_op jit(solution)/shard_map/pallas_call | solution.py:69
  103.4 16.6 %shard_map.300 = (bf16[768,2048]{1,0:T(8,128)(2,1)}, f32[768,512]{1,0:T(8,128)}, bf16[768,512]{1,0:T(8,128)(2,1)}, bf16[768,384]{1,0:T(8,128)(2,1)}, bf16[768,38...) custom-call(s32[3]{0:T(128)} %pad_add_fusion.scal, ...), custom_call_target="tpu_custom_call" | custom-call | flops 23000000512 | bytes 18098188 | tf_op jit(solution)/shard_map/pallas_call | solution.py:69
  121.2 1.1 collective-permute-start.28
  122.4 14.3 %collective-permute-done.26.refs_1_ = bf16[768,384]{1,0:T(8,128)(2,1)S(1)} collective-permute-done((bf16[768,384]{1,0:T(8,128)(2,1)}, bf16[768,384]{1,0:T(8,128)(2,1)S(1)}, u32[]{:S(2)}, u32[]{:S(2)}) %collective-permute-start.26) | collective-permute-done | bytes 589856 | tf_op jit(solution)/shard_map/ppermute | solution.py:1239
  136.7 9.2 %collective-permute-done.28.refs_3_ = bf16[768,384]{1,0:T(8,128)(2,1)S(1)} collective-permute-done((bf16[768,384]{1,0:T(8,128)(2,1)S(1)}, bf16[768,384]{1,0:T(8,128)(2,1)S(1)}, u32[]{:S(2)}, u32[]{:S(2)}) %collective-permute-start.28) | collective-permute-done | bytes 589856 | tf_op jit(solution)/shard_map/ppermute | solution.py:1239
  145.9 2.6 collective-permute-start.29
  148.5 1.7 collective-permute-start.30
  151.3 34.5 %shard_map.301 = (bf16[768,128]{1,0:T(8,128)(2,1)}, bf16[768,128]{1,0:T(8,128)(2,1)}, bf16[768,128]{1,0:T(8,128)(2,1)}, bf16[768,128]{1,0:T(8,128)(2,1)}, f32[3072,128]{1,0:T(8,128)}) custom-call(s32[3]{0:T(128)} %pad_add_fusion.scal, bf16[768,384]{1,0:T(8,128)(2,1)} %get-tuple-element.262.refs_0_, bf16[768,384]{1,0:T(8,128)(2,1)} %copy-done.25, ...), custom_call_target="tpu_custom_call" | custom-call | flops 41400000512 | bytes 4718604 | tf_op jit(solution)/shard_map/pallas_call | solution.py:69
  187.0 2.4 collective-permute-start.32
  190.4 4.6 collective-permute-done.32.refs_1_
  195.0 4.3 collective-permute-done.34.refs_3_
  200.8 24.3 %shard_map.302 = (bf16[768,512]{1,0:T(8,128)(2,1)}, f32[768,512]{1,0:T(8,128)}, bf16[768,128]{1,0:T(8,128)(2,1)}, bf16[768,128]{1,0:T(8,128)(2,1)}, bf16[768,128...) custom-call(s32[3]{0:T(128)} %pad_add_fusion.scal, ...), custom_call_target="tpu_custom_call" | custom-call | flops 23000000512 | bytes 18878476 | tf_op jit(solution)/shard_map/pallas_call | solution.py:69
  225.1 1.7 collective-permute-start.37
  227.3 10.3 %shard_map.303 = (bf16[16,288,256]{2,1,0:T(8,128)(2,1)}, bf16[16,288,256]{2,1,0:T(8,128)(2,1)}) custom-call(s32[3]{0:T(128)} %pad_add_fusion.scal, bf16[768,512]{1,0:T(8,128)(2,1)} %get-tuple-element.291.att_s, bf16[768,512]{1,0:T(8,128)(2,1)} %get-tuple-element.292.y5_s, bf16[768,2048]{1,0:T(8,128)(2,1)} %get-tuple-element.293.inner_s, ...), custom_call_target="tpu_custom_call" | custom-call | flops 11500000256 | bytes 14942220 | tf_op jit(solution)/shard_map/pallas_call | solution.py:69
  238.5 58.2 %shard_map.304 = (bf16[768,384]{1,0:T(8,128)(2,1)}, bf16[768,384]{1,0:T(8,128)(2,1)}, bf16[768,384]{1,0:T(8,128)(2,1)}, bf16[768,384]{1,0:T(8,128)(2,1)}) custom-call(s32[3]{0:T(128)} %pad_add_fusion.scal, bf16[768,384]{1,0:T(8,128)(2,1)} %get-tuple-element.262.refs_0_, bf16[768,384]{1,0:T(8,128)(2,1)} %copy-done.25, bf16[768,384]{1,0:T(8,128)(2,1)} %copy-done.26, ...), custom_call_target="tpu_custom_call" | custom-call | flops 66700001280 | bytes 7864332 | tf_op jit(solution)/shard_map/pallas_call | solution.py:69
  297.5 3.9 collective-permute-start.44
  301.3 1.9 collective-permute-start.41
  303.5 24.1 %collective-permute-done.44 = bf16[8,288,256]{2,1,0:T(8,128)(2,1)S(1)} collective-permute-done((bf16[8,288,256]{2,1,0:T(8,128)(2,1)S(1)}, bf16[8,288,256]{2,1,0:T(8,128)(2,1)S(1)}, u32[]{:S(2)}, u32[]{:S(2)}) %collective-permute-start.44) | collective-permute-done | bytes 1179680 | tf_op jit(solution)/shard_map/ppermute | solution.py:1076
  328.3 1.5 collective-permute-start.47
  329.7 6.5 %shard_map.305 = (f32[768,512]{1,0:T(8,128)}, bf16[768,256]{1,0:T(8,128)(2,1)}, bf16[768,1536]{1,0:T(8,128)(2,1)}, f32[1,512]{1,0:T(1,128)}) custom-call(s32[3]{0:T(128)} %pad_add_fusion.scal, bf16[768,384]{1,0:T(8,128)(2,1)} %get-tuple-element.314.refs_0_, bf16[768,384]{1,0:T(8,128)(2,1)} %copy-done.32, bf16[768,384]{1,0:T(8,128)(2,1)} %copy-done.34, ...), custom_call_target="tpu_custom_call" | custom-call | flops 6899999744 | bytes 11407372 | tf_op jit(solution)/shard_map/pallas_call | solution.py:69
  337.0 1.3 collective-permute-start.46
  338.2 4.5 collective-permute-start.45
  342.8 6.8 %shard_map.306 = (bf16[16,160,256]{2,1,0:T(8,128)(2,1)}, bf16[16,160,256]{2,1,0:T(8,128)(2,1)}) custom-call(s32[3]{0:T(128)} %pad_add_fusion.scal, bf16[768,512]{1,0:T(8,128)(2,1)} %get-tuple-element.322.y4_ref, bf16[768,1536]{1,0:T(8,128)(2,1)} %get-tuple-element.323.dqkv_s, bf16[768,2048]{1,0:T(8,128)(2,1)} %get-tuple-element.324.spread_ref, ...), custom_call_target="tpu_custom_call" | custom-call | flops 3449999872 | bytes 9306124 | tf_op jit(solution)/shard_map/pallas_call | solution.py:69
  349.9 1.2 collective-permute-start.50
  351.1 2.3 collective-permute-start.49
  353.4 1.8 collective-permute-start.52
  356.1 32.6 %shard_map.307 = (bf16[800,2048]{1,0:T(8,128)(2,1)}, bf16[768,768]{1,0:T(8,128)(2,1)}, f32[9,2048]{1,0:T(8,128)}, f32[1,2048]{1,0:T(1,128)}) custom-call(s32[3]{0:T(128)} %pad_add_fusion.scal, bf16[16,256]{1,0:T(8,128)(2,1)} %copy-done.47, bf16[768,256]{1,0:T(8,128)(2,1)} %get-tuple-element.321.db_ref, bf16[16,256]{1,0:T(8,128)(2,1)} %copy-done.46, ...), custom_call_target="tpu_custom_call" | custom-call | flops 50600001536 | bytes 16728076 | tf_op jit(solution)/shard_map/pallas_call | solution.py:69
  389.4 6.7 %shard_map.308 = (bf16[16,176,256]{2,1,0:T(8,128)(2,1)}, bf16[16,176,256]{2,1,0:T(8,128)(2,1)}) custom-call(s32[3]{0:T(128)} %pad_add_fusion.scal, bf16[800,2048]{1,0:T(8,128)(2,1)} %get-tuple-element.357.dl, bf16[768,768]{1,0:T(8,128)(2,1)} %get-tuple-element.342.st, bf16[800,512]{1,0:T(8,128)(2,1)} %get-tuple-element.231.y2_ref), custom_call_target="tpu_custom_call" | custom-call | flops 3449999872 | bytes 8159244 | tf_op jit(solution)/shard_map/pallas_call | solution.py:69
  396.3 2.8 collective-permute-start.53
  399.1 7.4 %shard_map.309 = (bf16[384,512]{1,0:T(8,128)(2,1)}, bf16[384,512]{1,0:T(8,128)(2,1)}, bf16[384,1024]{1,0:T(8,128)(2,1)}, f32[1,512]{1,0:T(1,128)}, f32[1,512]{1,0:T(1,128)}) custom-call(s32[3]{0:T(128)} %pad_add_fusion.scal, bf16[800,2048]{1,0:T(8,128)(2,1)} %get-tuple-element.357.dl, bf16[768,768]{1,0:T(8,128)(2,1)} %get-tuple-element.342.st, ...), custom_call_target="tpu_custom_call" | custom-call | flops 5750000128 | bytes 17276940 | tf_op jit(solution)/shard_map/pallas_call | solution.py:69
  410.1 7.3 %shard_map.310 = (bf16[384,512]{1,0:T(8,128)(2,1)}, bf16[384,512]{1,0:T(8,128)(2,1)}, bf16[384,1024]{1,0:T(8,128)(2,1)}, f32[1,512]{1,0:T(1,128)}, f32[1,512]{1,0:T(1,128)}) custom-call(s32[3]{0:T(128)} %pad_add_fusion.scal, bf16[800,2048]{1,0:T(8,128)(2,1)} %get-tuple-element.357.dl, bf16[768,768]{1,0:T(8,128)(2,1)} %get-tuple-element.342.st, ...), custom_call_target="tpu_custom_call" | custom-call | flops 5750000128 | bytes 17276940 | tf_op jit(solution)/shard_map/pallas_call | solution.py:69
  417.4 1.9 collective-permute-start.58
  419.3 4.7 shard_map.311
  425.3 5.9 %collective-permute-start.59 = (bf16[16,80,256]{2,1,0:T(8,128)(2,1)S(1)}, bf16[16,80,256]{2,1,0:T(8,128)(2,1)S(1)}, u32[]{:S(2)}, u32[]{:S(2)}) collective-permute-start(bf16[16,80,256]{2,1,0:T(8,128)(2,1)S(1)} %copy-done.22), channel_id=1, source_target_pairs={{0,1},{1,0},{2,3},{3,2},{4,5},{5,4},{6,7},{7,6},{8,9},{9,8},{10,11... | collective-permute-start | bytes 1966088 | tf_op jit(solution)/shard_map/ppermute | solution.py:1076
  433.2 1.3 collective-permute-start.61
  434.6 6.4 %collective-permute-start.62 = (bf16[4,80,256]{2,1,0:T(8,128)(2,1)S(1)}, bf16[4,80,256]{2,1,0:T(8,128)(2,1)S(1)}, u32[]{:S(2)}, u32[]{:S(2)}) collective-permute-start(bf16[4,80,256]{2,1,0:T(8,128)(2,1)S(1)} %get-tuple-element.401), channel_id=1, source_target_pairs={{0,6},{1,7},{2,4},{3,5},{4,2},{5,3},{6,0},{7,1},{8,14},{9,15},{10,... | collective-permute-start | bytes 491528 | tf_op jit(solution)/shard_map/ppermute | solution.py:1076
  441.1 2.4 collective-permute-done.61
  443.5 17.0 %collective-permute-done.60 = bf16[704,256]{1,0:T(8,128)(2,1)S(1)} collective-permute-done((bf16[704,256]{1,0:T(8,128)(2,1)S(1)}, bf16[704,256]{1,0:T(8,128)(2,1)S(1)}, u32[]{:S(2)}, u32[]{:S(2)}) %collective-permute-start.60) | collective-permute-done | bytes 360480 | tf_op jit(solution)/shard_map/ppermute | solution.py:1076
  462.2 2.2 collective-permute-start.65
  465.0 1.4 maximum_convert_fusion
  466.4 6.1 %collective-permute-done.64 = bf16[416,256]{1,0:T(8,128)(2,1)S(1)} collective-permute-done((bf16[416,256]{1,0:T(8,128)(2,1)S(1)}, bf16[416,256]{1,0:T(8,128)(2,1)S(1)}, u32[]{:S(2)}, u32[]{:S(2)}) %collective-permute-start.64) | collective-permute-done | bytes 213024 | tf_op jit(solution)/shard_map/ppermute | solution.py:1076
  472.9 10.1 %collective-permute-done.65 = bf16[416,256]{1,0:T(8,128)(2,1)S(1)} collective-permute-done((bf16[416,256]{1,0:T(8,128)(2,1)S(1)}, bf16[416,256]{1,0:T(8,128)(2,1)S(1)}, u32[]{:S(2)}, u32[]{:S(2)}) %collective-permute-start.65) | collective-permute-done | bytes 213024 | tf_op jit(solution)/shard_map/ppermute | solution.py:1076
  (294 shorter events, 41.0 us)
Async XLA Ops:
  6.4 9.7 %collective-permute-start.2 = (bf16[256,256]{1,0:T(8,128)(2,1)}, bf16[256,256]{1,0:T(8,128)(2,1)S(1)}, u32[]{:S(2)}, u32[]{:S(2)}) collective-permute-start(bf16[256,256]{1,0:T(8,128)(2,1)} %get-tuple-element.208), channel_id=1, source_target_pairs={{0,24},{1,25},{2,26},{3,27},{4,28},{5,29},{6,30},{7,31},{8,16},{9,... | collective-permute-start | bytes 393224 | tf_op jit(solution)/shard_map/ppermute | solution.py:1076
  11.4 12.5 %collective-permute-start.1 = (bf16[256,256]{1,0:T(8,128)(2,1)}, bf16[256,256]{1,0:T(8,128)(2,1)S(1)}, u32[]{:S(2)}, u32[]{:S(2)}) collective-permute-start(bf16[256,256]{1,0:T(8,128)(2,1)} %get-tuple-element.208), channel_id=1, source_target_pairs={{0,16},{1,17},{2,18},{3,19},{4,20},{5,21},{6,22},{7,23},{8,24},{9,... | collective-permute-start | bytes 393224 | tf_op jit(solution)/shard_map/ppermute | solution.py:1076
  11.4 12.5 %collective-permute-start = (bf16[256,256]{1,0:T(8,128)(2,1)}, bf16[256,256]{1,0:T(8,128)(2,1)S(1)}, u32[]{:S(2)}, u32[]{:S(2)}) collective-permute-start(bf16[256,256]{1,0:T(8,128)(2,1)} %get-tuple-element.208), channel_id=1, source_target_pairs={{0,8},{1,9},{2,10},{3,11},{4,12},{5,13},{6,14},{7,15},{8,0},{9,1},... | collective-permute-start | bytes 393224 | tf_op jit(solution)/shard_map/ppermute | solution.py:1076
  12.1 37.4 %collective-permute-start.5 = (bf16[784,512]{1,0:T(8,128)(2,1)S(1)}, bf16[784,512]{1,0:T(8,128)(2,1)S(1)}, u32[]{:S(2)}, u32[]{:S(2)}) collective-permute-start(bf16[784,512]{1,0:T(8,128)(2,1)S(1)} %pad_maximum_fusion.5), channel_id=1, source_target_pairs={{0,0},{8,4},{16,1},{24,5},{1,16},{9,20},{17,17},{25,21},{2,2},{10,... | collective-permute-start | bytes 2408456 | tf_op jit(solution)/shard_map/ppermute | solution.py:1224
  25.0 15.0 %collective-permute-start.4 = (bf16[4,128,256]{2,1,0:T(8,128)(2,1)S(1)}, bf16[4,128,256]{2,1,0:T(8,128)(2,1)S(1)}, u32[]{:S(2)}, u32[]{:S(2)}) collective-permute-start(bf16[4,128,256]{2,1,0:T(8,128)(2,1)S(1)} %get-tuple-element.409), channel_id=1, source_target_pairs={{0,2},{1,3},{2,0},{3,1},{4,6},{5,7},{6,4},{7,5},{8,10},{9,11},{10,... | collective-permute-start | bytes 786440 | tf_op jit(solution)/shard_map/ppermute | solution.py:1076
  26.3 23.0 %collective-permute-start.3 = (bf16[4,128,256]{2,1,0:T(8,128)(2,1)S(1)}, bf16[4,128,256]{2,1,0:T(8,128)(2,1)S(1)}, u32[]{:S(2)}, u32[]{:S(2)}) collective-permute-start(bf16[4,128,256]{2,1,0:T(8,128)(2,1)S(1)} %get-tuple-element.410), channel_id=1, source_target_pairs={{0,4},{1,5},{2,6},{3,7},{4,0},{5,1},{6,2},{7,3},{8,12},{9,13},{10,... | collective-permute-start | bytes 786440 | tf_op jit(solution)/shard_map/ppermute | solution.py:1076
  36.2 13.2 %collective-permute-start.7 = (bf16[16,512]{1,0:T(8,128)(2,1)S(1)}, bf16[16,512]{1,0:T(8,128)(2,1)S(1)}, u32[]{:S(2)}, u32[]{:S(2)}) collective-permute-start(bf16[16,512]{1,0:T(8,128)(2,1)S(1)} %get-tuple-element.399), channel_id=1, source_target_pairs={{8,0},{16,4},{24,1},{9,16},{17,20},{25,17},{10,2},{18,6},{26,3},{1... | collective-permute-start | bytes 49160 | tf_op jit(solution)/shard_map/ppermute | solution.py:1227
  37.5 12.1 %collective-permute-start.6 = (bf16[16,512]{1,0:T(8,128)(2,1)S(1)}, bf16[16,512]{1,0:T(8,128)(2,1)S(1)}, u32[]{:S(2)}, u32[]{:S(2)}) collective-permute-start(bf16[16,512]{1,0:T(8,128)(2,1)S(1)} %get-tuple-element.400), channel_id=1, source_target_pairs={{0,4},{8,1},{16,5},{1,20},{9,17},{17,21},{2,6},{10,3},{18,7},{3,22... | collective-permute-start | bytes 49160 | tf_op jit(solution)/shard_map/ppermute | solution.py:1227
  49.7 12.1 %collective-permute-start.12 = (bf16[160,256]{1,0:T(8,128)(2,1)S(1)}, bf16[160,256]{1,0:T(8,128)(2,1)S(1)}, u32[]{:S(2)}, u32[]{:S(2)}) collective-permute-start(bf16[160,256]{1,0:T(8,128)(2,1)S(1)} %copy-done.13), channel_id=1, source_target_pairs={{0,24},{1,25},{2,26},{3,27},{4,28},{5,29},{6,30},{7,31},{8,16},{9,... | collective-permute-start | bytes 245768 | tf_op jit(solution)/shard_map/ppermute | solution.py:1076
  52.3 9.4 %collective-permute-start.11 = (bf16[160,256]{1,0:T(8,128)(2,1)S(1)}, bf16[160,256]{1,0:T(8,128)(2,1)S(1)}, u32[]{:S(2)}, u32[]{:S(2)}) collective-permute-start(bf16[160,256]{1,0:T(8,128)(2,1)S(1)} %copy-done.13), channel_id=1, source_target_pairs={{0,16},{1,17},{2,18},{3,19},{4,20},{5,21},{6,22},{7,23},{8,24},{9,... | collective-permute-start | bytes 245768 | tf_op jit(solution)/shard_map/ppermute | solution.py:1076
  52.4 9.4 %collective-permute-start.10 = (bf16[160,256]{1,0:T(8,128)(2,1)S(1)}, bf16[160,256]{1,0:T(8,128)(2,1)S(1)}, u32[]{:S(2)}, u32[]{:S(2)}) collective-permute-start(bf16[160,256]{1,0:T(8,128)(2,1)S(1)} %copy-done.13), channel_id=1, source_target_pairs={{0,8},{1,9},{2,10},{3,11},{4,12},{5,13},{6,14},{7,15},{8,0},{9,1},... | collective-permute-start | bytes 245768 | tf_op jit(solution)/shard_map/ppermute | solution.py:1076
  54.1 11.9 %collective-permute-start.8 = (bf16[8,128,256]{2,1,0:T(8,128)(2,1)S(1)}, bf16[8,128,256]{2,1,0:T(8,128)(2,1)S(1)}, u32[]{:S(2)}, u32[]{:S(2)}) collective-permute-start(bf16[8,128,256]{2,1,0:T(8,128)(2,1)S(1)} %pad_maximum_fusion.13), channel_id=1, source_target_pairs={{0,2},{1,3},{2,0},{3,1},{4,6},{5,7},{6,4},{7,5},{8,10},{9,11},{10,... | collective-permute-start | bytes 1572872 | tf_op jit(solution)/shard_map/ppermute | solution.py:1076
  55.2 12.3 %collective-permute-start.9 = (bf16[8,128,256]{2,1,0:T(8,128)(2,1)S(1)}, bf16[8,128,256]{2,1,0:T(8,128)(2,1)S(1)}, u32[]{:S(2)}, u32[]{:S(2)}) collective-permute-start(bf16[8,128,256]{2,1,0:T(8,128)(2,1)S(1)} %pad_maximum_fusion.14), channel_id=1, source_target_pairs={{0,4},{1,5},{2,6},{3,7},{4,0},{5,1},{6,2},{7,3},{8,12},{9,13},{10,... | collective-permute-start | bytes 1572872 | tf_op jit(solution)/shard_map/ppermute | solution.py:1076
  67.7 7.6 %collective-permute-start.13 = (bf16[16,128,256]{2,1,0:T(8,128)(2,1)S(1)}, bf16[16,128,256]{2,1,0:T(8,128)(2,1)S(1)}, u32[]{:S(2)}, u32[]{:S(2)}) collective-permute-start(bf16[16,128,256]{2,1,0:T(8,128)(2,1)S(1)} %pad_maximum_fusion.2.p0), channel_id=1, source_target_pairs={{0,1},{1,0},{2,3},{3,2},{4,5},{5,4},{6,7},{7,6},{8,9},{9,8},{10,11... | collective-permute-start | bytes 3145736 | tf_op jit(solution)/shard_map/ppermute | solution.py:1076
  67.8 7.5 %collective-permute-start.14 = (bf16[16,128,256]{2,1,0:T(8,128)(2,1)S(1)}, bf16[16,128,256]{2,1,0:T(8,128)(2,1)}, u32[]{:S(2)}, u32[]{:S(2)}) collective-permute-start(bf16[16,128,256]{2,1,0:T(8,128)(2,1)S(1)} %pad_maximum_fusion.3.p2), channel_id=1, source_target_pairs={{0,1},{1,0},{2,3},{3,2},{4,5},{5,4},{6,7},{7,6},{8,9},{9,8},{10,11... | collective-permute-start | bytes 3145736 | tf_op jit(solution)/shard_map/ppermute | solution.py:1076
  75.3 10.7 %collective-permute-start.17 = (bf16[8,80,256]{2,1,0:T(8,128)(2,1)S(1)}, bf16[8,80,256]{2,1,0:T(8,128)(2,1)S(1)}, u32[]{:S(2)}, u32[]{:S(2)}) collective-permute-start(bf16[8,80,256]{2,1,0:T(8,128)(2,1)S(1)} %pad_maximum_fusion.18), channel_id=1, source_target_pairs={{0,2},{1,3},{2,0},{3,1},{4,6},{5,7},{6,4},{7,5},{8,10},{9,11},{10,... | collective-permute-start | bytes 983048 | tf_op jit(solution)/shard_map/ppermute | solution.py:1076
  76.4 9.7 %collective-permute-start.18 = (bf16[8,80,256]{2,1,0:T(8,128)(2,1)S(1)}, bf16[8,80,256]{2,1,0:T(8,128)(2,1)S(1)}, u32[]{:S(2)}, u32[]{:S(2)}) collective-permute-start(bf16[8,80,256]{2,1,0:T(8,128)(2,1)S(1)} %pad_maximum_fusion.19), channel_id=1, source_target_pairs={{0,4},{1,5},{2,6},{3,7},{4,0},{5,1},{6,2},{7,3},{8,12},{9,13},{10,... | collective-permute-start | bytes 983048 | tf_op jit(solution)/shard_map/ppermute | solution.py:1076
  86.9 14.9 %collective-permute-start.23 = (bf16[288,256]{1,0:T(8,128)(2,1)S(1)}, bf16[288,256]{1,0:T(8,128)(2,1)S(1)}, u32[]{:S(2)}, u32[]{:S(2)}) collective-permute-start(bf16[288,256]{1,0:T(8,128)(2,1)S(1)} %copy-done.12), channel_id=1, source_target_pairs={{0,24},{1,25},{2,26},{3,27},{4,28},{5,29},{6,30},{7,31},{8,16},{9,... | collective-permute-start | bytes 442376 | tf_op jit(solution)/shard_map/ppermute | solution.py:1076
  88.8 13.0 %collective-permute-start.22 = (bf16[288,256]{1,0:T(8,128)(2,1)S(1)}, bf16[288,256]{1,0:T(8,128)(2,1)S(1)}, u32[]{:S(2)}, u32[]{:S(2)}) collective-permute-start(bf16[288,256]{1,0:T(8,128)(2,1)S(1)} %copy-done.12), channel_id=1, source_target_pairs={{0,16},{1,17},{2,18},{3,19},{4,20},{5,21},{6,22},{7,23},{8,24},{9,... | collective-permute-start | bytes 442376 | tf_op jit(solution)/shard_map/ppermute | solution.py:1076
  88.8 13.0 %collective-permute-start.21 = (bf16[288,256]{1,0:T(8,128)(2,1)S(1)}, bf16[288,256]{1,0:T(8,128)(2,1)S(1)}, u32[]{:S(2)}, u32[]{:S(2)}) collective-permute-start(bf16[288,256]{1,0:T(8,128)(2,1)S(1)} %copy-done.12), channel_id=1, source_target_pairs={{0,8},{1,9},{2,10},{3,11},{4,12},{5,13},{6,14},{7,15},{8,0},{9,1},... | collective-permute-start | bytes 442376 | tf_op jit(solution)/shard_map/ppermute | solution.py:1076
  91.3 10.6 %collective-permute-start.19 = (bf16[16,80,256]{2,1,0:T(8,128)(2,1)S(1)}, bf16[16,80,256]{2,1,0:T(8,128)(2,1)S(1)}, u32[]{:S(2)}, u32[]{:S(2)}) collective-permute-start(bf16[16,80,256]{2,1,0:T(8,128)(2,1)S(1)} %pad_maximum_fusion.6.p0), channel_id=1, source_target_pairs={{0,1},{1,0},{2,3},{3,2},{4,5},{5,4},{6,7},{7,6},{8,9},{9,8},{10,11... | collective-permute-start | bytes 1966088 | tf_op jit(solution)/shard_map/ppermute | solution.py:1076
  91.3 10.6 %collective-permute-start.20 = (bf16[16,80,256]{2,1,0:T(8,128)(2,1)S(1)}, bf16[16,80,256]{2,1,0:T(8,128)(2,1)S(1)}, u32[]{:S(2)}, u32[]{:S(2)}) collective-permute-start(bf16[16,80,256]{2,1,0:T(8,128)(2,1)S(1)} %pad_maximum_fusion.7.p2), channel_id=1, source_target_pairs={{0,1},{1,0},{2,3},{3,2},{4,5},{5,4},{6,7},{7,6},{8,9},{9,8},{10,11... | collective-permute-start | bytes 1966088 | tf_op jit(solution)/shard_map/ppermute | solution.py:1076
  102.0 18.0 %collective-permute-start.25 = (bf16[4,144,256]{2,1,0:T(8,128)(2,1)S(1)}, bf16[4,144,256]{2,1,0:T(8,128)(2,1)S(1)}, u32[]{:S(2)}, u32[]{:S(2)}) collective-permute-start(bf16[4,144,256]{2,1,0:T(8,128)(2,1)S(1)} %get-tuple-element.407), channel_id=1, source_target_pairs={{0,2},{1,3},{2,0},{3,1},{4,6},{5,7},{6,4},{7,5},{8,10},{9,11},{10,... | collective-permute-start | bytes 884744 | tf_op jit(solution)/shard_map/ppermute | solution.py:1076
  103.1 17.0 %collective-permute-start.24 = (bf16[4,144,256]{2,1,0:T(8,128)(2,1)S(1)}, bf16[4,144,256]{2,1,0:T(8,128)(2,1)S(1)}, u32[]{:S(2)}, u32[]{:S(2)}) collective-permute-start(bf16[4,144,256]{2,1,0:T(8,128)(2,1)S(1)} %get-tuple-element.408), channel_id=1, source_target_pairs={{0,4},{1,5},{2,6},{3,7},{4,0},{5,1},{6,2},{7,3},{8,12},{9,13},{10,... | collective-permute-start | bytes 884744 | tf_op jit(solution)/shard_map/ppermute | solution.py:1076
  120.2 16.5 %collective-permute-start.26 = (bf16[768,384]{1,0:T(8,128)(2,1)}, bf16[768,384]{1,0:T(8,128)(2,1)S(1)}, u32[]{:S(2)}, u32[]{:S(2)}) collective-permute-start(bf16[768,384]{1,0:T(8,128)(2,1)} %get-tuple-element.255), channel_id=1, source_target_pairs={{0,4},{4,0},{1,5},{5,1},{16,20},{20,16},{17,21},{21,17},{2,6},{6,2... | collective-permute-start | bytes 1769480 | tf_op jit(solution)/shard_map/ppermute | solution.py:1239
  121.1 15.7 %collective-permute-start.27 = (bf16[768,384]{1,0:T(8,128)(2,1)S(1)}, bf16[768,384]{1,0:T(8,128)(2,1)S(1)}, u32[]{:S(2)}, u32[]{:S(2)}) collective-permute-start(bf16[768,384]{1,0:T(8,128)(2,1)S(1)} %copy-done.33), channel_id=1, source_target_pairs={{0,1},{4,5},{1,0},{5,4},{16,17},{20,21},{17,16},{21,20},{2,3},{6,7... | collective-permute-start | bytes 1769480 | tf_op jit(solution)/shard_map/ppermute | solution.py:1239
  121.2 24.7 %collective-permute-start.28 = (bf16[768,384]{1,0:T(8,128)(2,1)S(1)}, bf16[768,384]{1,0:T(8,128)(2,1)S(1)}, u32[]{:S(2)}, u32[]{:S(2)}) collective-permute-start(bf16[768,384]{1,0:T(8,128)(2,1)S(1)} %copy-done.31), channel_id=1, source_target_pairs={{0,5},{4,1},{1,4},{5,0},{16,21},{20,17},{17,20},{21,16},{2,7},{6,3... | collective-permute-start | bytes 1769480 | tf_op jit(solution)/shard_map/ppermute | solution.py:1239
  145.9 39.8 %collective-permute-start.29 = (bf16[8,144,256]{2,1,0:T(8,128)(2,1)S(1)}, bf16[8,144,256]{2,1,0:T(8,128)(2,1)S(1)}, u32[]{:S(2)}, u32[]{:S(2)}) collective-permute-start(bf16[8,144,256]{2,1,0:T(8,128)(2,1)S(1)} %pad_maximum_fusion.9), channel_id=1, source_target_pairs={{0,2},{1,3},{2,0},{3,1},{4,6},{5,7},{6,4},{7,5},{8,10},{9,11},{10,... | collective-permute-start | bytes 1769480 | tf_op jit(solution)/shard_map/ppermute | solution.py:1076
  148.5 37.4 %collective-permute-start.30 = (bf16[8,144,256]{2,1,0:T(8,128)(2,1)S(1)}, bf16[8,144,256]{2,1,0:T(8,128)(2,1)S(1)}, u32[]{:S(2)}, u32[]{:S(2)}) collective-permute-start(bf16[8,144,256]{2,1,0:T(8,128)(2,1)S(1)} %pad_maximum_fusion.10), channel_id=1, source_target_pairs={{0,4},{1,5},{2,6},{3,7},{4,0},{5,1},{6,2},{7,3},{8,12},{9,13},{10,... | collective-permute-start | bytes 1769480 | tf_op jit(solution)/shard_map/ppermute | solution.py:1076
  150.3 35.8 %collective-permute-start.31 = (bf16[768,512]{1,0:T(8,128)(2,1)S(1)}, bf16[768,512]{1,0:T(8,128)(2,1)S(1)}, u32[]{:S(2)}, u32[]{:S(2)}) collective-permute-start(bf16[768,512]{1,0:T(8,128)(2,1)S(1)} %bitcast.131), channel_id=1, source_target_pairs={{0,0},{8,4},{16,1},{24,5},{1,16},{9,20},{17,17},{25,21},{2,2},{10,... | collective-permute-start | bytes 2359304 | tf_op jit(solution)/shard_map/ppermute | solution.py:1224
  186.0 13.3 %collective-permute-start.35 = (bf16[16,144,256]{2,1,0:T(8,128)(2,1)S(1)}, bf16[16,144,256]{2,1,0:T(8,128)(2,1)S(1)}, u32[]{:S(2)}, u32[]{:S(2)}) collective-permute-start(bf16[16,144,256]{2,1,0:T(8,128)(2,1)S(1)} %pad_maximum_fusion.refs_6_), channel_id=1, source_target_pairs={{0,1},{1,0},{2,3},{3,2},{4,5},{5,4},{6,7},{7,6},{8,9},{9,8},{10,11... | collective-permute-start | bytes 3538952 | tf_op jit(solution)/shard_map/ppermute | solution.py:1076
  186.9 12.5 %collective-permute-start.36 = (bf16[16,144,256]{2,1,0:T(8,128)(2,1)S(1)}, bf16[16,144,256]{2,1,0:T(8,128)(2,1)S(1)}, u32[]{:S(2)}, u32[]{:S(2)}) collective-permute-start(bf16[16,144,256]{2,1,0:T(8,128)(2,1)S(1)} %pad_maximum_fusion.1.refs_8_), channel_id=1, source_target_pairs={{0,1},{1,0},{2,3},{3,2},{4,5},{5,4},{6,7},{7,6},{8,9},{9,8},{10,11... | collective-permute-start | bytes 3538952 | tf_op jit(solution)/shard_map/ppermute | solution.py:1076
  187.0 8.0 %collective-permute-start.32 = (bf16[768,128]{1,0:T(8,128)(2,1)S(1)}, bf16[768,128]{1,0:T(8,128)(2,1)S(1)}, u32[]{:S(2)}, u32[]{:S(2)}) collective-permute-start(bf16[768,128]{1,0:T(8,128)(2,1)S(1)} %copy-done.37), channel_id=1, source_target_pairs={{0,4},{4,0},{1,5},{5,1},{16,20},{20,16},{17,21},{21,17},{2,6},{6,2... | collective-permute-start | bytes 589832 | tf_op jit(solution)/shard_map/ppermute | solution.py:1239
  189.9 9.4 %collective-permute-start.34 = (bf16[768,128]{1,0:T(8,128)(2,1)S(1)}, bf16[768,128]{1,0:T(8,128)(2,1)S(1)}, u32[]{:S(2)}, u32[]{:S(2)}) collective-permute-start(bf16[768,128]{1,0:T(8,128)(2,1)S(1)} %copy-done.39), channel_id=1, source_target_pairs={{0,5},{4,1},{1,4},{5,0},{16,21},{20,17},{17,20},{21,16},{2,7},{6,3... | collective-permute-start | bytes 589832 | tf_op jit(solution)/shard_map/ppermute | solution.py:1239
  225.1 12.5 %collective-permute-start.37 = (bf16[768,128]{1,0:T(8,128)(2,1)}, bf16[768,128]{1,0:T(8,128)(2,1)S(1)}, u32[]{:S(2)}, u32[]{:S(2)}) collective-permute-start(bf16[768,128]{1,0:T(8,128)(2,1)} %get-tuple-element.288), channel_id=1, source_target_pairs={{0,4},{4,0},{1,5},{5,1},{16,20},{20,16},{17,21},{21,17},{2,6},{6,2... | collective-permute-start | bytes 589832 | tf_op jit(solution)/shard_map/ppermute | solution.py:1239
  226.9 10.8 %collective-permute-start.38 = (bf16[768,128]{1,0:T(8,128)(2,1)}, bf16[768,128]{1,0:T(8,128)(2,1)S(1)}, u32[]{:S(2)}, u32[]{:S(2)}) collective-permute-start(bf16[768,128]{1,0:T(8,128)(2,1)} %get-tuple-element.289), channel_id=1, source_target_pairs={{0,1},{4,5},{1,0},{5,4},{16,17},{20,21},{17,16},{21,20},{2,3},{6,7... | collective-permute-start | bytes 589832 | tf_op jit(solution)/shard_map/ppermute | solution.py:1239
  226.9 10.8 %collective-permute-start.39 = (bf16[768,128]{1,0:T(8,128)(2,1)}, bf16[768,128]{1,0:T(8,128)(2,1)S(1)}, u32[]{:S(2)}, u32[]{:S(2)}) collective-permute-start(bf16[768,128]{1,0:T(8,128)(2,1)} %get-tuple-element.290), channel_id=1, source_target_pairs={{0,5},{4,1},{1,4},{5,0},{16,21},{20,17},{17,20},{21,16},{2,7},{6,3... | collective-permute-start | bytes 589832 | tf_op jit(solution)/shard_map/ppermute | solution.py:1239
  237.7 59.0 %collective-permute-start.40 = (bf16[16,288,256]{2,1,0:T(8,128)(2,1)}, bf16[16,288,256]{2,1,0:T(8,128)(2,1)S(1)}, u32[]{:S(2)}, u32[]{:S(2)}) collective-permute-start(bf16[16,288,256]{2,1,0:T(8,128)(2,1)} %get-tuple-element.308), channel_id=1, source_target_pairs={{0,1},{1,0},{2,3},{3,2},{4,5},{5,4},{6,7},{7,6},{8,9},{9,8},{10,11... | collective-permute-start | bytes 7077896 | tf_op jit(solution)/shard_map/ppermute | solution.py:1076
  297.5 30.1 %collective-permute-start.44 = (bf16[8,288,256]{2,1,0:T(8,128)(2,1)S(1)}, bf16[8,288,256]{2,1,0:T(8,128)(2,1)S(1)}, u32[]{:S(2)}, u32[]{:S(2)}) collective-permute-start(bf16[8,288,256]{2,1,0:T(8,128)(2,1)S(1)} %slice.314), channel_id=1, source_target_pairs={{0,2},{1,3},{2,0},{3,1},{4,6},{5,7},{6,4},{7,5},{8,10},{9,11},{10,... | collective-permute-start | bytes 3538952 | tf_op jit(solution)/shard_map/ppermute | solution.py:1076
  301.3 26.6 %collective-permute-start.41 = (bf16[768,384]{1,0:T(8,128)(2,1)S(1)}, bf16[768,384]{1,0:T(8,128)(2,1)S(1)}, u32[]{:S(2)}, u32[]{:S(2)}) collective-permute-start(bf16[768,384]{1,0:T(8,128)(2,1)S(1)} %copy-done.30), channel_id=1, source_target_pairs={{0,4},{4,0},{1,5},{5,1},{16,20},{20,16},{17,21},{21,17},{2,6},{6,2... | collective-permute-start | bytes 1769480 | tf_op jit(solution)/shard_map/ppermute | solution.py:1239
  303.2 24.7 %collective-permute-start.42 = (bf16[768,384]{1,0:T(8,128)(2,1)S(1)}, bf16[768,384]{1,0:T(8,128)(2,1)S(1)}, u32[]{:S(2)}, u32[]{:S(2)}) collective-permute-start(bf16[768,384]{1,0:T(8,128)(2,1)S(1)} %copy-done.29), channel_id=1, source_target_pairs={{0,1},{4,5},{1,0},{5,4},{16,17},{20,21},{17,16},{21,20},{2,3},{6,7... | collective-permute-start | bytes 1769480 | tf_op jit(solution)/shard_map/ppermute | solution.py:1239
  303.2 25.0 %collective-permute-start.43 = (bf16[768,384]{1,0:T(8,128)(2,1)S(1)}, bf16[768,384]{1,0:T(8,128)(2,1)S(1)}, u32[]{:S(2)}, u32[]{:S(2)}) collective-permute-start(bf16[768,384]{1,0:T(8,128)(2,1)S(1)} %copy-done.28), channel_id=1, source_target_pairs={{0,5},{4,1},{1,4},{5,0},{16,21},{20,17},{17,20},{21,16},{2,7},{6,3... | collective-permute-start | bytes 1769480 | tf_op jit(solution)/shard_map/ppermute | solution.py:1239
  328.3 21.3 %collective-permute-start.47 = (bf16[4,288,256]{2,1,0:T(8,128)(2,1)S(1)}, bf16[4,288,256]{2,1,0:T(8,128)(2,1)S(1)}, u32[]{:S(2)}, u32[]{:S(2)}) collective-permute-start(bf16[4,288,256]{2,1,0:T(8,128)(2,1)S(1)} %slice.318), channel_id=1, source_target_pairs={{0,4},{1,5},{2,6},{3,7},{4,0},{5,1},{6,2},{7,3},{8,12},{9,13},{10,... | collective-permute-start | bytes 1769480 | tf_op jit(solution)/shard_map/ppermute | solution.py:1076
  337.0 12.8 %collective-permute-start.46 = (bf16[16,256]{1,0:T(8,128)(2,1)S(1)}, bf16[16,256]{1,0:T(8,128)(2,1)S(1)}, u32[]{:S(2)}, u32[]{:S(2)}) collective-permute-start(bf16[16,256]{1,0:T(8,128)(2,1)S(1)} %get-tuple-element.428), channel_id=1, source_target_pairs={{4,0},{1,4},{5,1},{20,16},{17,20},{21,17},{6,2},{3,6},{7,3},{22,18... | collective-permute-start | bytes 24584 | tf_op jit(solution)/shard_map/ppermute | solution.py:1235
  338.2 11.5 %collective-permute-start.45 = (bf16[16,256]{1,0:T(8,128)(2,1)S(1)}, bf16[16,256]{1,0:T(8,128)(2,1)S(1)}, u32[]{:S(2)}, u32[]{:S(2)}) collective-permute-start(bf16[16,256]{1,0:T(8,128)(2,1)S(1)} %get-tuple-element.429), channel_id=1, source_target_pairs={{0,4},{4,1},{1,5},{16,20},{20,17},{17,21},{2,6},{6,3},{3,7},{18,22... | collective-permute-start | bytes 24584 | tf_op jit(solution)/shard_map/ppermute | solution.py:1235
  349.8 38.9 %collective-permute-start.48 = (bf16[288,256]{1,0:T(8,128)(2,1)S(1)}, bf16[288,256]{1,0:T(8,128)(2,1)S(1)}, u32[]{:S(2)}, u32[]{:S(2)}) collective-permute-start(bf16[288,256]{1,0:T(8,128)(2,1)S(1)} %get-tuple-element.404), channel_id=1, source_target_pairs={{0,8},{1,9},{2,10},{3,11},{4,12},{5,13},{6,14},{7,15},{8,0},{9,1},... | collective-permute-start | bytes 442376 | tf_op jit(solution)/shard_map/ppermute | solution.py:1076
  349.9 38.9 %collective-permute-start.50 = (bf16[288,256]{1,0:T(8,128)(2,1)S(1)}, bf16[288,256]{1,0:T(8,128)(2,1)S(1)}, u32[]{:S(2)}, u32[]{:S(2)}) collective-permute-start(bf16[288,256]{1,0:T(8,128)(2,1)S(1)} %get-tuple-element.405), channel_id=1, source_target_pairs={{0,24},{1,25},{2,26},{3,27},{4,28},{5,29},{6,30},{7,31},{8,16},{9,... | collective-permute-start | bytes 442376 | tf_op jit(solution)/shard_map/ppermute | solution.py:1076
  351.1 37.7 %collective-permute-start.49 = (bf16[288,256]{1,0:T(8,128)(2,1)S(1)}, bf16[288,256]{1,0:T(8,128)(2,1)S(1)}, u32[]{:S(2)}, u32[]{:S(2)}) collective-permute-start(bf16[288,256]{1,0:T(8,128)(2,1)S(1)} %get-tuple-element.406), channel_id=1, source_target_pairs={{0,16},{1,17},{2,18},{3,19},{4,20},{5,21},{6,22},{7,23},{8,24},{9,... | collective-permute-start | bytes 442376 | tf_op jit(solution)/shard_map/ppermute | solution.py:1076
  353.4 36.0 %collective-permute-start.52 = (bf16[768,512]{1,0:T(8,128)(2,1)}, bf16[768,512]{1,0:T(8,128)(2,1)S(1)}, u32[]{:S(2)}, u32[]{:S(2)}) collective-permute-start(bf16[768,512]{1,0:T(8,128)(2,1)} %get-tuple-element.339), channel_id=1, source_target_pairs={{0,0},{4,8},{1,16},{5,24},{16,1},{20,9},{17,17},{21,25},{2,2},{6,1... | collective-permute-start | bytes 2359304 | tf_op jit(solution)/shard_map/ppermute | solution.py:1232
  355.1 33.7 %collective-permute-start.51 = (bf16[16,160,256]{2,1,0:T(8,128)(2,1)}, bf16[16,160,256]{2,1,0:T(8,128)(2,1)S(1)}, u32[]{:S(2)}, u32[]{:S(2)}) collective-permute-start(bf16[16,160,256]{2,1,0:T(8,128)(2,1)} %get-tuple-element.338), channel_id=1, source_target_pairs={{0,1},{1,0},{2,3},{3,2},{4,5},{5,4},{6,7},{7,6},{8,9},{9,8},{10,11... | collective-permute-start | bytes 3932168 | tf_op jit(solution)/shard_map/ppermute | solution.py:1076
  396.1 11.2 %collective-permute-start.55 = (bf16[16,176,256]{2,1,0:T(8,128)(2,1)}, bf16[16,176,256]{2,1,0:T(8,128)(2,1)S(1)}, u32[]{:S(2)}, u32[]{:S(2)}) collective-permute-start(bf16[16,176,256]{2,1,0:T(8,128)(2,1)} %get-tuple-element.356), channel_id=1, source_target_pairs={{0,1},{1,0},{2,3},{3,2},{4,5},{5,4},{6,7},{7,6},{8,9},{9,8},{10,11... | collective-permute-start | bytes 4325384 | tf_op jit(solution)/shard_map/ppermute | solution.py:1076
  396.2 10.9 %collective-permute-start.54 = (bf16[8,80,256]{2,1,0:T(8,128)(2,1)S(1)}, bf16[8,80,256]{2,1,0:T(8,128)(2,1)S(1)}, u32[]{:S(2)}, u32[]{:S(2)}) collective-permute-start(bf16[8,80,256]{2,1,0:T(8,128)(2,1)S(1)} %slice.328), channel_id=1, source_target_pairs={{0,4},{1,5},{2,6},{3,7},{4,0},{5,1},{6,2},{7,3},{8,12},{9,13},{10,... | collective-permute-start | bytes 983048 | tf_op jit(solution)/shard_map/ppermute | solution.py:1076
  396.3 10.9 %collective-permute-start.53 = (bf16[8,80,256]{2,1,0:T(8,128)(2,1)S(1)}, bf16[8,80,256]{2,1,0:T(8,128)(2,1)S(1)}, u32[]{:S(2)}, u32[]{:S(2)}) collective-permute-start(bf16[8,80,256]{2,1,0:T(8,128)(2,1)S(1)} %slice.326), channel_id=1, source_target_pairs={{0,2},{1,3},{2,0},{3,1},{4,6},{5,7},{6,4},{7,5},{8,10},{9,11},{10,... | collective-permute-start | bytes 983048 | tf_op jit(solution)/shard_map/ppermute | solution.py:1076
  408.5 15.5 %collective-permute-start.57 = (bf16[960,256]{1,0:T(8,128)(2,1)S(1)}, bf16[960,256]{1,0:T(8,128)(2,1)S(1)}, u32[]{:S(2)}, u32[]{:S(2)}) collective-permute-start(bf16[960,256]{1,0:T(8,128)(2,1)S(1)} %pad_maximum_fusion.15), channel_id=1, source_target_pairs={{0,4},{1,5},{2,6},{3,7},{4,0},{5,1},{6,2},{7,3},{8,12},{9,13},{10,... | collective-permute-start | bytes 1474568 | tf_op jit(solution)/shard_map/ppermute | solution.py:1076
  409.3 14.9 %collective-permute-start.56 = (bf16[1088,256]{1,0:T(8,128)(2,1)S(1)}, bf16[1088,256]{1,0:T(8,128)(2,1)S(1)}, u32[]{:S(2)}, u32[]{:S(2)}) collective-permute-start(bf16[1088,256]{1,0:T(8,128)(2,1)S(1)} %pad_maximum_fusion.11), channel_id=1, source_target_pairs={{0,2},{1,3},{2,0},{3,1},{4,6},{5,7},{6,4},{7,5},{8,10},{9,11},{10,... | collective-permute-start | bytes 1671176 | tf_op jit(solution)/shard_map/ppermute | solution.py:1076
  417.4 7.8 %collective-permute-start.58 = (bf16[384,512]{1,0:T(8,128)(2,1)}, bf16[384,512]{1,0:T(8,128)(2,1)S(1)}, u32[]{:S(2)}, u32[]{:S(2)}) collective-permute-start(bf16[384,512]{1,0:T(8,128)(2,1)} %get-tuple-element.377), channel_id=1, source_target_pairs={{0,0},{4,8},{1,16},{5,24},{16,1},{20,9},{17,17},{21,25},{2,2},{6,1... | collective-permute-start | bytes 1179656 | tf_op jit(solution)/shard_map/ppermute | solution.py:1232
  425.3 7.6 %collective-permute-start.59 = (bf16[16,80,256]{2,1,0:T(8,128)(2,1)S(1)}, bf16[16,80,256]{2,1,0:T(8,128)(2,1)S(1)}, u32[]{:S(2)}, u32[]{:S(2)}) collective-permute-start(bf16[16,80,256]{2,1,0:T(8,128)(2,1)S(1)} %copy-done.22), channel_id=1, source_target_pairs={{0,1},{1,0},{2,3},{3,2},{4,5},{5,4},{6,7},{7,6},{8,9},{9,8},{10,11... | collective-permute-start | bytes 1966088 | tf_op jit(solution)/shard_map/ppermute | solution.py:1076
  431.2 29.5 %collective-permute-start.63 = (bf16[384,512]{1,0:T(8,128)(2,1)S(1)}, bf16[384,512]{1,0:T(8,128)(2,1)S(1)}, u32[]{:S(2)}, u32[]{:S(2)}) collective-permute-start(bf16[384,512]{1,0:T(8,128)(2,1)S(1)} %copy-done.36), channel_id=1, source_target_pairs={{0,0},{4,8},{1,16},{5,24},{16,1},{20,9},{17,17},{21,25},{2,2},{6,1... | collective-permute-start | bytes 1179656 | tf_op jit(solution)/shard_map/ppermute | solution.py:1232
  433.2 10.3 %collective-permute-start.61 = (bf16[640,256]{1,0:T(8,128)(2,1)S(1)}, bf16[640,256]{1,0:T(8,128)(2,1)S(1)}, u32[]{:S(2)}, u32[]{:S(2)}) collective-permute-start(bf16[640,256]{1,0:T(8,128)(2,1)S(1)} %pad_maximum_fusion.20), channel_id=1, source_target_pairs={{0,2},{1,3},{2,0},{3,1},{4,6},{5,7},{6,4},{7,5},{8,10},{9,11},{10,... | collective-permute-start | bytes 983048 | tf_op jit(solution)/shard_map/ppermute | solution.py:1076
  434.6 26.1 %collective-permute-start.62 = (bf16[4,80,256]{2,1,0:T(8,128)(2,1)S(1)}, bf16[4,80,256]{2,1,0:T(8,128)(2,1)S(1)}, u32[]{:S(2)}, u32[]{:S(2)}) collective-permute-start(bf16[4,80,256]{2,1,0:T(8,128)(2,1)S(1)} %get-tuple-element.401), channel_id=1, source_target_pairs={{0,6},{1,7},{2,4},{3,5},{4,2},{5,3},{6,0},{7,1},{8,14},{9,15},{10,... | collective-permute-start | bytes 491528 | tf_op jit(solution)/shard_map/ppermute | solution.py:1076
  441.0 19.6 %collective-permute-start.60 = (bf16[704,256]{1,0:T(8,128)(2,1)S(1)}, bf16[704,256]{1,0:T(8,128)(2,1)S(1)}, u32[]{:S(2)}, u32[]{:S(2)}) collective-permute-start(bf16[704,256]{1,0:T(8,128)(2,1)S(1)} %pad_maximum_fusion.16), channel_id=1, source_target_pairs={{0,4},{1,5},{2,6},{3,7},{4,0},{5,1},{6,2},{7,3},{8,12},{9,13},{10,... | collective-permute-start | bytes 1081352 | tf_op jit(solution)/shard_map/ppermute | solution.py:1076
  460.9 11.6 %collective-permute-start.64 = (bf16[416,256]{1,0:T(8,128)(2,1)S(1)}, bf16[416,256]{1,0:T(8,128)(2,1)S(1)}, u32[]{:S(2)}, u32[]{:S(2)}) collective-permute-start(bf16[416,256]{1,0:T(8,128)(2,1)S(1)} %get-tuple-element.396), channel_id=1, source_target_pairs={{0,8},{1,9},{2,10},{3,11},{4,12},{5,13},{6,14},{7,15},{8,0},{9,1},... | collective-permute-start | bytes 638984 | tf_op jit(solution)/shard_map/ppermute | solution.py:1076
  461.7 11.2 %collective-permute-start.66 = (bf16[416,256]{1,0:T(8,128)(2,1)S(1)}, bf16[416,256]{1,0:T(8,128)(2,1)S(1)}, u32[]{:S(2)}, u32[]{:S(2)}) collective-permute-start(bf16[416,256]{1,0:T(8,128)(2,1)S(1)} %get-tuple-element.397), channel_id=1, source_target_pairs={{0,24},{1,25},{2,26},{3,27},{4,28},{5,29},{6,30},{7,31},{8,16},{9,... | collective-permute-start | bytes 638984 | tf_op jit(solution)/shard_map/ppermute | solution.py:1076
  462.2 20.8 %collective-permute-start.65 = (bf16[416,256]{1,0:T(8,128)(2,1)S(1)}, bf16[416,256]{1,0:T(8,128)(2,1)S(1)}, u32[]{:S(2)}, u32[]{:S(2)}) collective-permute-start(bf16[416,256]{1,0:T(8,128)(2,1)S(1)} %get-tuple-element.398), channel_id=1, source_target_pairs={{0,16},{1,17},{2,18},{3,19},{4,20},{5,21},{6,22},{7,23},{8,24},{9,... | collective-permute-start | bytes 638984 | tf_op jit(solution)/shard_map/ppermute | solution.py:1076
  (53 other events, 404.1 us)
